TPU v7x, 32 devices: a whole 2x2x4 slice. The times are simulated.
32 devices in a mesh: plane: 2 (over x), coil: 16 (over z, y, core).
Axes of the slice: x: 2, y: 2, z: 4, core: 2. Of those that a mesh axis runs over, the one named last changes fastest.
Arguments:
- image: float32 [512, 8, 512], P(('plane', 'coil')), parts along dimension 0, may hold values from -6 to 6
- sens: float32 [512, 32, 512], P(('plane', 'coil')), parts along dimension 0, may hold values from -0.75 to 0.75
- kspace: float32 [512, 256, 512], P('plane', 'coil'), parts along dimension 0, may hold values from -6 to 6
- mask: int32 [8, 256], replicated, may hold values 0 or 1
Outputs:
- recon: float32 [512, 8, 512], P(('plane', 'coil')), parts along dimension 0
There are 2 independent parts, one for each index of `plane`. A program takes and returns all parts, laid end to end along the dimension named above; an argument that names none is the same for every part. Nothing has to cross between parts.
Inputs may be any that keep to these rules, and one draw needn't show every extreme that they name: mask[f, ky] is 1 where phase-encode line ky is sampled in frame f, else 0.
All inputs are finite; a program needn't handle non-finite values.
Results may differ from a plain program's by a relative error of at most 0.0001.
Values sent between devices are 32-bit elements; how exact they have to be, the bound alone decides.
No kernel may reach another device: no remote copies, remote signals or barrier semaphores. Data moves between devices by JAX's collectives and lax.ppermute only.
A program may use at most 128 MiB of HBM per device.

v0:
```python
import jax
import jax.numpy as jnp
from jax import lax
from jax.sharding import PartitionSpec as P

OUTER = 2
INNER = 2


step_size = 0.5
tv_weight = 0.1
dual_step = 1.25
highest = lax.Precision.HIGHEST


def shifted(block, axis, distance):
    devices = range(lax.axis_size(axis))
    route = [(i - distance, i) for i in devices if i - distance in devices]
    return lax.ppermute(block, axis, route)


def dft_tables(length):
    index = lax.iota(jnp.int32, length)
    product = index[:, None] * index[None, :] % length
    angle = 2.0 * jnp.pi / length * product.astype(jnp.float32)
    scale = 1.0 / jnp.sqrt(jnp.float32(length))
    return (jnp.cos(angle) * scale, -jnp.sin(angle) * scale)


def column_matrix(cos_part, sin_part):
    upper = jnp.concatenate([cos_part, sin_part], 1)
    lower = jnp.concatenate([-sin_part, cos_part], 1)
    return jnp.concatenate([upper, lower], 0)


def swap_parts(field):
    half = field.shape[-1] // 2
    return jnp.concatenate([-field[..., half:], field[..., :half]], -1)


def mul_packed(left, right):
    half = left.shape[-1] // 2
    left_re, left_im = (left[..., :half], left[..., half:])
    right_re, right_im = (right[..., :half], right[..., half:])
    return jnp.concatenate(
        [left_re * right_re - left_im * right_im, left_re * right_im + left_im * right_re], -1
    )


def mul_conj(left, right):
    half = left.shape[-1] // 2
    left_re, left_im = (left[..., :half], left[..., half:])
    right_re, right_im = (right[..., :half], right[..., half:])
    return jnp.concatenate(
        [left_re * right_re + left_im * right_im, left_re * right_im - left_im * right_re], -1
    )


def rows_apply(cos_part, sin_part, field):
    first = jnp.einsum(
        "ky,ypz->kpz", cos_part, field, precision=highest, preferred_element_type=jnp.float32
    )
    second = jnp.einsum(
        "ky,ypz->kpz",
        sin_part,
        swap_parts(field),
        precision=highest,
        preferred_element_type=jnp.float32,
    )
    return first + second


def cols_apply(matrix, field):
    shape_in = field.shape
    flat = field.reshape(-1, shape_in[-1])
    return jnp.dot(flat, matrix, precision=highest, preferred_element_type=jnp.float32).reshape(
        shape_in
    )


def pair_rows(proj_re, proj_im, field):
    first = jnp.einsum(
        "pay,ypz->apz", proj_re, field, precision=highest, preferred_element_type=jnp.float32
    )
    second = jnp.einsum(
        "pay,ypz->apz",
        proj_im,
        swap_parts(field),
        precision=highest,
        preferred_element_type=jnp.float32,
    )
    return first + second


def forward_diff(field, keep_rows):
    after = shifted(field[:1], "coil", -1)
    following = jnp.concatenate([field[1:], after], 0)
    diff_rows = jnp.where(keep_rows, following - field, 0.0)
    diff_time = jnp.concatenate([field[:, 1:] - field[:, :-1], jnp.zeros_like(field[:, :1])], 1)
    return (diff_time, diff_rows)


def adjoint_diff(dual_time, dual_rows, keep_rows):
    before = shifted(dual_rows[-1:], "coil", 1)
    keep_time = (lax.iota(jnp.int32, dual_time.shape[1]) < dual_time.shape[1] - 1)[None, :, None]
    from_time = jnp.concatenate(
        [jnp.zeros_like(dual_time[:, :1]), dual_time[:, :-1]], 1
    ) - jnp.where(keep_time, dual_time, 0.0)
    from_rows = jnp.concatenate([before, dual_rows[:-1]], 0) - jnp.where(keep_rows, dual_rows, 0.0)
    return from_time + from_rows


def per_device(image, sens, kspace, mask):
    rows_dev, frame_count, packed = image.shape
    coil_count = sens.shape[1]
    length, pair_count, unused = kspace.shape
    half = packed // 2
    device = lax.axis_index("coil")
    global_rows = device * rows_dev + lax.iota(jnp.int32, rows_dev)
    keep_rows = (global_rows < length - 1)[:, None, None]
    frame_ids = (device * pair_count + lax.iota(jnp.int32, pair_count)) % frame_count
    onehot = (frame_ids[:, None] == lax.iota(jnp.int32, frame_count)[None, :]).astype(jnp.float32)
    mask_pairs = jnp.dot(
        onehot, mask.astype(jnp.float32), precision=highest, preferred_element_type=jnp.float32
    )
    mask_rows = jnp.transpose(mask_pairs)
    sampled = mask_rows[:, :, None]
    row_cos, row_sin = dft_tables(length)
    col_cos, col_sin = dft_tables(half)
    adjoint_cols = column_matrix(col_cos, -col_sin)
    repeated = jnp.broadcast_to(sens[:, :, None, :], (rows_dev, coil_count, frame_count, packed))
    maps_pairs = lax.all_to_all(
        repeated.reshape(rows_dev, coil_count * frame_count, packed),
        "coil",
        split_axis=1,
        concat_axis=0,
        tiled=True,
    )
    proj_re = jnp.einsum(
        "ka,kp,ky->pay",
        row_cos,
        mask_rows,
        row_cos,
        precision=highest,
        preferred_element_type=jnp.float32,
    )
    proj_re = proj_re + jnp.einsum(
        "ka,kp,ky->pay",
        row_sin,
        mask_rows,
        row_sin,
        precision=highest,
        preferred_element_type=jnp.float32,
    )
    proj_im = jnp.einsum(
        "ka,kp,ky->pay",
        row_cos,
        mask_rows,
        row_sin,
        precision=highest,
        preferred_element_type=jnp.float32,
    )
    proj_im = proj_im - jnp.einsum(
        "ka,kp,ky->pay",
        row_sin,
        mask_rows,
        row_cos,
        precision=highest,
        preferred_element_type=jnp.float32,
    )
    base = cols_apply(adjoint_cols, rows_apply(row_cos, -row_sin, sampled * kspace))
    field = image
    for sweep in range(OUTER):
        chosen = jnp.einsum(
            "rfz,pf->rpz",
            lax.all_gather(field, "coil", axis=0, tiled=True),
            onehot,
            precision=highest,
            preferred_element_type=jnp.float32,
        )
        coil_images = mul_packed(maps_pairs, chosen)
        coil_grads = pair_rows(proj_re, proj_im, coil_images) - base
        weighted = mul_conj(maps_pairs, coil_grads)
        gradient = lax.psum_scatter(
            jnp.einsum(
                "rpz,pf->rfz",
                weighted,
                onehot,
                precision=highest,
                preferred_element_type=jnp.float32,
            ),
            "coil",
            scatter_dimension=0,
            tiled=True,
        )
        target = field - step_size * gradient
        dual_time = jnp.zeros_like(target)
        dual_rows = jnp.zeros_like(target)
        for repeat in range(INNER):
            if repeat == 0:
                primal = target
            else:
                primal = target - tv_weight * adjoint_diff(dual_time, dual_rows, keep_rows)
            diff_time, diff_rows = forward_diff(primal, keep_rows)
            dual_time = jnp.clip(dual_time + dual_step * diff_time, -1.0, 1.0)
            dual_rows = jnp.clip(dual_rows + dual_step * diff_rows, -1.0, 1.0)
        field = target - tv_weight * adjoint_diff(dual_time, dual_rows, keep_rows)
    return field


def solution(mesh):
    return jax.shard_map(
        per_device,
        mesh=mesh,
        in_specs=(
            P(("plane", "coil"), None, None),
            P(("plane", "coil"), None, None),
            P("plane", "coil", None),
            P(),
        ),
        out_specs=P(("plane", "coil"), None, None),
        check_vma=False,
    )
```

profile of v0, /device:TPU:0, one launch (start us, length us, event | category | flops | bytes accessed | tf_op | source)
XLA Modules:
  0.0 705.2 jit_solution(16049533103693490658)
XLA Ops:
  12.7 7.6 %all-to-all-start = ((f32[16,256,512]{2,0,1:T(8,128)}), f32[16,256,512]{2,0,1:T(8,128)}, u32[]{:S(2)}, u32[]{:S(2)}) async-start(f32[16,256,512]{2,0,1:T(8,128)} %bitcast.60), calls=%async_computation | async-start | bytes 16777216 | tf_op jit(solution)/shard_map/all_to_all | solution.py:132
  32.8 7.5 %fusion.42 = f32[16,256,256]{2,1,0:T(8,128)} fusion(f32[16,256,256]{2,1,0:T(8,128)S(1)} %fusion.22, f32[256,256]{0,1:T(8,128)S(1)} %copy.35, f32[256,16]{0,1:T(8,128)S(1)} %convolution_bitcast_fusion.2), kind=kOutput, calls=%fused_computation.52 | convolution fusion | flops 3224371200 | bytes 8667136 | tf_op jit(solution)/shard_map/ka,kp,ky->pay/dot_general | solution.py:155
  55.0 9.7 %fusion.91 = f32[256,16,512]{2,0,1:T(8,128)S(1)} fusion(f32[256,16,512]{2,0,1:T(8,128)S(1)} %copy_multiply_fusion), kind=kOutput, calls=%fused_computation.116 | convolution fusion | flops 6443433984 | bytes 16777216 | tf_op jit(solution)/shard_map/ky,ypz->kpz/dot_general | solution.py:60
  64.7 12.3 %fusion.30 = f32[256,16,512]{2,0,1:T(8,128)} fusion(f32[256,16,512]{2,0,1:T(8,128)S(1)} %fusion.91, f32[256,16,256]{2,0,1:T(8,128)} %get-tuple-element.16, f32[256,16,256]{2,0,1:T(8,128)S(1)} %get-tuple-element.15), kind=kOutput, calls=%fused_computation.46 | convolution fusion | flops 6447759360 | bytes 25165824 | tf_op jit(solution)/shard_map/ky,ypz->kpz/dot_general | solution.py:63
  77.0 95.6 %all-gather.3.cloned.1.call-done = f32[256,8,512]{2,1,0:T(8,128)} async-done(((f32[16,8,512]{2,1,0:T(8,128)}), f32[256,8,512]{2,1,0:T(8,128)}) %all-gather.3.cloned.1.call-update) | async-done | bytes 4194320 | tf_op jit(solution)/shard_map/all_gather | solution.py:176
  172.6 7.6 %convolution_bitcast_fusion.1 = f32[256,16,512]{2,1,0:T(8,128)} fusion(f32[256,8,512]{2,1,0:T(8,128)} %all-gather.3.cloned.1.call-done, s32[16]{0:T(128)S(1)} %and_select_fusion), kind=kOutput, calls=%fused_computation.48 | convolution fusion | flops 201326720 | bytes 12582976 | tf_op jit(solution)/shard_map/rfz,pf->rpz/dot_general | solution.py:174
  180.2 16.1 %all-to-all-done = f32[16,256,512]{2,0,1:T(8,128)} async-done(((f32[16,256,512]{2,0,1:T(8,128)}), f32[16,256,512]{2,0,1:T(8,128)}, u32[]{:S(2)}, u32[]{:S(2)}) %all-to-all-start) | async-done | bytes 8388640 | tf_op jit(solution)/shard_map/all_to_all | solution.py:132
  196.3 10.1 %copy.34 = f32[16,16,16,512]{3,2,1,0:T(8,128)S(1)} copy(f32[16,16,16,512]{3,1,2,0:T(8,128)} %bitcast.4) | data formatting | bytes 16777216 | tf_op jit(solution)/shard_map/all_to_all | solution.py:132
  213.5 10.3 %pad_maximum_fusion.1 = (f32[256,16,512]{2,1,0:T(8,128)S(1)}, f32[256,16,512]{2,1,0:T(8,128)}) fusion(f32[256,16,256]{2,1,0:T(8,128)} %get-tuple-element.14, f32[256,16,256]{2,1,0:T(8,128)} %get-tuple-element.7, f32[256,16,256]{2,1,0:T(8,128)} %get-tuple-element.8), kind=kLoop, calls=%fused_computation.1 | loop fusion | flops 4194304 | bytes 29360128 | tf_op jit(solution)/shard_map/concatenate | solution.py:38
  223.8 18.6 %fusion.18 = f32[16,512,256]{2,1,0:T(8,128)} fusion(f32[16,256,256]{2,1,0:T(8,128)S(1)} %copy-done.1, f32[256,16,512]{2,1,0:T(8,128)S(1)} %get-tuple-element.19), kind=kOutput, calls=%fused_computation.25 | convolution fusion | flops 6442450944 | bytes 20971520 | tf_op jit(solution)/shard_map/pay,ypz->apz/dot_general | solution.py:85
  242.4 10.5 %copy.40 = f32[16,512,256]{1,0,2:T(8,128)} copy(f32[16,512,256]{2,1,0:T(8,128)} %fusion.18) | data formatting | bytes 16777216 | tf_op jit(solution)/shard_map/pay,ypz->apz/dot_general | solution.py:85
  252.9 23.8 %fusion.20 = f32[16,512,256]{2,1,0:T(8,128)} fusion(f32[16,256,256]{2,1,0:T(8,128)} %fusion.39, f32[256,16,512]{2,1,0:T(8,128)} %get-tuple-element.20), kind=kOutput, calls=%fused_computation.27 | convolution fusion | flops 6442450944 | bytes 20971520 | tf_op jit(solution)/shard_map/pay,ypz->apz/dot_general | solution.py:82
  276.7 10.5 %copy.39 = f32[16,512,256]{1,0,2:T(8,128)} copy(f32[16,512,256]{2,1,0:T(8,128)} %fusion.20) | data formatting | bytes 16777216 | tf_op jit(solution)/shard_map/pay,ypz->apz/dot_general | solution.py:82
  287.2 27.0 %bitcast_subtract_fusion.1 = (f32[256,16,512]{2,1,0:T(8,128)}, f32[256,16,512]{2,1,0:T(8,128)}) fusion(f32[16,512,256]{1,0,2:T(8,128)} %copy.39, f32[16,512,256]{1,0,2:T(8,128)} %copy.40, f32[256,256]{1,0:T(8,128)S(1)} %get-tuple-element.24, f32[256,256]{1,0:T(8,128)S(1)} %get-tuple-element.23, f32[256,256]{1,0:T(8,128)S(1)} %fusion.98, ...), kind=kOutput, calls=%fused_computation.17 | convolution fusion | flops 12889882624 | bytes 42729472 | tf_op jit(solution)/shard_map/dot_general | solution.py:76
  326.9 104.2 %reduce-scatter.3.cloned.1.call-done = f32[16,8,512]{2,1,0:T(8,128)} async-done(((f32[256,8,512]{2,1,0:T(8,128)}), f32[16,8,512]{2,1,0:T(8,128)}) %reduce-scatter.3.cloned.1.call-update) | async-done | bytes 262160 | tf_op jit(solution)/shard_map/reduce_scatter | solution.py:184
  448.7 52.6 %all-gather.5.cloned.1.call-done = f32[256,8,512]{2,1,0:T(8,128)} async-done(((f32[16,8,512]{2,1,0:T(8,128)}), f32[256,8,512]{2,1,0:T(8,128)}) %all-gather.5.cloned.1.call-update) | async-done | bytes 4194320 | tf_op jit(solution)/shard_map/all_gather | solution.py:176
  508.1 8.2 %fusion.147 = (f32[256,16,256]{2,1,0:T(8,128)}, f32[256,16,256]{2,1,0:T(8,128)}, f32[256,16,256]{2,1,0:T(8,128)}) fusion(f32[256,16,512]{2,1,0:T(8,128)S(1)} %convolution_bitcast_fusion, f32[256,16,512]{2,1,0:T(8,128)} %bitcast.58), kind=kLoop, calls=%fused_computation.181 | loop fusion | flops 7340032 | bytes 29360128 | tf_op jit(solution)/shard_map/neg | solution.py:38
  516.3 10.2 %pad_maximum_fusion.3 = (f32[256,16,512]{2,1,0:T(8,128)S(1)}, f32[256,16,512]{2,1,0:T(8,128)}) fusion(f32[256,16,256]{2,1,0:T(8,128)} %get-tuple-element.11, f32[256,16,256]{2,1,0:T(8,128)} %get-tuple-element.5, f32[256,16,256]{2,1,0:T(8,128)} %get-tuple-element.6), kind=kLoop, calls=%fused_computation.11 | loop fusion | flops 4194304 | bytes 29360128 | tf_op jit(solution)/shard_map/concatenate | solution.py:38
  526.5 18.4 %fusion.14 = f32[16,512,256]{2,1,0:T(8,128)} fusion(f32[16,256,256]{2,1,0:T(8,128)S(1)} %copy-done.2, f32[256,16,512]{2,1,0:T(8,128)S(1)} %get-tuple-element.17), kind=kOutput, calls=%fused_computation.20 | convolution fusion | flops 6442450944 | bytes 20971520 | tf_op jit(solution)/shard_map/pay,ypz->apz/dot_general | solution.py:85
  544.8 10.5 %copy.46 = f32[16,512,256]{1,0,2:T(8,128)} copy(f32[16,512,256]{2,1,0:T(8,128)} %fusion.14) | data formatting | bytes 16777216 | tf_op jit(solution)/shard_map/pay,ypz->apz/dot_general | solution.py:85
  555.3 23.8 %fusion.16 = f32[16,512,256]{2,1,0:T(8,128)} fusion(f32[16,256,256]{2,1,0:T(8,128)} %fusion.39, f32[256,16,512]{2,1,0:T(8,128)} %get-tuple-element.18), kind=kOutput, calls=%fused_computation.22 | convolution fusion | flops 6442450944 | bytes 20971520 | tf_op jit(solution)/shard_map/pay,ypz->apz/dot_general | solution.py:82
  579.1 10.5 %copy.45 = f32[16,512,256]{1,0,2:T(8,128)} copy(f32[16,512,256]{2,1,0:T(8,128)} %fusion.16) | data formatting | bytes 16777216 | tf_op jit(solution)/shard_map/pay,ypz->apz/dot_general | solution.py:82
  589.6 9.8 %bitcast_subtract_fusion = f32[256,16,512]{2,1,0:T(8,128)S(1)} fusion(f32[256,16,512]{2,1,0:T(8,128)} %get-tuple-element.22, f32[16,512,256]{1,0,2:T(8,128)} %copy.45, f32[16,512,256]{1,0,2:T(8,128)} %copy.46), kind=kLoop, calls=%fused_computation.16 | loop fusion | flops 4194304 | bytes 33554432 | tf_op jit(solution)/shard_map/sub | solution.py:182
  609.3 71.4 %reduce-scatter.5.cloned.1.call-done = f32[16,8,512]{2,1,0:T(8,128)} async-done(((f32[256,8,512]{2,1,0:T(8,128)}), f32[16,8,512]{2,1,0:T(8,128)}) %reduce-scatter.5.cloned.1.call-update) | async-done | bytes 262160 | tf_op jit(solution)/shard_map/reduce_scatter | solution.py:184
  (98 shorter events, 104.5 us)
Async XLA Ops:
  12.7 10.7 %copy-start.6 = (s32[8,256]{1,0:T(8,128)S(1)}, s32[8,256]{1,0:T(8,128)}, u32[]{:S(2)}) copy-start(s32[8,256]{1,0:T(8,128)} %param.7) | copy-start | bytes 24580
  12.7 183.6 %all-to-all-start = ((f32[16,256,512]{2,0,1:T(8,128)}), f32[16,256,512]{2,0,1:T(8,128)}, u32[]{:S(2)}, u32[]{:S(2)}) async-start(f32[16,256,512]{2,0,1:T(8,128)} %bitcast.60), calls=%async_computation | async-start | bytes 16777216 | tf_op jit(solution)/shard_map/all_to_all | solution.py:132
  20.3 152.3 %all-gather.3.cloned.1.call-start = ((), (), s32[]{:S(2)}) async-start(), calls=%async_computation.3 | async-start | bytes 4456448 | tf_op jit(solution)/shard_map/all_gather | solution.py:176
  21.0 410.1 %reduce-scatter.3.cloned.1.call-start = ((), (), s32[]{:S(2)}) async-start(), calls=%async_computation.4 | async-start | bytes 4456448 | tf_op jit(solution)/shard_map/reduce_scatter | solution.py:184
  32.8 14.7 %slice-start = ((s8[8388608]{0:T(1024)(128)(4,1)}), s8[4194304]{0:T(1024)(128)(4,1)S(1)}, s32[]{:S(2)}) async-start(s8[8388608]{0:T(1024)(128)(4,1)} %bitcast.61), calls=%async_computation.7 | async-start | bytes 8388608
  40.3 7.1 %slice-start.1 = ((s8[8388608]{0:T(1024)(128)(4,1)}), s8[4194304]{0:T(1024)(128)(4,1)S(1)}, s32[]{:S(2)}) async-start(s8[8388608]{0:T(1024)(128)(4,1)} %bitcast.61), calls=%async_computation.8 | async-start | bytes 8388608
  196.3 10.1 %copy-start.3 = (f32[256,16,512]{2,1,0:T(8,128)S(1)}, f32[256,16,512]{2,1,0:T(8,128)}, u32[]{:S(2)}) copy-start(f32[256,16,512]{2,1,0:T(8,128)} %convolution_bitcast_fusion.1) | copy-start | bytes 25165828
  206.4 7.1 %copy-start = (f32[16,16,16,512]{3,2,1,0:T(8,128)}, f32[16,16,16,512]{3,2,1,0:T(8,128)S(1)}, u32[]{:S(2)}) copy-start(f32[16,16,16,512]{3,2,1,0:T(8,128)S(1)} %copy.34) | copy-start | bytes 25165828
  213.5 10.3 %copy-start.1 = (f32[16,256,256]{2,1,0:T(8,128)S(1)}, f32[16,256,256]{2,1,0:T(8,128)}, u32[]{:S(2)}) copy-start(f32[16,256,256]{2,1,0:T(8,128)} %fusion.42) | copy-start | bytes 12582916
  326.8 104.3 %copy-start.5 = (f32[16,8,512]{2,1,0:T(8,128)S(1)}, f32[16,8,512]{2,1,0:T(8,128)}, u32[]{:S(2)}) copy-start(f32[16,8,512]{2,1,0:T(8,128)} %param.4) | copy-start | bytes 786436
  326.8 174.5 %all-gather.5.cloned.1.call-start = ((), (), s32[]{:S(2)}) async-start(), calls=%async_computation.5 | async-start | bytes 4456448 | tf_op jit(solution)/shard_map/all_gather | solution.py:176
  432.1 3.1 collective-permute-start
  435.3 3.8 collective-permute-start.1
  439.3 3.1 collective-permute-start.2
  442.5 5.3 collective-permute-start.3
  448.7 232.1 %reduce-scatter.5.cloned.1.call-start = ((), (), s32[]{:S(2)}) async-start(), calls=%async_computation.6 | async-start | bytes 4456448 | tf_op jit(solution)/shard_map/reduce_scatter | solution.py:184
  516.3 10.2 %copy-start.2 = (f32[16,256,256]{2,1,0:T(8,128)S(1)}, f32[16,256,256]{2,1,0:T(8,128)}, u32[]{:S(2)}) copy-start(f32[16,256,256]{2,1,0:T(8,128)} %fusion.42) | copy-start | bytes 12582916
  609.3 71.5 %copy-start.4 = (f32[16,8,512]{2,1,0:T(8,128)S(1)}, f32[16,8,512]{2,1,0:T(8,128)}, u32[]{:S(2)}) copy-start(f32[16,8,512]{2,1,0:T(8,128)} %fusion.74) | copy-start | bytes 786436
  681.7 3.1 collective-permute-start.4
  684.9 3.8 collective-permute-start.5
  688.9 3.1 collective-permute-start.6
  692.1 5.3 collective-permute-start.7
Sparse Core Ops, SparseCore 0:
  23.3 149.2 all-gather.2
  326.9 104.1 reduce-scatter.2
  448.8 52.4 all-gather.4
  609.4 71.2 reduce-scatter.4
where the time goes:
time: 717 us; the launch traced here: 705 us
  waiting for transfers between devices  351 us (49%)
  matrix products  183 us (26%)
  other arithmetic  71.3 us (10%)
  local copies, waits for them, and re-layouts  58.7 us (8%)
  starting transfers between devices  27.8 us (4%)
  between operations  14 us (2%)
    reduce_scatter x2, waiting for transfers between devices, per_device(): lax.psum_scatter(jnp.einsum('rpz,pf->rfz', weighted, onehot, precision=hi...  176 us
    all_gather x2, waiting for transfers between devices, per_device(): lax.all_gather(field, 'coil', axis=0, tiled=True)  148 us
    dot_general x2, matrix products, pair_rows(): jnp.einsum('pay,ypz->apz', proj_re, field, precision=highest, preferred_e...  47.6 us
    dot_general x2, matrix products, pair_rows(): jnp.einsum('pay,ypz->apz', proj_im, swap_parts(field), precision=highest,...  37 us
    dot_general x1, matrix products, cols_apply(): jnp.dot(flat, matrix, precision=highest, preferred_element_type=jnp.float32)  27 us
    dot_general x2, local copies, waits for them, and re-layouts, pair_rows(): jnp.einsum('pay,ypz->apz', proj_im, swap_parts(field), precision=highest,...  21 us
    dot_general x2, local copies, waits for them, and re-layouts, pair_rows(): jnp.einsum('pay,ypz->apz', proj_re, field, precision=highest, preferred_e...  20.9 us
    concatenate x2, other arithmetic, swap_parts(): return jnp.concatenate([-field[..., half:], field[..., :half]], -1)  20.5 us
  transfers between devices with their start and end apart: 13, of which 13 were waited for; matrix products, arithmetic and copies ran while one was open for 9% of the time, Pallas kernels for 0%

commit v1 on v0

v1 whole, which is shorter than its diff:
```python
import functools

import jax
import jax.numpy as jnp
import ml_dtypes
import numpy as np
from jax import lax
from jax.experimental import pallas as pl
from jax.experimental.pallas import tpu as pltpu
from jax.sharding import PartitionSpec as P

OUTER = 2
INNER = 2
LANES = 128
VMEM_LIMIT = 48 * 1024 * 1024

step_size = 0.5
tv_weight = 0.1
dual_step = 1.25
highest = lax.Precision.HIGHEST


def two_terms(table):
    first = table.astype(ml_dtypes.bfloat16)
    second = (table - first.astype(np.float64)).astype(ml_dtypes.bfloat16)
    return first, second


def dft(out_index, in_index, length):
    product = np.outer(out_index, in_index) % length
    return np.exp(2j * np.pi / length * product)


def packed_left(matrix):
    return np.block([[matrix.real, -matrix.imag], [matrix.imag, matrix.real]])


def packed_right(matrix):
    return packed_left(matrix).T


def split(value):
    first = value.astype(jnp.bfloat16)
    second = (value - first.astype(jnp.float32)).astype(jnp.bfloat16)
    return first, second


def dot3(left, right, contract=((1,), (0,))):
    dims = (contract, ((), ()))

    def dot(a, b):
        return lax.dot_general(a, b, dims, preferred_element_type=jnp.float32)

    return dot(left[0], right[0]) + (dot(left[0], right[1]) + dot(left[1], right[0]))


def lane_exchange(parts, width):
    parts = list(parts)
    lane = lax.broadcasted_iota(jnp.int32, parts[0].shape, parts[0].ndim - 1)
    axis = parts[0].ndim - 1
    bit = 1
    while bit < len(parts):
        odd = (lane // width) & bit != 0
        for s in range(len(parts)):
            if s & bit:
                continue
            low, high = parts[s], parts[s | bit]
            parts[s] = jnp.where(odd, pltpu.roll(high, width * bit, axis), low)
            parts[s | bit] = jnp.where(odd, high, pltpu.roll(low, LANES - width * bit, axis))
        bit *= 2
    return parts


def roll_last(value, distance):
    shape = value.shape
    flat = value.reshape(-1, shape[-1])
    return pltpu.roll(flat, distance % shape[-1], 1).reshape(shape)


def tv_step(target):
    length = target.shape[-1]
    row = lax.broadcasted_iota(jnp.int32, target.shape, target.ndim - 1)
    last, first = row == length - 1, row == 0
    nothing = jnp.zeros_like(target[:1])

    def adjoint(dual_time, dual_rows):
        from_time = jnp.concatenate([nothing, dual_time[:-1]], 0) - jnp.concatenate(
            [dual_time[:-1], nothing], 0
        )
        from_rows = jnp.where(first, 0.0, roll_last(dual_rows, 1)) - jnp.where(last, 0.0, dual_rows)
        return from_time + from_rows

    dual_time = jnp.zeros_like(target)
    dual_rows = jnp.zeros_like(target)
    primal = target
    for repeat in range(INNER):
        diff_time = jnp.concatenate([primal[1:] - primal[:-1], nothing], 0)
        diff_rows = jnp.where(last, 0.0, roll_last(primal, -1) - primal)
        dual_time = jnp.clip(dual_time + dual_step * diff_time, -1.0, 1.0)
        dual_rows = jnp.clip(dual_rows + dual_step * diff_rows, -1.0, 1.0)
        primal = target - tv_weight * adjoint(dual_time, dual_rows)
    return primal


def normal_frame(maps_ref, field_re, field_im, tables):
    coils, _, cols, length = maps_ref.shape
    half = length // 2
    maps_re, maps_im = maps_ref[:, 0], maps_ref[:, 1]
    u_re = maps_re * field_re[None] - maps_im * field_im[None]
    u_im = maps_re * field_im[None] + maps_im * field_re[None]
    flat_re = u_re.reshape(coils * cols, length)
    flat_im = u_im.reshape(coils * cols, length)
    outs = []
    for sign, table in zip((1.0, -1.0), tables):
        packed = jnp.concatenate(
            [
                flat_re[:, :half] + sign * flat_re[:, half:],
                flat_im[:, :half] + sign * flat_im[:, half:],
            ],
            1,
        )
        outs.append(dot3(split(packed), table))
    plus, minus = outs
    v_re = jnp.concatenate(
        [plus[:, :half] + minus[:, :half], plus[:, :half] - minus[:, :half]], 1
    ).reshape(coils, cols, length)
    v_im = jnp.concatenate(
        [plus[:, half:] + minus[:, half:], plus[:, half:] - minus[:, half:]], 1
    ).reshape(coils, cols, length)
    return (
        jnp.sum(maps_re * v_re + maps_im * v_im, 0),
        jnp.sum(maps_re * v_im - maps_im * v_re, 0),
    )


def coil_blocks_kernel(coils, *refs):
    *tiles, out_ref = refs
    devices, own, rows, _ = out_ref.shape
    for d in range(devices):
        for c in range(own):
            for t, ref in enumerate(tiles):
                out_ref[d, c, :, t * LANES : (t + 1) * LANES] = ref[
                    pl.ds(d * own + c, rows, stride=coils), :
                ]


def column_blocks_kernel(coils, frames, chunk_of, *refs):
    *tiles, out_ref = refs
    sens_tiles, image_tiles = tiles[: len(tiles) // 2], tiles[len(tiles) // 2 :]
    devices, groups, _, cols, _ = out_ref.shape
    rows = sens_tiles[0].shape[0] // coils
    per = LANES // rows
    half = len(sens_tiles) // 2
    for g in range(groups):
        if g * per < coils:
            tiles, count, base = sens_tiles, coils, g * per
        else:
            tiles, count, base = image_tiles, frames, g * per - coils
        for t, ref in enumerate(tiles):
            turned = jnp.concatenate(
                [ref[pl.ds(base + c, rows, stride=count), :] for c in range(per)], 0
            ).T
            for d in range(devices):
                at = chunk_of[d] * cols - t % half * LANES
                if 0 <= at < LANES:
                    out_ref[d, g, t // half] = turned[at : at + cols]


def mask_tables_kernel(mask_ref, in_hi, in_lo, out_hi, out_lo, hi_ref, lo_ref):
    for side in range(2):
        row = mask_ref[0, side : side + 1, :].astype(jnp.bfloat16)
        left = (in_hi[side] * row, in_lo[side] * row)
        hi_ref[0, side], lo_ref[0, side] = split(dot3(left, (out_hi[side], out_lo[side])))


def base_kernel(pairs, *refs):
    *tiles, mask_ref, col_hi, col_lo, row_hi, row_lo, out_ref = refs
    p = pl.program_id(0)
    length = out_ref.shape[-1]
    half_cols = out_ref.shape[-2]
    half = length // 2
    data = jnp.concatenate(
        [
            jnp.concatenate([ref[pl.ds(at + p, half, stride=2 * pairs), :] for ref in tiles], 1)
            for at in (0, pairs)
        ],
        0,
    )
    columns = dot3((col_hi[...], col_lo[...]), split(data), ((1,), (1,)))
    columns = columns * mask_ref[0]
    re, im = columns[:half_cols], columns[half_cols:]
    even, odd = [
        dot3(
            split(jnp.concatenate([re[:, at : at + half], im[:, at : at + half]], 1)),
            (row_hi[side], row_lo[side]),
        )
        for side, at in enumerate((0, half))
    ]
    out_ref[0, 0] = jnp.concatenate([even[:, :half] + odd[:, :half], even[:, :half] - odd[:, :half]], 1)
    out_ref[0, 1] = jnp.concatenate([even[:, half:] + odd[:, half:], even[:, half:] - odd[:, half:]], 1)


def weigh_kernel(bit_ref, maps_ref, base_ref, keep_ref, send_ref, turned):
    devices, own, rows, packed = maps_ref.shape
    half_cols = packed // 2
    length = devices * rows

    @pl.when(pl.program_id(0) == 0)
    def _():
        for c in range(own):
            whole = maps_ref[:, c].reshape(length, packed).T
            turned[c, 0] = whole[:half_cols]
            turned[c, 1] = whole[half_cols:]

    bit = bit_ref[0]
    span = half_cols // 2
    blocks = devices // 2
    for ref, which in ((send_ref, 1 - bit), (keep_ref, bit)):
        at = pl.ds(pl.multiple_of(which * span, span), span)
        total_re = total_im = None
        for c in range(own):
            s_re, s_im = turned[c, 0, at, :], turned[c, 1, at, :]
            b_re, b_im = base_ref[c, 0, 0, at, :], base_ref[c, 0, 1, at, :]
            t_re = s_re * b_re + s_im * b_im
            t_im = s_re * b_im - s_im * b_re
            total_re = t_re if c == 0 else total_re + t_re
            total_im = t_im if c == 0 else total_im + t_im
        ref[:, 0, 0] = total_re.reshape(blocks, span // blocks, length)
        ref[:, 0, 1] = total_im.reshape(blocks, span // blocks, length)


def first_normal_kernel(coils, got_ref, hi_ref, lo_ref, maps_out, field_out, grad_out):
    devices, groups, _, cols, lanes = got_ref.shape
    frames = field_out.shape[0]
    per = (coils + frames) // groups
    width = lanes // per
    for g in range(groups):
        out, base = (maps_out, g * per) if g * per < coils else (field_out, g * per - coils)
        for h in range(devices // per):
            exchanged = lane_exchange([got_ref[h * per + s, g] for s in range(per)], width)
            for c in range(per):
                out[base + c, :, :, h * lanes : (h + 1) * lanes] = exchanged[c]

    def one(f, _):
        tables = [(hi_ref[f, side], lo_ref[f, side]) for side in range(2)]
        grad_out[f, 0], grad_out[f, 1] = normal_frame(
            maps_out, field_out[f, 0], field_out[f, 1], tables
        )
        return 0

    lax.fori_loop(0, frames, one, 0)


def steps_kernel(field_ref, grad_ref, b0_ref, b1_ref, maps_ref, hi_ref, lo_ref, out_ref, field, grad):
    frames, _, cols, length = field_ref.shape
    devices, _, _, lanes = out_ref.shape
    data_term = jnp.concatenate([b0_ref[...], b1_ref[...]], 0)
    field[...] = tv_step(field_ref[...] - step_size * (grad_ref[...] - data_term))
    for sweep in range(1, OUTER):

        def one(f, _):
            tables = [(hi_ref[f, side], lo_ref[f, side]) for side in range(2)]
            grad[f, 0], grad[f, 1] = normal_frame(maps_ref, field[f, 0], field[f, 1], tables)
            return 0

        lax.fori_loop(0, frames, one, 0)
        field[...] = tv_step(field[...] - step_size * (grad[...] - data_term))
    per = frames
    for h in range(devices // per):
        parts = [field[f, :, :, h * lanes : (h + 1) * lanes] for f in range(per)]
        exchanged = lane_exchange(parts, lanes // per)
        for s in range(per):
            out_ref[h * per + s] = exchanged[s]


def rows_out_kernel(chunk_of, frames, got_ref, out_ref, tiles):
    devices, _, cols, lanes = got_ref.shape
    count = tiles.shape[0]
    rows = lanes // frames
    order = sorted(range(devices), key=lambda d: chunk_of[d])
    each = LANES // cols
    for t in range(count):
        at = t % (count // 2) * each
        turned = jnp.concatenate([got_ref[d, t // (count // 2)] for d in order[at : at + each]], 0).T
        for f in range(frames):
            tiles[t, pl.ds(f, rows, stride=frames), :] = turned[f * rows : (f + 1) * rows]
        out_ref[:, t * LANES : (t + 1) * LANES] = tiles[t]


def params(**more):
    return pltpu.CompilerParams(vmem_limit_bytes=VMEM_LIMIT, **more)


def cost(flops, moved):
    return pl.CostEstimate(flops=int(flops), bytes_accessed=int(moved), transcendentals=0)


def whole(shape):
    return pl.BlockSpec(shape, lambda *_: (0,) * len(shape))


def lane_tiles(rows, lanes):
    return [
        pl.BlockSpec((rows, LANES), lambda *_, t=t: (0, t), pipeline_mode=pl.Buffered(1))
        for t in range(lanes // LANES)
    ]


def f32(*shape):
    return jax.ShapeDtypeStruct(shape, jnp.float32)


def scatter_sum(keep, send, order, device):
    devices = lax.axis_size("coil")
    bits = len(order)
    rest = keep.shape[1:]
    lead = [2] * bits
    lead[order[0]] = 1
    route = lambda bit: [(i, i ^ (1 << bit)) for i in range(devices)]
    value = (keep + lax.ppermute(send, "coil", route(order[0]))).reshape(*lead, *rest)
    for bit in order[1:]:
        mine = (device >> bit) & 1
        keep = lax.dynamic_index_in_dim(value, mine, bit, keepdims=True)
        send = lax.dynamic_index_in_dim(value, 1 - mine, bit, keepdims=True)
        value = keep + lax.ppermute(send, "coil", route(bit))
    return value.reshape(rest)


def kernel_path(image, sens, kspace, mask):
    rows, frames, packed = image.shape
    coils = sens.shape[1]
    length, pairs, _ = kspace.shape
    half = packed // 2
    hl = length // 2
    devices = lax.axis_size("coil")
    device = lax.axis_index("coil")
    bits = devices.bit_length() - 1
    own = pairs // frames
    cols = half // devices
    per = LANES // rows
    groups = (coils + frames) // per
    chunk_of = [sum(((d >> b) & 1) << (bits - 1 - b) for b in range(bits)) for d in range(devices)]

    k = np.arange(length)
    z = np.arange(half)
    y = np.arange(hl)
    col_hi, col_lo = two_terms(packed_left(dft(z, z, half) / np.sqrt(half)))
    lanes_k = [k[0::2], k[1::2]]
    inverse = [packed_right(dft(y, ks, length)) for ks in lanes_k]
    row_hi, row_lo = two_terms(np.stack(inverse) / np.sqrt(length))
    forward = [packed_right(dft(ks, y, length).conj()) for ks in lanes_k]
    in_hi, in_lo = two_terms(np.stack(forward) / np.sqrt(hl))
    out_hi, out_lo = two_terms(np.stack(inverse) / np.sqrt(hl) * 0.5)

    sampled = mask.astype(jnp.float32)
    mask_even, mask_odd = sampled[:, 0::2], sampled[:, 1::2]
    mask_lanes = jnp.concatenate([mask_even, mask_odd], 1)[:, None, :]
    mask_packed = jnp.stack(
        [jnp.concatenate([mask_even] * 2, 1), jnp.concatenate([mask_odd] * 2, 1)], 1
    )

    sens_rows = sens.reshape(rows * coils, packed)
    image_rows = image.reshape(rows * frames, packed)

    with jax.named_scope("coil_maps"):
        blocks = pl.pallas_call(
            functools.partial(coil_blocks_kernel, coils),
            grid=(1,),
            out_shape=f32(devices, own, rows, packed),
            in_specs=lane_tiles(rows * coils, packed),
            out_specs=whole((devices, own, rows, packed)),
            compiler_params=params(),
            cost_estimate=cost(0, 2 * sens.size * 4),
        )(*[sens_rows] * (packed // LANES))
        coil_maps = lax.all_to_all(blocks, "coil", 0, 0, tiled=True)

    with jax.named_scope("column_maps"):
        blocks = pl.pallas_call(
            functools.partial(column_blocks_kernel, coils, frames, chunk_of),
            grid=(1,),
            out_shape=f32(devices, groups, 2, cols, LANES),
            in_specs=lane_tiles(rows * coils, packed) + lane_tiles(rows * frames, packed),
            out_specs=whole((devices, groups, 2, cols, LANES)),
            compiler_params=params(),
            cost_estimate=cost(0, 2 * (sens.size + image.size) * 4),
        )(*[sens_rows] * (packed // LANES), *[image_rows] * (packed // LANES))
        column_maps = lax.all_to_all(blocks, "coil", 0, 0, tiled=True)

    with jax.named_scope("mask_tables"):
        table = jax.ShapeDtypeStruct((frames, 2, length, length), jnp.bfloat16)
        block = pl.BlockSpec((1, 2, length, length), lambda f: (f, 0, 0, 0))
        table_hi, table_lo = pl.pallas_call(
            mask_tables_kernel,
            grid=(frames,),
            out_shape=(table, table),
            in_specs=[pl.BlockSpec((1, 2, length), lambda f: (f, 0, 0))]
            + [whole((2, length, length))] * 4,
            out_specs=(block, block),
            compiler_params=params(),
            cost_estimate=cost(2 * 3 * 2 * frames * length**3, frames * 8 * length**2),
        )(mask_packed, in_hi, in_lo, out_hi, out_lo)

    with jax.named_scope("data_transform"):
        base = pl.pallas_call(
            functools.partial(base_kernel, pairs),
            grid=(pairs,),
            out_shape=f32(pairs, 2, half, length),
            in_specs=lane_tiles(length * pairs, packed)
            + [
                pl.BlockSpec((1, 1, length), lambda p: (p % frames, 0, 0)),
                whole((packed, packed)),
                whole((packed, packed)),
                whole((2, length, length)),
                whole((2, length, length)),
            ],
            out_specs=pl.BlockSpec((1, 2, half, length), lambda p: (p, 0, 0, 0)),
            compiler_params=params(),
            cost_estimate=cost(pairs * 6 * 6 * half * half * length, 2 * kspace.size * 4),
        )(
            *[kspace.reshape(length * pairs, packed)] * (packed // LANES),
            mask_lanes,
            col_hi,
            col_lo,
            row_hi,
            row_lo,
        )
        base = base.reshape(own, frames, 2, half, length)

    with jax.named_scope("data_term"):
        bit = (device & 1).astype(jnp.int32)[None]
        streams = 2
        count = frames // streams
        orders = [list(range(bits)), [0] + list(range(2, bits)) + [1]]
        terms = []
        for stream in range(streams):
            start = stream * count
            out = f32(devices // 2, count, 2, cols, length)
            block = pl.BlockSpec((devices // 2, 1, 2, cols, length), lambda i: (0, i, 0, 0, 0))
            keep, send = pl.pallas_call(
                weigh_kernel,
                grid=(count,),
                out_shape=(out, out),
                in_specs=[
                    pl.BlockSpec(memory_space=pltpu.SMEM),
                    whole((devices, own, rows, packed)),
                    pl.BlockSpec(
                        (own, 1, 2, half, length), lambda i, start=start: (0, start + i, 0, 0, 0)
                    ),
                ],
                out_specs=(block, block),
                scratch_shapes=[pltpu.VMEM((own, 2, half, length), jnp.float32)],
                compiler_params=params(),
                cost_estimate=cost(0, base.size * 4 // 2 + 2 * out.size * 4),
            )(bit, coil_maps, base)
            terms.append(scatter_sum(keep, send, orders[stream], device))

    with jax.named_scope("first_gradient"):
        field = f32(frames, 2, cols, length)
        normal_cost = 6 * 2 * frames * coils * cols * length * length
        maps, field0, grad0 = pl.pallas_call(
            functools.partial(first_normal_kernel, coils),
            out_shape=(f32(coils, 2, cols, length), field, field),
            compiler_params=params(),
            cost_estimate=cost(normal_cost, 4 * sens.size * 4),
        )(column_maps, table_hi, table_lo)

    with jax.named_scope("outer_steps"):
        blocks = pl.pallas_call(
            steps_kernel,
            out_shape=f32(devices, 2, cols, LANES),
            scratch_shapes=[pltpu.VMEM(field.shape, jnp.float32)] * 2,
            compiler_params=params(),
            cost_estimate=cost(normal_cost, 4 * sens.size * 4),
        )(field0, grad0, terms[0], terms[1], maps, table_hi, table_lo)

    with jax.named_scope("result_rows"):
        got = lax.all_to_all(blocks, "coil", 0, 0, tiled=True)
        recon = pl.pallas_call(
            functools.partial(rows_out_kernel, chunk_of, frames),
            out_shape=f32(rows * frames, packed),
            scratch_shapes=[pltpu.VMEM((packed // LANES, rows * frames, LANES), jnp.float32)],
            compiler_params=params(),
            cost_estimate=cost(0, 2 * image.size * 4),
        )(got)
    return recon.reshape(rows, frames, packed)


def einsum(form, left, right):
    return jnp.einsum(form, left, right, precision=highest, preferred_element_type=jnp.float32)


def complex_einsum(form, left, right):
    (a, b), (c, d) = left, right
    return (
        einsum(form, a, c) - einsum(form, b, d),
        einsum(form, a, d) + einsum(form, b, c),
    )


def general_path(image, sens, kspace, mask):
    rows, frames, packed = image.shape
    coils = sens.shape[1]
    length, pairs, _ = kspace.shape
    half = packed // 2
    devices = lax.axis_size("coil")
    device = lax.axis_index("coil")
    cols = half // devices

    def table(size):
        values = dft(np.arange(size), np.arange(size), size) / np.sqrt(size)
        return jnp.asarray(values.real, jnp.float32), jnp.asarray(values.imag, jnp.float32)

    inverse_rows, inverse_cols = table(length), table(half)
    forward_rows = (inverse_rows[0], -inverse_rows[1])

    both = jnp.concatenate([sens, image], 1).reshape(rows, coils + frames, 2, devices, cols)
    both = lax.all_to_all(both.transpose(3, 1, 2, 4, 0), "coil", 0, 0, tiled=True)
    both = both.transpose(1, 2, 3, 0, 4).reshape(coils + frames, 2, cols, length)
    maps, field = both[:coils], both[coils:]

    own = max(1, pairs // frames)
    repeats = devices * own // coils
    spread = jnp.repeat(sens.reshape(rows, coils // own, own, packed), repeats, axis=1)
    spread = spread.transpose(1, 0, 2, 3)
    coil_maps = lax.all_to_all(spread, "coil", 0, 0, tiled=True).reshape(length, own, packed)

    ids = device * pairs + lax.iota(jnp.int32, pairs)
    onehot = (ids[:, None] % frames == lax.iota(jnp.int32, frames)[None, :]).astype(jnp.float32)
    sampled = mask.astype(jnp.float32)
    data = einsum("pf,fk->kp", onehot, sampled)[:, :, None] * kspace
    data = (data[..., :half], data[..., half:])
    data = complex_einsum("kpz,zx->kpx", data, inverse_cols)
    data = complex_einsum("yk,kpx->ypx", inverse_rows, data)
    pair_maps = jnp.repeat(coil_maps, pairs // own, axis=1)
    m_re, m_im = pair_maps[..., :half], pair_maps[..., half:]
    weighted = jnp.stack(
        [m_re * data[0] + m_im * data[1], m_re * data[1] - m_im * data[0]], 2
    ).reshape(length, pairs, 2, devices, cols)
    term = einsum("ypcdx,pf->dfcxy", weighted, onehot)
    term = lax.psum_scatter(term, "coil", scatter_dimension=0, tiled=True)[0]

    masked = (
        sampled[:, :, None] * forward_rows[0][None],
        sampled[:, :, None] * forward_rows[1][None],
    )
    project = complex_einsum("yk,fkv->fyv", inverse_rows, masked)
    for sweep in range(OUTER):
        u_re = maps[:, None, 0] * field[None, :, 0] - maps[:, None, 1] * field[None, :, 1]
        u_im = maps[:, None, 0] * field[None, :, 1] + maps[:, None, 1] * field[None, :, 0]
        v_re, v_im = complex_einsum("fyv,cfxv->cfxy", project, (u_re, u_im))
        grad = jnp.stack(
            [
                jnp.sum(maps[:, None, 0] * v_re + maps[:, None, 1] * v_im, 0),
                jnp.sum(maps[:, None, 0] * v_im - maps[:, None, 1] * v_re, 0),
            ],
            1,
        )
        target = field - step_size * (grad - term)
        dual_time = jnp.zeros_like(target)
        dual_rows = jnp.zeros_like(target)
        field = target
        for repeat in range(INNER):
            diff_time = jnp.concatenate([field[1:] - field[:-1], jnp.zeros_like(field[:1])], 0)
            diff_rows = jnp.concatenate(
                [field[..., 1:] - field[..., :-1], jnp.zeros_like(field[..., :1])], -1
            )
            dual_time = jnp.clip(dual_time + dual_step * diff_time, -1.0, 1.0)
            dual_rows = jnp.clip(dual_rows + dual_step * diff_rows, -1.0, 1.0)
            inner_time, inner_rows = dual_time[:-1], dual_rows[..., :-1]
            none_time, none_rows = jnp.zeros_like(field[:1]), jnp.zeros_like(field[..., :1])
            divergence = (
                jnp.concatenate([none_time, inner_time], 0)
                - jnp.concatenate([inner_time, none_time], 0)
                + jnp.concatenate([none_rows, inner_rows], -1)
                - jnp.concatenate([inner_rows, none_rows], -1)
            )
            field = target - tv_weight * divergence

    result = field.reshape(frames, 2, cols, devices, rows).transpose(3, 0, 1, 2, 4)
    result = lax.all_to_all(result, "coil", 0, 0, tiled=True)
    return result.transpose(4, 1, 2, 0, 3).reshape(rows, frames, packed)


def fits_kernels(image, sens, kspace, devices):
    rows, frames, packed = image.shape
    coils = sens.shape[1]
    length, pairs, _ = kspace.shape
    per = LANES // rows
    return (
        devices & (devices - 1) == 0
        and devices >= 4
        and rows % 8 == 0
        and rows * per == LANES
        and frames == per
        and frames % 2 == 0
        and coils % per == 0
        and devices % per == 0
        and pairs % frames == 0
        and pairs * devices == coils * frames
        and length == 2 * LANES
        and packed % (16 * devices) == 0
        and packed % (4 * LANES) == 0
    )


def per_device(image, sens, kspace, mask):
    if fits_kernels(image, sens, kspace, lax.axis_size("coil")):
        return kernel_path(image, sens, kspace, mask)
    return general_path(image, sens, kspace, mask)


def solution(mesh):
    return jax.shard_map(
        per_device,
        mesh=mesh,
        in_specs=(
            P(("plane", "coil"), None, None),
            P(("plane", "coil"), None, None),
            P("plane", "coil", None),
            P(),
        ),
        out_specs=P(("plane", "coil"), None, None),
        check_vma=False,
    )
```

time: 717 us -> 156 us (0.22); the launches traced: 705 us -> 155 us
  waiting for transfers between devices: 351 us -> 40.5 us
  matrix products: 183 us -> 0 us
  Pallas kernels: 0 us -> 66.4 us
  other arithmetic: 71.3 us -> 5.46 us
  local copies, waits for them, and re-layouts: 58.7 us -> 6.5 us
  blocking collectives: 0 us -> 13.9 us
  between operations: 14 us -> 0.33 us
    dot_general x16 -> x0, matrix products: 183 us -> none  [the longest x2 47.6 us: pair_rows(): jnp.einsum('pay,ypz->apz', proj_re, field, precision=highest, preferred_e...]
    reduce_scatter x2 -> x0, waiting for transfers between devices: 176 us -> none  [per_device(): lax.psum_scatter(jnp.einsum('rpz,pf->rfz', weighted, onehot, precision=hi...]
    all_gather x2 -> x0, waiting for transfers between devices: 148 us -> none  [per_device(): lax.all_gather(field, 'coil', axis=0, tiled=True)]
    pallas_call x0 -> x9, Pallas kernels: none -> 66.4 us  [the longest x1 31.4 us: kernel_path(): pl.pallas_call(functools.partial(base_kernel, pairs), grid=(pairs,), out_...]
    dot_general x4 -> x0, local copies, waits for them, and re-layouts: 41.9 us -> none  [the longest x2 21 us: pair_rows(): jnp.einsum('pay,ypz->apz', proj_im, swap_parts(field), precision=highest,...]
    concatenate x2 -> x1, other arithmetic: 20.5 us -> 0.01 us  [kernel_path(): mask_lanes = jnp.concatenate([mask_even, mask_odd], 1)[:, None, :]]
    neg x4 -> x0, other arithmetic: 18.8 us -> none  [the longest x3 17.8 us: swap_parts(): return jnp.concatenate([-field[..., half:], field[..., :half]], -1)]
    sub x11 -> x0, other arithmetic: 13.9 us -> none  [the longest x1 9.82 us: per_device(): coil_grads = pair_rows(proj_re, proj_im, coil_images) - base]
  transfers between devices with their start and end apart: 13 -> 10, of which waited for: 13 -> 5; matrix products, arithmetic and copies ran while one was open for 9% -> 4% of each run, Pallas kernels for 0% -> 36%
where the time goes in v1:
time: 156 us; the launch traced here: 155 us
  Pallas kernels  66.4 us (43%)
  waiting for transfers between devices  40.5 us (26%)
  starting transfers between devices  21.9 us (14%)
  blocking collectives  13.9 us (9%)
  local copies, waits for them, and re-layouts  6.5 us (4%)
  other arithmetic  5.46 us (4%)
    pallas_call x1, Pallas kernels, kernel_path(): pl.pallas_call(functools.partial(base_kernel, pairs), grid=(pairs,), out_...  31.4 us
    all_to_all x1, waiting for transfers between devices, kernel_path(): coil_maps = lax.all_to_all(blocks, 'coil', 0, 0, tiled=True)  20.5 us
    ppermute x6, waiting for transfers between devices, scatter_sum(): value = keep + lax.ppermute(send, 'coil', route(bit))  19.9 us
    all_to_all x1, blocking collectives, kernel_path(): got = lax.all_to_all(blocks, 'coil', 0, 0, tiled=True)  13.9 us
    pallas_call x1, Pallas kernels, kernel_path(): pl.pallas_call(functools.partial(first_normal_kernel, coils), out_shape=(...  9.38 us
    pallas_call x2, Pallas kernels, kernel_path(): pl.pallas_call(weigh_kernel, grid=(count,), out_shape=(out, out), in_spec...  9.35 us
    pallas_call x1, Pallas kernels, kernel_path(): pl.pallas_call(steps_kernel, out_shape=f32(devices, 2, cols, LANES), scra...  8.68 us
    all_to_all x1, starting transfers between devices, kernel_path(): coil_maps = lax.all_to_all(blocks, 'coil', 0, 0, tiled=True)  7.52 us
  transfers between devices with their start and end apart: 10, of which 5 were waited for; matrix products, arithmetic and copies ran while one was open for 4% of the time, Pallas kernels for 36%

profile of v1, /device:TPU:0, one launch (start us, length us, event | category | flops | bytes accessed | tf_op | source)
XLA Modules:
  0.0 154.9 jit_solution(8284827237231068464)
XLA Ops:
  0.0 1.2 copy-done
  1.2 1.7 %coil_maps.1 = f32[16,2,16,512]{3,2,1,0:T(8,128)} custom-call(f32[512,512]{1,0:T(8,128)S(1)} %bitcast.16, f32[512,512]{1,0:T(8,128)S(1)} %bitcast.17, f32[512,512]{1,0:T(8,128)S(1)} %bitcast.18, f32[512,512]{1,0:T(8,128)S(1)} %bitcast.19), custom_call_target="tpu_custom_call" | custom-call | bytes 2097152 | tf_op jit(solution)/shard_map/coil_maps/pallas_call | solution.py:366
  2.9 7.5 %all-to-all-start.1 = ((f32[16,2,16,512]{3,2,1,0:T(8,128)}), f32[16,2,16,512]{3,2,1,0:T(8,128)S(1)}, u32[]{:S(2)}, u32[]{:S(2)}) async-start(f32[16,2,16,512]{3,2,1,0:T(8,128)} %coil_maps.1), calls=%async_computation.1 | async-start | bytes 2097152 | tf_op jit(solution)/shard_map/coil_maps/all_to_all | solution.py:375
  10.9 1.9 %column_maps.1 = f32[16,5,2,16,128]{4,3,2,1,0:T(8,128)} custom-call(f32[512,512]{1,0:T(8,128)S(1)} %bitcast.20, f32[512,512]{1,0:T(8,128)S(1)} %bitcast.21, f32[512,512]{1,0:T(8,128)S(1)} %bitcast.22, f32[512,512]{1,0:T(8,128)S(1)} %bitcast.23, f32[128,512]{1,0:T(8,128)S(1)} %bitcast.24, f32[128,512]{1,0:T(8,128)S(1)} %bitcast.25, f32[128,512]{1,0:T(8,128)S(1)} %bitcast.26, ...), custom_call_target="tpu_custom_call" | custom-call | bytes 2621440 | tf_op jit(solution)/shard_map/column_maps/pallas_call | solution.py:378
  12.8 20.5 %all-to-all-done.1.maps_ref = f32[16,2,16,512]{3,2,1,0:T(8,128)S(1)} async-done(((f32[16,2,16,512]{3,2,1,0:T(8,128)}), f32[16,2,16,512]{3,2,1,0:T(8,128)S(1)}, u32[]{:S(2)}, u32[]{:S(2)}) %all-to-all-start.1) | async-done | bytes 1048608 | tf_op jit(solution)/shard_map/coil_maps/all_to_all | solution.py:375
  33.4 6.9 %all-to-all-start = ((f32[16,5,2,16,128]{4,3,2,1,0:T(8,128)}), f32[16,5,2,16,128]{4,3,2,1,0:T(8,128)S(1)}, u32[]{:S(2)}, u32[]{:S(2)}) async-start(f32[16,5,2,16,128]{4,3,2,1,0:T(8,128)} %column_maps.1), calls=%async_computation | async-start | bytes 2621440 | tf_op jit(solution)/shard_map/column_maps/all_to_all | solution.py:387
  42.2 31.4 %data_transform.1 = f32[16,2,256,256]{3,2,1,0:T(8,128)} custom-call(f32[4096,512]{1,0:T(8,128)} %bitcast.28, f32[4096,512]{1,0:T(8,128)} %bitcast.29, f32[4096,512]{1,0:T(8,128)} %bitcast.30, f32[4096,512]{1,0:T(8,128)} %bitcast.31, f32[8,1,256]{2,1,0:T(1,128)S(1)} %broadcast_in_dim.7.refs_4_, bf16[512,512]{1,0:T(8,128)(2,1)S(1)} %copy-done.4, ...), custom_call_target="tpu_custom_call" | custom-call | flops 9663676416 | bytes 16777216 | tf_op jit(solution)/shard_map/data_transform/pallas_call | solution.py:404
  73.6 4.7 %data_term.3 = (f32[8,4,2,16,256]{4,3,2,1,0:T(8,128)S(1)}, f32[8,4,2,16,256]{4,3,2,1,0:T(8,128)}) custom-call(s32[1]{0:T(128)} %bitcast.4.bit_ref, f32[16,2,16,512]{3,2,1,0:T(8,128)S(1)} %all-to-all-done.1.maps_ref, f32[2,8,2,256,256]{4,3,2,1,0:T(8,128)} %bitcast.32), custom_call_target="tpu_custom_call" | custom-call | bytes 6291456 | tf_op jit(solution)/shard_map/data_term/pallas_call | solution.py:439
  78.7 4.7 %data_term.2 = (f32[8,4,2,16,256]{4,3,2,1,0:T(8,128)S(1)}, f32[8,4,2,16,256]{4,3,2,1,0:T(8,128)}) custom-call(s32[1]{0:T(128)} %bitcast.4.bit_ref, f32[16,2,16,512]{3,2,1,0:T(8,128)S(1)} %all-to-all-done.1.maps_ref, f32[2,8,2,256,256]{4,3,2,1,0:T(8,128)} %bitcast.33), custom_call_target="tpu_custom_call" | custom-call | bytes 6291456 | tf_op jit(solution)/shard_map/data_term/pallas_call | solution.py:439
  83.8 1.9 %add.67 = f32[8,4,2,16,256]{4,3,2,1,0:T(8,128)S(1)} add(f32[8,4,2,16,256]{4,3,2,1,0:T(8,128)} %copy-done.3, f32[8,4,2,16,256]{4,3,2,1,0:T(8,128)} %collective-permute-done.4) | non-fusion elementwise | flops 262144 | bytes 3145728 | tf_op jit(solution)/shard_map/data_term/add | solution.py:320
  85.7 1.0 constant_dynamic-slice_fusion.2
  86.9 1.7 %collective-permute-start.5 = (f32[1,2,1,2,4,2,16,256]{7,6,5,4,3,2,1,0:T(8,128)}, f32[1,2,1,2,4,2,16,256]{7,6,5,4,3,2,1,0:T(8,128)}, u32[]{:S(2)}, u32[]{:S(2)}) collective-permute-start(f32[1,2,1,2,4,2,16,256]{7,6,5,4,3,2,1,0:T(8,128)} %constant_dynamic-slice_fusion.2), channel_id=1, source_target_pairs={{0,4},{1,5},{2,6},{3,7},{4,0},{5,1},{6,2},{7,3},{8,12},{9,13},{10,... | collective-permute-start | bytes 1572872 | tf_op jit(solution)/shard_map/data_term/ppermute | solution.py:325
  88.6 3.1 %mask_tables.1 = (bf16[8,2,256,256]{3,2,1,0:T(8,128)(2,1)S(1)}, bf16[8,2,256,256]{3,2,1,0:T(8,128)(2,1)S(1)}) custom-call(f32[8,2,256]{2,1,0:T(2,128)S(1)} %copy.13.mask_ref, bf16[2,256,256]{2,1,0:T(8,128)(2,1)S(1)} %copy-done.8, bf16[2,256,256]{2,1,0:T(8,128)(2,1)S(1)} %copy-done.9, bf16[2,256,256]{2,1,0:T(8,128)(2,1)S(1)} %copy-done.10, ...), custom_call_target="tpu_custom_call" | custom-call | flops 1610612736 | bytes 4194304 | tf_op jit(solution)/shard_map/mask_tables/pallas_call | solution.py:392
  91.7 2.2 %add.57 = f32[8,4,2,16,256]{4,3,2,1,0:T(8,128)S(1)} add(f32[8,4,2,16,256]{4,3,2,1,0:T(8,128)S(1)} %get-tuple-element.18, f32[8,4,2,16,256]{4,3,2,1,0:T(8,128)} %collective-permute-done) | non-fusion elementwise | flops 262144 | bytes 3145728 | tf_op jit(solution)/shard_map/data_term/add | solution.py:320
  94.0 1.5 collective-permute-start.1
  95.5 1.6 %copy-done.13 = bf16[8,2,256,256]{3,2,1,0:T(8,128)(2,1)S(1)} copy-done((bf16[8,2,256,256]{3,2,1,0:T(8,128)(2,1)S(1)}, bf16[8,2,256,256]{3,2,1,0:T(8,128)(2,1)}, u32[]{:S(2)}) %copy-start.13) | copy-done | bytes 2097176
  97.1 9.4 %first_gradient.1 = (f32[32,2,16,256]{3,2,1,0:T(8,128)S(1)}, f32[8,2,16,256]{3,2,1,0:T(8,128)S(1)}, f32[8,2,16,256]{3,2,1,0:T(8,128)S(1)}) custom-call(f32[16,5,2,16,128]{4,3,2,1,0:T(8,128)S(1)} %all-to-all-done.got_ref, bf16[8,2,256,256]{3,2,1,0:T(8,128)(2,1)S(1)} %copy-done.13, bf16[8,2,256,256]{3,2,1,0:T(8,128)(2,1)} %copy-done.14), custom_call_target="tpu_custom_call" | custom-call | flops 3221225472 | bytes 4194304 | tf_op jit(solution)/shard_map/first_gradient/pallas_call | solution.py:460
  106.5 1.1 dynamic-slice_add_fusion
  107.7 2.4 %collective-permute-start.6 = (f32[1,2,1,1,4,2,16,256]{7,6,5,4,3,2,1,0:T(8,128)S(1)}, f32[1,2,1,1,4,2,16,256]{7,6,5,4,3,2,1,0:T(8,128)S(1)}, u32[]{:S(2)}, u32[]{:S(2)}) collective-permute-start(f32[1,2,1,1,4,2,16,256]{7,6,5,4,3,2,1,0:T(8,128)S(1)} %constant_dynamic-slice_fusion.1), channel_id=1, source_target_pairs={{0,8},{1,9},{2,10},{3,11},{4,12},{5,13},{6,14},{7,15},{8,0},{9,1},... | collective-permute-start | bytes 786440 | tf_op jit(solution)/shard_map/data_term/ppermute | solution.py:325
  110.9 11.5 %collective-permute-done.6 = f32[1,2,1,1,4,2,16,256]{7,6,5,4,3,2,1,0:T(8,128)S(1)} collective-permute-done((f32[1,2,1,1,4,2,16,256]{7,6,5,4,3,2,1,0:T(8,128)S(1)}, f32[1,2,1,1,4,2,16,256]{7,6,5,4,3,2,1,0:T(8,128)S(1)}, u32[]{:S(2)}, u32[]{:S(2)}) %collective-permute-start.6) | collective-permute-done | bytes 262176 | tf_op jit(solution)/shard_map/data_term/ppermute | solution.py:325
  123.7 4.2 %collective-permute-done.7 = f32[1,1,1,1,4,2,16,256]{7,6,5,4,3,2,1,0:T(8,128)S(1)} collective-permute-done((f32[1,1,1,1,4,2,16,256]{7,6,5,4,3,2,1,0:T(8,128)S(1)}, f32[1,1,1,1,4,2,16,256]{7,6,5,4,3,2,1,0:T(8,128)S(1)}, u32[]{:S(2)}, u32[]{:S(2)}) %collective-permute-start.7) | collective-permute-done | bytes 131104 | tf_op jit(solution)/shard_map/data_term/ppermute | solution.py:325
  127.9 3.5 %collective-permute-done.3 = f32[1,1,1,1,4,2,16,256]{7,6,5,4,3,2,1,0:T(8,128)S(1)} collective-permute-done((f32[1,1,1,1,4,2,16,256]{7,6,5,4,3,2,1,0:T(8,128)S(1)}, f32[1,1,1,1,4,2,16,256]{7,6,5,4,3,2,1,0:T(8,128)S(1)}, u32[]{:S(2)}, u32[]{:S(2)}) %collective-permute-start.3) | collective-permute-done | bytes 131104 | tf_op jit(solution)/shard_map/data_term/ppermute | solution.py:325
  131.5 8.7 %outer_steps.1 = f32[16,2,16,128]{3,2,1,0:T(8,128)S(1)} custom-call(f32[8,2,16,256]{3,2,1,0:T(8,128)S(1)} %get-tuple-element.16.field_ref, f32[8,2,16,256]{3,2,1,0:T(8,128)S(1)} %get-tuple-element.17.grad_ref, f32[4,2,16,256]{3,2,1,0:T(8,128)S(1)} %add_bitcast_fusion.1.b0_ref, f32[4,2,16,256]{3,2,1,0:T(8,128)S(1)} %add_bitcast_fusion.b1_ref, ...), custom_call_target="tpu_custom_call" | custom-call | flops 3221225472 | bytes 4194304 | tf_op jit(solution)/shard_map/outer_steps/pallas_call | solution.py:468
  140.1 13.9 %all_to_all.15.got_ref = f32[16,2,16,128]{3,2,1,0:T(8,128)S(1)} all-to-all(f32[16,2,16,128]{3,2,1,0:T(8,128)S(1)} %outer_steps.1), channel_id=1, replica_groups=mesh['plane'=2,'coil'=16] {'coil'}, dimensions={0} | all-to-all | bytes 524288 | tf_op jit(solution)/shard_map/result_rows/all_to_all | solution.py:477
  (63 shorter events, 6.4 us)
Async XLA Ops:
  2.9 7.5 %copy-start.17 = (s32[8,256]{1,0:T(8,128)S(1)}, s32[8,256]{1,0:T(8,128)}, u32[]{:S(2)}) copy-start(s32[8,256]{1,0:T(8,128)} %param.15) | copy-start | bytes 24580
  2.9 8.0 %copy-start.1 = (f32[16,32,512]{2,1,0:T(8,128)S(1)}, f32[16,32,512]{2,1,0:T(8,128)}, u32[]{:S(2)}) copy-start(f32[16,32,512]{2,1,0:T(8,128)} %param.13) | copy-start | bytes 3145732
  2.9 8.0 %copy-start.2 = (f32[16,8,512]{2,1,0:T(8,128)S(1)}, f32[16,8,512]{2,1,0:T(8,128)}, u32[]{:S(2)}) copy-start(f32[16,8,512]{2,1,0:T(8,128)} %param.12) | copy-start | bytes 786436
  2.9 30.5 %all-to-all-start.1 = ((f32[16,2,16,512]{3,2,1,0:T(8,128)}), f32[16,2,16,512]{3,2,1,0:T(8,128)S(1)}, u32[]{:S(2)}, u32[]{:S(2)}) async-start(f32[16,2,16,512]{3,2,1,0:T(8,128)} %coil_maps.1), calls=%async_computation.1 | async-start | bytes 2097152 | tf_op jit(solution)/shard_map/coil_maps/all_to_all | solution.py:375
  12.8 27.4 %copy-start.4 = (bf16[512,512]{1,0:T(8,128)(2,1)S(1)}, bf16[512,512]{1,0:T(8,128)(2,1)}, u32[]{:S(2)}) copy-start(bf16[512,512]{1,0:T(8,128)(2,1)} %constant.70.clone.refs_5_) | copy-start | bytes 1572868
  12.8 27.5 %copy-start.5 = (bf16[512,512]{1,0:T(8,128)(2,1)S(1)}, bf16[512,512]{1,0:T(8,128)(2,1)}, u32[]{:S(2)}) copy-start(bf16[512,512]{1,0:T(8,128)(2,1)} %constant.71.clone.refs_6_) | copy-start | bytes 1572868
  33.4 62.2 %all-to-all-start = ((f32[16,5,2,16,128]{4,3,2,1,0:T(8,128)}), f32[16,5,2,16,128]{4,3,2,1,0:T(8,128)S(1)}, u32[]{:S(2)}, u32[]{:S(2)}) async-start(f32[16,5,2,16,128]{4,3,2,1,0:T(8,128)} %column_maps.1), calls=%async_computation | async-start | bytes 2621440 | tf_op jit(solution)/shard_map/column_maps/all_to_all | solution.py:387
  78.3 5.1 %copy-start.3 = (f32[8,4,2,16,256]{4,3,2,1,0:T(8,128)}, f32[8,4,2,16,256]{4,3,2,1,0:T(8,128)S(1)}, u32[]{:S(2)}) copy-start(f32[8,4,2,16,256]{4,3,2,1,0:T(8,128)S(1)} %get-tuple-element.20) | copy-start | bytes 3145732
  78.3 5.5 %collective-permute-start.4 = (f32[8,4,2,16,256]{4,3,2,1,0:T(8,128)}, f32[8,4,2,16,256]{4,3,2,1,0:T(8,128)}, u32[]{:S(2)}, u32[]{:S(2)}) collective-permute-start(f32[8,4,2,16,256]{4,3,2,1,0:T(8,128)} %get-tuple-element.21), channel_id=1, source_target_pairs={{0,1},{1,0},{2,3},{3,2},{4,5},{5,4},{6,7},{7,6},{8,9},{9,8},{10,11... | collective-permute-start | bytes 3145736 | tf_op jit(solution)/shard_map/data_term/ppermute | solution.py:320
  83.4 8.3 %collective-permute-start = (f32[8,4,2,16,256]{4,3,2,1,0:T(8,128)}, f32[8,4,2,16,256]{4,3,2,1,0:T(8,128)}, u32[]{:S(2)}, u32[]{:S(2)}) collective-permute-start(f32[8,4,2,16,256]{4,3,2,1,0:T(8,128)} %get-tuple-element.19), channel_id=1, source_target_pairs={{0,1},{1,0},{2,3},{3,2},{4,5},{5,4},{6,7},{7,6},{8,9},{9,8},{10,11... | collective-permute-start | bytes 3145736 | tf_op jit(solution)/shard_map/data_term/ppermute | solution.py:320
  83.8 4.8 %copy-start.8 = (bf16[2,256,256]{2,1,0:T(8,128)(2,1)S(1)}, bf16[2,256,256]{2,1,0:T(8,128)(2,1)}, u32[]{:S(2)}) copy-start(bf16[2,256,256]{2,1,0:T(8,128)(2,1)} %constant.66.clone.in_hi) | copy-start | bytes 786436
  83.8 4.8 %copy-start.9 = (bf16[2,256,256]{2,1,0:T(8,128)(2,1)S(1)}, bf16[2,256,256]{2,1,0:T(8,128)(2,1)}, u32[]{:S(2)}) copy-start(bf16[2,256,256]{2,1,0:T(8,128)(2,1)} %constant.67.clone.in_lo) | copy-start | bytes 786436
  83.8 4.8 %copy-start.10 = (bf16[2,256,256]{2,1,0:T(8,128)(2,1)S(1)}, bf16[2,256,256]{2,1,0:T(8,128)(2,1)}, u32[]{:S(2)}) copy-start(bf16[2,256,256]{2,1,0:T(8,128)(2,1)} %constant.68.clone.out_hi) | copy-start | bytes 786436
  83.8 4.7 %copy-start.11 = (bf16[2,256,256]{2,1,0:T(8,128)(2,1)S(1)}, bf16[2,256,256]{2,1,0:T(8,128)(2,1)}, u32[]{:S(2)}) copy-start(bf16[2,256,256]{2,1,0:T(8,128)(2,1)} %constant.69.clone.out_lo) | copy-start | bytes 786436
  86.9 19.6 %collective-permute-start.5 = (f32[1,2,1,2,4,2,16,256]{7,6,5,4,3,2,1,0:T(8,128)}, f32[1,2,1,2,4,2,16,256]{7,6,5,4,3,2,1,0:T(8,128)}, u32[]{:S(2)}, u32[]{:S(2)}) collective-permute-start(f32[1,2,1,2,4,2,16,256]{7,6,5,4,3,2,1,0:T(8,128)} %constant_dynamic-slice_fusion.2), channel_id=1, source_target_pairs={{0,4},{1,5},{2,6},{3,7},{4,0},{5,1},{6,2},{7,3},{8,12},{9,13},{10,... | collective-permute-start | bytes 1572872 | tf_op jit(solution)/shard_map/data_term/ppermute | solution.py:325
  91.6 2.3 %copy-start.12 = (bf16[8,2,256,256]{3,2,1,0:T(8,128)(2,1)}, bf16[8,2,256,256]{3,2,1,0:T(8,128)(2,1)S(1)}, u32[]{:S(2)}) copy-start(bf16[8,2,256,256]{3,2,1,0:T(8,128)(2,1)S(1)} %get-tuple-element.14.hi_ref) | copy-start | bytes 6291460
  91.7 2.3 %copy-start.14 = (bf16[8,2,256,256]{3,2,1,0:T(8,128)(2,1)}, bf16[8,2,256,256]{3,2,1,0:T(8,128)(2,1)S(1)}, u32[]{:S(2)}) copy-start(bf16[8,2,256,256]{3,2,1,0:T(8,128)(2,1)S(1)} %get-tuple-element.15.lo_ref) | copy-start | bytes 6291460
  94.0 16.1 %collective-permute-start.1 = (f32[1,1,2,2,4,2,16,256]{7,6,5,4,3,2,1,0:T(8,128)S(1)}, f32[1,1,2,2,4,2,16,256]{7,6,5,4,3,2,1,0:T(8,128)S(1)}, u32[]{:S(2)}, u32[]{:S(2)}) collective-permute-start(f32[1,1,2,2,4,2,16,256]{7,6,5,4,3,2,1,0:T(8,128)S(1)} %constant_dynamic-slice_fusion.5), channel_id=1, source_target_pairs={{0,2},{1,3},{2,0},{3,1},{4,6},{5,7},{6,4},{7,5},{8,10},{9,11},{10,... | collective-permute-start | bytes 1572872 | tf_op jit(solution)/shard_map/data_term/ppermute | solution.py:325
  95.5 1.6 %copy-start.13 = (bf16[8,2,256,256]{3,2,1,0:T(8,128)(2,1)S(1)}, bf16[8,2,256,256]{3,2,1,0:T(8,128)(2,1)}, u32[]{:S(2)}) copy-start(bf16[8,2,256,256]{3,2,1,0:T(8,128)(2,1)} %copy-done.12) | copy-start | bytes 6291460
  97.1 9.4 %copy-start.16 = (f32[8,4,2,16,256]{4,3,2,1,0:T(8,128)S(1)}, f32[8,4,2,16,256]{4,3,2,1,0:T(8,128)}, u32[]{:S(2)}) copy-start(f32[8,4,2,16,256]{4,3,2,1,0:T(8,128)} %copy-done.15) | copy-start | bytes 3145732
  107.7 14.7 %collective-permute-start.6 = (f32[1,2,1,1,4,2,16,256]{7,6,5,4,3,2,1,0:T(8,128)S(1)}, f32[1,2,1,1,4,2,16,256]{7,6,5,4,3,2,1,0:T(8,128)S(1)}, u32[]{:S(2)}, u32[]{:S(2)}) collective-permute-start(f32[1,2,1,1,4,2,16,256]{7,6,5,4,3,2,1,0:T(8,128)S(1)} %constant_dynamic-slice_fusion.1), channel_id=1, source_target_pairs={{0,8},{1,9},{2,10},{3,11},{4,12},{5,13},{6,14},{7,15},{8,0},{9,1},... | collective-permute-start | bytes 786440 | tf_op jit(solution)/shard_map/data_term/ppermute | solution.py:325
  110.3 13.3 %collective-permute-start.2 = (f32[1,1,1,2,4,2,16,256]{7,6,5,4,3,2,1,0:T(8,128)S(1)}, f32[1,1,1,2,4,2,16,256]{7,6,5,4,3,2,1,0:T(8,128)S(1)}, u32[]{:S(2)}, u32[]{:S(2)}) collective-permute-start(f32[1,1,1,2,4,2,16,256]{7,6,5,4,3,2,1,0:T(8,128)S(1)} %constant_dynamic-slice_fusion.4), channel_id=1, source_target_pairs={{0,4},{1,5},{2,6},{3,7},{4,0},{5,1},{6,2},{7,3},{8,12},{9,13},{10,... | collective-permute-start | bytes 786440 | tf_op jit(solution)/shard_map/data_term/ppermute | solution.py:325
  122.5 5.4 %collective-permute-start.7 = (f32[1,1,1,1,4,2,16,256]{7,6,5,4,3,2,1,0:T(8,128)S(1)}, f32[1,1,1,1,4,2,16,256]{7,6,5,4,3,2,1,0:T(8,128)S(1)}, u32[]{:S(2)}, u32[]{:S(2)}) collective-permute-start(f32[1,1,1,1,4,2,16,256]{7,6,5,4,3,2,1,0:T(8,128)S(1)} %constant_dynamic-slice_fusion), channel_id=1, source_target_pairs={{0,2},{1,3},{2,0},{3,1},{4,6},{5,7},{6,4},{7,5},{8,10},{9,11},{10,... | collective-permute-start | bytes 393224 | tf_op jit(solution)/shard_map/data_term/ppermute | solution.py:325
  123.7 7.8 %collective-permute-start.3 = (f32[1,1,1,1,4,2,16,256]{7,6,5,4,3,2,1,0:T(8,128)S(1)}, f32[1,1,1,1,4,2,16,256]{7,6,5,4,3,2,1,0:T(8,128)S(1)}, u32[]{:S(2)}, u32[]{:S(2)}) collective-permute-start(f32[1,1,1,1,4,2,16,256]{7,6,5,4,3,2,1,0:T(8,128)S(1)} %constant_dynamic-slice_fusion.3), channel_id=1, source_target_pairs={{0,8},{1,9},{2,10},{3,11},{4,12},{5,13},{6,14},{7,15},{8,0},{9,1},... | collective-permute-start | bytes 393224 | tf_op jit(solution)/shard_map/data_term/ppermute | solution.py:325
  (4 other events, 4.3 us)

commit v2 on v1

--- a/solution.py
+++ b/solution.py
@@ -173,31 +173,56 @@
         hi_ref[0, side], lo_ref[0, side] = split(dot3(left, (out_hi[side], out_lo[side])))
 
 
-def base_kernel(pairs, *refs):
-    *tiles, mask_ref, col_hi, col_lo, row_hi, row_lo, out_ref = refs
-    p = pl.program_id(0)
-    length = out_ref.shape[-1]
-    half_cols = out_ref.shape[-2]
+def base_kernel(kspace_ref, mask_ref, col_hi, col_lo, row_hi, row_lo, out_ref, data, arrived):
+    own, _, _, half_cols, length = out_ref.shape
     half = length // 2
-    data = jnp.concatenate(
-        [
-            jnp.concatenate([ref[pl.ds(at + p, half, stride=2 * pairs), :] for ref in tiles], 1)
-            for at in (0, pairs)
-        ],
-        0,
-    )
-    columns = dot3((col_hi[...], col_lo[...]), split(data), ((1,), (1,)))
-    columns = columns * mask_ref[0]
-    re, im = columns[:half_cols], columns[half_cols:]
-    even, odd = [
-        dot3(
-            split(jnp.concatenate([re[:, at : at + half], im[:, at : at + half]], 1)),
-            (row_hi[side], row_lo[side]),
+    frame, frames = pl.program_id(0), pl.num_programs(0)
+
+    def fetch(f, slot):
+        return [
+            pltpu.make_async_copy(
+                kspace_ref.at[:, odd, f + c * frames, :],
+                data.at[slot, c, pl.ds(odd * half, half)],
+                arrived.at[slot, c, odd],
+            )
+            for c in range(own)
+            for odd in range(2)
+        ]
+
+    @pl.when(frame == 0)
+    def _():
+        for copy in fetch(0, 0):
+            copy.start()
+
+    @pl.when(frame + 1 < frames)
+    def _():
+        for copy in fetch(frame + 1, (frame + 1) % 2):
+            copy.start()
+
+    slot = frame % 2
+    for copy in fetch(frame, slot):
+        copy.wait()
+    columns = [
+        dot3((col_hi[...], col_lo[...]), split(data[slot, c]), ((1,), (1,))) * mask_ref[0]
+        for c in range(own)
+    ]
+    sides = []
+    for odd in range(2):
+        at = odd * half
+        stacked = jnp.concatenate(
+            [
+                jnp.concatenate([v[:half_cols, at : at + half], v[half_cols:, at : at + half]], 1)
+                for v in columns
+            ],
+            0,
         )
-        for side, at in enumerate((0, half))
-    ]
-    out_ref[0, 0] = jnp.concatenate([even[:, :half] + odd[:, :half], even[:, :half] - odd[:, :half]], 1)
-    out_ref[0, 1] = jnp.concatenate([even[:, half:] + odd[:, half:], even[:, half:] - odd[:, half:]], 1)
+        sides.append(dot3(split(stacked), (row_hi[odd], row_lo[odd])))
+    for c in range(own):
+        even, odd = [side[c * half_cols : (c + 1) * half_cols] for side in sides]
+        for part in range(2):
+            e = even[:, part * half : (part + 1) * half]
+            o = odd[:, part * half : (part + 1) * half]
+            out_ref[c, 0, part] = jnp.concatenate([e + o, e - o], 1)
 
 
 def weigh_kernel(bit_ref, maps_ref, base_ref, keep_ref, send_ref, turned):
@@ -375,7 +400,7 @@
         coil_maps = lax.all_to_all(blocks, "coil", 0, 0, tiled=True)
 
     with jax.named_scope("column_maps"):
-        blocks = pl.pallas_call(
+        column_blocks = pl.pallas_call(
             functools.partial(column_blocks_kernel, coils, frames, chunk_of),
             grid=(1,),
             out_shape=f32(devices, groups, 2, cols, LANES),
@@ -384,7 +409,6 @@
             compiler_params=params(),
             cost_estimate=cost(0, 2 * (sens.size + image.size) * 4),
         )(*[sens_rows] * (packed // LANES), *[image_rows] * (packed // LANES))
-        column_maps = lax.all_to_all(blocks, "coil", 0, 0, tiled=True)
 
     with jax.named_scope("mask_tables"):
         table = jax.ShapeDtypeStruct((frames, 2, length, length), jnp.bfloat16)
@@ -402,29 +426,33 @@
 
     with jax.named_scope("data_transform"):
         base = pl.pallas_call(
-            functools.partial(base_kernel, pairs),
-            grid=(pairs,),
-            out_shape=f32(pairs, 2, half, length),
-            in_specs=lane_tiles(length * pairs, packed)
-            + [
-                pl.BlockSpec((1, 1, length), lambda p: (p % frames, 0, 0)),
+            base_kernel,
+            grid=(frames,),
+            out_shape=f32(own, frames, 2, half, length),
+            in_specs=[
+                pl.BlockSpec(memory_space=pl.ANY),
+                pl.BlockSpec((1, 1, length), lambda f: (f, 0, 0)),
                 whole((packed, packed)),
                 whole((packed, packed)),
                 whole((2, length, length)),
                 whole((2, length, length)),
             ],
-            out_specs=pl.BlockSpec((1, 2, half, length), lambda p: (p, 0, 0, 0)),
+            out_specs=pl.BlockSpec((own, 1, 2, half, length), lambda f: (0, f, 0, 0, 0)),
+            scratch_shapes=[
+                pltpu.VMEM((2, own, length, packed), jnp.float32),
+                pltpu.SemaphoreType.DMA((2, own, 2)),
+            ],
             compiler_params=params(),
             cost_estimate=cost(pairs * 6 * 6 * half * half * length, 2 * kspace.size * 4),
         )(
-            *[kspace.reshape(length * pairs, packed)] * (packed // LANES),
-            mask_lanes,
-            col_hi,
-            col_lo,
-            row_hi,
-            row_lo,
+            kspace.reshape(hl, 2, pairs, packed), mask_lanes, col_hi, col_lo, row_hi, row_lo
         )
-        base = base.reshape(own, frames, 2, half, length)
+
+    column_blocks, base, table_hi, table_lo = lax.optimization_barrier(
+        (column_blocks, base, table_hi, table_lo)
+    )
+    with jax.named_scope("column_maps"):
+        column_maps = lax.all_to_all(column_blocks, "coil", 0, 0, tiled=True)
 
     with jax.named_scope("data_term"):
         bit = (device & 1).astype(jnp.int32)[None]

time: 156 us -> 133 us (0.85)
  Pallas kernels: 66.4 us -> 50.9 us
  waiting for transfers between devices: 40.5 us -> 28.8 us
  starting transfers between devices: 21.9 us -> 25.9 us
  blocking collectives: 13.9 us -> 16.1 us
    all_to_all x1, waiting for transfers between devices: 20.5 us -> 1.08 us  [kernel_path(): coil_maps = lax.all_to_all(blocks, 'coil', 0, 0, tiled=True)]
    pallas_call x1, Pallas kernels: 31.4 us -> 16.1 us  [kernel_path(): pl.pallas_call(base_kernel, grid=(frames,), out_shape=f32(own, frames, 2,...]
    all_to_all x1, waiting for transfers between devices: 0.01 us -> 9.29 us  [kernel_path(): column_maps = lax.all_to_all(column_blocks, 'coil', 0, 0, tiled=True)]
    ppermute x6, starting transfers between devices: 6.69 us -> 10.7 us  [scatter_sum(): value = keep + lax.ppermute(send, 'coil', route(bit))]
    all_to_all x1, blocking collectives: 13.9 us -> 16.1 us  [kernel_path(): got = lax.all_to_all(blocks, 'coil', 0, 0, tiled=True)]
  transfers between devices with their start and end apart: 10 -> 10, of which waited for: 5 -> 6; matrix products, arithmetic and copies ran while one was open for 4% -> 5% of each run, Pallas kernels for 36% -> 30%
where the time goes in v2:
time: 133 us; the launch traced here: 132 us
  Pallas kernels  50.9 us (38%)
  waiting for transfers between devices  28.8 us (22%)
  starting transfers between devices  25.9 us (19%)
  blocking collectives  16.1 us (12%)
  local copies, waits for them, and re-layouts  5.25 us (4%)
  other arithmetic  4.62 us (3%)
    ppermute x6, waiting for transfers between devices, scatter_sum(): value = keep + lax.ppermute(send, 'coil', route(bit))  18.4 us
    pallas_call x1, Pallas kernels, kernel_path(): pl.pallas_call(base_kernel, grid=(frames,), out_shape=f32(own, frames, 2,...  16.1 us
    all_to_all x1, blocking collectives, kernel_path(): got = lax.all_to_all(blocks, 'coil', 0, 0, tiled=True)  16.1 us
    ppermute x6, starting transfers between devices, scatter_sum(): value = keep + lax.ppermute(send, 'coil', route(bit))  10.7 us
    pallas_call x2, Pallas kernels, kernel_path(): pl.pallas_call(weigh_kernel, grid=(count,), out_shape=(out, out), in_spec...  9.38 us
    all_to_all x1, waiting for transfers between devices, kernel_path(): column_maps = lax.all_to_all(column_blocks, 'coil', 0, 0, tiled=True)  9.29 us
    pallas_call x1, Pallas kernels, kernel_path(): pl.pallas_call(functools.partial(first_normal_kernel, coils), out_shape=(...  9.29 us
    pallas_call x1, Pallas kernels, kernel_path(): pl.pallas_call(steps_kernel, out_shape=f32(devices, 2, cols, LANES), scra...  8.68 us
  transfers between devices with their start and end apart: 10, of which 6 were waited for; matrix products, arithmetic and copies ran while one was open for 5% of the time, Pallas kernels for 30%

profile of v2, /device:TPU:0, one launch (start us, length us, event | category | flops | bytes accessed | tf_op | source)
XLA Modules:
  0.0 131.9 jit_solution(8693134471809122911)
XLA Ops:
  0.0 1.2 copy-done
  1.2 1.6 %coil_maps.1 = f32[16,2,16,512]{3,2,1,0:T(8,128)} custom-call(f32[512,512]{1,0:T(8,128)S(1)} %bitcast.15, f32[512,512]{1,0:T(8,128)S(1)} %bitcast.16, f32[512,512]{1,0:T(8,128)S(1)} %bitcast.17, f32[512,512]{1,0:T(8,128)S(1)} %bitcast.18), custom_call_target="tpu_custom_call" | custom-call | bytes 2097152 | tf_op jit(solution)/shard_map/coil_maps/pallas_call | solution.py:391
  2.9 7.5 %all-to-all-start.1 = ((f32[16,2,16,512]{3,2,1,0:T(8,128)}), f32[16,2,16,512]{3,2,1,0:T(8,128)S(1)}, u32[]{:S(2)}, u32[]{:S(2)}) async-start(f32[16,2,16,512]{3,2,1,0:T(8,128)} %coil_maps.1), calls=%async_computation.1 | async-start | bytes 2097152 | tf_op jit(solution)/shard_map/coil_maps/all_to_all | solution.py:400
  11.0 1.9 %column_maps.1 = f32[16,5,2,16,128]{4,3,2,1,0:T(8,128)} custom-call(f32[512,512]{1,0:T(8,128)S(1)} %bitcast.19, f32[512,512]{1,0:T(8,128)S(1)} %bitcast.20, f32[512,512]{1,0:T(8,128)S(1)} %bitcast.21, f32[512,512]{1,0:T(8,128)S(1)} %bitcast.22, f32[128,512]{1,0:T(8,128)S(1)} %bitcast.23, f32[128,512]{1,0:T(8,128)S(1)} %bitcast.24, f32[128,512]{1,0:T(8,128)S(1)} %bitcast.25, ...), custom_call_target="tpu_custom_call" | custom-call | bytes 2621440 | tf_op jit(solution)/shard_map/column_maps/pallas_call | solution.py:403
  13.0 3.1 %mask_tables.1 = (bf16[8,2,256,256]{3,2,1,0:T(8,128)(2,1)S(1)}, bf16[8,2,256,256]{3,2,1,0:T(8,128)(2,1)S(1)}) custom-call(f32[8,2,256]{2,1,0:T(2,128)S(1)} %pad_maximum_fusion.mask_ref, bf16[2,256,256]{2,1,0:T(8,128)(2,1)S(1)} %copy-done.6, bf16[2,256,256]{2,1,0:T(8,128)(2,1)S(1)} %copy-done.9, bf16[2,256,256]{2,1,0:T(8,128)(2,1)S(1)} %copy-done.10, ...), custom_call_target="tpu_custom_call" | custom-call | flops 1610612736 | bytes 4194304 | tf_op jit(solution)/shard_map/mask_tables/pallas_call | solution.py:416
  16.1 16.1 %data_transform.1.base_ref = f32[2,8,2,256,256]{4,3,2,1,0:T(8,128)} custom-call(f32[128,2,16,512]{3,2,1,0:T(8,128)} %bitcast.31, f32[8,1,256]{2,1,0:T(1,128)S(1)} %copy.13.mask_ref, bf16[512,512]{1,0:T(8,128)(2,1)S(1)} %copy-done.4, bf16[512,512]{1,0:T(8,128)(2,1)S(1)} %copy-done.5, bf16[2,256,256]{2,1,0:T(8,128)(2,1)S(1)} %copy-done.7, ...), custom_call_target="tpu_custom_call" | custom-call | flops 9663676416 | bytes 16777216 | tf_op jit(solution)/shard_map/data_transform/pallas_call | solution.py:428
  33.3 6.9 %all-to-all-start = ((f32[16,5,2,16,128]{4,3,2,1,0:T(8,128)}), f32[16,5,2,16,128]{4,3,2,1,0:T(8,128)S(1)}, u32[]{:S(2)}, u32[]{:S(2)}) async-start(f32[16,5,2,16,128]{4,3,2,1,0:T(8,128)} %column_maps.1), calls=%async_computation | async-start | bytes 2621440 | tf_op jit(solution)/shard_map/column_maps/all_to_all | solution.py:455
  40.2 4.7 %data_term.3 = (f32[8,4,2,16,256]{4,3,2,1,0:T(8,128)S(1)}, f32[8,4,2,16,256]{4,3,2,1,0:T(8,128)}) custom-call(s32[1]{0:T(128)} %bitcast.5.bit_ref, f32[16,2,16,512]{3,2,1,0:T(8,128)S(1)} %all-to-all-done.1.maps_ref, f32[2,8,2,256,256]{4,3,2,1,0:T(8,128)} %data_transform.1.base_ref), custom_call_target="tpu_custom_call" | custom-call | bytes 6291456 | tf_op jit(solution)/shard_map/data_term/pallas_call | solution.py:467
  45.4 4.6 %data_term.2 = (f32[8,4,2,16,256]{4,3,2,1,0:T(8,128)S(1)}, f32[8,4,2,16,256]{4,3,2,1,0:T(8,128)}) custom-call(s32[1]{0:T(128)} %bitcast.5.bit_ref, f32[16,2,16,512]{3,2,1,0:T(8,128)S(1)} %all-to-all-done.1.maps_ref, f32[2,8,2,256,256]{4,3,2,1,0:T(8,128)} %data_transform.1.base_ref), custom_call_target="tpu_custom_call" | custom-call | bytes 6291456 | tf_op jit(solution)/shard_map/data_term/pallas_call | solution.py:467
  50.4 1.8 %add.67 = f32[8,4,2,16,256]{4,3,2,1,0:T(8,128)S(1)} add(f32[8,4,2,16,256]{4,3,2,1,0:T(8,128)} %copy-done.3, f32[8,4,2,16,256]{4,3,2,1,0:T(8,128)} %collective-permute-done.4) | non-fusion elementwise | flops 262144 | bytes 3145728 | tf_op jit(solution)/shard_map/data_term/add | solution.py:345
  53.0 1.7 %collective-permute-start.5 = (f32[1,2,1,2,4,2,16,256]{7,6,5,4,3,2,1,0:T(8,128)}, f32[1,2,1,2,4,2,16,256]{7,6,5,4,3,2,1,0:T(8,128)}, u32[]{:S(2)}, u32[]{:S(2)}) collective-permute-start(f32[1,2,1,2,4,2,16,256]{7,6,5,4,3,2,1,0:T(8,128)} %constant_dynamic-slice_fusion.2), channel_id=1, source_target_pairs={{0,4},{1,5},{2,6},{3,7},{4,0},{5,1},{6,2},{7,3},{8,12},{9,13},{10,... | collective-permute-start | bytes 1572872 | tf_op jit(solution)/shard_map/data_term/ppermute | solution.py:350
  54.7 1.4 %add.57 = f32[8,4,2,16,256]{4,3,2,1,0:T(8,128)S(1)} add(f32[8,4,2,16,256]{4,3,2,1,0:T(8,128)S(1)} %get-tuple-element.26, f32[8,4,2,16,256]{4,3,2,1,0:T(8,128)} %collective-permute-done) | non-fusion elementwise | flops 262144 | bytes 3145728 | tf_op jit(solution)/shard_map/data_term/add | solution.py:345
  57.1 1.5 %collective-permute-start.1 = (f32[1,1,2,2,4,2,16,256]{7,6,5,4,3,2,1,0:T(8,128)S(1)}, f32[1,1,2,2,4,2,16,256]{7,6,5,4,3,2,1,0:T(8,128)S(1)}, u32[]{:S(2)}, u32[]{:S(2)}) collective-permute-start(f32[1,1,2,2,4,2,16,256]{7,6,5,4,3,2,1,0:T(8,128)S(1)} %constant_dynamic-slice_fusion.5), channel_id=1, source_target_pairs={{0,2},{1,3},{2,0},{3,1},{4,6},{5,7},{6,4},{7,5},{8,10},{9,11},{10,... | collective-permute-start | bytes 1572872 | tf_op jit(solution)/shard_map/data_term/ppermute | solution.py:350
  58.6 9.3 %all-to-all-done.got_ref = f32[16,5,2,16,128]{4,3,2,1,0:T(8,128)S(1)} async-done(((f32[16,5,2,16,128]{4,3,2,1,0:T(8,128)}), f32[16,5,2,16,128]{4,3,2,1,0:T(8,128)S(1)}, u32[]{:S(2)}, u32[]{:S(2)}) %all-to-all-start) | async-done | bytes 1310752 | tf_op jit(solution)/shard_map/column_maps/all_to_all | solution.py:455
  67.8 1.6 %copy-done.13 = bf16[8,2,256,256]{3,2,1,0:T(8,128)(2,1)S(1)} copy-done((bf16[8,2,256,256]{3,2,1,0:T(8,128)(2,1)S(1)}, bf16[8,2,256,256]{3,2,1,0:T(8,128)(2,1)}, u32[]{:S(2)}) %copy-start.13) | copy-done | bytes 2097176
  69.4 9.3 %first_gradient.1 = (f32[32,2,16,256]{3,2,1,0:T(8,128)S(1)}, f32[8,2,16,256]{3,2,1,0:T(8,128)S(1)}, f32[8,2,16,256]{3,2,1,0:T(8,128)S(1)}) custom-call(f32[16,5,2,16,128]{4,3,2,1,0:T(8,128)S(1)} %all-to-all-done.got_ref, bf16[8,2,256,256]{3,2,1,0:T(8,128)(2,1)S(1)} %copy-done.13, bf16[8,2,256,256]{3,2,1,0:T(8,128)(2,1)} %copy-done.14), custom_call_target="tpu_custom_call" | custom-call | flops 3221225472 | bytes 4194304 | tf_op jit(solution)/shard_map/first_gradient/pallas_call | solution.py:488
  78.8 1.2 dynamic-slice_add_fusion
  80.0 6.2 %collective-permute-start.6 = (f32[1,2,1,1,4,2,16,256]{7,6,5,4,3,2,1,0:T(8,128)S(1)}, f32[1,2,1,1,4,2,16,256]{7,6,5,4,3,2,1,0:T(8,128)S(1)}, u32[]{:S(2)}, u32[]{:S(2)}) collective-permute-start(f32[1,2,1,1,4,2,16,256]{7,6,5,4,3,2,1,0:T(8,128)S(1)} %constant_dynamic-slice_fusion.1), channel_id=1, source_target_pairs={{0,8},{1,9},{2,10},{3,11},{4,12},{5,13},{6,14},{7,15},{8,0},{9,1},... | collective-permute-start | bytes 786440 | tf_op jit(solution)/shard_map/data_term/ppermute | solution.py:350
  86.5 11.5 %collective-permute-done.6 = f32[1,2,1,1,4,2,16,256]{7,6,5,4,3,2,1,0:T(8,128)S(1)} collective-permute-done((f32[1,2,1,1,4,2,16,256]{7,6,5,4,3,2,1,0:T(8,128)S(1)}, f32[1,2,1,1,4,2,16,256]{7,6,5,4,3,2,1,0:T(8,128)S(1)}, u32[]{:S(2)}, u32[]{:S(2)}) %collective-permute-start.6) | collective-permute-done | bytes 262176 | tf_op jit(solution)/shard_map/data_term/ppermute | solution.py:350
  98.5 1.2 collective-permute-start.3
  99.7 3.4 %collective-permute-done.7 = f32[1,1,1,1,4,2,16,256]{7,6,5,4,3,2,1,0:T(8,128)S(1)} collective-permute-done((f32[1,1,1,1,4,2,16,256]{7,6,5,4,3,2,1,0:T(8,128)S(1)}, f32[1,1,1,1,4,2,16,256]{7,6,5,4,3,2,1,0:T(8,128)S(1)}, u32[]{:S(2)}, u32[]{:S(2)}) %collective-permute-start.7) | collective-permute-done | bytes 131104 | tf_op jit(solution)/shard_map/data_term/ppermute | solution.py:350
  103.1 3.2 %collective-permute-done.3 = f32[1,1,1,1,4,2,16,256]{7,6,5,4,3,2,1,0:T(8,128)S(1)} collective-permute-done((f32[1,1,1,1,4,2,16,256]{7,6,5,4,3,2,1,0:T(8,128)S(1)}, f32[1,1,1,1,4,2,16,256]{7,6,5,4,3,2,1,0:T(8,128)S(1)}, u32[]{:S(2)}, u32[]{:S(2)}) %collective-permute-start.3) | collective-permute-done | bytes 131104 | tf_op jit(solution)/shard_map/data_term/ppermute | solution.py:350
  106.3 8.7 %outer_steps.1 = f32[16,2,16,128]{3,2,1,0:T(8,128)S(1)} custom-call(f32[8,2,16,256]{3,2,1,0:T(8,128)S(1)} %get-tuple-element.23.field_ref, f32[8,2,16,256]{3,2,1,0:T(8,128)S(1)} %get-tuple-element.24.grad_ref, f32[4,2,16,256]{3,2,1,0:T(8,128)S(1)} %add_bitcast_fusion.1.b0_ref, f32[4,2,16,256]{3,2,1,0:T(8,128)S(1)} %add_bitcast_fusion.b1_ref, ...), custom_call_target="tpu_custom_call" | custom-call | flops 3221225472 | bytes 4194304 | tf_op jit(solution)/shard_map/outer_steps/pallas_call | solution.py:496
  115.0 16.1 %all_to_all.15.got_ref = f32[16,2,16,128]{3,2,1,0:T(8,128)S(1)} all-to-all(f32[16,2,16,128]{3,2,1,0:T(8,128)S(1)} %outer_steps.1), channel_id=1, replica_groups=mesh['plane'=2,'coil'=16] {'coil'}, dimensions={0} | all-to-all | bytes 524288 | tf_op jit(solution)/shard_map/result_rows/all_to_all | solution.py:505
  (64 shorter events, 5.8 us)
Async XLA Ops:
  2.9 7.5 %copy-start.17 = (s32[8,256]{1,0:T(8,128)S(1)}, s32[8,256]{1,0:T(8,128)}, u32[]{:S(2)}) copy-start(s32[8,256]{1,0:T(8,128)} %param.15) | copy-start | bytes 24580
  2.9 8.0 %copy-start.1 = (f32[16,32,512]{2,1,0:T(8,128)S(1)}, f32[16,32,512]{2,1,0:T(8,128)}, u32[]{:S(2)}) copy-start(f32[16,32,512]{2,1,0:T(8,128)} %param.13) | copy-start | bytes 3145732
  2.9 8.0 %copy-start.2 = (f32[16,8,512]{2,1,0:T(8,128)S(1)}, f32[16,8,512]{2,1,0:T(8,128)}, u32[]{:S(2)}) copy-start(f32[16,8,512]{2,1,0:T(8,128)} %param.12) | copy-start | bytes 786436
  2.9 30.5 %all-to-all-start.1 = ((f32[16,2,16,512]{3,2,1,0:T(8,128)}), f32[16,2,16,512]{3,2,1,0:T(8,128)S(1)}, u32[]{:S(2)}, u32[]{:S(2)}) async-start(f32[16,2,16,512]{3,2,1,0:T(8,128)} %coil_maps.1), calls=%async_computation.1 | async-start | bytes 2097152 | tf_op jit(solution)/shard_map/coil_maps/all_to_all | solution.py:400
  10.9 2.0 %copy-start.6 = (bf16[2,256,256]{2,1,0:T(8,128)(2,1)S(1)}, bf16[2,256,256]{2,1,0:T(8,128)(2,1)}, u32[]{:S(2)}) copy-start(bf16[2,256,256]{2,1,0:T(8,128)(2,1)} %constant.66.clone.in_hi) | copy-start | bytes 786436
  10.9 2.0 %copy-start.9 = (bf16[2,256,256]{2,1,0:T(8,128)(2,1)S(1)}, bf16[2,256,256]{2,1,0:T(8,128)(2,1)}, u32[]{:S(2)}) copy-start(bf16[2,256,256]{2,1,0:T(8,128)(2,1)} %constant.67.clone.in_lo) | copy-start | bytes 786436
  10.9 2.0 %copy-start.10 = (bf16[2,256,256]{2,1,0:T(8,128)(2,1)S(1)}, bf16[2,256,256]{2,1,0:T(8,128)(2,1)}, u32[]{:S(2)}) copy-start(bf16[2,256,256]{2,1,0:T(8,128)(2,1)} %constant.68.clone.out_hi) | copy-start | bytes 786436
  12.9 3.1 %copy-start.4 = (bf16[512,512]{1,0:T(8,128)(2,1)S(1)}, bf16[512,512]{1,0:T(8,128)(2,1)}, u32[]{:S(2)}) copy-start(bf16[512,512]{1,0:T(8,128)(2,1)} %constant.70.clone.col_hi) | copy-start | bytes 1572868
  12.9 3.1 %copy-start.5 = (bf16[512,512]{1,0:T(8,128)(2,1)S(1)}, bf16[512,512]{1,0:T(8,128)(2,1)}, u32[]{:S(2)}) copy-start(bf16[512,512]{1,0:T(8,128)(2,1)} %constant.71.clone.col_lo) | copy-start | bytes 1572868
  13.0 3.1 %copy-start.7 = (bf16[2,256,256]{2,1,0:T(8,128)(2,1)S(1)}, bf16[2,256,256]{2,1,0:T(8,128)(2,1)}, u32[]{:S(2)}) copy-start(bf16[2,256,256]{2,1,0:T(8,128)(2,1)} %constant.72.clone.row_hi) | copy-start | bytes 786436
  13.0 3.1 %copy-start.8 = (bf16[2,256,256]{2,1,0:T(8,128)(2,1)S(1)}, bf16[2,256,256]{2,1,0:T(8,128)(2,1)}, u32[]{:S(2)}) copy-start(bf16[2,256,256]{2,1,0:T(8,128)(2,1)} %constant.73.clone.row_lo) | copy-start | bytes 786436
  16.1 16.2 %copy-start.12 = (bf16[8,2,256,256]{3,2,1,0:T(8,128)(2,1)}, bf16[8,2,256,256]{3,2,1,0:T(8,128)(2,1)S(1)}, u32[]{:S(2)}) copy-start(bf16[8,2,256,256]{3,2,1,0:T(8,128)(2,1)S(1)} %get-tuple-element.21.hi_ref) | copy-start | bytes 6291460
  16.1 16.2 %copy-start.14 = (bf16[8,2,256,256]{3,2,1,0:T(8,128)(2,1)}, bf16[8,2,256,256]{3,2,1,0:T(8,128)(2,1)S(1)}, u32[]{:S(2)}) copy-start(bf16[8,2,256,256]{3,2,1,0:T(8,128)(2,1)S(1)} %get-tuple-element.22.lo_ref) | copy-start | bytes 6291460
  33.3 34.5 %all-to-all-start = ((f32[16,5,2,16,128]{4,3,2,1,0:T(8,128)}), f32[16,5,2,16,128]{4,3,2,1,0:T(8,128)S(1)}, u32[]{:S(2)}, u32[]{:S(2)}) async-start(f32[16,5,2,16,128]{4,3,2,1,0:T(8,128)} %column_maps.1), calls=%async_computation | async-start | bytes 2621440 | tf_op jit(solution)/shard_map/column_maps/all_to_all | solution.py:455
  45.0 5.0 %copy-start.3 = (f32[8,4,2,16,256]{4,3,2,1,0:T(8,128)}, f32[8,4,2,16,256]{4,3,2,1,0:T(8,128)S(1)}, u32[]{:S(2)}) copy-start(f32[8,4,2,16,256]{4,3,2,1,0:T(8,128)S(1)} %get-tuple-element.28) | copy-start | bytes 3145732
  45.0 5.4 %collective-permute-start.4 = (f32[8,4,2,16,256]{4,3,2,1,0:T(8,128)}, f32[8,4,2,16,256]{4,3,2,1,0:T(8,128)}, u32[]{:S(2)}, u32[]{:S(2)}) collective-permute-start(f32[8,4,2,16,256]{4,3,2,1,0:T(8,128)} %get-tuple-element.29), channel_id=1, source_target_pairs={{0,1},{1,0},{2,3},{3,2},{4,5},{5,4},{6,7},{7,6},{8,9},{9,8},{10,11... | collective-permute-start | bytes 3145736 | tf_op jit(solution)/shard_map/data_term/ppermute | solution.py:345
  50.0 4.7 %collective-permute-start = (f32[8,4,2,16,256]{4,3,2,1,0:T(8,128)}, f32[8,4,2,16,256]{4,3,2,1,0:T(8,128)}, u32[]{:S(2)}, u32[]{:S(2)}) collective-permute-start(f32[8,4,2,16,256]{4,3,2,1,0:T(8,128)} %get-tuple-element.27), channel_id=1, source_target_pairs={{0,1},{1,0},{2,3},{3,2},{4,5},{5,4},{6,7},{7,6},{8,9},{9,8},{10,11... | collective-permute-start | bytes 3145736 | tf_op jit(solution)/shard_map/data_term/ppermute | solution.py:345
  53.0 25.7 %collective-permute-start.5 = (f32[1,2,1,2,4,2,16,256]{7,6,5,4,3,2,1,0:T(8,128)}, f32[1,2,1,2,4,2,16,256]{7,6,5,4,3,2,1,0:T(8,128)}, u32[]{:S(2)}, u32[]{:S(2)}) collective-permute-start(f32[1,2,1,2,4,2,16,256]{7,6,5,4,3,2,1,0:T(8,128)} %constant_dynamic-slice_fusion.2), channel_id=1, source_target_pairs={{0,4},{1,5},{2,6},{3,7},{4,0},{5,1},{6,2},{7,3},{8,12},{9,13},{10,... | collective-permute-start | bytes 1572872 | tf_op jit(solution)/shard_map/data_term/ppermute | solution.py:350
  57.1 29.2 %collective-permute-start.1 = (f32[1,1,2,2,4,2,16,256]{7,6,5,4,3,2,1,0:T(8,128)S(1)}, f32[1,1,2,2,4,2,16,256]{7,6,5,4,3,2,1,0:T(8,128)S(1)}, u32[]{:S(2)}, u32[]{:S(2)}) collective-permute-start(f32[1,1,2,2,4,2,16,256]{7,6,5,4,3,2,1,0:T(8,128)S(1)} %constant_dynamic-slice_fusion.5), channel_id=1, source_target_pairs={{0,2},{1,3},{2,0},{3,1},{4,6},{5,7},{6,4},{7,5},{8,10},{9,11},{10,... | collective-permute-start | bytes 1572872 | tf_op jit(solution)/shard_map/data_term/ppermute | solution.py:350
  78.7 7.5 %copy-start.16 = (f32[8,4,2,16,256]{4,3,2,1,0:T(8,128)S(1)}, f32[8,4,2,16,256]{4,3,2,1,0:T(8,128)}, u32[]{:S(2)}) copy-start(f32[8,4,2,16,256]{4,3,2,1,0:T(8,128)} %copy-done.15) | copy-start | bytes 3145732
  80.0 18.0 %collective-permute-start.6 = (f32[1,2,1,1,4,2,16,256]{7,6,5,4,3,2,1,0:T(8,128)S(1)}, f32[1,2,1,1,4,2,16,256]{7,6,5,4,3,2,1,0:T(8,128)S(1)}, u32[]{:S(2)}, u32[]{:S(2)}) collective-permute-start(f32[1,2,1,1,4,2,16,256]{7,6,5,4,3,2,1,0:T(8,128)S(1)} %constant_dynamic-slice_fusion.1), channel_id=1, source_target_pairs={{0,8},{1,9},{2,10},{3,11},{4,12},{5,13},{6,14},{7,15},{8,0},{9,1},... | collective-permute-start | bytes 786440 | tf_op jit(solution)/shard_map/data_term/ppermute | solution.py:350
  86.4 12.0 %collective-permute-start.2 = (f32[1,1,1,2,4,2,16,256]{7,6,5,4,3,2,1,0:T(8,128)S(1)}, f32[1,1,1,2,4,2,16,256]{7,6,5,4,3,2,1,0:T(8,128)S(1)}, u32[]{:S(2)}, u32[]{:S(2)}) collective-permute-start(f32[1,1,1,2,4,2,16,256]{7,6,5,4,3,2,1,0:T(8,128)S(1)} %constant_dynamic-slice_fusion.4), channel_id=1, source_target_pairs={{0,4},{1,5},{2,6},{3,7},{4,0},{5,1},{6,2},{7,3},{8,12},{9,13},{10,... | collective-permute-start | bytes 786440 | tf_op jit(solution)/shard_map/data_term/ppermute | solution.py:350
  98.0 5.0 %collective-permute-start.7 = (f32[1,1,1,1,4,2,16,256]{7,6,5,4,3,2,1,0:T(8,128)S(1)}, f32[1,1,1,1,4,2,16,256]{7,6,5,4,3,2,1,0:T(8,128)S(1)}, u32[]{:S(2)}, u32[]{:S(2)}) collective-permute-start(f32[1,1,1,1,4,2,16,256]{7,6,5,4,3,2,1,0:T(8,128)S(1)} %constant_dynamic-slice_fusion), channel_id=1, source_target_pairs={{0,2},{1,3},{2,0},{3,1},{4,6},{5,7},{6,4},{7,5},{8,10},{9,11},{10,... | collective-permute-start | bytes 393224 | tf_op jit(solution)/shard_map/data_term/ppermute | solution.py:350
  98.5 7.8 %collective-permute-start.3 = (f32[1,1,1,1,4,2,16,256]{7,6,5,4,3,2,1,0:T(8,128)S(1)}, f32[1,1,1,1,4,2,16,256]{7,6,5,4,3,2,1,0:T(8,128)S(1)}, u32[]{:S(2)}, u32[]{:S(2)}) collective-permute-start(f32[1,1,1,1,4,2,16,256]{7,6,5,4,3,2,1,0:T(8,128)S(1)} %constant_dynamic-slice_fusion.3), channel_id=1, source_target_pairs={{0,8},{1,9},{2,10},{3,11},{4,12},{5,13},{6,14},{7,15},{8,0},{9,1},... | collective-permute-start | bytes 393224 | tf_op jit(solution)/shard_map/data_term/ppermute | solution.py:350
  (4 other events, 5.8 us)

commit v3 on v2

--- a/solution.py
+++ b/solution.py
@@ -12,7 +12,8 @@
 OUTER = 2
 INNER = 2
 LANES = 128
-VMEM_LIMIT = 48 * 1024 * 1024
+VMEM_LIMIT = 16 * 1024 * 1024
+TRANSFORM_LIMIT = 52 * 1024 * 1024
 
 step_size = 0.5
 tv_weight = 0.1
@@ -100,6 +101,38 @@
         dual_rows = jnp.clip(dual_rows + dual_step * diff_rows, -1.0, 1.0)
         primal = target - tv_weight * adjoint(dual_time, dual_rows)
     return primal
+
+
+def mask_responses(mask_ref, wave_hi, wave_lo, out_ref):
+    for side in range(2):
+        mask = mask_ref[side].astype(jnp.bfloat16)
+        terms = [
+            jnp.dot(mask, wave[side], preferred_element_type=jnp.float32)
+            for wave in (wave_hi, wave_lo)
+        ]
+        out_ref[side] = terms[0] + terms[1]
+
+
+def frame_tables(response_ref, f):
+    half = response_ref.shape[-1] // 2
+    tables = []
+    for side in range(2):
+        row = response_ref[side, pl.ds(f, 1), :]
+        parts = []
+        for at in (0, half):
+            spread = jnp.broadcast_to(row[:, at : at + half], (half, half))
+            turned = pltpu.roll(spread, 0, 1, stride=1, stride_axis=0)
+            if side:
+                before = lax.broadcasted_iota(jnp.int32, (half, half), 1) < (
+                    lax.broadcasted_iota(jnp.int32, (half, half), 0)
+                )
+                turned = jnp.where(before, -turned, turned)
+            parts.append(turned)
+        re, im = parts
+        tables.append(
+            split(jnp.concatenate([jnp.concatenate([re, im], 1), jnp.concatenate([-im, re], 1)], 0))
+        )
+    return tables
 
 
 def normal_frame(maps_ref, field_re, field_im, tables):
@@ -166,22 +199,17 @@
                     out_ref[d, g, t // half] = turned[at : at + cols]
 
 
-def mask_tables_kernel(mask_ref, in_hi, in_lo, out_hi, out_lo, hi_ref, lo_ref):
-    for side in range(2):
-        row = mask_ref[0, side : side + 1, :].astype(jnp.bfloat16)
-        left = (in_hi[side] * row, in_lo[side] * row)
-        hi_ref[0, side], lo_ref[0, side] = split(dot3(left, (out_hi[side], out_lo[side])))
-
-
-def base_kernel(kspace_ref, mask_ref, col_hi, col_lo, row_hi, row_lo, out_ref, data, arrived):
+def base_kernel(
+    start, frames, kspace_ref, mask_ref, col_hi, col_lo, row_hi, row_lo, out_ref, data, arrived
+):
     own, _, _, half_cols, length = out_ref.shape
     half = length // 2
-    frame, frames = pl.program_id(0), pl.num_programs(0)
+    frame = pl.program_id(0)
 
     def fetch(f, slot):
         return [
             pltpu.make_async_copy(
-                kspace_ref.at[:, odd, f + c * frames, :],
+                kspace_ref.at[:, odd, start + f + c * frames, :],
                 data.at[slot, c, pl.ds(odd * half, half)],
                 arrived.at[slot, c, odd],
             )
@@ -194,7 +222,7 @@
         for copy in fetch(0, 0):
             copy.start()
 
-    @pl.when(frame + 1 < frames)
+    @pl.when(frame + 1 < pl.num_programs(0))
     def _():
         for copy in fetch(frame + 1, (frame + 1) % 2):
             copy.start()
@@ -254,7 +282,10 @@
         ref[:, 0, 1] = total_im.reshape(blocks, span // blocks, length)
 
 
-def first_normal_kernel(coils, got_ref, hi_ref, lo_ref, maps_out, field_out, grad_out):
+def first_normal_kernel(
+    coils, got_ref, mask_ref, wave_hi, wave_lo, maps_out, field_out, grad_out, responses
+):
+    mask_responses(mask_ref, wave_hi, wave_lo, responses)
     devices, groups, _, cols, lanes = got_ref.shape
     frames = field_out.shape[0]
     per = (coils + frames) // groups
@@ -267,25 +298,27 @@
                 out[base + c, :, :, h * lanes : (h + 1) * lanes] = exchanged[c]
 
     def one(f, _):
-        tables = [(hi_ref[f, side], lo_ref[f, side]) for side in range(2)]
         grad_out[f, 0], grad_out[f, 1] = normal_frame(
-            maps_out, field_out[f, 0], field_out[f, 1], tables
+            maps_out, field_out[f, 0], field_out[f, 1], frame_tables(responses, f)
         )
         return 0
 
     lax.fori_loop(0, frames, one, 0)
 
 
-def steps_kernel(field_ref, grad_ref, b0_ref, b1_ref, maps_ref, hi_ref, lo_ref, out_ref, field, grad):
+def steps_kernel(field_ref, grad_ref, b0_ref, b1_ref, maps_ref, mask_ref, *refs):
+    wave_hi, wave_lo, out_ref, field, grad, responses = refs
     frames, _, cols, length = field_ref.shape
     devices, _, _, lanes = out_ref.shape
+    mask_responses(mask_ref, wave_hi, wave_lo, responses)
     data_term = jnp.concatenate([b0_ref[...], b1_ref[...]], 0)
     field[...] = tv_step(field_ref[...] - step_size * (grad_ref[...] - data_term))
     for sweep in range(1, OUTER):
 
         def one(f, _):
-            tables = [(hi_ref[f, side], lo_ref[f, side]) for side in range(2)]
-            grad[f, 0], grad[f, 1] = normal_frame(maps_ref, field[f, 0], field[f, 1], tables)
+            grad[f, 0], grad[f, 1] = normal_frame(
+                maps_ref, field[f, 0], field[f, 1], frame_tables(responses, f)
+            )
             return 0
 
         lax.fori_loop(0, frames, one, 0)
@@ -312,8 +345,8 @@
         out_ref[:, t * LANES : (t + 1) * LANES] = tiles[t]
 
 
-def params(**more):
-    return pltpu.CompilerParams(vmem_limit_bytes=VMEM_LIMIT, **more)
+def params(limit=VMEM_LIMIT):
+    return pltpu.CompilerParams(vmem_limit_bytes=limit)
 
 
 def cost(flops, moved):
@@ -335,20 +368,21 @@
     return jax.ShapeDtypeStruct(shape, jnp.float32)
 
 
-def scatter_sum(keep, send, order, device):
+def exchange(send, bit):
     devices = lax.axis_size("coil")
-    bits = len(order)
-    rest = keep.shape[1:]
-    lead = [2] * bits
-    lead[order[0]] = 1
-    route = lambda bit: [(i, i ^ (1 << bit)) for i in range(devices)]
-    value = (keep + lax.ppermute(send, "coil", route(order[0]))).reshape(*lead, *rest)
-    for bit in order[1:]:
-        mine = (device >> bit) & 1
-        keep = lax.dynamic_index_in_dim(value, mine, bit, keepdims=True)
-        send = lax.dynamic_index_in_dim(value, 1 - mine, bit, keepdims=True)
-        value = keep + lax.ppermute(send, "coil", route(bit))
-    return value.reshape(rest)
+    return lax.ppermute(send, "coil", [(i, i ^ (1 << bit)) for i in range(devices)])
+
+
+def halve(keep, got, bit, device):
+    mine = (device >> bit) & 1
+
+    def part(which):
+        return lax.dynamic_index_in_dim(
+            keep, which, bit, keepdims=True
+        ) + lax.dynamic_index_in_dim(got, which, bit, keepdims=True)
+
+    send = part(1 - mine)
+    return part(mine), send
 
 
 def kernel_path(image, sens, kspace, mask):
@@ -373,16 +407,12 @@
     lanes_k = [k[0::2], k[1::2]]
     inverse = [packed_right(dft(y, ks, length)) for ks in lanes_k]
     row_hi, row_lo = two_terms(np.stack(inverse) / np.sqrt(length))
-    forward = [packed_right(dft(ks, y, length).conj()) for ks in lanes_k]
-    in_hi, in_lo = two_terms(np.stack(forward) / np.sqrt(hl))
-    out_hi, out_lo = two_terms(np.stack(inverse) / np.sqrt(hl) * 0.5)
+    waves = [dft(ks, y, length) * 0.5 / hl for ks in lanes_k]
+    wave_hi, wave_lo = two_terms(np.stack([np.concatenate([w.real, w.imag], 1) for w in waves]))
 
     sampled = mask.astype(jnp.float32)
-    mask_even, mask_odd = sampled[:, 0::2], sampled[:, 1::2]
-    mask_lanes = jnp.concatenate([mask_even, mask_odd], 1)[:, None, :]
-    mask_packed = jnp.stack(
-        [jnp.concatenate([mask_even] * 2, 1), jnp.concatenate([mask_odd] * 2, 1)], 1
-    )
+    mask_sides = jnp.stack([sampled[:, 0::2], sampled[:, 1::2]])
+    mask_lanes = jnp.concatenate([mask_sides[0], mask_sides[1]], 1)[:, None, :]
 
     sens_rows = sens.reshape(rows * coils, packed)
     image_rows = image.reshape(rows * frames, packed)
@@ -410,58 +440,59 @@
             cost_estimate=cost(0, 2 * (sens.size + image.size) * 4),
         )(*[sens_rows] * (packed // LANES), *[image_rows] * (packed // LANES))
 
-    with jax.named_scope("mask_tables"):
-        table = jax.ShapeDtypeStruct((frames, 2, length, length), jnp.bfloat16)
-        block = pl.BlockSpec((1, 2, length, length), lambda f: (f, 0, 0, 0))
-        table_hi, table_lo = pl.pallas_call(
-            mask_tables_kernel,
-            grid=(frames,),
-            out_shape=(table, table),
-            in_specs=[pl.BlockSpec((1, 2, length), lambda f: (f, 0, 0))]
-            + [whole((2, length, length))] * 4,
-            out_specs=(block, block),
+    streams = 2
+    count = frames // streams
+    with jax.named_scope("data_transform"):
+        bases = [
+            pl.pallas_call(
+                functools.partial(base_kernel, start, frames),
+                grid=(count,),
+                out_shape=f32(own, count, 2, half, length),
+                in_specs=[
+                    pl.BlockSpec(memory_space=pl.ANY),
+                    pl.BlockSpec((1, 1, length), lambda f, start=start: (start + f, 0, 0)),
+                    whole((packed, packed)),
+                    whole((packed, packed)),
+                    whole((2, length, length)),
+                    whole((2, length, length)),
+                ],
+                out_specs=pl.BlockSpec((own, 1, 2, half, length), lambda f: (0, f, 0, 0, 0)),
+                scratch_shapes=[
+                    pltpu.VMEM((2, own, length, packed), jnp.float32),
+                    pltpu.SemaphoreType.DMA((2, own, 2)),
+                ],
+                compiler_params=params(TRANSFORM_LIMIT),
+                cost_estimate=cost(
+                    pairs * 6 * 6 * half * half * length // streams, 2 * kspace.size * 4 // streams
+                ),
+            )(kspace.reshape(hl, 2, pairs, packed), mask_lanes, col_hi, col_lo, row_hi, row_lo)
+            for start in range(0, frames, count)
+        ]
+
+    field = f32(frames, 2, cols, length)
+    normal_cost = 6 * 2 * frames * coils * cols * length * length
+
+    responses = pltpu.VMEM((2, frames, length), jnp.float32)
+
+    def first_gradient(column_maps):
+        return pl.pallas_call(
+            functools.partial(first_normal_kernel, coils),
+            out_shape=(f32(coils, 2, cols, length), field, field),
+            scratch_shapes=[responses],
             compiler_params=params(),
-            cost_estimate=cost(2 * 3 * 2 * frames * length**3, frames * 8 * length**2),
-        )(mask_packed, in_hi, in_lo, out_hi, out_lo)
-
-    with jax.named_scope("data_transform"):
-        base = pl.pallas_call(
-            base_kernel,
-            grid=(frames,),
-            out_shape=f32(own, frames, 2, half, length),
-            in_specs=[
-                pl.BlockSpec(memory_space=pl.ANY),
-                pl.BlockSpec((1, 1, length), lambda f: (f, 0, 0)),
-                whole((packed, packed)),
-                whole((packed, packed)),
-                whole((2, length, length)),
-                whole((2, length, length)),
-            ],
-            out_specs=pl.BlockSpec((own, 1, 2, half, length), lambda f: (0, f, 0, 0, 0)),
-            scratch_shapes=[
-                pltpu.VMEM((2, own, length, packed), jnp.float32),
-                pltpu.SemaphoreType.DMA((2, own, 2)),
-            ],
-            compiler_params=params(),
-            cost_estimate=cost(pairs * 6 * 6 * half * half * length, 2 * kspace.size * 4),
-        )(
-            kspace.reshape(hl, 2, pairs, packed), mask_lanes, col_hi, col_lo, row_hi, row_lo
-        )
-
-    column_blocks, base, table_hi, table_lo = lax.optimization_barrier(
-        (column_blocks, base, table_hi, table_lo)
-    )
+            cost_estimate=cost(normal_cost, 4 * sens.size * 4),
+            name="first_gradient",
+        )(column_maps, mask_sides, wave_hi, wave_lo)
+
+    column_blocks, bases = lax.optimization_barrier((column_blocks, bases))
     with jax.named_scope("column_maps"):
         column_maps = lax.all_to_all(column_blocks, "coil", 0, 0, tiled=True)
 
     with jax.named_scope("data_term"):
         bit = (device & 1).astype(jnp.int32)[None]
-        streams = 2
-        count = frames // streams
         orders = [list(range(bits)), [0] + list(range(2, bits)) + [1]]
         terms = []
         for stream in range(streams):
-            start = stream * count
             out = f32(devices // 2, count, 2, cols, length)
             block = pl.BlockSpec((devices // 2, 1, 2, cols, length), lambda i: (0, i, 0, 0, 0))
             keep, send = pl.pallas_call(
@@ -471,35 +502,36 @@
                 in_specs=[
                     pl.BlockSpec(memory_space=pltpu.SMEM),
                     whole((devices, own, rows, packed)),
-                    pl.BlockSpec(
-                        (own, 1, 2, half, length), lambda i, start=start: (0, start + i, 0, 0, 0)
-                    ),
+                    pl.BlockSpec((own, 1, 2, half, length), lambda i: (0, i, 0, 0, 0)),
                 ],
                 out_specs=(block, block),
                 scratch_shapes=[pltpu.VMEM((own, 2, half, length), jnp.float32)],
                 compiler_params=params(),
-                cost_estimate=cost(0, base.size * 4 // 2 + 2 * out.size * 4),
-            )(bit, coil_maps, base)
-            terms.append(scatter_sum(keep, send, orders[stream], device))
-
-    with jax.named_scope("first_gradient"):
-        field = f32(frames, 2, cols, length)
-        normal_cost = 6 * 2 * frames * coils * cols * length * length
-        maps, field0, grad0 = pl.pallas_call(
-            functools.partial(first_normal_kernel, coils),
-            out_shape=(f32(coils, 2, cols, length), field, field),
-            compiler_params=params(),
-            cost_estimate=cost(normal_cost, 4 * sens.size * 4),
-        )(column_maps, table_hi, table_lo)
+                cost_estimate=cost(0, bases[stream].size * 4 + 2 * out.size * 4),
+            )(bit, coil_maps, bases[stream])
+            lead = [1] + [2] * (bits - 1)
+            got = exchange(send, 0).reshape(*lead, *keep.shape[1:])
+            terms.append((keep.reshape(got.shape), got))
+        for step in range(1, bits):
+            halves = [halve(*terms[i], orders[i][step], device) for i in range(streams)]
+            if step == 2:
+                column_maps, halves = lax.optimization_barrier((column_maps, halves))
+            terms = [
+                (keep, exchange(send, orders[i][step])) for i, (keep, send) in enumerate(halves)
+            ]
+            if step == 2:
+                maps, field0, grad0 = first_gradient(column_maps)
+                terms, grad0 = lax.optimization_barrier((terms, grad0))
+        terms = [(keep + got).reshape(count, 2, cols, length) for keep, got in terms]
 
     with jax.named_scope("outer_steps"):
         blocks = pl.pallas_call(
             steps_kernel,
             out_shape=f32(devices, 2, cols, LANES),
-            scratch_shapes=[pltpu.VMEM(field.shape, jnp.float32)] * 2,
+            scratch_shapes=[pltpu.VMEM(field.shape, jnp.float32)] * 2 + [responses],
             compiler_params=params(),
             cost_estimate=cost(normal_cost, 4 * sens.size * 4),
-        )(field0, grad0, terms[0], terms[1], maps, table_hi, table_lo)
+        )(field0, grad0, terms[0], terms[1], maps, mask_sides, wave_hi, wave_lo)
 
     with jax.named_scope("result_rows"):
         got = lax.all_to_all(blocks, "coil", 0, 0, tiled=True)

time: 133 us -> 124 us (0.932)
  Pallas kernels: 50.9 us -> 43.7 us
  other arithmetic: 4.62 us -> 8.03 us
  blocking collectives: 16.1 us -> 13.9 us
  starting transfers between devices: 25.9 us -> 24 us
    all_to_all x1, waiting for transfers between devices: 9.29 us -> 0.01 us  [kernel_path(): column_maps = lax.all_to_all(column_blocks, 'coil', 0, 0, tiled=True)]
    ppermute x8, waiting for transfers between devices: 18.4 us -> 26.4 us  [exchange(): lax.ppermute(send, 'coil', [(i, i ^ 1 << bit) for i in range(devices)])]
    pallas_call x2, Pallas kernels: 9.38 us -> 5.15 us  [kernel_path(): pl.pallas_call(weigh_kernel, grid=(count,), out_shape=(out, out), in_spec...]
    add x6, other arithmetic: 4.56 us -> 7.96 us  [part(): lax.dynamic_index_in_dim(keep, which, bit, keepdims=True)]
    pallas_call x3, Pallas kernels: 28.5 us -> 26 us  [the longest x2 17.4 us: kernel_path(): pl.pallas_call(functools.partial(base_kernel, start, frames), grid=(count...]
    all_to_all x1, blocking collectives: 16.1 us -> 13.9 us  [kernel_path(): got = lax.all_to_all(blocks, 'coil', 0, 0, tiled=True)]
    all_to_all x1, waiting for transfers between devices: 1.08 us -> 3.03 us  [kernel_path(): coil_maps = lax.all_to_all(blocks, 'coil', 0, 0, tiled=True)]
    ppermute x8, starting transfers between devices: 11.5 us -> 9.6 us  [exchange(): lax.ppermute(send, 'coil', [(i, i ^ 1 << bit) for i in range(devices)])]
  transfers between devices with their start and end apart: 10 -> 10, of which waited for: 6 -> 6; matrix products, arithmetic and copies ran while one was open for 5% -> 7% of each run, Pallas kernels for 30% -> 27%
where the time goes in v3:
time: 124 us; the launch traced here: 123 us
  Pallas kernels  43.7 us (35%)
  waiting for transfers between devices  29.4 us (24%)
  starting transfers between devices  24 us (19%)
  blocking collectives  13.9 us (11%)
  other arithmetic  8.03 us (6%)
  local copies, waits for them, and re-layouts  4.02 us (3%)
    ppermute x8, waiting for transfers between devices, exchange(): lax.ppermute(send, 'coil', [(i, i ^ 1 << bit) for i in range(devices)])  26.4 us
    pallas_call x2, Pallas kernels, kernel_path(): pl.pallas_call(functools.partial(base_kernel, start, frames), grid=(count...  17.4 us
    all_to_all x1, blocking collectives, kernel_path(): got = lax.all_to_all(blocks, 'coil', 0, 0, tiled=True)  13.9 us
    ppermute x8, starting transfers between devices, exchange(): lax.ppermute(send, 'coil', [(i, i ^ 1 << bit) for i in range(devices)])  9.6 us
    pallas_call x1, Pallas kernels, first_gradient(): pl.pallas_call(functools.partial(first_normal_kernel, coils), out_shape=(...  8.63 us
    pallas_call x1, Pallas kernels, kernel_path(): pl.pallas_call(steps_kernel, out_shape=f32(devices, 2, cols, LANES), scra...  8.03 us
    add x6, other arithmetic, part(): lax.dynamic_index_in_dim(keep, which, bit, keepdims=True)  7.96 us
    all_to_all x1, starting transfers between devices, kernel_path(): coil_maps = lax.all_to_all(blocks, 'coil', 0, 0, tiled=True)  7.52 us
  transfers between devices with their start and end apart: 10, of which 6 were waited for; matrix products, arithmetic and copies ran while one was open for 7% of the time, Pallas kernels for 27%

profile of v3, /device:TPU:0, one launch (start us, length us, event | category | flops | bytes accessed | tf_op | source)
XLA Modules:
  0.0 123.2 jit_solution(12339144316031251768)
XLA Ops:
  0.0 1.2 copy-done
  1.2 1.6 %coil_maps.1 = f32[16,2,16,512]{3,2,1,0:T(8,128)} custom-call(f32[512,512]{1,0:T(8,128)S(1)} %bitcast.17, f32[512,512]{1,0:T(8,128)S(1)} %bitcast.18, f32[512,512]{1,0:T(8,128)S(1)} %bitcast.19, f32[512,512]{1,0:T(8,128)S(1)} %bitcast.20), custom_call_target="tpu_custom_call" | custom-call | bytes 2097152 | tf_op jit(solution)/shard_map/coil_maps/pallas_call | solution.py:421
  2.9 7.5 %all-to-all-start.1 = ((f32[16,2,16,512]{3,2,1,0:T(8,128)}), f32[16,2,16,512]{3,2,1,0:T(8,128)S(1)}, u32[]{:S(2)}, u32[]{:S(2)}) async-start(f32[16,2,16,512]{3,2,1,0:T(8,128)} %coil_maps.1), calls=%async_computation.1 | async-start | bytes 2097152 | tf_op jit(solution)/shard_map/coil_maps/all_to_all | solution.py:430
  10.9 2.0 %column_maps.1 = f32[16,5,2,16,128]{4,3,2,1,0:T(8,128)} custom-call(f32[512,512]{1,0:T(8,128)S(1)} %bitcast.21, f32[512,512]{1,0:T(8,128)S(1)} %bitcast.22, f32[512,512]{1,0:T(8,128)S(1)} %bitcast.23, f32[512,512]{1,0:T(8,128)S(1)} %bitcast.24, f32[128,512]{1,0:T(8,128)S(1)} %bitcast.25, f32[128,512]{1,0:T(8,128)S(1)} %bitcast.26, f32[128,512]{1,0:T(8,128)S(1)} %bitcast.27, ...), custom_call_target="tpu_custom_call" | custom-call | bytes 2621440 | tf_op jit(solution)/shard_map/column_maps/pallas_call | solution.py:433
  12.9 8.8 %data_transform.2.base_ref = f32[2,4,2,256,256]{4,3,2,1,0:T(8,128)} custom-call(f32[128,2,16,512]{3,2,1,0:T(8,128)} %bitcast.33, f32[8,1,256]{2,1,0:T(1,128)S(1)} %copy.11.mask_ref, bf16[512,512]{1,0:T(8,128)(2,1)S(1)} %copy-done.6, bf16[512,512]{1,0:T(8,128)(2,1)S(1)} %copy-done.7, bf16[2,256,256]{2,1,0:T(8,128)(2,1)S(1)} %copy-done.8, ...), custom_call_target="tpu_custom_call" | custom-call | flops 4831838208 | bytes 8388608 | tf_op jit(solution)/shard_map/data_transform/pallas_call | solution.py:447
  21.6 8.7 %data_transform.3.base_ref = f32[2,4,2,256,256]{4,3,2,1,0:T(8,128)} custom-call(f32[128,2,16,512]{3,2,1,0:T(8,128)} %bitcast.34, f32[8,1,256]{2,1,0:T(1,128)S(1)} %copy.11.mask_ref, bf16[512,512]{1,0:T(8,128)(2,1)S(1)} %copy-done.6, bf16[512,512]{1,0:T(8,128)(2,1)S(1)} %copy-done.7, bf16[2,256,256]{2,1,0:T(8,128)(2,1)S(1)} %copy-done.8, ...), custom_call_target="tpu_custom_call" | custom-call | flops 4831838208 | bytes 8388608 | tf_op jit(solution)/shard_map/data_transform/pallas_call | solution.py:447
  30.3 3.0 %all-to-all-done.1.maps_ref = f32[16,2,16,512]{3,2,1,0:T(8,128)S(1)} async-done(((f32[16,2,16,512]{3,2,1,0:T(8,128)}), f32[16,2,16,512]{3,2,1,0:T(8,128)S(1)}, u32[]{:S(2)}, u32[]{:S(2)}) %all-to-all-start.1) | async-done | bytes 1048608 | tf_op jit(solution)/shard_map/coil_maps/all_to_all | solution.py:430
  33.3 6.9 %all-to-all-start = ((f32[16,5,2,16,128]{4,3,2,1,0:T(8,128)}), f32[16,5,2,16,128]{4,3,2,1,0:T(8,128)S(1)}, u32[]{:S(2)}, u32[]{:S(2)}) async-start(f32[16,5,2,16,128]{4,3,2,1,0:T(8,128)} %column_maps.1), calls=%async_computation | async-start | bytes 2621440 | tf_op jit(solution)/shard_map/column_maps/all_to_all | solution.py:489
  40.2 2.3 %copy-done.4 = f32[2,4,2,256,256]{4,3,2,1,0:T(8,128)S(1)} copy-done((f32[2,4,2,256,256]{4,3,2,1,0:T(8,128)S(1)}, f32[2,4,2,256,256]{4,3,2,1,0:T(8,128)}, u32[]{:S(2)}) %copy-start.4) | copy-done | bytes 4194328
  42.6 2.6 %data_term.2 = (f32[8,4,2,16,256]{4,3,2,1,0:T(8,128)S(1)}, f32[8,4,2,16,256]{4,3,2,1,0:T(8,128)}) custom-call(s32[1]{0:T(128)} %bitcast.4.bit_ref, f32[16,2,16,512]{3,2,1,0:T(8,128)S(1)} %all-to-all-done.1.maps_ref, f32[2,4,2,256,256]{4,3,2,1,0:T(8,128)S(1)} %copy-done.4), custom_call_target="tpu_custom_call" | custom-call | bytes 6291456 | tf_op jit(solution)/shard_map/data_term/pallas_call | solution.py:498
  45.6 2.6 %data_term.3 = (f32[8,4,2,16,256]{4,3,2,1,0:T(8,128)S(1)}, f32[8,4,2,16,256]{4,3,2,1,0:T(8,128)}) custom-call(s32[1]{0:T(128)} %bitcast.4.bit_ref, f32[16,2,16,512]{3,2,1,0:T(8,128)S(1)} %all-to-all-done.1.maps_ref, f32[2,4,2,256,256]{4,3,2,1,0:T(8,128)S(1)} %copy-done.3), custom_call_target="tpu_custom_call" | custom-call | bytes 6291456 | tf_op jit(solution)/shard_map/data_term/pallas_call | solution.py:498
  48.2 2.6 %dynamic-slice_add_fusion.3 = (f32[1,1,2,2,4,2,16,256]{7,6,5,4,3,2,1,0:T(8,128)S(1)}, f32[1,1,2,2,4,2,16,256]{7,6,5,4,3,2,1,0:T(8,128)}) fusion(f32[1,2,2,2,4,2,16,256]{7,6,5,4,3,2,1,0:T(8,128)} %bitcast.6, s32[]{:T(128)S(6)} %select_n.42, f32[1,2,2,2,4,2,16,256]{7,6,5,4,3,2,1,0:T(8,128)} %bitcast.30, s32[]{:T(128)S(6)} %select_n.44), kind=kLoop, calls=%fused_computation.3 | loop fusion | flops 262144 | bytes 3145736 | tf_op jit(solution)/shard_map/data_term/add | solution.py:380
  50.9 1.9 %collective-permute-start.1 = (f32[1,1,2,2,4,2,16,256]{7,6,5,4,3,2,1,0:T(8,128)}, f32[1,1,2,2,4,2,16,256]{7,6,5,4,3,2,1,0:T(8,128)}, u32[]{:S(2)}, u32[]{:S(2)}) collective-permute-start(f32[1,1,2,2,4,2,16,256]{7,6,5,4,3,2,1,0:T(8,128)} %get-tuple-element.48), channel_id=1, source_target_pairs={{0,2},{1,3},{2,0},{3,1},{4,6},{5,7},{6,4},{7,5},{8,10},{9,11},{10,... | collective-permute-start | bytes 1572872 | tf_op jit(solution)/shard_map/data_term/ppermute | solution.py:373
  52.8 2.4 %dynamic-slice_add_fusion.1 = (f32[1,2,1,2,4,2,16,256]{7,6,5,4,3,2,1,0:T(8,128)}, f32[1,2,1,2,4,2,16,256]{7,6,5,4,3,2,1,0:T(8,128)}) fusion(f32[1,2,2,2,4,2,16,256]{7,6,5,4,3,2,1,0:T(8,128)} %bitcast.8, s32[]{:T(128)S(6)} %select_n.43, f32[1,2,2,2,4,2,16,256]{7,6,5,4,3,2,1,0:T(8,128)S(1)} %bitcast.29, s32[]{:T(128)S(6)} %select_n.45), kind=kLoop, calls=%fused_computation.1 | loop fusion | flops 262144 | bytes 3145736 | tf_op jit(solution)/shard_map/data_term/add | solution.py:380
  55.2 1.5 %collective-permute-start.3 = (f32[1,2,1,2,4,2,16,256]{7,6,5,4,3,2,1,0:T(8,128)}, f32[1,2,1,2,4,2,16,256]{7,6,5,4,3,2,1,0:T(8,128)S(1)}, u32[]{:S(2)}, u32[]{:S(2)}) collective-permute-start(f32[1,2,1,2,4,2,16,256]{7,6,5,4,3,2,1,0:T(8,128)} %get-tuple-element.46), channel_id=1, source_target_pairs={{0,4},{1,5},{2,6},{3,7},{4,0},{5,1},{6,2},{7,3},{8,12},{9,13},{10,... | collective-permute-start | bytes 1572872 | tf_op jit(solution)/shard_map/data_term/ppermute | solution.py:373
  56.6 14.6 %collective-permute-done.1 = f32[1,1,2,2,4,2,16,256]{7,6,5,4,3,2,1,0:T(8,128)} collective-permute-done((f32[1,1,2,2,4,2,16,256]{7,6,5,4,3,2,1,0:T(8,128)}, f32[1,1,2,2,4,2,16,256]{7,6,5,4,3,2,1,0:T(8,128)}, u32[]{:S(2)}, u32[]{:S(2)}) %collective-permute-start.1) | collective-permute-done | bytes 524320 | tf_op jit(solution)/shard_map/data_term/ppermute | solution.py:373
  72.3 3.3 %collective-permute-done.3 = f32[1,2,1,2,4,2,16,256]{7,6,5,4,3,2,1,0:T(8,128)S(1)} collective-permute-done((f32[1,2,1,2,4,2,16,256]{7,6,5,4,3,2,1,0:T(8,128)}, f32[1,2,1,2,4,2,16,256]{7,6,5,4,3,2,1,0:T(8,128)S(1)}, u32[]{:S(2)}, u32[]{:S(2)}) %collective-permute-start.3) | collective-permute-done | bytes 524320 | tf_op jit(solution)/shard_map/data_term/ppermute | solution.py:373
  75.6 1.8 %dynamic-slice_add_fusion.4 = (f32[1,2,1,1,4,2,16,256]{7,6,5,4,3,2,1,0:T(8,128)}, f32[1,2,1,1,4,2,16,256]{7,6,5,4,3,2,1,0:T(8,128)S(1)}) fusion(f32[1,2,1,2,4,2,16,256]{7,6,5,4,3,2,1,0:T(8,128)S(1)} %collective-permute-done.3, s32[]{:T(128)S(6)} %select_n.47, f32[1,2,1,2,4,2,16,256]{7,6,5,4,3,2,1,0:T(8,128)} %get-tuple-element.45, s32[]{:T(128)S(6)} %select_n.46), kind=kLoop, calls=%fused_computation.4 | loop fusion | flops 131072 | bytes 1572872 | tf_op jit(solution)/shard_map/data_term/add | solution.py:380
  78.1 3.8 %collective-permute-start.5 = (f32[1,2,1,1,4,2,16,256]{7,6,5,4,3,2,1,0:T(8,128)}, f32[1,2,1,1,4,2,16,256]{7,6,5,4,3,2,1,0:T(8,128)S(1)}, u32[]{:S(2)}, u32[]{:S(2)}) collective-permute-start(f32[1,2,1,1,4,2,16,256]{7,6,5,4,3,2,1,0:T(8,128)} %get-tuple-element.37), channel_id=1, source_target_pairs={{0,8},{1,9},{2,10},{3,11},{4,12},{5,13},{6,14},{7,15},{8,0},{9,1},... | collective-permute-start | bytes 786440 | tf_op jit(solution)/shard_map/data_term/ppermute | solution.py:373
  82.0 8.6 %first_gradient.1 = (f32[32,2,16,256]{3,2,1,0:T(8,128)S(1)}, f32[8,2,16,256]{3,2,1,0:T(8,128)S(1)}, f32[8,2,16,256]{3,2,1,0:T(8,128)S(1)}) custom-call(f32[16,5,2,16,128]{4,3,2,1,0:T(8,128)S(1)} %all-to-all-done.got_ref, f32[2,8,128]{2,1,0:T(8,128)S(1)} %pad_maximum_fusion.mask_ref, bf16[2,128,256]{2,1,0:T(8,128)(2,1)S(1)} %copy-done.10, ...), custom_call_target="tpu_custom_call" | custom-call | flops 3221225472 | bytes 4194304 | tf_op jit(solution)/shard_map/data_term/first_gradient/pallas_call | solution.py:478
  90.9 2.1 %collective-permute-done.5 = f32[1,2,1,1,4,2,16,256]{7,6,5,4,3,2,1,0:T(8,128)S(1)} collective-permute-done((f32[1,2,1,1,4,2,16,256]{7,6,5,4,3,2,1,0:T(8,128)}, f32[1,2,1,1,4,2,16,256]{7,6,5,4,3,2,1,0:T(8,128)S(1)}, u32[]{:S(2)}, u32[]{:S(2)}) %collective-permute-start.5) | collective-permute-done | bytes 262176 | tf_op jit(solution)/shard_map/data_term/ppermute | solution.py:373
  94.3 6.0 %collective-permute-done.6 = f32[1,1,1,1,4,2,16,256]{7,6,5,4,3,2,1,0:T(8,128)S(1)} collective-permute-done((f32[1,1,1,1,4,2,16,256]{7,6,5,4,3,2,1,0:T(8,128)S(1)}, f32[1,1,1,1,4,2,16,256]{7,6,5,4,3,2,1,0:T(8,128)S(1)}, u32[]{:S(2)}, u32[]{:S(2)}) %collective-permute-start.6) | collective-permute-done | bytes 131104 | tf_op jit(solution)/shard_map/data_term/ppermute | solution.py:373
  100.4 8.0 %outer_steps.1 = f32[16,2,16,128]{3,2,1,0:T(8,128)S(1)} custom-call(f32[8,2,16,256]{3,2,1,0:T(8,128)S(1)} %get-tuple-element.33.field_ref, f32[8,2,16,256]{3,2,1,0:T(8,128)S(1)} %get-tuple-element.39.grad_ref, f32[4,2,16,256]{3,2,1,0:T(8,128)S(1)} %add_bitcast_fusion.1.b0_ref, f32[4,2,16,256]{3,2,1,0:T(8,128)S(1)} %add_bitcast_fusion.b1_ref, ...), custom_call_target="tpu_custom_call" | custom-call | flops 3221225472 | bytes 4194304 | tf_op jit(solution)/shard_map/outer_steps/pallas_call | solution.py:528
  108.4 13.9 %all_to_all.15.got_ref = f32[16,2,16,128]{3,2,1,0:T(8,128)S(1)} all-to-all(f32[16,2,16,128]{3,2,1,0:T(8,128)S(1)} %outer_steps.1), channel_id=1, replica_groups=mesh['plane'=2,'coil'=16] {'coil'}, dimensions={0} | all-to-all | bytes 524288 | tf_op jit(solution)/shard_map/result_rows/all_to_all | solution.py:537
  (46 shorter events, 5.3 us)
Async XLA Ops:
  0.0 1.2 copy-start
  1.2 9.2 %copy-start.12 = (s32[8,256]{1,0:T(8,128)S(1)}, s32[8,256]{1,0:T(8,128)}, u32[]{:S(2)}) copy-start(s32[8,256]{1,0:T(8,128)} %param.13) | copy-start | bytes 24580
  1.2 9.6 %copy-start.1 = (f32[16,32,512]{2,1,0:T(8,128)S(1)}, f32[16,32,512]{2,1,0:T(8,128)}, u32[]{:S(2)}) copy-start(f32[16,32,512]{2,1,0:T(8,128)} %param.11) | copy-start | bytes 3145732
  1.2 9.6 %copy-start.2 = (f32[16,8,512]{2,1,0:T(8,128)S(1)}, f32[16,8,512]{2,1,0:T(8,128)}, u32[]{:S(2)}) copy-start(f32[16,8,512]{2,1,0:T(8,128)} %param.10) | copy-start | bytes 786436
  2.9 10.0 %copy-start.6 = (bf16[512,512]{1,0:T(8,128)(2,1)S(1)}, bf16[512,512]{1,0:T(8,128)(2,1)}, u32[]{:S(2)}) copy-start(bf16[512,512]{1,0:T(8,128)(2,1)} %constant.86.clone.col_hi) | copy-start | bytes 1572868
  2.9 10.0 %copy-start.7 = (bf16[512,512]{1,0:T(8,128)(2,1)S(1)}, bf16[512,512]{1,0:T(8,128)(2,1)}, u32[]{:S(2)}) copy-start(bf16[512,512]{1,0:T(8,128)(2,1)} %constant.87.clone.col_lo) | copy-start | bytes 1572868
  2.9 30.5 %all-to-all-start.1 = ((f32[16,2,16,512]{3,2,1,0:T(8,128)}), f32[16,2,16,512]{3,2,1,0:T(8,128)S(1)}, u32[]{:S(2)}, u32[]{:S(2)}) async-start(f32[16,2,16,512]{3,2,1,0:T(8,128)} %coil_maps.1), calls=%async_computation.1 | async-start | bytes 2097152 | tf_op jit(solution)/shard_map/coil_maps/all_to_all | solution.py:430
  10.8 2.0 %copy-start.8 = (bf16[2,256,256]{2,1,0:T(8,128)(2,1)S(1)}, bf16[2,256,256]{2,1,0:T(8,128)(2,1)}, u32[]{:S(2)}) copy-start(bf16[2,256,256]{2,1,0:T(8,128)(2,1)} %constant.88.clone.row_hi) | copy-start | bytes 786436
  10.8 2.0 %copy-start.9 = (bf16[2,256,256]{2,1,0:T(8,128)(2,1)S(1)}, bf16[2,256,256]{2,1,0:T(8,128)(2,1)}, u32[]{:S(2)}) copy-start(bf16[2,256,256]{2,1,0:T(8,128)(2,1)} %constant.89.clone.row_lo) | copy-start | bytes 786436
  33.3 44.1 %all-to-all-start = ((f32[16,5,2,16,128]{4,3,2,1,0:T(8,128)}), f32[16,5,2,16,128]{4,3,2,1,0:T(8,128)S(1)}, u32[]{:S(2)}, u32[]{:S(2)}) async-start(f32[16,5,2,16,128]{4,3,2,1,0:T(8,128)} %column_maps.1), calls=%async_computation | async-start | bytes 2621440 | tf_op jit(solution)/shard_map/column_maps/all_to_all | solution.py:489
  40.2 5.3 %copy-start.3 = (f32[2,4,2,256,256]{4,3,2,1,0:T(8,128)S(1)}, f32[2,4,2,256,256]{4,3,2,1,0:T(8,128)}, u32[]{:S(2)}) copy-start(f32[2,4,2,256,256]{4,3,2,1,0:T(8,128)} %data_transform.3.base_ref) | copy-start | bytes 12582916
  40.2 2.3 %copy-start.4 = (f32[2,4,2,256,256]{4,3,2,1,0:T(8,128)S(1)}, f32[2,4,2,256,256]{4,3,2,1,0:T(8,128)}, u32[]{:S(2)}) copy-start(f32[2,4,2,256,256]{4,3,2,1,0:T(8,128)} %data_transform.2.base_ref) | copy-start | bytes 12582916
  45.1 3.0 %copy-start.5 = (f32[8,4,2,16,256]{4,3,2,1,0:T(8,128)}, f32[8,4,2,16,256]{4,3,2,1,0:T(8,128)S(1)}, u32[]{:S(2)}) copy-start(f32[8,4,2,16,256]{4,3,2,1,0:T(8,128)S(1)} %get-tuple-element.27) | copy-start | bytes 3145732
  45.1 3.1 %collective-permute-start = (f32[8,4,2,16,256]{4,3,2,1,0:T(8,128)}, f32[8,4,2,16,256]{4,3,2,1,0:T(8,128)}, u32[]{:S(2)}, u32[]{:S(2)}) collective-permute-start(f32[8,4,2,16,256]{4,3,2,1,0:T(8,128)} %get-tuple-element.28), channel_id=1, source_target_pairs={{0,1},{1,0},{2,3},{3,2},{4,5},{5,4},{6,7},{7,6},{8,9},{9,8},{10,11... | collective-permute-start | bytes 3145736 | tf_op jit(solution)/shard_map/data_term/ppermute | solution.py:373
  48.1 4.7 %collective-permute-start.2 = (f32[8,4,2,16,256]{4,3,2,1,0:T(8,128)}, f32[8,4,2,16,256]{4,3,2,1,0:T(8,128)}, u32[]{:S(2)}, u32[]{:S(2)}) collective-permute-start(f32[8,4,2,16,256]{4,3,2,1,0:T(8,128)} %get-tuple-element.31), channel_id=1, source_target_pairs={{0,1},{1,0},{2,3},{3,2},{4,5},{5,4},{6,7},{7,6},{8,9},{9,8},{10,11... | collective-permute-start | bytes 3145736 | tf_op jit(solution)/shard_map/data_term/ppermute | solution.py:373
  48.2 33.7 %copy-start.10 = (bf16[2,128,256]{2,1,0:T(8,128)(2,1)S(1)}, bf16[2,128,256]{2,1,0:T(8,128)(2,1)}, u32[]{:S(2)}) copy-start(bf16[2,128,256]{2,1,0:T(8,128)(2,1)} %constant.90.clone.wave_hi.refs_0_) | copy-start | bytes 393220
  48.2 33.7 %copy-start.11 = (bf16[2,128,256]{2,1,0:T(8,128)(2,1)S(1)}, bf16[2,128,256]{2,1,0:T(8,128)(2,1)}, u32[]{:S(2)}) copy-start(bf16[2,128,256]{2,1,0:T(8,128)(2,1)} %constant.91.clone.wave_lo.refs_1_) | copy-start | bytes 393220
  50.9 20.3 %collective-permute-start.1 = (f32[1,1,2,2,4,2,16,256]{7,6,5,4,3,2,1,0:T(8,128)}, f32[1,1,2,2,4,2,16,256]{7,6,5,4,3,2,1,0:T(8,128)}, u32[]{:S(2)}, u32[]{:S(2)}) collective-permute-start(f32[1,1,2,2,4,2,16,256]{7,6,5,4,3,2,1,0:T(8,128)} %get-tuple-element.48), channel_id=1, source_target_pairs={{0,2},{1,3},{2,0},{3,1},{4,6},{5,7},{6,4},{7,5},{8,10},{9,11},{10,... | collective-permute-start | bytes 1572872 | tf_op jit(solution)/shard_map/data_term/ppermute | solution.py:373
  55.2 20.5 %collective-permute-start.3 = (f32[1,2,1,2,4,2,16,256]{7,6,5,4,3,2,1,0:T(8,128)}, f32[1,2,1,2,4,2,16,256]{7,6,5,4,3,2,1,0:T(8,128)S(1)}, u32[]{:S(2)}, u32[]{:S(2)}) collective-permute-start(f32[1,2,1,2,4,2,16,256]{7,6,5,4,3,2,1,0:T(8,128)} %get-tuple-element.46), channel_id=1, source_target_pairs={{0,4},{1,5},{2,6},{3,7},{4,0},{5,1},{6,2},{7,3},{8,12},{9,13},{10,... | collective-permute-start | bytes 1572872 | tf_op jit(solution)/shard_map/data_term/ppermute | solution.py:373
  77.5 13.4 %collective-permute-start.4 = (f32[1,1,1,2,4,2,16,256]{7,6,5,4,3,2,1,0:T(8,128)S(1)}, f32[1,1,1,2,4,2,16,256]{7,6,5,4,3,2,1,0:T(8,128)S(1)}, u32[]{:S(2)}, u32[]{:S(2)}) collective-permute-start(f32[1,1,1,2,4,2,16,256]{7,6,5,4,3,2,1,0:T(8,128)S(1)} %get-tuple-element.35), channel_id=1, source_target_pairs={{0,4},{1,5},{2,6},{3,7},{4,0},{5,1},{6,2},{7,3},{8,12},{9,13},{10,... | collective-permute-start | bytes 786440 | tf_op jit(solution)/shard_map/data_term/ppermute | solution.py:373
  78.1 14.9 %collective-permute-start.5 = (f32[1,2,1,1,4,2,16,256]{7,6,5,4,3,2,1,0:T(8,128)}, f32[1,2,1,1,4,2,16,256]{7,6,5,4,3,2,1,0:T(8,128)S(1)}, u32[]{:S(2)}, u32[]{:S(2)}) collective-permute-start(f32[1,2,1,1,4,2,16,256]{7,6,5,4,3,2,1,0:T(8,128)} %get-tuple-element.37), channel_id=1, source_target_pairs={{0,8},{1,9},{2,10},{3,11},{4,12},{5,13},{6,14},{7,15},{8,0},{9,1},... | collective-permute-start | bytes 786440 | tf_op jit(solution)/shard_map/data_term/ppermute | solution.py:373
  93.0 7.3 %collective-permute-start.6 = (f32[1,1,1,1,4,2,16,256]{7,6,5,4,3,2,1,0:T(8,128)S(1)}, f32[1,1,1,1,4,2,16,256]{7,6,5,4,3,2,1,0:T(8,128)S(1)}, u32[]{:S(2)}, u32[]{:S(2)}) collective-permute-start(f32[1,1,1,1,4,2,16,256]{7,6,5,4,3,2,1,0:T(8,128)S(1)} %dynamic-slice_add_fusion.9), channel_id=1, source_target_pairs={{0,8},{1,9},{2,10},{3,11},{4,12},{5,13},{6,14},{7,15},{8,0},{9,1},... | collective-permute-start | bytes 393224 | tf_op jit(solution)/shard_map/data_term/ppermute | solution.py:373
  93.2 7.2 %collective-permute-start.7 = (f32[1,1,1,1,4,2,16,256]{7,6,5,4,3,2,1,0:T(8,128)S(1)}, f32[1,1,1,1,4,2,16,256]{7,6,5,4,3,2,1,0:T(8,128)S(1)}, u32[]{:S(2)}, u32[]{:S(2)}) collective-permute-start(f32[1,1,1,1,4,2,16,256]{7,6,5,4,3,2,1,0:T(8,128)S(1)} %dynamic-slice_add_fusion.8), channel_id=1, source_target_pairs={{0,2},{1,3},{2,0},{3,1},{4,6},{5,7},{6,4},{7,5},{8,10},{9,11},{10,... | collective-permute-start | bytes 393224 | tf_op jit(solution)/shard_map/data_term/ppermute | solution.py:373

commit v4 on v3

--- a/solution.py
+++ b/solution.py
@@ -14,6 +14,7 @@
 LANES = 128
 VMEM_LIMIT = 16 * 1024 * 1024
 TRANSFORM_LIMIT = 52 * 1024 * 1024
+WEIGH_LIMIT = 60 * 1024 * 1024
 
 step_size = 0.5
 tv_weight = 0.1
@@ -167,42 +168,54 @@
 
 
 def coil_blocks_kernel(coils, *refs):
-    *tiles, out_ref = refs
-    devices, own, rows, _ = out_ref.shape
+    *tiles, before, out_ref = refs
+    del before
+    devices, pair_coils, rows, lanes = out_ref.shape
+    halves = len(tiles) // 2
+    each = lanes // (2 * LANES)
     for d in range(devices):
-        for c in range(own):
-            for t, ref in enumerate(tiles):
-                out_ref[d, c, :, t * LANES : (t + 1) * LANES] = ref[
-                    pl.ds(d * own + c, rows, stride=coils), :
-                ]
-
-
-def column_blocks_kernel(coils, frames, chunk_of, *refs):
-    *tiles, out_ref = refs
+        for c in range(pair_coils):
+            for part in range(2):
+                for t in range(each):
+                    at = (part * each + t) * LANES
+                    out_ref[d, c, :, at : at + LANES] = tiles[part * halves + (d & 1) * each + t][
+                        pl.ds((d >> 1) * pair_coils + c, rows, stride=coils), :
+                    ]
+
+
+def with_bit(index, bit, value):
+    return ((index >> bit) << (bit + 1)) | (value << bit) | (index & ((1 << bit) - 1))
+
+
+def column_blocks_kernel(coils, frames, chunk_of, level, device_ref, *refs):
+    *tiles, keep_ref, send_ref, turned = refs
     sens_tiles, image_tiles = tiles[: len(tiles) // 2], tiles[len(tiles) // 2 :]
-    devices, groups, _, cols, _ = out_ref.shape
+    blocks, groups, _, cols, _ = keep_ref.shape
     rows = sens_tiles[0].shape[0] // coils
     per = LANES // rows
     half = len(sens_tiles) // 2
+    mine = (device_ref[0] >> level) & 1
+    far = chunk_of[1 << level] * cols
     for g in range(groups):
         if g * per < coils:
             tiles, count, base = sens_tiles, coils, g * per
         else:
             tiles, count, base = image_tiles, frames, g * per - coils
         for t, ref in enumerate(tiles):
-            turned = jnp.concatenate(
+            turned[t // half, pl.ds(t % half * LANES, LANES)] = jnp.concatenate(
                 [ref[pl.ds(base + c, rows, stride=count), :] for c in range(per)], 0
             ).T
-            for d in range(devices):
-                at = chunk_of[d] * cols - t % half * LANES
-                if 0 <= at < LANES:
-                    out_ref[d, g, t // half] = turned[at : at + cols]
-
-
-def base_kernel(
-    start, frames, kspace_ref, mask_ref, col_hi, col_lo, row_hi, row_lo, out_ref, data, arrived
-):
-    own, _, _, half_cols, length = out_ref.shape
+        for out, side in ((keep_ref, mine), (send_ref, 1 - mine)):
+            for e in range(blocks):
+                at = pl.multiple_of(chunk_of[with_bit(e, level, 0)] * cols + side * far, cols)
+                for part in range(2):
+                    out[e, g, part] = turned[part, pl.ds(at, cols)]
+
+
+def base_kernel(start, frames, device_ref, kspace_ref, mask_ref, *refs):
+    col_hi, col_lo, row_hi, row_lo, keep_ref, send_ref, data, near_hi, near_lo, arrived = refs
+    own, _, _, span, length = keep_ref.shape
+    bit = device_ref[0] & 1
     half = length // 2
     frame = pl.program_id(0)
 
@@ -221,6 +234,11 @@
     def _():
         for copy in fetch(0, 0):
             copy.start()
+        for far, near in ((col_hi, near_hi), (col_lo, near_lo)):
+            for i, which in enumerate((bit, 1 - bit)):
+                for part in range(2):
+                    at = pl.multiple_of((2 * part + which) * span, span)
+                    near[pl.ds((2 * i + part) * span, span)] = far[pl.ds(at, span)]
 
     @pl.when(frame + 1 < pl.num_programs(0))
     def _():
@@ -231,88 +249,130 @@
     for copy in fetch(frame, slot):
         copy.wait()
     columns = [
-        dot3((col_hi[...], col_lo[...]), split(data[slot, c]), ((1,), (1,))) * mask_ref[0]
+        dot3((near_hi[...], near_lo[...]), split(data[slot, c]), ((1,), (1,))) * mask_ref[0]
         for c in range(own)
     ]
+    blocks = [v[2 * i * span : (2 * i + 2) * span] for v in columns for i in range(2)]
     sides = []
     for odd in range(2):
         at = odd * half
         stacked = jnp.concatenate(
             [
-                jnp.concatenate([v[:half_cols, at : at + half], v[half_cols:, at : at + half]], 1)
-                for v in columns
+                jnp.concatenate([v[:span, at : at + half], v[span:, at : at + half]], 1)
+                for v in blocks
             ],
             0,
         )
         sides.append(dot3(split(stacked), (row_hi[odd], row_lo[odd])))
     for c in range(own):
-        even, odd = [side[c * half_cols : (c + 1) * half_cols] for side in sides]
-        for part in range(2):
-            e = even[:, part * half : (part + 1) * half]
-            o = odd[:, part * half : (part + 1) * half]
-            out_ref[c, 0, part] = jnp.concatenate([e + o, e - o], 1)
-
-
-def weigh_kernel(bit_ref, maps_ref, base_ref, keep_ref, send_ref, turned):
-    devices, own, rows, packed = maps_ref.shape
-    half_cols = packed // 2
-    length = devices * rows
-
-    @pl.when(pl.program_id(0) == 0)
-    def _():
-        for c in range(own):
-            whole = maps_ref[:, c].reshape(length, packed).T
-            turned[c, 0] = whole[:half_cols]
-            turned[c, 1] = whole[half_cols:]
-
-    bit = bit_ref[0]
-    span = half_cols // 2
-    blocks = devices // 2
-    for ref, which in ((send_ref, 1 - bit), (keep_ref, bit)):
-        at = pl.ds(pl.multiple_of(which * span, span), span)
-        total_re = total_im = None
-        for c in range(own):
-            s_re, s_im = turned[c, 0, at, :], turned[c, 1, at, :]
-            b_re, b_im = base_ref[c, 0, 0, at, :], base_ref[c, 0, 1, at, :]
-            t_re = s_re * b_re + s_im * b_im
-            t_im = s_re * b_im - s_im * b_re
-            total_re = t_re if c == 0 else total_re + t_re
-            total_im = t_im if c == 0 else total_im + t_im
-        ref[:, 0, 0] = total_re.reshape(blocks, span // blocks, length)
-        ref[:, 0, 1] = total_im.reshape(blocks, span // blocks, length)
-
-
-def first_normal_kernel(
-    coils, got_ref, mask_ref, wave_hi, wave_lo, maps_out, field_out, grad_out, responses
-):
+        for i, ref in enumerate((keep_ref, send_ref)):
+            rows = (2 * c + i) * span
+            even, odd = [side[rows : rows + span] for side in sides]
+            for part in range(2):
+                e = even[:, part * half : (part + 1) * half]
+                o = odd[:, part * half : (part + 1) * half]
+                ref[c, 0, part] = jnp.concatenate([e + o, e - o], 1)
+
+
+def weigh_kernel(outer, level, device_ref, maps_ref, kept_ref, got_ref, keep_out, send_out, *refs):
+    turned, kept, got, keep, send, arrived, left = refs
+    devices, pair_coils, rows, lanes = maps_ref.shape
+    own, count = got_ref.shape[:2]
+    inner, _, _, cols, length = keep.shape
+    inner //= outer
+
+    copies = [
+        [
+            pltpu.make_async_copy(src.at[:, f], dst.at[:, f], arrived.at[i, f])
+            for i, (src, dst) in enumerate(((kept_ref, kept), (got_ref, got)))
+        ]
+        for f in range(count)
+    ]
+    for pair in copies:
+        for copy in pair:
+            copy.start()
+    for c in range(pair_coils):
+        one = maps_ref[:, c].reshape(length, lanes).T
+        turned[c, 0] = one[: lanes // 2]
+        turned[c, 1] = one[lanes // 2 :]
+
+    bit, mine = device_ref[0] & 1, (device_ref[0] >> level) & 1
+    span = inner * cols
+    results = []
+    for f in range(count):
+        for copy in copies[f]:
+            copy.wait()
+        for ref, which in ((send, 1 - mine), (keep, mine)):
+            for i in range(outer):
+                at = pl.ds(pl.multiple_of((2 * i + which) * span, span), span)
+                total_re = total_im = 0.0
+                for base, first in ((kept, bit * own), (got, (1 - bit) * own)):
+                    for c in range(own):
+                        s_re, s_im = turned[first + c, 0, at, :], turned[first + c, 1, at, :]
+                        b_re, b_im = base[c, f, 0, at, :], base[c, f, 1, at, :]
+                        total_re += s_re * b_re + s_im * b_im
+                        total_im += s_re * b_im - s_im * b_re
+                here = slice(i * inner, (i + 1) * inner)
+                ref[here, f, 0] = total_re.reshape(inner, cols, length)
+                ref[here, f, 1] = total_im.reshape(inner, cols, length)
+        for i, (src, dst) in enumerate(((send, send_out), (keep, keep_out))):
+            results.append(pltpu.make_async_copy(src.at[:, f], dst.at[:, f], left.at[i, f]))
+            results[-1].start()
+    for copy in results:
+        copy.wait()
+
+
+def first_normal_kernel(coils, level, device_ref, got_ref, mask_ref, wave_hi, wave_lo, *refs):
+    maps_out, field_out, grad_out, responses = refs[-4:]
     mask_responses(mask_ref, wave_hi, wave_lo, responses)
-    devices, groups, _, cols, lanes = got_ref.shape
+    blocks, _, groups, _, cols, lanes = got_ref.shape
+    devices = 2 * blocks
+    mine = (device_ref[0] >> level) & 1
     frames = field_out.shape[0]
+
+    def block(s, g):
+        e = ((s >> (level + 1)) << level) | (s & ((1 << level) - 1))
+        return got_ref[e, ((s >> level) & 1) ^ mine, g]
+
     per = (coils + frames) // groups
     width = lanes // per
     for g in range(groups):
         out, base = (maps_out, g * per) if g * per < coils else (field_out, g * per - coils)
         for h in range(devices // per):
-            exchanged = lane_exchange([got_ref[h * per + s, g] for s in range(per)], width)
+            exchanged = lane_exchange([block(h * per + s, g) for s in range(per)], width)
             for c in range(per):
                 out[base + c, :, :, h * lanes : (h + 1) * lanes] = exchanged[c]
 
-    def one(f, _):
-        grad_out[f, 0], grad_out[f, 1] = normal_frame(
-            maps_out, field_out[f, 0], field_out[f, 1], frame_tables(responses, f)
+    gradient_frames(0, maps_out, field_out, responses, grad_out)
+
+
+def gradient_frames(start, maps_ref, field_ref, responses, grad_out):
+    def one(i, _):
+        f = start + i
+        grad_out[i, 0], grad_out[i, 1] = normal_frame(
+            maps_ref, field_ref[f, 0], field_ref[f, 1], frame_tables(responses, f)
         )
         return 0
 
-    lax.fori_loop(0, frames, one, 0)
-
-
-def steps_kernel(field_ref, grad_ref, b0_ref, b1_ref, maps_ref, mask_ref, *refs):
-    wave_hi, wave_lo, out_ref, field, grad, responses = refs
+    lax.fori_loop(0, grad_out.shape[0], one, 0)
+
+
+def second_normal_kernel(start, maps_ref, field_ref, mask_ref, wave_hi, wave_lo, *refs):
+    grad_out, responses = refs[-2:]
+    mask_responses(mask_ref, wave_hi, wave_lo, responses)
+    gradient_frames(start, maps_ref, field_ref, responses, grad_out)
+
+
+def steps_kernel(field_ref, grad0_ref, grad1_ref, maps_ref, mask_ref, *refs):
+    wave_hi, wave_lo, *terms, out_ref, field, grad, responses = refs
     frames, _, cols, length = field_ref.shape
     devices, _, _, lanes = out_ref.shape
     mask_responses(mask_ref, wave_hi, wave_lo, responses)
-    data_term = jnp.concatenate([b0_ref[...], b1_ref[...]], 0)
-    field[...] = tv_step(field_ref[...] - step_size * (grad_ref[...] - data_term))
+    data_term = jnp.concatenate(
+        [keep[...] + got[...] for keep, got in zip(terms[0::2], terms[1::2])], 0
+    )
+    first = jnp.concatenate([grad0_ref[...], grad1_ref[...]], 0)
+    field[...] = tv_step(field_ref[...] - step_size * (first - data_term))
     for sweep in range(1, OUTER):
 
         def one(f, _):
@@ -378,8 +438,8 @@
 
     def part(which):
         return lax.dynamic_index_in_dim(
-            keep, which, bit, keepdims=True
-        ) + lax.dynamic_index_in_dim(got, which, bit, keepdims=True)
+            keep, which, bit - 1, keepdims=True
+        ) + lax.dynamic_index_in_dim(got, which, bit - 1, keepdims=True)
 
     send = part(1 - mine)
     return part(mine), send
@@ -417,112 +477,167 @@
     sens_rows = sens.reshape(rows * coils, packed)
     image_rows = image.reshape(rows * frames, packed)
 
+    with jax.named_scope("column_maps"):
+        level = 1
+        block = (devices // 2, groups, 2, cols, LANES)
+        column_keep, column_send = pl.pallas_call(
+            functools.partial(column_blocks_kernel, coils, frames, chunk_of, level),
+            grid=(1,),
+            out_shape=(f32(*block),) * 2,
+            in_specs=[pl.BlockSpec(memory_space=pltpu.SMEM)]
+            + lane_tiles(rows * coils, packed)
+            + lane_tiles(rows * frames, packed),
+            out_specs=(whole(block),) * 2,
+            scratch_shapes=[pltpu.VMEM((2, half, LANES), jnp.float32)],
+            compiler_params=params(),
+            cost_estimate=cost(0, 2 * (sens.size + image.size) * 4),
+        )(device[None], *[sens_rows] * (packed // LANES), *[image_rows] * (packed // LANES))
+        column_blocks = jnp.stack([column_keep, exchange(column_send, level)], 1)
+        sides = [[with_bit(e, level, side) for e in range(devices // 2)] for side in range(2)]
+
     with jax.named_scope("coil_maps"):
         blocks = pl.pallas_call(
             functools.partial(coil_blocks_kernel, coils),
             grid=(1,),
-            out_shape=f32(devices, own, rows, packed),
-            in_specs=lane_tiles(rows * coils, packed),
-            out_specs=whole((devices, own, rows, packed)),
+            out_shape=f32(devices, 2 * own, rows, half),
+            in_specs=lane_tiles(rows * coils, packed) + [pl.BlockSpec(memory_space=pl.ANY)],
+            out_specs=whole((devices, 2 * own, rows, half)),
             compiler_params=params(),
             cost_estimate=cost(0, 2 * sens.size * 4),
-        )(*[sens_rows] * (packed // LANES))
+        )(*[sens_rows] * (packed // LANES), column_send)
+        blocks, device = lax.optimization_barrier((blocks, device))
         coil_maps = lax.all_to_all(blocks, "coil", 0, 0, tiled=True)
 
-    with jax.named_scope("column_maps"):
-        column_blocks = pl.pallas_call(
-            functools.partial(column_blocks_kernel, coils, frames, chunk_of),
-            grid=(1,),
-            out_shape=f32(devices, groups, 2, cols, LANES),
-            in_specs=lane_tiles(rows * coils, packed) + lane_tiles(rows * frames, packed),
-            out_specs=whole((devices, groups, 2, cols, LANES)),
-            compiler_params=params(),
-            cost_estimate=cost(0, 2 * (sens.size + image.size) * 4),
-        )(*[sens_rows] * (packed // LANES), *[image_rows] * (packed // LANES))
-
-    streams = 2
-    count = frames // streams
-    with jax.named_scope("data_transform"):
-        bases = [
-            pl.pallas_call(
+    plans = [
+        (frames // 2, list(range(1, bits))),
+        (frames // 2, list(range(1, bits))),
+    ]
+    firsts = [sum(count for count, _ in plans[:i]) for i in range(len(plans))]
+    span = half // 2
+    smem = pl.BlockSpec(memory_space=pltpu.SMEM)
+    kept, got = [], []
+    for start, (count, _) in zip(firsts, plans):
+        with jax.named_scope("data_transform"):
+            block = pl.BlockSpec((own, 1, 2, span, length), lambda f: (0, f, 0, 0, 0))
+            keep, send = pl.pallas_call(
                 functools.partial(base_kernel, start, frames),
                 grid=(count,),
-                out_shape=f32(own, count, 2, half, length),
+                out_shape=(f32(own, count, 2, span, length),) * 2,
                 in_specs=[
-                    pl.BlockSpec(memory_space=pl.ANY),
+                    smem,
+                    pl.BlockSpec(memory_space=pltpu.HBM),
                     pl.BlockSpec((1, 1, length), lambda f, start=start: (start + f, 0, 0)),
                     whole((packed, packed)),
                     whole((packed, packed)),
                     whole((2, length, length)),
                     whole((2, length, length)),
                 ],
-                out_specs=pl.BlockSpec((own, 1, 2, half, length), lambda f: (0, f, 0, 0, 0)),
+                out_specs=(block, block),
                 scratch_shapes=[
                     pltpu.VMEM((2, own, length, packed), jnp.float32),
+                    pltpu.VMEM((packed, packed), jnp.bfloat16),
+                    pltpu.VMEM((packed, packed), jnp.bfloat16),
                     pltpu.SemaphoreType.DMA((2, own, 2)),
                 ],
                 compiler_params=params(TRANSFORM_LIMIT),
                 cost_estimate=cost(
-                    pairs * 6 * 6 * half * half * length // streams, 2 * kspace.size * 4 // streams
+                    own * count * 36 * half * half * length, 16 * own * count * half * length
                 ),
-            )(kspace.reshape(hl, 2, pairs, packed), mask_lanes, col_hi, col_lo, row_hi, row_lo)
-            for start in range(0, frames, count)
-        ]
+            )(
+                device[None],
+                kspace.reshape(hl, 2, pairs, packed),
+                mask_lanes,
+                col_hi,
+                col_lo,
+                row_hi,
+                row_lo,
+            )
+        if len(kept) == len(plans) - 1:
+            column_blocks, send = lax.optimization_barrier((column_blocks, send))
+        kept.append(keep)
+        got.append(exchange(send, 0))
+    with jax.named_scope("column_maps"):
+        column_maps = lax.all_to_all(
+            column_blocks, "coil", 0, 0, tiled=True, axis_index_groups=sides
+        )
 
     field = f32(frames, 2, cols, length)
     normal_cost = 6 * 2 * frames * coils * cols * length * length
 
     responses = pltpu.VMEM((2, frames, length), jnp.float32)
 
-    def first_gradient(column_maps):
+    part = f32(frames // 2, 2, cols, length)
+    anywhere = pl.BlockSpec(memory_space=pl.ANY)
+
+    def second_gradient(maps, field0, before):
         return pl.pallas_call(
-            functools.partial(first_normal_kernel, coils),
-            out_shape=(f32(coils, 2, cols, length), field, field),
+            functools.partial(second_normal_kernel, frames // 2),
+            in_specs=[pl.BlockSpec(memory_space=pltpu.VMEM)] * 5 + [anywhere] * len(before),
+            out_shape=part,
             scratch_shapes=[responses],
             compiler_params=params(),
-            cost_estimate=cost(normal_cost, 4 * sens.size * 4),
+            cost_estimate=cost(normal_cost // 2, 2 * sens.size * 4),
+            name="second_gradient",
+        )(maps, field0, mask_sides, wave_hi, wave_lo, *before)
+
+    def first_gradient(column_maps, before):
+        return pl.pallas_call(
+            functools.partial(first_normal_kernel, coils, level),
+            in_specs=[smem]
+            + [pl.BlockSpec(memory_space=pltpu.VMEM)] * 4
+            + [pl.BlockSpec(memory_space=pl.ANY)] * len(before),
+            out_shape=(f32(coils, 2, cols, length), field, part),
+            scratch_shapes=[responses],
+            compiler_params=params(),
+            cost_estimate=cost(normal_cost // 2, 4 * sens.size * 4),
             name="first_gradient",
-        )(column_maps, mask_sides, wave_hi, wave_lo)
-
-    column_blocks, bases = lax.optimization_barrier((column_blocks, bases))
-    with jax.named_scope("column_maps"):
-        column_maps = lax.all_to_all(column_blocks, "coil", 0, 0, tiled=True)
+        )(device[None], column_maps, mask_sides, wave_hi, wave_lo, *before)
 
     with jax.named_scope("data_term"):
-        bit = (device & 1).astype(jnp.int32)[None]
-        orders = [list(range(bits)), [0] + list(range(2, bits)) + [1]]
         terms = []
-        for stream in range(streams):
-            out = f32(devices // 2, count, 2, cols, length)
-            block = pl.BlockSpec((devices // 2, 1, 2, cols, length), lambda i: (0, i, 0, 0, 0))
+        for stream, (count, order) in enumerate(plans):
+            outer = 2 ** (order[0] - 1)
+            out = f32(devices // 4, count, 2, cols, length)
+            vmem, anywhere = pl.BlockSpec(memory_space=pltpu.VMEM), pl.BlockSpec(memory_space=pl.ANY)
+            base = pltpu.VMEM((own, count, 2, span, length), jnp.float32)
+            term = pltpu.VMEM(out.shape, jnp.float32)
             keep, send = pl.pallas_call(
-                weigh_kernel,
-                grid=(count,),
+                functools.partial(weigh_kernel, outer, order[0]),
                 out_shape=(out, out),
-                in_specs=[
-                    pl.BlockSpec(memory_space=pltpu.SMEM),
-                    whole((devices, own, rows, packed)),
-                    pl.BlockSpec((own, 1, 2, half, length), lambda i: (0, i, 0, 0, 0)),
+                in_specs=[smem, vmem, anywhere, anywhere],
+                out_specs=(anywhere, anywhere),
+                scratch_shapes=[
+                    pltpu.VMEM((2 * own, 2, span, length), jnp.float32),
+                    base,
+                    base,
+                    term,
+                    term,
+                    pltpu.SemaphoreType.DMA((2, count)),
+                    pltpu.SemaphoreType.DMA((2, count)),
                 ],
-                out_specs=(block, block),
-                scratch_shapes=[pltpu.VMEM((own, 2, half, length), jnp.float32)],
-                compiler_params=params(),
-                cost_estimate=cost(0, bases[stream].size * 4 + 2 * out.size * 4),
-            )(bit, coil_maps, bases[stream])
-            lead = [1] + [2] * (bits - 1)
-            got = exchange(send, 0).reshape(*lead, *keep.shape[1:])
-            terms.append((keep.reshape(got.shape), got))
-        for step in range(1, bits):
-            halves = [halve(*terms[i], orders[i][step], device) for i in range(streams)]
-            if step == 2:
-                column_maps, halves = lax.optimization_barrier((column_maps, halves))
-            terms = [
-                (keep, exchange(send, orders[i][step])) for i, (keep, send) in enumerate(halves)
-            ]
-            if step == 2:
-                maps, field0, grad0 = first_gradient(column_maps)
-                terms, grad0 = lax.optimization_barrier((terms, grad0))
-        terms = [(keep + got).reshape(count, 2, cols, length) for keep, got in terms]
+                compiler_params=params(WEIGH_LIMIT),
+                cost_estimate=cost(0, 2 * kept[stream].size * 4 + 2 * out.size * 4),
+            )(device[None], coil_maps, kept[stream], got[stream])
+            dims = [2] * (bits - 1)
+            dims[order[0] - 1] = 1
+            received = exchange(send, order[0]).reshape(*dims, *keep.shape[1:])
+            terms.append((keep.reshape(received.shape), received))
+        sent = [None] * len(plans)
+
+        def advance(stream, step):
+            order = plans[stream][1]
+            keep, sent[stream] = halve(*terms[stream], order[step], device)
+            terms[stream] = (keep, exchange(sent[stream], order[step]))
+
+        for step in range(1, bits - 2):
+            for stream in range(len(plans)):
+                advance(stream, step)
+        advance(0, bits - 2)
+        maps, field0, early = first_gradient(column_maps, sent)
+        terms[1], early = lax.optimization_barrier((terms[1], early))
+        advance(1, bits - 2)
+        late = second_gradient(maps, field0, sent[1:])
+        terms = [value.reshape(-1, 2, cols, length) for term in terms for value in term]
 
     with jax.named_scope("outer_steps"):
         blocks = pl.pallas_call(
@@ -531,7 +646,7 @@
             scratch_shapes=[pltpu.VMEM(field.shape, jnp.float32)] * 2 + [responses],
             compiler_params=params(),
             cost_estimate=cost(normal_cost, 4 * sens.size * 4),
-        )(field0, grad0, terms[0], terms[1], maps, mask_sides, wave_hi, wave_lo)
+        )(field0, early, late, maps, mask_sides, wave_hi, wave_lo, *terms)
 
     with jax.named_scope("result_rows"):
         got = lax.all_to_all(blocks, "coil", 0, 0, tiled=True)

time: 124 us -> 119 us (0.960)
  other arithmetic: 8.03 us -> 3.64 us
  Pallas kernels: 43.7 us -> 46.7 us
  waiting for transfers between devices: 29.4 us -> 27.2 us
    add x6 -> x2, other arithmetic: 7.96 us -> 2.38 us  [part(): lax.dynamic_index_in_dim(keep, which, bit - 1, keepdims=True)]
    pallas_call x3 -> x4, Pallas kernels: 13.8 us -> 17.6 us  [the longest x2 8.73 us: kernel_path(): pl.pallas_call(functools.partial(weigh_kernel, outer, order[0]), out_shap...]
    all_to_all x1, waiting for transfers between devices: 3.03 us -> 0.01 us  [kernel_path(): coil_maps = lax.all_to_all(blocks, 'coil', 0, 0, tiled=True)]
    all_to_all x1, starting transfers between devices: 6.86 us -> 4.66 us  [kernel_path(): lax.all_to_all(column_blocks, 'coil', 0, 0, tiled=True, axis_index_groups...]
    ppermute x8 -> x9, starting transfers between devices: 9.6 us -> 11.3 us  [exchange(): lax.ppermute(send, 'coil', [(i, i ^ 1 << bit) for i in range(devices)])]
    ppermute x8 -> x9, waiting for transfers between devices: 26.4 us -> 27.2 us  [exchange(): lax.ppermute(send, 'coil', [(i, i ^ 1 << bit) for i in range(devices)])]
    unnamed x26 -> x22, local copies, waits for them, and re-layouts: 3.6 us -> 3.72 us
  transfers between devices with their start and end apart: 10 -> 11, of which waited for: 6 -> 6; matrix products, arithmetic and copies ran while one was open for 7% -> 3% of each run, Pallas kernels for 27% -> 30%
where the time goes in v4:
time: 119 us
  Pallas kernels  46.7 us (39%)
  waiting for transfers between devices  27.2 us (23%)
  starting transfers between devices  23.6 us (20%)
  blocking collectives  13.2 us (11%)
  local copies, waits for them, and re-layouts  4.14 us (3%)
  other arithmetic  3.64 us (3%)
    ppermute x9, waiting for transfers between devices, exchange(): lax.ppermute(send, 'coil', [(i, i ^ 1 << bit) for i in range(devices)])  27.2 us
    pallas_call x2, Pallas kernels, kernel_path(): pl.pallas_call(functools.partial(base_kernel, start, frames), grid=(count...  17.5 us
    all_to_all x1, blocking collectives, kernel_path(): got = lax.all_to_all(blocks, 'coil', 0, 0, tiled=True)  13.2 us
    ppermute x9, starting transfers between devices, exchange(): lax.ppermute(send, 'coil', [(i, i ^ 1 << bit) for i in range(devices)])  11.3 us
    pallas_call x2, Pallas kernels, kernel_path(): pl.pallas_call(functools.partial(weigh_kernel, outer, order[0]), out_shap...  8.73 us
    pallas_call x1, Pallas kernels, kernel_path(): pl.pallas_call(steps_kernel, out_shape=f32(devices, 2, cols, LANES), scra...  8.09 us
    all_to_all x1, starting transfers between devices, kernel_path(): coil_maps = lax.all_to_all(blocks, 'coil', 0, 0, tiled=True)  7.58 us
    pallas_call x1, Pallas kernels, first_gradient(): pl.pallas_call(functools.partial(first_normal_kernel, coils, level), in_s...  5.31 us
  transfers between devices with their start and end apart: 11, of which 6 were waited for; matrix products, arithmetic and copies ran while one was open for 3% of the time, Pallas kernels for 30%

profile of v4, /device:TPU:0, one launch (start us, length us, event | category | flops | bytes accessed | tf_op | source)
XLA Modules:
  0.0 118.6 jit_solution(3915451917031259770)
XLA Ops:
  0.0 1.2 %copy-done = f32[16,32,512]{2,1,0:T(8,128)S(1)} copy-done((f32[16,32,512]{2,1,0:T(8,128)S(1)}, f32[16,32,512]{2,1,0:T(8,128)}, u32[]{:S(2)}) %copy-start) | copy-done | bytes 1048600
  3.4 1.7 %coil_maps.1 = f32[16,4,16,256]{3,2,1,0:T(8,128)} custom-call(f32[512,512]{1,0:T(8,128)S(1)} %bitcast.26, f32[512,512]{1,0:T(8,128)S(1)} %bitcast.27, f32[512,512]{1,0:T(8,128)S(1)} %bitcast.28, f32[512,512]{1,0:T(8,128)S(1)} %bitcast.29, f32[8,5,2,16,128]{4,3,2,1,0:T(8,128)S(1)} %get-tuple-element.25.refs_4_), custom_call_target="tpu_custom_call" | custom-call | bytes 2097152 | tf_op jit(solution)/shard_map/coil_maps/pallas_call | solution.py:499
  5.1 7.6 %all-to-all-start.1 = ((f32[16,4,16,256]{3,2,1,0:T(8,128)}), f32[16,4,16,256]{3,2,1,0:T(8,128)}, u32[]{:S(2)}, u32[]{:S(2)}) async-start(f32[16,4,16,256]{3,2,1,0:T(8,128)} %coil_maps.1), calls=%async_computation.1 | async-start | bytes 2097152 | tf_op jit(solution)/shard_map/coil_maps/all_to_all | solution.py:509
  12.7 1.9 %collective-permute-start = (f32[8,5,2,16,128]{4,3,2,1,0:T(8,128)S(1)}, f32[8,5,2,16,128]{4,3,2,1,0:T(8,128)S(1)}, u32[]{:S(2)}, u32[]{:S(2)}) collective-permute-start(f32[8,5,2,16,128]{4,3,2,1,0:T(8,128)S(1)} %get-tuple-element.25.refs_4_), channel_id=1, source_target_pairs={{0,2},{1,3},{2,0},{3,1},{4,6},{5,7},{6,4},{7,5},{8,10},{9,11},{10,... | collective-permute-start | bytes 1966088 | tf_op jit(solution)/shard_map/column_maps/ppermute | solution.py:433
  15.0 8.8 %data_transform.3 = (f32[2,4,2,128,256]{4,3,2,1,0:T(8,128)}, f32[2,4,2,128,256]{4,3,2,1,0:T(8,128)}) custom-call(s32[1]{0:T(128)} %bitcast.3.device_ref, f32[128,2,16,512]{3,2,1,0:T(8,128)} %bitcast.43, f32[8,1,256]{2,1,0:T(1,128)S(1)} %copy.11.mask_ref, bf16[512,512]{1,0:T(8,128)(2,1)S(1)} %copy-done.4, bf16[512,512]{1,0:T(8,128)(2,1)S(1)} %copy-done.3, ...), custom_call_target="tpu_custom_call" | custom-call | flops 4831838208 | bytes 8388608 | tf_op jit(solution)/shard_map/data_transform/pallas_call | solution.py:522
  23.9 8.7 %data_transform.2 = (f32[2,4,2,128,256]{4,3,2,1,0:T(8,128)}, f32[2,4,2,128,256]{4,3,2,1,0:T(8,128)}) custom-call(s32[1]{0:T(128)} %bitcast.3.device_ref, f32[128,2,16,512]{3,2,1,0:T(8,128)} %bitcast.44, f32[8,1,256]{2,1,0:T(1,128)S(1)} %copy.11.mask_ref, bf16[512,512]{1,0:T(8,128)(2,1)S(1)} %copy-done.4, bf16[512,512]{1,0:T(8,128)(2,1)S(1)} %copy-done.3, ...), custom_call_target="tpu_custom_call" | custom-call | flops 4831838208 | bytes 8388608 | tf_op jit(solution)/shard_map/data_transform/pallas_call | solution.py:522
  32.6 8.4 %collective-permute-done = f32[8,5,2,16,128]{4,3,2,1,0:T(8,128)S(1)} collective-permute-done((f32[8,5,2,16,128]{4,3,2,1,0:T(8,128)S(1)}, f32[8,5,2,16,128]{4,3,2,1,0:T(8,128)S(1)}, u32[]{:S(2)}, u32[]{:S(2)}) %collective-permute-start) | collective-permute-done | bytes 655392 | tf_op jit(solution)/shard_map/column_maps/ppermute | solution.py:433
  42.2 4.7 %all-to-all-start = ((f32[8,2,5,2,16,128]{5,4,3,2,1,0:T(8,128)}), f32[8,2,5,2,16,128]{5,4,3,2,1,0:T(8,128)S(1)}, u32[]{:S(2)}, u32[]{:S(2)}) async-start(f32[8,2,5,2,16,128]{5,4,3,2,1,0:T(8,128)} %pad_maximum_fusion), calls=%async_computation | async-start | bytes 2621440 | tf_op jit(solution)/shard_map/column_maps/all_to_all | solution.py:560
  46.9 4.4 %data_term.2 = (f32[4,4,2,16,256]{4,3,2,1,0:T(8,128)}, f32[4,4,2,16,256]{4,3,2,1,0:T(8,128)}) custom-call(s32[1]{0:T(128)} %bitcast.3.device_ref, f32[16,4,16,256]{3,2,1,0:T(8,128)} %all-to-all-done.1.maps_ref, f32[2,4,2,128,256]{4,3,2,1,0:T(8,128)} %get-tuple-element.31.kept_ref, f32[2,4,2,128,256]{4,3,2,1,0:T(8,128)} %collective-permute-done.1.got_ref), custom_call_target="tpu_custom_call" | custom-call | bytes 5242880 | tf_op jit(solution)/shard_map/data_term/pallas_call | solution.py:604
  51.9 1.3 %copy-done.9 = f32[2,4,2,128,256]{4,3,2,1,0:T(8,128)} copy-done((f32[2,4,2,128,256]{4,3,2,1,0:T(8,128)}, f32[2,4,2,128,256]{4,3,2,1,0:T(8,128)S(1)}, u32[]{:S(2)}) %copy-start.9) | copy-done | bytes 2097176
  53.2 4.4 %data_term.3 = (f32[4,4,2,16,256]{4,3,2,1,0:T(8,128)}, f32[4,4,2,16,256]{4,3,2,1,0:T(8,128)}) custom-call(s32[1]{0:T(128)} %bitcast.3.device_ref, f32[16,4,16,256]{3,2,1,0:T(8,128)} %all-to-all-done.1.maps_ref, f32[2,4,2,128,256]{4,3,2,1,0:T(8,128)} %get-tuple-element.35.kept_ref, f32[2,4,2,128,256]{4,3,2,1,0:T(8,128)} %copy-done.9), custom_call_target="tpu_custom_call" | custom-call | bytes 5242880 | tf_op jit(solution)/shard_map/data_term/pallas_call | solution.py:604
  57.6 1.5 %collective-permute-start.5 = (f32[4,4,2,16,256]{4,3,2,1,0:T(8,128)}, f32[4,4,2,16,256]{4,3,2,1,0:T(8,128)S(1)}, u32[]{:S(2)}, u32[]{:S(2)}) collective-permute-start(f32[4,4,2,16,256]{4,3,2,1,0:T(8,128)} %get-tuple-element.38), channel_id=1, source_target_pairs={{0,2},{1,3},{2,0},{3,1},{4,6},{5,7},{6,4},{7,5},{8,10},{9,11},{10,... | collective-permute-start | bytes 1572872 | tf_op jit(solution)/shard_map/data_term/ppermute | solution.py:433
  59.1 7.2 %collective-permute-done.2 = f32[4,4,2,16,256]{4,3,2,1,0:T(8,128)} collective-permute-done((f32[4,4,2,16,256]{4,3,2,1,0:T(8,128)}, f32[4,4,2,16,256]{4,3,2,1,0:T(8,128)}, u32[]{:S(2)}, u32[]{:S(2)}) %collective-permute-start.2) | collective-permute-done | bytes 524320 | tf_op jit(solution)/shard_map/data_term/ppermute | solution.py:433
  66.4 1.3 %dynamic-slice_add_fusion.3 = (f32[1,1,2,4,2,16,256]{6,5,4,3,2,1,0:T(8,128)S(1)}, f32[1,1,2,4,2,16,256]{6,5,4,3,2,1,0:T(8,128)S(1)}) fusion(f32[1,2,2,4,2,16,256]{6,5,4,3,2,1,0:T(8,128)} %bitcast.11, s32[]{:T(128)S(6)} %select_n.26, f32[1,2,2,4,2,16,256]{6,5,4,3,2,1,0:T(8,128)} %bitcast.40, s32[]{:T(128)S(6)} %select_n.28), kind=kLoop, calls=%fused_computation.4 | loop fusion | flops 131072 | bytes 1572872 | tf_op jit(solution)/shard_map/data_term/add | solution.py:440
  67.6 2.1 %collective-permute-start.3 = (f32[1,1,2,4,2,16,256]{6,5,4,3,2,1,0:T(8,128)S(1)}, f32[1,1,2,4,2,16,256]{6,5,4,3,2,1,0:T(8,128)S(1)}, u32[]{:S(2)}, u32[]{:S(2)}) collective-permute-start(f32[1,1,2,4,2,16,256]{6,5,4,3,2,1,0:T(8,128)S(1)} %get-tuple-element.48), channel_id=1, source_target_pairs={{0,4},{1,5},{2,6},{3,7},{4,0},{5,1},{6,2},{7,3},{8,12},{9,13},{10,... | collective-permute-start | bytes 786440 | tf_op jit(solution)/shard_map/data_term/ppermute | solution.py:433
  69.8 7.3 %collective-permute-done.5 = f32[4,4,2,16,256]{4,3,2,1,0:T(8,128)S(1)} collective-permute-done((f32[4,4,2,16,256]{4,3,2,1,0:T(8,128)}, f32[4,4,2,16,256]{4,3,2,1,0:T(8,128)S(1)}, u32[]{:S(2)}, u32[]{:S(2)}) %collective-permute-start.5) | collective-permute-done | bytes 524320 | tf_op jit(solution)/shard_map/data_term/ppermute | solution.py:433
  78.2 1.7 %collective-permute-start.6 = (f32[1,1,2,4,2,16,256]{6,5,4,3,2,1,0:T(8,128)S(1)}, f32[1,1,2,4,2,16,256]{6,5,4,3,2,1,0:T(8,128)S(1)}, u32[]{:S(2)}, u32[]{:S(2)}) collective-permute-start(f32[1,1,2,4,2,16,256]{6,5,4,3,2,1,0:T(8,128)S(1)} %get-tuple-element.46.refs_1_), channel_id=1, source_target_pairs={{0,4},{1,5},{2,6},{3,7},{4,0},{5,1},{6,2},{7,3},{8,12},{9,13},{10,... | collective-permute-start | bytes 786440 | tf_op jit(solution)/shard_map/data_term/ppermute | solution.py:433
  80.3 2.2 %collective-permute-start.7 = (f32[1,1,1,4,2,16,256]{6,5,4,3,2,1,0:T(8,128)S(1)}, f32[1,1,1,4,2,16,256]{6,5,4,3,2,1,0:T(8,128)S(1)}, u32[]{:S(2)}, u32[]{:S(2)}) collective-permute-start(f32[1,1,1,4,2,16,256]{6,5,4,3,2,1,0:T(8,128)S(1)} %get-tuple-element.52.refs_0_), channel_id=1, source_target_pairs={{0,8},{1,9},{2,10},{3,11},{4,12},{5,13},{6,14},{7,15},{8,0},{9,1},... | collective-permute-start | bytes 393224 | tf_op jit(solution)/shard_map/data_term/ppermute | solution.py:433
  82.4 5.3 %first_gradient.1 = (f32[32,2,16,256]{3,2,1,0:T(8,128)S(1)}, f32[8,2,16,256]{3,2,1,0:T(8,128)S(1)}, f32[4,2,16,256]{3,2,1,0:T(8,128)S(1)}) custom-call(s32[1]{0:T(128)} %bitcast.3.device_ref, f32[8,2,5,2,16,128]{5,4,3,2,1,0:T(8,128)S(1)} %all-to-all-done.got_ref, f32[2,8,128]{2,1,0:T(8,128)S(1)} %pad_maximum_fusion.1.mask_ref, ...), custom_call_target="tpu_custom_call" | custom-call | flops 1610612736 | bytes 4194304 | tf_op jit(solution)/shard_map/data_term/first_gradient/pallas_call | solution.py:584
  87.8 1.3 %collective-permute-done.6 = f32[1,1,2,4,2,16,256]{6,5,4,3,2,1,0:T(8,128)S(1)} collective-permute-done((f32[1,1,2,4,2,16,256]{6,5,4,3,2,1,0:T(8,128)S(1)}, f32[1,1,2,4,2,16,256]{6,5,4,3,2,1,0:T(8,128)S(1)}, u32[]{:S(2)}, u32[]{:S(2)}) %collective-permute-start.6) | collective-permute-done | bytes 262176 | tf_op jit(solution)/shard_map/data_term/ppermute | solution.py:433
  90.3 3.5 %second_gradient.1.grad1_ref = f32[4,2,16,256]{3,2,1,0:T(8,128)S(1)} custom-call(f32[32,2,16,256]{3,2,1,0:T(8,128)S(1)} %get-tuple-element.42.maps_ref, f32[8,2,16,256]{3,2,1,0:T(8,128)S(1)} %get-tuple-element.39.field_ref, f32[2,8,128]{2,1,0:T(8,128)S(1)} %pad_maximum_fusion.1.mask_ref, bf16[2,128,256]{2,1,0:T(8,128)(2,1)S(1)} %copy-done.8, ...), custom_call_target="tpu_custom_call" | custom-call | flops 1610612736 | bytes 2097152 | tf_op jit(solution)/shard_map/data_term/second_gradient/pallas_call | solution.py:573
  93.8 2.7 %collective-permute-done.8 = f32[1,1,1,4,2,16,256]{6,5,4,3,2,1,0:T(8,128)S(1)} collective-permute-done((f32[1,1,1,4,2,16,256]{6,5,4,3,2,1,0:T(8,128)S(1)}, f32[1,1,1,4,2,16,256]{6,5,4,3,2,1,0:T(8,128)S(1)}, u32[]{:S(2)}, u32[]{:S(2)}) %collective-permute-start.8) | collective-permute-done | bytes 131104 | tf_op jit(solution)/shard_map/data_term/ppermute | solution.py:433
  96.5 8.1 %outer_steps.1 = f32[16,2,16,128]{3,2,1,0:T(8,128)S(1)} custom-call(f32[8,2,16,256]{3,2,1,0:T(8,128)S(1)} %get-tuple-element.39.field_ref, f32[4,2,16,256]{3,2,1,0:T(8,128)S(1)} %get-tuple-element.41.grad0_ref, f32[4,2,16,256]{3,2,1,0:T(8,128)S(1)} %second_gradient.1.grad1_ref, f32[32,2,16,256]{3,2,1,0:T(8,128)S(1)} %get-tuple-element.42.maps_ref, ...), custom_call_target="tpu_custom_call" | custom-call | flops 3221225472 | bytes 4194304 | tf_op jit(solution)/shard_map/outer_steps/pallas_call | solution.py:643
  104.6 13.2 %all_to_all.15.got_ref = f32[16,2,16,128]{3,2,1,0:T(8,128)S(1)} all-to-all(f32[16,2,16,128]{3,2,1,0:T(8,128)S(1)} %outer_steps.1), channel_id=1, replica_groups=mesh['plane'=2,'coil'=16] {'coil'}, dimensions={0} | all-to-all | bytes 524288 | tf_op jit(solution)/shard_map/result_rows/all_to_all | solution.py:652
  (42 shorter events, 8.1 us)
Async XLA Ops:
  0.0 1.2 %copy-start = (f32[16,32,512]{2,1,0:T(8,128)S(1)}, f32[16,32,512]{2,1,0:T(8,128)}, u32[]{:S(2)}) copy-start(f32[16,32,512]{2,1,0:T(8,128)} %param.11) | copy-start | bytes 3145732
  1.2 0.9 copy-start.2
  2.2 1.2 %copy-start.1 = (f32[16,32,512]{2,1,0:T(8,128)S(1)}, f32[16,32,512]{2,1,0:T(8,128)}, u32[]{:S(2)}) copy-start(f32[16,32,512]{2,1,0:T(8,128)} %param.11) | copy-start | bytes 3145732
  5.1 9.5 %copy-start.10 = (s32[8,256]{1,0:T(8,128)S(1)}, s32[8,256]{1,0:T(8,128)}, u32[]{:S(2)}) copy-start(s32[8,256]{1,0:T(8,128)} %param.13) | copy-start | bytes 24580
  5.1 9.9 %copy-start.3 = (bf16[512,512]{1,0:T(8,128)(2,1)S(1)}, bf16[512,512]{1,0:T(8,128)(2,1)}, u32[]{:S(2)}) copy-start(bf16[512,512]{1,0:T(8,128)(2,1)} %constant.62.clone.refs_1_) | copy-start | bytes 1572868
  5.1 9.9 %copy-start.4 = (bf16[512,512]{1,0:T(8,128)(2,1)S(1)}, bf16[512,512]{1,0:T(8,128)(2,1)}, u32[]{:S(2)}) copy-start(bf16[512,512]{1,0:T(8,128)(2,1)} %constant.61.clone.refs_0_) | copy-start | bytes 1572868
  5.1 10.0 %copy-start.5 = (bf16[2,256,256]{2,1,0:T(8,128)(2,1)S(1)}, bf16[2,256,256]{2,1,0:T(8,128)(2,1)}, u32[]{:S(2)}) copy-start(bf16[2,256,256]{2,1,0:T(8,128)(2,1)} %constant.64.clone.refs_3_) | copy-start | bytes 786436
  5.1 10.0 %copy-start.6 = (bf16[2,256,256]{2,1,0:T(8,128)(2,1)S(1)}, bf16[2,256,256]{2,1,0:T(8,128)(2,1)}, u32[]{:S(2)}) copy-start(bf16[2,256,256]{2,1,0:T(8,128)(2,1)} %constant.63.clone.refs_2_) | copy-start | bytes 786436
  5.1 37.1 %all-to-all-start.1 = ((f32[16,4,16,256]{3,2,1,0:T(8,128)}), f32[16,4,16,256]{3,2,1,0:T(8,128)}, u32[]{:S(2)}, u32[]{:S(2)}) async-start(f32[16,4,16,256]{3,2,1,0:T(8,128)} %coil_maps.1), calls=%async_computation.1 | async-start | bytes 2097152 | tf_op jit(solution)/shard_map/coil_maps/all_to_all | solution.py:509
  12.7 28.4 %collective-permute-start = (f32[8,5,2,16,128]{4,3,2,1,0:T(8,128)S(1)}, f32[8,5,2,16,128]{4,3,2,1,0:T(8,128)S(1)}, u32[]{:S(2)}, u32[]{:S(2)}) collective-permute-start(f32[8,5,2,16,128]{4,3,2,1,0:T(8,128)S(1)} %get-tuple-element.25.refs_4_), channel_id=1, source_target_pairs={{0,2},{1,3},{2,0},{3,1},{4,6},{5,7},{6,4},{7,5},{8,10},{9,11},{10,... | collective-permute-start | bytes 1966088 | tf_op jit(solution)/shard_map/column_maps/ppermute | solution.py:433
  23.8 23.1 %collective-permute-start.1 = (f32[2,4,2,128,256]{4,3,2,1,0:T(8,128)}, f32[2,4,2,128,256]{4,3,2,1,0:T(8,128)}, u32[]{:S(2)}, u32[]{:S(2)}) collective-permute-start(f32[2,4,2,128,256]{4,3,2,1,0:T(8,128)} %get-tuple-element.32), channel_id=1, source_target_pairs={{0,1},{1,0},{2,3},{3,2},{4,5},{5,4},{6,7},{7,6},{8,9},{9,8},{10,11... | collective-permute-start | bytes 6291464 | tf_op jit(solution)/shard_map/ppermute | solution.py:433
  42.2 9.7 %collective-permute-start.4 = (f32[2,4,2,128,256]{4,3,2,1,0:T(8,128)}, f32[2,4,2,128,256]{4,3,2,1,0:T(8,128)S(1)}, u32[]{:S(2)}, u32[]{:S(2)}) collective-permute-start(f32[2,4,2,128,256]{4,3,2,1,0:T(8,128)} %get-tuple-element.36), channel_id=1, source_target_pairs={{0,1},{1,0},{2,3},{3,2},{4,5},{5,4},{6,7},{7,6},{8,9},{9,8},{10,11... | collective-permute-start | bytes 6291464 | tf_op jit(solution)/shard_map/ppermute | solution.py:433
  42.2 40.2 %all-to-all-start = ((f32[8,2,5,2,16,128]{5,4,3,2,1,0:T(8,128)}), f32[8,2,5,2,16,128]{5,4,3,2,1,0:T(8,128)S(1)}, u32[]{:S(2)}, u32[]{:S(2)}) async-start(f32[8,2,5,2,16,128]{5,4,3,2,1,0:T(8,128)} %pad_maximum_fusion), calls=%async_computation | async-start | bytes 2621440 | tf_op jit(solution)/shard_map/column_maps/all_to_all | solution.py:560
  51.3 15.1 %collective-permute-start.2 = (f32[4,4,2,16,256]{4,3,2,1,0:T(8,128)}, f32[4,4,2,16,256]{4,3,2,1,0:T(8,128)}, u32[]{:S(2)}, u32[]{:S(2)}) collective-permute-start(f32[4,4,2,16,256]{4,3,2,1,0:T(8,128)} %get-tuple-element.34), channel_id=1, source_target_pairs={{0,2},{1,3},{2,0},{3,1},{4,6},{5,7},{6,4},{7,5},{8,10},{9,11},{10,... | collective-permute-start | bytes 1572872 | tf_op jit(solution)/shard_map/data_term/ppermute | solution.py:433
  51.9 1.3 %copy-start.9 = (f32[2,4,2,128,256]{4,3,2,1,0:T(8,128)}, f32[2,4,2,128,256]{4,3,2,1,0:T(8,128)S(1)}, u32[]{:S(2)}) copy-start(f32[2,4,2,128,256]{4,3,2,1,0:T(8,128)S(1)} %collective-permute-done.4.got_ref) | copy-start | bytes 6291460
  57.6 24.8 %copy-start.7 = (bf16[2,128,256]{2,1,0:T(8,128)(2,1)S(1)}, bf16[2,128,256]{2,1,0:T(8,128)(2,1)}, u32[]{:S(2)}) copy-start(bf16[2,128,256]{2,1,0:T(8,128)(2,1)} %constant.66.clone.wave_lo.refs_1_) | copy-start | bytes 393220
  57.6 24.8 %copy-start.8 = (bf16[2,128,256]{2,1,0:T(8,128)(2,1)S(1)}, bf16[2,128,256]{2,1,0:T(8,128)(2,1)}, u32[]{:S(2)}) copy-start(bf16[2,128,256]{2,1,0:T(8,128)(2,1)} %constant.65.clone.wave_hi.refs_0_) | copy-start | bytes 393220
  57.6 19.5 %collective-permute-start.5 = (f32[4,4,2,16,256]{4,3,2,1,0:T(8,128)}, f32[4,4,2,16,256]{4,3,2,1,0:T(8,128)S(1)}, u32[]{:S(2)}, u32[]{:S(2)}) collective-permute-start(f32[4,4,2,16,256]{4,3,2,1,0:T(8,128)} %get-tuple-element.38), channel_id=1, source_target_pairs={{0,2},{1,3},{2,0},{3,1},{4,6},{5,7},{6,4},{7,5},{8,10},{9,11},{10,... | collective-permute-start | bytes 1572872 | tf_op jit(solution)/shard_map/data_term/ppermute | solution.py:433
  67.6 12.6 %collective-permute-start.3 = (f32[1,1,2,4,2,16,256]{6,5,4,3,2,1,0:T(8,128)S(1)}, f32[1,1,2,4,2,16,256]{6,5,4,3,2,1,0:T(8,128)S(1)}, u32[]{:S(2)}, u32[]{:S(2)}) collective-permute-start(f32[1,1,2,4,2,16,256]{6,5,4,3,2,1,0:T(8,128)S(1)} %get-tuple-element.48), channel_id=1, source_target_pairs={{0,4},{1,5},{2,6},{3,7},{4,0},{5,1},{6,2},{7,3},{8,12},{9,13},{10,... | collective-permute-start | bytes 786440 | tf_op jit(solution)/shard_map/data_term/ppermute | solution.py:433
  78.2 10.8 %collective-permute-start.6 = (f32[1,1,2,4,2,16,256]{6,5,4,3,2,1,0:T(8,128)S(1)}, f32[1,1,2,4,2,16,256]{6,5,4,3,2,1,0:T(8,128)S(1)}, u32[]{:S(2)}, u32[]{:S(2)}) collective-permute-start(f32[1,1,2,4,2,16,256]{6,5,4,3,2,1,0:T(8,128)S(1)} %get-tuple-element.46.refs_1_), channel_id=1, source_target_pairs={{0,4},{1,5},{2,6},{3,7},{4,0},{5,1},{6,2},{7,3},{8,12},{9,13},{10,... | collective-permute-start | bytes 786440 | tf_op jit(solution)/shard_map/data_term/ppermute | solution.py:433
  80.3 13.5 %collective-permute-start.7 = (f32[1,1,1,4,2,16,256]{6,5,4,3,2,1,0:T(8,128)S(1)}, f32[1,1,1,4,2,16,256]{6,5,4,3,2,1,0:T(8,128)S(1)}, u32[]{:S(2)}, u32[]{:S(2)}) collective-permute-start(f32[1,1,1,4,2,16,256]{6,5,4,3,2,1,0:T(8,128)S(1)} %get-tuple-element.52.refs_0_), channel_id=1, source_target_pairs={{0,8},{1,9},{2,10},{3,11},{4,12},{5,13},{6,14},{7,15},{8,0},{9,1},... | collective-permute-start | bytes 393224 | tf_op jit(solution)/shard_map/data_term/ppermute | solution.py:433
  89.1 7.4 %collective-permute-start.8 = (f32[1,1,1,4,2,16,256]{6,5,4,3,2,1,0:T(8,128)S(1)}, f32[1,1,1,4,2,16,256]{6,5,4,3,2,1,0:T(8,128)S(1)}, u32[]{:S(2)}, u32[]{:S(2)}) collective-permute-start(f32[1,1,1,4,2,16,256]{6,5,4,3,2,1,0:T(8,128)S(1)} %get-tuple-element.50.refs_0_), channel_id=1, source_target_pairs={{0,8},{1,9},{2,10},{3,11},{4,12},{5,13},{6,14},{7,15},{8,0},{9,1},... | collective-permute-start | bytes 393224 | tf_op jit(solution)/shard_map/data_term/ppermute | solution.py:433

commit v5 on v4

--- a/solution.py
+++ b/solution.py
@@ -50,10 +50,12 @@
 def dot3(left, right, contract=((1,), (0,))):
     dims = (contract, ((), ()))
 
-    def dot(a, b):
-        return lax.dot_general(a, b, dims, preferred_element_type=jnp.float32)
-
-    return dot(left[0], right[0]) + (dot(left[0], right[1]) + dot(left[1], right[0]))
+    return lax.dot_general(
+        jnp.concatenate([left[0], left[0], left[1]], contract[0][0]),
+        jnp.concatenate([right[0], right[1], right[0]], contract[1][0]),
+        dims,
+        preferred_element_type=jnp.float32,
+    )
 
 
 def lane_exchange(parts, width):
@@ -168,8 +170,7 @@
 
 
 def coil_blocks_kernel(coils, *refs):
-    *tiles, before, out_ref = refs
-    del before
+    *tiles, out_ref = refs
     devices, pair_coils, rows, lanes = out_ref.shape
     halves = len(tiles) // 2
     each = lanes // (2 * LANES)
@@ -354,7 +355,7 @@
         )
         return 0
 
-    lax.fori_loop(0, grad_out.shape[0], one, 0)
+    lax.fori_loop(0, grad_out.shape[0], one, 0, unroll=2)
 
 
 def second_normal_kernel(start, maps_ref, field_ref, mask_ref, wave_hi, wave_lo, *refs):
@@ -381,7 +382,7 @@
             )
             return 0
 
-        lax.fori_loop(0, frames, one, 0)
+        lax.fori_loop(0, frames, one, 0, unroll=2)
         field[...] = tv_step(field[...] - step_size * (grad[...] - data_term))
     per = frames
     for h in range(devices // per):
@@ -476,6 +477,19 @@
 
     sens_rows = sens.reshape(rows * coils, packed)
     image_rows = image.reshape(rows * frames, packed)
+
+    with jax.named_scope("coil_maps"):
+        blocks = pl.pallas_call(
+            functools.partial(coil_blocks_kernel, coils),
+            grid=(1,),
+            out_shape=f32(devices, 2 * own, rows, half),
+            in_specs=lane_tiles(rows * coils, packed),
+            out_specs=whole((devices, 2 * own, rows, half)),
+            compiler_params=params(),
+            cost_estimate=cost(0, 2 * sens.size * 4),
+        )(*[sens_rows] * (packed // LANES))
+        blocks, device = lax.optimization_barrier((blocks, device))
+        coil_maps = lax.all_to_all(blocks, "coil", 0, 0, tiled=True)
 
     with jax.named_scope("column_maps"):
         level = 1
@@ -494,19 +508,6 @@
         )(device[None], *[sens_rows] * (packed // LANES), *[image_rows] * (packed // LANES))
         column_blocks = jnp.stack([column_keep, exchange(column_send, level)], 1)
         sides = [[with_bit(e, level, side) for e in range(devices // 2)] for side in range(2)]
-
-    with jax.named_scope("coil_maps"):
-        blocks = pl.pallas_call(
-            functools.partial(coil_blocks_kernel, coils),
-            grid=(1,),
-            out_shape=f32(devices, 2 * own, rows, half),
-            in_specs=lane_tiles(rows * coils, packed) + [pl.BlockSpec(memory_space=pl.ANY)],
-            out_specs=whole((devices, 2 * own, rows, half)),
-            compiler_params=params(),
-            cost_estimate=cost(0, 2 * sens.size * 4),
-        )(*[sens_rows] * (packed // LANES), column_send)
-        blocks, device = lax.optimization_barrier((blocks, device))
-        coil_maps = lax.all_to_all(blocks, "coil", 0, 0, tiled=True)
 
     plans = [
         (frames // 2, list(range(1, bits))),

time: 119 us -> 116 us (0.975)
  Pallas kernels: 46.7 us -> 44.3 us
  waiting for transfers between devices: 27.2 us -> 25.4 us
    ppermute x9, waiting for transfers between devices: 27.2 us -> 25.4 us  [exchange(): lax.ppermute(send, 'coil', [(i, i ^ 1 << bit) for i in range(devices)])]
  transfers between devices with their start and end apart: 11 -> 11, of which waited for: 6 -> 6; matrix products, arithmetic and copies ran while one was open for 3% -> 4% of each run, Pallas kernels for 30% -> 30%
where the time goes in v5:
time: 116 us; the launch traced here: 115 us
  Pallas kernels  44.3 us (38%)
  waiting for transfers between devices  25.4 us (22%)
  starting transfers between devices  23.6 us (20%)
  blocking collectives  13.2 us (11%)
  local copies, waits for them, and re-layouts  4.99 us (4%)
  other arithmetic  3.64 us (3%)
    ppermute x9, waiting for transfers between devices, exchange(): lax.ppermute(send, 'coil', [(i, i ^ 1 << bit) for i in range(devices)])  25.4 us
    pallas_call x2, Pallas kernels, kernel_path(): pl.pallas_call(functools.partial(base_kernel, start, frames), grid=(count...  17.3 us
    all_to_all x1, blocking collectives, kernel_path(): got = lax.all_to_all(blocks, 'coil', 0, 0, tiled=True)  13.2 us
    ppermute x9, starting transfers between devices, exchange(): lax.ppermute(send, 'coil', [(i, i ^ 1 << bit) for i in range(devices)])  11.4 us
    pallas_call x2, Pallas kernels, kernel_path(): pl.pallas_call(functools.partial(weigh_kernel, outer, order[0]), out_shap...  8.73 us
    all_to_all x1, starting transfers between devices, kernel_path(): coil_maps = lax.all_to_all(blocks, 'coil', 0, 0, tiled=True)  7.57 us
    pallas_call x1, Pallas kernels, kernel_path(): pl.pallas_call(steps_kernel, out_shape=f32(devices, 2, cols, LANES), scra...  6.99 us
    pallas_call x1, Pallas kernels, first_gradient(): pl.pallas_call(functools.partial(first_normal_kernel, coils, level), in_s...  4.77 us
  transfers between devices with their start and end apart: 11, of which 6 were waited for; matrix products, arithmetic and copies ran while one was open for 4% of the time, Pallas kernels for 30%

profile of v5, /device:TPU:0, one launch (start us, length us, event | category | flops | bytes accessed | tf_op | source)
XLA Modules:
  0.0 115.3 jit_solution(1315026976973556241)
XLA Ops:
  0.0 1.2 %copy-done = f32[16,32,512]{2,1,0:T(8,128)S(1)} copy-done((f32[16,32,512]{2,1,0:T(8,128)S(1)}, f32[16,32,512]{2,1,0:T(8,128)}, u32[]{:S(2)}) %copy-start) | copy-done | bytes 1048600
  1.2 1.7 %coil_maps.1 = f32[16,4,16,256]{3,2,1,0:T(8,128)} custom-call(f32[512,512]{1,0:T(8,128)S(1)} %bitcast.21, f32[512,512]{1,0:T(8,128)S(1)} %bitcast.22, f32[512,512]{1,0:T(8,128)S(1)} %bitcast.23, f32[512,512]{1,0:T(8,128)S(1)} %bitcast.24), custom_call_target="tpu_custom_call" | custom-call | bytes 2097152 | tf_op jit(solution)/shard_map/coil_maps/pallas_call | solution.py:482
  2.9 7.6 %all-to-all-start.1 = ((f32[16,4,16,256]{3,2,1,0:T(8,128)}), f32[16,4,16,256]{3,2,1,0:T(8,128)}, u32[]{:S(2)}, u32[]{:S(2)}) async-start(f32[16,4,16,256]{3,2,1,0:T(8,128)} %coil_maps.1), calls=%async_computation.1 | async-start | bytes 2097152 | tf_op jit(solution)/shard_map/coil_maps/all_to_all | solution.py:492
  11.5 1.9 %collective-permute-start = (f32[8,5,2,16,128]{4,3,2,1,0:T(8,128)S(1)}, f32[8,5,2,16,128]{4,3,2,1,0:T(8,128)S(1)}, u32[]{:S(2)}, u32[]{:S(2)}) collective-permute-start(f32[8,5,2,16,128]{4,3,2,1,0:T(8,128)S(1)} %get-tuple-element.27), channel_id=1, source_target_pairs={{0,2},{1,3},{2,0},{3,1},{4,6},{5,7},{6,4},{7,5},{8,10},{9,11},{10,... | collective-permute-start | bytes 1966088 | tf_op jit(solution)/shard_map/column_maps/ppermute | solution.py:434
  15.9 8.6 %data_transform.3 = (f32[2,4,2,128,256]{4,3,2,1,0:T(8,128)}, f32[2,4,2,128,256]{4,3,2,1,0:T(8,128)}) custom-call(s32[1]{0:T(128)} %bitcast.1.device_ref, f32[128,2,16,512]{3,2,1,0:T(8,128)} %bitcast.42, f32[8,1,256]{2,1,0:T(1,128)S(1)} %copy.11.mask_ref, bf16[512,512]{1,0:T(8,128)(2,1)S(1)} %copy-done.4, bf16[512,512]{1,0:T(8,128)(2,1)S(1)} %copy-done.3, ...), custom_call_target="tpu_custom_call" | custom-call | flops 4831838208 | bytes 8388608 | tf_op jit(solution)/shard_map/data_transform/pallas_call | solution.py:523
  24.7 8.6 %data_transform.2 = (f32[2,4,2,128,256]{4,3,2,1,0:T(8,128)}, f32[2,4,2,128,256]{4,3,2,1,0:T(8,128)}) custom-call(s32[1]{0:T(128)} %bitcast.1.device_ref, f32[128,2,16,512]{3,2,1,0:T(8,128)} %bitcast.43, f32[8,1,256]{2,1,0:T(1,128)S(1)} %copy.11.mask_ref, bf16[512,512]{1,0:T(8,128)(2,1)S(1)} %copy-done.4, bf16[512,512]{1,0:T(8,128)(2,1)S(1)} %copy-done.3, ...), custom_call_target="tpu_custom_call" | custom-call | flops 4831838208 | bytes 8388608 | tf_op jit(solution)/shard_map/data_transform/pallas_call | solution.py:523
  33.3 5.5 %collective-permute-done = f32[8,5,2,16,128]{4,3,2,1,0:T(8,128)S(1)} collective-permute-done((f32[8,5,2,16,128]{4,3,2,1,0:T(8,128)S(1)}, f32[8,5,2,16,128]{4,3,2,1,0:T(8,128)S(1)}, u32[]{:S(2)}, u32[]{:S(2)}) %collective-permute-start) | collective-permute-done | bytes 655392 | tf_op jit(solution)/shard_map/column_maps/ppermute | solution.py:434
  40.0 4.7 %all-to-all-start = ((f32[8,2,5,2,16,128]{5,4,3,2,1,0:T(8,128)}), f32[8,2,5,2,16,128]{5,4,3,2,1,0:T(8,128)S(1)}, u32[]{:S(2)}, u32[]{:S(2)}) async-start(f32[8,2,5,2,16,128]{5,4,3,2,1,0:T(8,128)} %pad_maximum_fusion), calls=%async_computation | async-start | bytes 2621440 | tf_op jit(solution)/shard_map/column_maps/all_to_all | solution.py:561
  44.7 4.4 %data_term.2 = (f32[4,4,2,16,256]{4,3,2,1,0:T(8,128)}, f32[4,4,2,16,256]{4,3,2,1,0:T(8,128)}) custom-call(s32[1]{0:T(128)} %bitcast.1.device_ref, f32[16,4,16,256]{3,2,1,0:T(8,128)} %all-to-all-done.1.maps_ref, f32[2,4,2,128,256]{4,3,2,1,0:T(8,128)} %get-tuple-element.31.kept_ref, f32[2,4,2,128,256]{4,3,2,1,0:T(8,128)} %collective-permute-done.1.got_ref), custom_call_target="tpu_custom_call" | custom-call | bytes 5242880 | tf_op jit(solution)/shard_map/data_term/pallas_call | solution.py:605
  49.7 1.3 %copy-done.9 = f32[2,4,2,128,256]{4,3,2,1,0:T(8,128)} copy-done((f32[2,4,2,128,256]{4,3,2,1,0:T(8,128)}, f32[2,4,2,128,256]{4,3,2,1,0:T(8,128)S(1)}, u32[]{:S(2)}) %copy-start.9) | copy-done | bytes 2097176
  51.0 4.4 %data_term.3 = (f32[4,4,2,16,256]{4,3,2,1,0:T(8,128)}, f32[4,4,2,16,256]{4,3,2,1,0:T(8,128)}) custom-call(s32[1]{0:T(128)} %bitcast.1.device_ref, f32[16,4,16,256]{3,2,1,0:T(8,128)} %all-to-all-done.1.maps_ref, f32[2,4,2,128,256]{4,3,2,1,0:T(8,128)} %get-tuple-element.35.kept_ref, f32[2,4,2,128,256]{4,3,2,1,0:T(8,128)} %copy-done.9), custom_call_target="tpu_custom_call" | custom-call | bytes 5242880 | tf_op jit(solution)/shard_map/data_term/pallas_call | solution.py:605
  55.4 1.5 %collective-permute-start.5 = (f32[4,4,2,16,256]{4,3,2,1,0:T(8,128)}, f32[4,4,2,16,256]{4,3,2,1,0:T(8,128)S(1)}, u32[]{:S(2)}, u32[]{:S(2)}) collective-permute-start(f32[4,4,2,16,256]{4,3,2,1,0:T(8,128)} %get-tuple-element.38), channel_id=1, source_target_pairs={{0,2},{1,3},{2,0},{3,1},{4,6},{5,7},{6,4},{7,5},{8,10},{9,11},{10,... | collective-permute-start | bytes 1572872 | tf_op jit(solution)/shard_map/data_term/ppermute | solution.py:434
  56.9 7.2 %collective-permute-done.2 = f32[4,4,2,16,256]{4,3,2,1,0:T(8,128)} collective-permute-done((f32[4,4,2,16,256]{4,3,2,1,0:T(8,128)}, f32[4,4,2,16,256]{4,3,2,1,0:T(8,128)}, u32[]{:S(2)}, u32[]{:S(2)}) %collective-permute-start.2) | collective-permute-done | bytes 524320 | tf_op jit(solution)/shard_map/data_term/ppermute | solution.py:434
  64.2 1.3 %dynamic-slice_add_fusion.3 = (f32[1,1,2,4,2,16,256]{6,5,4,3,2,1,0:T(8,128)S(1)}, f32[1,1,2,4,2,16,256]{6,5,4,3,2,1,0:T(8,128)S(1)}) fusion(f32[1,2,2,4,2,16,256]{6,5,4,3,2,1,0:T(8,128)} %bitcast.10, s32[]{:T(128)S(6)} %select_n.26, f32[1,2,2,4,2,16,256]{6,5,4,3,2,1,0:T(8,128)} %bitcast.39, s32[]{:T(128)S(6)} %select_n.28), kind=kLoop, calls=%fused_computation.4 | loop fusion | flops 131072 | bytes 1572872 | tf_op jit(solution)/shard_map/data_term/add | solution.py:441
  65.4 2.1 %collective-permute-start.3 = (f32[1,1,2,4,2,16,256]{6,5,4,3,2,1,0:T(8,128)S(1)}, f32[1,1,2,4,2,16,256]{6,5,4,3,2,1,0:T(8,128)S(1)}, u32[]{:S(2)}, u32[]{:S(2)}) collective-permute-start(f32[1,1,2,4,2,16,256]{6,5,4,3,2,1,0:T(8,128)S(1)} %get-tuple-element.48), channel_id=1, source_target_pairs={{0,4},{1,5},{2,6},{3,7},{4,0},{5,1},{6,2},{7,3},{8,12},{9,13},{10,... | collective-permute-start | bytes 786440 | tf_op jit(solution)/shard_map/data_term/ppermute | solution.py:434
  67.6 7.3 %collective-permute-done.5 = f32[4,4,2,16,256]{4,3,2,1,0:T(8,128)S(1)} collective-permute-done((f32[4,4,2,16,256]{4,3,2,1,0:T(8,128)}, f32[4,4,2,16,256]{4,3,2,1,0:T(8,128)S(1)}, u32[]{:S(2)}, u32[]{:S(2)}) %collective-permute-start.5) | collective-permute-done | bytes 524320 | tf_op jit(solution)/shard_map/data_term/ppermute | solution.py:434
  76.0 1.7 %collective-permute-start.6 = (f32[1,1,2,4,2,16,256]{6,5,4,3,2,1,0:T(8,128)S(1)}, f32[1,1,2,4,2,16,256]{6,5,4,3,2,1,0:T(8,128)S(1)}, u32[]{:S(2)}, u32[]{:S(2)}) collective-permute-start(f32[1,1,2,4,2,16,256]{6,5,4,3,2,1,0:T(8,128)S(1)} %get-tuple-element.46.refs_1_), channel_id=1, source_target_pairs={{0,4},{1,5},{2,6},{3,7},{4,0},{5,1},{6,2},{7,3},{8,12},{9,13},{10,... | collective-permute-start | bytes 786440 | tf_op jit(solution)/shard_map/data_term/ppermute | solution.py:434
  78.1 2.2 %collective-permute-start.7 = (f32[1,1,1,4,2,16,256]{6,5,4,3,2,1,0:T(8,128)S(1)}, f32[1,1,1,4,2,16,256]{6,5,4,3,2,1,0:T(8,128)S(1)}, u32[]{:S(2)}, u32[]{:S(2)}) collective-permute-start(f32[1,1,1,4,2,16,256]{6,5,4,3,2,1,0:T(8,128)S(1)} %get-tuple-element.52.refs_0_), channel_id=1, source_target_pairs={{0,8},{1,9},{2,10},{3,11},{4,12},{5,13},{6,14},{7,15},{8,0},{9,1},... | collective-permute-start | bytes 393224 | tf_op jit(solution)/shard_map/data_term/ppermute | solution.py:434
  80.2 4.8 %first_gradient.1 = (f32[32,2,16,256]{3,2,1,0:T(8,128)S(1)}, f32[8,2,16,256]{3,2,1,0:T(8,128)S(1)}, f32[4,2,16,256]{3,2,1,0:T(8,128)S(1)}) custom-call(s32[1]{0:T(128)} %bitcast.1.device_ref, f32[8,2,5,2,16,128]{5,4,3,2,1,0:T(8,128)S(1)} %all-to-all-done.got_ref, f32[2,8,128]{2,1,0:T(8,128)S(1)} %pad_maximum_fusion.1.mask_ref, ...), custom_call_target="tpu_custom_call" | custom-call | flops 1610612736 | bytes 4194304 | tf_op jit(solution)/shard_map/data_term/first_gradient/pallas_call | solution.py:585
  85.0 1.8 %collective-permute-done.6 = f32[1,1,2,4,2,16,256]{6,5,4,3,2,1,0:T(8,128)S(1)} collective-permute-done((f32[1,1,2,4,2,16,256]{6,5,4,3,2,1,0:T(8,128)S(1)}, f32[1,1,2,4,2,16,256]{6,5,4,3,2,1,0:T(8,128)S(1)}, u32[]{:S(2)}, u32[]{:S(2)}) %collective-permute-start.6) | collective-permute-done | bytes 262176 | tf_op jit(solution)/shard_map/data_term/ppermute | solution.py:434
  88.1 3.0 %second_gradient.1.grad1_ref = f32[4,2,16,256]{3,2,1,0:T(8,128)S(1)} custom-call(f32[32,2,16,256]{3,2,1,0:T(8,128)S(1)} %get-tuple-element.42.maps_ref, f32[8,2,16,256]{3,2,1,0:T(8,128)S(1)} %get-tuple-element.39.field_ref, f32[2,8,128]{2,1,0:T(8,128)S(1)} %pad_maximum_fusion.1.mask_ref, bf16[2,128,256]{2,1,0:T(8,128)(2,1)S(1)} %copy-done.8, ...), custom_call_target="tpu_custom_call" | custom-call | flops 1610612736 | bytes 2097152 | tf_op jit(solution)/shard_map/data_term/second_gradient/pallas_call | solution.py:574
  91.0 3.2 %collective-permute-done.8 = f32[1,1,1,4,2,16,256]{6,5,4,3,2,1,0:T(8,128)S(1)} collective-permute-done((f32[1,1,1,4,2,16,256]{6,5,4,3,2,1,0:T(8,128)S(1)}, f32[1,1,1,4,2,16,256]{6,5,4,3,2,1,0:T(8,128)S(1)}, u32[]{:S(2)}, u32[]{:S(2)}) %collective-permute-start.8) | collective-permute-done | bytes 131104 | tf_op jit(solution)/shard_map/data_term/ppermute | solution.py:434
  94.3 7.0 %outer_steps.1 = f32[16,2,16,128]{3,2,1,0:T(8,128)S(1)} custom-call(f32[8,2,16,256]{3,2,1,0:T(8,128)S(1)} %get-tuple-element.39.field_ref, f32[4,2,16,256]{3,2,1,0:T(8,128)S(1)} %get-tuple-element.41.grad0_ref, f32[4,2,16,256]{3,2,1,0:T(8,128)S(1)} %second_gradient.1.grad1_ref, f32[32,2,16,256]{3,2,1,0:T(8,128)S(1)} %get-tuple-element.42.maps_ref, ...), custom_call_target="tpu_custom_call" | custom-call | flops 3221225472 | bytes 4194304 | tf_op jit(solution)/shard_map/outer_steps/pallas_call | solution.py:644
  101.3 13.2 %all_to_all.15.got_ref = f32[16,2,16,128]{3,2,1,0:T(8,128)S(1)} all-to-all(f32[16,2,16,128]{3,2,1,0:T(8,128)S(1)} %outer_steps.1), channel_id=1, replica_groups=mesh['plane'=2,'coil'=16] {'coil'}, dimensions={0} | all-to-all | bytes 524288 | tf_op jit(solution)/shard_map/result_rows/all_to_all | solution.py:653
  (42 shorter events, 8.9 us)
Async XLA Ops:
  0.0 1.2 %copy-start = (f32[16,32,512]{2,1,0:T(8,128)S(1)}, f32[16,32,512]{2,1,0:T(8,128)}, u32[]{:S(2)}) copy-start(f32[16,32,512]{2,1,0:T(8,128)} %param.11) | copy-start | bytes 3145732
  2.9 7.6 %copy-start.1 = (f32[16,32,512]{2,1,0:T(8,128)S(1)}, f32[16,32,512]{2,1,0:T(8,128)}, u32[]{:S(2)}) copy-start(f32[16,32,512]{2,1,0:T(8,128)} %param.11) | copy-start | bytes 3145732
  2.9 7.6 %copy-start.2 = (f32[16,8,512]{2,1,0:T(8,128)S(1)}, f32[16,8,512]{2,1,0:T(8,128)}, u32[]{:S(2)}) copy-start(f32[16,8,512]{2,1,0:T(8,128)} %param.10) | copy-start | bytes 786436
  2.9 37.1 %all-to-all-start.1 = ((f32[16,4,16,256]{3,2,1,0:T(8,128)}), f32[16,4,16,256]{3,2,1,0:T(8,128)}, u32[]{:S(2)}, u32[]{:S(2)}) async-start(f32[16,4,16,256]{3,2,1,0:T(8,128)} %coil_maps.1), calls=%async_computation.1 | async-start | bytes 2097152 | tf_op jit(solution)/shard_map/coil_maps/all_to_all | solution.py:492
  10.5 3.0 %copy-start.10 = (s32[8,256]{1,0:T(8,128)S(1)}, s32[8,256]{1,0:T(8,128)}, u32[]{:S(2)}) copy-start(s32[8,256]{1,0:T(8,128)} %param.13) | copy-start | bytes 24580
  10.5 3.4 %copy-start.3 = (bf16[512,512]{1,0:T(8,128)(2,1)S(1)}, bf16[512,512]{1,0:T(8,128)(2,1)}, u32[]{:S(2)}) copy-start(bf16[512,512]{1,0:T(8,128)(2,1)} %constant.62.clone.refs_1_) | copy-start | bytes 1572868
  10.5 3.4 %copy-start.5 = (bf16[2,256,256]{2,1,0:T(8,128)(2,1)S(1)}, bf16[2,256,256]{2,1,0:T(8,128)(2,1)}, u32[]{:S(2)}) copy-start(bf16[2,256,256]{2,1,0:T(8,128)(2,1)} %constant.64.clone.refs_3_) | copy-start | bytes 786436
  11.5 27.3 %collective-permute-start = (f32[8,5,2,16,128]{4,3,2,1,0:T(8,128)S(1)}, f32[8,5,2,16,128]{4,3,2,1,0:T(8,128)S(1)}, u32[]{:S(2)}, u32[]{:S(2)}) collective-permute-start(f32[8,5,2,16,128]{4,3,2,1,0:T(8,128)S(1)} %get-tuple-element.27), channel_id=1, source_target_pairs={{0,2},{1,3},{2,0},{3,1},{4,6},{5,7},{6,4},{7,5},{8,10},{9,11},{10,... | collective-permute-start | bytes 1966088 | tf_op jit(solution)/shard_map/column_maps/ppermute | solution.py:434
  14.0 1.0 copy-start.4
  15.0 0.9 copy-start.6
  24.6 20.1 %collective-permute-start.1 = (f32[2,4,2,128,256]{4,3,2,1,0:T(8,128)}, f32[2,4,2,128,256]{4,3,2,1,0:T(8,128)}, u32[]{:S(2)}, u32[]{:S(2)}) collective-permute-start(f32[2,4,2,128,256]{4,3,2,1,0:T(8,128)} %get-tuple-element.32), channel_id=1, source_target_pairs={{0,1},{1,0},{2,3},{3,2},{4,5},{5,4},{6,7},{7,6},{8,9},{9,8},{10,11... | collective-permute-start | bytes 6291464 | tf_op jit(solution)/shard_map/ppermute | solution.py:434
  40.0 9.7 %collective-permute-start.4 = (f32[2,4,2,128,256]{4,3,2,1,0:T(8,128)}, f32[2,4,2,128,256]{4,3,2,1,0:T(8,128)S(1)}, u32[]{:S(2)}, u32[]{:S(2)}) collective-permute-start(f32[2,4,2,128,256]{4,3,2,1,0:T(8,128)} %get-tuple-element.36), channel_id=1, source_target_pairs={{0,1},{1,0},{2,3},{3,2},{4,5},{5,4},{6,7},{7,6},{8,9},{9,8},{10,11... | collective-permute-start | bytes 6291464 | tf_op jit(solution)/shard_map/ppermute | solution.py:434
  40.0 40.2 %all-to-all-start = ((f32[8,2,5,2,16,128]{5,4,3,2,1,0:T(8,128)}), f32[8,2,5,2,16,128]{5,4,3,2,1,0:T(8,128)S(1)}, u32[]{:S(2)}, u32[]{:S(2)}) async-start(f32[8,2,5,2,16,128]{5,4,3,2,1,0:T(8,128)} %pad_maximum_fusion), calls=%async_computation | async-start | bytes 2621440 | tf_op jit(solution)/shard_map/column_maps/all_to_all | solution.py:561
  49.1 15.1 %collective-permute-start.2 = (f32[4,4,2,16,256]{4,3,2,1,0:T(8,128)}, f32[4,4,2,16,256]{4,3,2,1,0:T(8,128)}, u32[]{:S(2)}, u32[]{:S(2)}) collective-permute-start(f32[4,4,2,16,256]{4,3,2,1,0:T(8,128)} %get-tuple-element.34), channel_id=1, source_target_pairs={{0,2},{1,3},{2,0},{3,1},{4,6},{5,7},{6,4},{7,5},{8,10},{9,11},{10,... | collective-permute-start | bytes 1572872 | tf_op jit(solution)/shard_map/data_term/ppermute | solution.py:434
  49.7 1.3 %copy-start.9 = (f32[2,4,2,128,256]{4,3,2,1,0:T(8,128)}, f32[2,4,2,128,256]{4,3,2,1,0:T(8,128)S(1)}, u32[]{:S(2)}) copy-start(f32[2,4,2,128,256]{4,3,2,1,0:T(8,128)S(1)} %collective-permute-done.4.got_ref) | copy-start | bytes 6291460
  55.4 24.8 %copy-start.7 = (bf16[2,128,256]{2,1,0:T(8,128)(2,1)S(1)}, bf16[2,128,256]{2,1,0:T(8,128)(2,1)}, u32[]{:S(2)}) copy-start(bf16[2,128,256]{2,1,0:T(8,128)(2,1)} %constant.66.clone.wave_lo.refs_1_) | copy-start | bytes 393220
  55.4 24.8 %copy-start.8 = (bf16[2,128,256]{2,1,0:T(8,128)(2,1)S(1)}, bf16[2,128,256]{2,1,0:T(8,128)(2,1)}, u32[]{:S(2)}) copy-start(bf16[2,128,256]{2,1,0:T(8,128)(2,1)} %constant.65.clone.wave_hi.refs_0_) | copy-start | bytes 393220
  55.4 19.5 %collective-permute-start.5 = (f32[4,4,2,16,256]{4,3,2,1,0:T(8,128)}, f32[4,4,2,16,256]{4,3,2,1,0:T(8,128)S(1)}, u32[]{:S(2)}, u32[]{:S(2)}) collective-permute-start(f32[4,4,2,16,256]{4,3,2,1,0:T(8,128)} %get-tuple-element.38), channel_id=1, source_target_pairs={{0,2},{1,3},{2,0},{3,1},{4,6},{5,7},{6,4},{7,5},{8,10},{9,11},{10,... | collective-permute-start | bytes 1572872 | tf_op jit(solution)/shard_map/data_term/ppermute | solution.py:434
  65.4 12.6 %collective-permute-start.3 = (f32[1,1,2,4,2,16,256]{6,5,4,3,2,1,0:T(8,128)S(1)}, f32[1,1,2,4,2,16,256]{6,5,4,3,2,1,0:T(8,128)S(1)}, u32[]{:S(2)}, u32[]{:S(2)}) collective-permute-start(f32[1,1,2,4,2,16,256]{6,5,4,3,2,1,0:T(8,128)S(1)} %get-tuple-element.48), channel_id=1, source_target_pairs={{0,4},{1,5},{2,6},{3,7},{4,0},{5,1},{6,2},{7,3},{8,12},{9,13},{10,... | collective-permute-start | bytes 786440 | tf_op jit(solution)/shard_map/data_term/ppermute | solution.py:434
  76.0 10.8 %collective-permute-start.6 = (f32[1,1,2,4,2,16,256]{6,5,4,3,2,1,0:T(8,128)S(1)}, f32[1,1,2,4,2,16,256]{6,5,4,3,2,1,0:T(8,128)S(1)}, u32[]{:S(2)}, u32[]{:S(2)}) collective-permute-start(f32[1,1,2,4,2,16,256]{6,5,4,3,2,1,0:T(8,128)S(1)} %get-tuple-element.46.refs_1_), channel_id=1, source_target_pairs={{0,4},{1,5},{2,6},{3,7},{4,0},{5,1},{6,2},{7,3},{8,12},{9,13},{10,... | collective-permute-start | bytes 786440 | tf_op jit(solution)/shard_map/data_term/ppermute | solution.py:434
  78.1 13.0 %collective-permute-start.7 = (f32[1,1,1,4,2,16,256]{6,5,4,3,2,1,0:T(8,128)S(1)}, f32[1,1,1,4,2,16,256]{6,5,4,3,2,1,0:T(8,128)S(1)}, u32[]{:S(2)}, u32[]{:S(2)}) collective-permute-start(f32[1,1,1,4,2,16,256]{6,5,4,3,2,1,0:T(8,128)S(1)} %get-tuple-element.52.refs_0_), channel_id=1, source_target_pairs={{0,8},{1,9},{2,10},{3,11},{4,12},{5,13},{6,14},{7,15},{8,0},{9,1},... | collective-permute-start | bytes 393224 | tf_op jit(solution)/shard_map/data_term/ppermute | solution.py:434
  86.9 7.4 %collective-permute-start.8 = (f32[1,1,1,4,2,16,256]{6,5,4,3,2,1,0:T(8,128)S(1)}, f32[1,1,1,4,2,16,256]{6,5,4,3,2,1,0:T(8,128)S(1)}, u32[]{:S(2)}, u32[]{:S(2)}) collective-permute-start(f32[1,1,1,4,2,16,256]{6,5,4,3,2,1,0:T(8,128)S(1)} %get-tuple-element.50.refs_0_), channel_id=1, source_target_pairs={{0,8},{1,9},{2,10},{3,11},{4,12},{5,13},{6,14},{7,15},{8,0},{9,1},... | collective-permute-start | bytes 393224 | tf_op jit(solution)/shard_map/data_term/ppermute | solution.py:434

commit v6 on v5

--- a/solution.py
+++ b/solution.py
@@ -191,7 +191,8 @@
 def column_blocks_kernel(coils, frames, chunk_of, level, device_ref, *refs):
     *tiles, keep_ref, send_ref, turned = refs
     sens_tiles, image_tiles = tiles[: len(tiles) // 2], tiles[len(tiles) // 2 :]
-    blocks, groups, _, cols, _ = keep_ref.shape
+    blocks, early, _, cols, _ = send_ref.shape
+    groups = (keep_ref.shape[1] + early) // 2
     rows = sens_tiles[0].shape[0] // coils
     per = LANES // rows
     half = len(sens_tiles) // 2
@@ -206,11 +207,12 @@
             turned[t // half, pl.ds(t % half * LANES, LANES)] = jnp.concatenate(
                 [ref[pl.ds(base + c, rows, stride=count), :] for c in range(per)], 0
             ).T
-        for out, side in ((keep_ref, mine), (send_ref, 1 - mine)):
+        other = (send_ref, g) if g < early else (keep_ref, g + groups - early)
+        for (out, unit), side in (((keep_ref, g), mine), (other, 1 - mine)):
             for e in range(blocks):
                 at = pl.multiple_of(chunk_of[with_bit(e, level, 0)] * cols + side * far, cols)
                 for part in range(2):
-                    out[e, g, part] = turned[part, pl.ds(at, cols)]
+                    out[e, unit, part] = turned[part, pl.ds(at, cols)]
 
 
 def base_kernel(start, frames, device_ref, kspace_ref, mask_ref, *refs):
@@ -275,65 +277,76 @@
                 ref[c, 0, part] = jnp.concatenate([e + o, e - o], 1)
 
 
-def weigh_kernel(outer, level, device_ref, maps_ref, kept_ref, got_ref, keep_out, send_out, *refs):
-    turned, kept, got, keep, send, arrived, left = refs
+def weigh_kernel(outer, level, flip, device_ref, maps_ref, kept_ref, got_ref, out_ref, *refs):
+    turned, kept, got, total, arrived, left = refs
     devices, pair_coils, rows, lanes = maps_ref.shape
     own, count = got_ref.shape[:2]
-    inner, _, _, cols, length = keep.shape
+    inner, _, _, cols, length = total.shape
     inner //= outer
+    span = inner * cols
+    bit, which = device_ref[0] & 1, ((device_ref[0] >> level) & 1) ^ flip
+    far = [pl.multiple_of((2 * i + which) * span, span) for i in range(outer)]
 
     copies = [
         [
-            pltpu.make_async_copy(src.at[:, f], dst.at[:, f], arrived.at[i, f])
-            for i, (src, dst) in enumerate(((kept_ref, kept), (got_ref, got)))
+            pltpu.make_async_copy(
+                src.at[:, f, :, pl.ds(far[i], span)],
+                dst.at[:, f, :, pl.ds(i * span, span)],
+                arrived.at[j, f, i],
+            )
+            for j, (src, dst) in enumerate(((kept_ref, kept), (got_ref, got)))
+            for i in range(outer)
         ]
         for f in range(count)
     ]
-    for pair in copies:
-        for copy in pair:
+    for group in copies:
+        for copy in group:
             copy.start()
     for c in range(pair_coils):
         one = maps_ref[:, c].reshape(length, lanes).T
         turned[c, 0] = one[: lanes // 2]
         turned[c, 1] = one[lanes // 2 :]
 
-    bit, mine = device_ref[0] & 1, (device_ref[0] >> level) & 1
-    span = inner * cols
     results = []
     for f in range(count):
         for copy in copies[f]:
             copy.wait()
-        for ref, which in ((send, 1 - mine), (keep, mine)):
-            for i in range(outer):
-                at = pl.ds(pl.multiple_of((2 * i + which) * span, span), span)
-                total_re = total_im = 0.0
-                for base, first in ((kept, bit * own), (got, (1 - bit) * own)):
-                    for c in range(own):
-                        s_re, s_im = turned[first + c, 0, at, :], turned[first + c, 1, at, :]
-                        b_re, b_im = base[c, f, 0, at, :], base[c, f, 1, at, :]
-                        total_re += s_re * b_re + s_im * b_im
-                        total_im += s_re * b_im - s_im * b_re
-                here = slice(i * inner, (i + 1) * inner)
-                ref[here, f, 0] = total_re.reshape(inner, cols, length)
-                ref[here, f, 1] = total_im.reshape(inner, cols, length)
-        for i, (src, dst) in enumerate(((send, send_out), (keep, keep_out))):
-            results.append(pltpu.make_async_copy(src.at[:, f], dst.at[:, f], left.at[i, f]))
-            results[-1].start()
+        for i in range(outer):
+            here = slice(i * span, (i + 1) * span)
+            total_re = total_im = 0.0
+            for base, first in ((kept, bit * own), (got, (1 - bit) * own)):
+                for c in range(own):
+                    s_re = turned[first + c, 0, pl.ds(far[i], span), :]
+                    s_im = turned[first + c, 1, pl.ds(far[i], span), :]
+                    b_re, b_im = base[c, f, 0, here, :], base[c, f, 1, here, :]
+                    total_re += s_re * b_re + s_im * b_im
+                    total_im += s_re * b_im - s_im * b_re
+            total[i * inner : (i + 1) * inner, f, 0] = total_re.reshape(inner, cols, length)
+            total[i * inner : (i + 1) * inner, f, 1] = total_im.reshape(inner, cols, length)
+        results.append(pltpu.make_async_copy(total.at[:, f], out_ref.at[:, f], left.at[f]))
+        results[-1].start()
     for copy in results:
         copy.wait()
 
 
-def first_normal_kernel(coils, level, device_ref, got_ref, mask_ref, wave_hi, wave_lo, *refs):
+def first_normal_kernel(
+    coils, level, device_ref, got_ref, late_ref, mask_ref, wave_hi, wave_lo, *refs
+):
     maps_out, field_out, grad_out, responses = refs[-4:]
     mask_responses(mask_ref, wave_hi, wave_lo, responses)
-    blocks, _, groups, _, cols, lanes = got_ref.shape
+    blocks, units, _, cols, lanes = got_ref.shape
+    groups = units // 2
+    early = groups - late_ref.shape[1]
     devices = 2 * blocks
     mine = (device_ref[0] >> level) & 1
     frames = field_out.shape[0]
 
     def block(s, g):
         e = ((s >> (level + 1)) << level) | (s & ((1 << level) - 1))
-        return got_ref[e, ((s >> level) & 1) ^ mine, g]
+        across = ((s >> level) & 1) ^ mine
+        if g < early:
+            return got_ref[e, g + across * (units - early)]
+        return jnp.where(across == 0, got_ref[e, g], late_ref[e, g - early])
 
     per = (coils + frames) // groups
     width = lanes // per
@@ -344,27 +357,16 @@
             for c in range(per):
                 out[base + c, :, :, h * lanes : (h + 1) * lanes] = exchanged[c]
 
-    gradient_frames(0, maps_out, field_out, responses, grad_out)
-
-
-def gradient_frames(start, maps_ref, field_ref, responses, grad_out):
-    def one(i, _):
-        f = start + i
-        grad_out[i, 0], grad_out[i, 1] = normal_frame(
-            maps_ref, field_ref[f, 0], field_ref[f, 1], frame_tables(responses, f)
+    def one(f, _):
+        grad_out[f, 0], grad_out[f, 1] = normal_frame(
+            maps_out, field_out[f, 0], field_out[f, 1], frame_tables(responses, f)
         )
         return 0
 
-    lax.fori_loop(0, grad_out.shape[0], one, 0, unroll=2)
-
-
-def second_normal_kernel(start, maps_ref, field_ref, mask_ref, wave_hi, wave_lo, *refs):
-    grad_out, responses = refs[-2:]
-    mask_responses(mask_ref, wave_hi, wave_lo, responses)
-    gradient_frames(start, maps_ref, field_ref, responses, grad_out)
-
-
-def steps_kernel(field_ref, grad0_ref, grad1_ref, maps_ref, mask_ref, *refs):
+    lax.fori_loop(0, frames, one, 0, unroll=2)
+
+
+def steps_kernel(field_ref, grad_ref, maps_ref, mask_ref, *refs):
     wave_hi, wave_lo, *terms, out_ref, field, grad, responses = refs
     frames, _, cols, length = field_ref.shape
     devices, _, _, lanes = out_ref.shape
@@ -372,8 +374,7 @@
     data_term = jnp.concatenate(
         [keep[...] + got[...] for keep, got in zip(terms[0::2], terms[1::2])], 0
     )
-    first = jnp.concatenate([grad0_ref[...], grad1_ref[...]], 0)
-    field[...] = tv_step(field_ref[...] - step_size * (first - data_term))
+    field[...] = tv_step(field_ref[...] - step_size * (grad_ref[...] - data_term))
     for sweep in range(1, OUTER):
 
         def one(f, _):
@@ -493,20 +494,23 @@
 
     with jax.named_scope("column_maps"):
         level = 1
-        block = (devices // 2, groups, 2, cols, LANES)
+        early = (groups + 1) // 2
+        keep_block = (devices // 2, 2 * groups - early, 2, cols, LANES)
+        send_block = (devices // 2, early, 2, cols, LANES)
         column_keep, column_send = pl.pallas_call(
             functools.partial(column_blocks_kernel, coils, frames, chunk_of, level),
             grid=(1,),
-            out_shape=(f32(*block),) * 2,
+            out_shape=(f32(*keep_block), f32(*send_block)),
             in_specs=[pl.BlockSpec(memory_space=pltpu.SMEM)]
             + lane_tiles(rows * coils, packed)
             + lane_tiles(rows * frames, packed),
-            out_specs=(whole(block),) * 2,
+            out_specs=(whole(keep_block), whole(send_block)),
             scratch_shapes=[pltpu.VMEM((2, half, LANES), jnp.float32)],
             compiler_params=params(),
             cost_estimate=cost(0, 2 * (sens.size + image.size) * 4),
         )(device[None], *[sens_rows] * (packed // LANES), *[image_rows] * (packed // LANES))
-        column_blocks = jnp.stack([column_keep, exchange(column_send, level)], 1)
+        column_send, device = lax.optimization_barrier((column_send, device))
+        column_blocks = jnp.concatenate([column_keep, exchange(column_send, level)], 1)
         sides = [[with_bit(e, level, side) for e in range(devices // 2)] for side in range(2)]
 
     plans = [
@@ -561,68 +565,58 @@
         column_maps = lax.all_to_all(
             column_blocks, "coil", 0, 0, tiled=True, axis_index_groups=sides
         )
+        column_late = exchange(column_maps[:, groups : 2 * groups - early], level)
 
     field = f32(frames, 2, cols, length)
     normal_cost = 6 * 2 * frames * coils * cols * length * length
 
     responses = pltpu.VMEM((2, frames, length), jnp.float32)
 
-    part = f32(frames // 2, 2, cols, length)
     anywhere = pl.BlockSpec(memory_space=pl.ANY)
-
-    def second_gradient(maps, field0, before):
-        return pl.pallas_call(
-            functools.partial(second_normal_kernel, frames // 2),
-            in_specs=[pl.BlockSpec(memory_space=pltpu.VMEM)] * 5 + [anywhere] * len(before),
-            out_shape=part,
-            scratch_shapes=[responses],
-            compiler_params=params(),
-            cost_estimate=cost(normal_cost // 2, 2 * sens.size * 4),
-            name="second_gradient",
-        )(maps, field0, mask_sides, wave_hi, wave_lo, *before)
 
     def first_gradient(column_maps, before):
         return pl.pallas_call(
             functools.partial(first_normal_kernel, coils, level),
             in_specs=[smem]
-            + [pl.BlockSpec(memory_space=pltpu.VMEM)] * 4
+            + [pl.BlockSpec(memory_space=pltpu.VMEM)] * 5
             + [pl.BlockSpec(memory_space=pl.ANY)] * len(before),
-            out_shape=(f32(coils, 2, cols, length), field, part),
+            out_shape=(f32(coils, 2, cols, length), field, field),
             scratch_shapes=[responses],
             compiler_params=params(),
-            cost_estimate=cost(normal_cost // 2, 4 * sens.size * 4),
+            cost_estimate=cost(normal_cost, 4 * sens.size * 4),
             name="first_gradient",
-        )(device[None], column_maps, mask_sides, wave_hi, wave_lo, *before)
+        )(device[None], column_maps, column_late, mask_sides, wave_hi, wave_lo, *before)
 
     with jax.named_scope("data_term"):
-        terms = []
-        for stream, (count, order) in enumerate(plans):
+
+        def weigh(stream, flip):
+            count, order = plans[stream]
             outer = 2 ** (order[0] - 1)
             out = f32(devices // 4, count, 2, cols, length)
             vmem, anywhere = pl.BlockSpec(memory_space=pltpu.VMEM), pl.BlockSpec(memory_space=pl.ANY)
-            base = pltpu.VMEM((own, count, 2, span, length), jnp.float32)
-            term = pltpu.VMEM(out.shape, jnp.float32)
-            keep, send = pl.pallas_call(
-                functools.partial(weigh_kernel, outer, order[0]),
-                out_shape=(out, out),
+            base = pltpu.VMEM((own, count, 2, span // 2, length), jnp.float32)
+            value = pl.pallas_call(
+                functools.partial(weigh_kernel, outer, order[0], flip),
+                out_shape=out,
                 in_specs=[smem, vmem, anywhere, anywhere],
-                out_specs=(anywhere, anywhere),
+                out_specs=anywhere,
                 scratch_shapes=[
                     pltpu.VMEM((2 * own, 2, span, length), jnp.float32),
                     base,
                     base,
-                    term,
-                    term,
-                    pltpu.SemaphoreType.DMA((2, count)),
-                    pltpu.SemaphoreType.DMA((2, count)),
+                    pltpu.VMEM(out.shape, jnp.float32),
+                    pltpu.SemaphoreType.DMA((2, count, outer)),
+                    pltpu.SemaphoreType.DMA((count,)),
                 ],
                 compiler_params=params(WEIGH_LIMIT),
-                cost_estimate=cost(0, 2 * kept[stream].size * 4 + 2 * out.size * 4),
+                cost_estimate=cost(0, kept[stream].size * 4 + out.size * 4),
             )(device[None], coil_maps, kept[stream], got[stream])
             dims = [2] * (bits - 1)
             dims[order[0] - 1] = 1
-            received = exchange(send, order[0]).reshape(*dims, *keep.shape[1:])
-            terms.append((keep.reshape(received.shape), received))
+            return value.reshape(*dims, *out.shape[1:])
+
+        received = [exchange(weigh(i, 1), plans[i][1][0]) for i in range(len(plans))]
+        terms = [(weigh(i, 0), received[i]) for i in range(len(plans))]
         sent = [None] * len(plans)
 
         def advance(stream, step):
@@ -630,14 +624,10 @@
             keep, sent[stream] = halve(*terms[stream], order[step], device)
             terms[stream] = (keep, exchange(sent[stream], order[step]))
 
-        for step in range(1, bits - 2):
+        for step in range(1, bits - 1):
             for stream in range(len(plans)):
                 advance(stream, step)
-        advance(0, bits - 2)
-        maps, field0, early = first_gradient(column_maps, sent)
-        terms[1], early = lax.optimization_barrier((terms[1], early))
-        advance(1, bits - 2)
-        late = second_gradient(maps, field0, sent[1:])
+        maps, field0, grad0 = first_gradient(column_maps, sent)
         terms = [value.reshape(-1, 2, cols, length) for term in terms for value in term]
 
     with jax.named_scope("outer_steps"):
@@ -647,7 +637,7 @@
             scratch_shapes=[pltpu.VMEM(field.shape, jnp.float32)] * 2 + [responses],
             compiler_params=params(),
             cost_estimate=cost(normal_cost, 4 * sens.size * 4),
-        )(field0, early, late, maps, mask_sides, wave_hi, wave_lo, *terms)
+        )(field0, grad0, maps, mask_sides, wave_hi, wave_lo, *terms)
 
     with jax.named_scope("result_rows"):
         got = lax.all_to_all(blocks, "coil", 0, 0, tiled=True)

time: 116 us -> 113 us (0.974)
  waiting for transfers between devices: 25.4 us -> 13.3 us
  Pallas kernels: 44.3 us -> 49.4 us
  starting transfers between devices: 23.6 us -> 25.5 us
    ppermute x9 -> x10, waiting for transfers between devices: 25.4 us -> 13.3 us  [exchange(): lax.ppermute(send, 'coil', [(i, i ^ 1 << bit) for i in range(devices)])]
    pallas_call x1, Pallas kernels: 4.77 us -> 7.45 us  [first_gradient(): pl.pallas_call(functools.partial(first_normal_kernel, coils, level), in_s...]
    pallas_call x3 -> x4, Pallas kernels: 11.7 us -> 14.4 us  [weigh(): pl.pallas_call(functools.partial(weigh_kernel, outer, order[0], flip), ou...]
    ppermute x9 -> x10, starting transfers between devices: 11.4 us -> 13 us  [exchange(): lax.ppermute(send, 'coil', [(i, i ^ 1 << bit) for i in range(devices)])]
    another operation x1 -> x0, other arithmetic: 1.18 us -> none  [kernel_path(): column_blocks = jnp.stack([column_keep, exchange(column_send, level)], 1)]
    concatenate x0 -> x1, other arithmetic: none -> 1.18 us  [kernel_path(): jnp.concatenate([column_keep, exchange(column_send, level)], 1)]
    unnamed x22 -> x24, local copies, waits for them, and re-layouts: 4.57 us -> 4.65 us
  transfers between devices with their start and end apart: 11 -> 12, of which waited for: 6 -> 4; matrix products, arithmetic and copies ran while one was open for 4% -> 4% of each run, Pallas kernels for 30% -> 36%
where the time goes in v6:
time: 113 us; the launch traced here: 112 us
  Pallas kernels  49.4 us (44%)
  starting transfers between devices  25.5 us (23%)
  blocking collectives  14.2 us (13%)
  waiting for transfers between devices  13.3 us (12%)
  local copies, waits for them, and re-layouts  5.09 us (5%)
  other arithmetic  4.19 us (4%)
    pallas_call x2, Pallas kernels, kernel_path(): pl.pallas_call(functools.partial(base_kernel, start, frames), grid=(count...  17.2 us
    pallas_call x4, Pallas kernels, weigh(): pl.pallas_call(functools.partial(weigh_kernel, outer, order[0], flip), ou...  14.4 us
    all_to_all x1, blocking collectives, kernel_path(): got = lax.all_to_all(blocks, 'coil', 0, 0, tiled=True)  14.2 us
    ppermute x10, waiting for transfers between devices, exchange(): lax.ppermute(send, 'coil', [(i, i ^ 1 << bit) for i in range(devices)])  13.3 us
    ppermute x10, starting transfers between devices, exchange(): lax.ppermute(send, 'coil', [(i, i ^ 1 << bit) for i in range(devices)])  13 us
    all_to_all x1, starting transfers between devices, kernel_path(): coil_maps = lax.all_to_all(blocks, 'coil', 0, 0, tiled=True)  7.57 us
    pallas_call x1, Pallas kernels, first_gradient(): pl.pallas_call(functools.partial(first_normal_kernel, coils, level), in_s...  7.45 us
    pallas_call x1, Pallas kernels, kernel_path(): pl.pallas_call(steps_kernel, out_shape=f32(devices, 2, cols, LANES), scra...  6.84 us
  transfers between devices with their start and end apart: 12, of which 4 were waited for; matrix products, arithmetic and copies ran while one was open for 4% of the time, Pallas kernels for 36%

profile of v6, /device:TPU:0, one launch (start us, length us, event | category | flops | bytes accessed | tf_op | source)
XLA Modules:
  0.0 111.9 jit_solution(9007718055589990320)
XLA Ops:
  0.0 1.2 %copy-done = f32[16,32,512]{2,1,0:T(8,128)S(1)} copy-done((f32[16,32,512]{2,1,0:T(8,128)S(1)}, f32[16,32,512]{2,1,0:T(8,128)}, u32[]{:S(2)}) %copy-start) | copy-done | bytes 1048600
  1.2 1.7 %coil_maps.1 = f32[16,4,16,256]{3,2,1,0:T(8,128)} custom-call(f32[512,512]{1,0:T(8,128)S(1)} %bitcast.20, f32[512,512]{1,0:T(8,128)S(1)} %bitcast.21, f32[512,512]{1,0:T(8,128)S(1)} %bitcast.22, f32[512,512]{1,0:T(8,128)S(1)} %bitcast.23), custom_call_target="tpu_custom_call" | custom-call | bytes 2097152 | tf_op jit(solution)/shard_map/coil_maps/pallas_call | solution.py:483
  2.9 7.6 %all-to-all-start.1 = ((f32[16,4,16,256]{3,2,1,0:T(8,128)}), f32[16,4,16,256]{3,2,1,0:T(8,128)}, u32[]{:S(2)}, u32[]{:S(2)}) async-start(f32[16,4,16,256]{3,2,1,0:T(8,128)} %coil_maps.1), calls=%async_computation.1 | async-start | bytes 2097152 | tf_op jit(solution)/shard_map/coil_maps/all_to_all | solution.py:493
  11.5 1.9 %collective-permute-start = (f32[8,3,2,16,128]{4,3,2,1,0:T(8,128)S(1)}, f32[8,3,2,16,128]{4,3,2,1,0:T(8,128)S(1)}, u32[]{:S(2)}, u32[]{:S(2)}) collective-permute-start(f32[8,3,2,16,128]{4,3,2,1,0:T(8,128)S(1)} %get-tuple-element.24), channel_id=1, source_target_pairs={{0,2},{1,3},{2,0},{3,1},{4,6},{5,7},{6,4},{7,5},{8,10},{9,11},{10,... | collective-permute-start | bytes 1179656 | tf_op jit(solution)/shard_map/column_maps/ppermute | solution.py:435
  15.9 8.6 %data_transform.3 = (f32[2,4,2,128,256]{4,3,2,1,0:T(8,128)}, f32[2,4,2,128,256]{4,3,2,1,0:T(8,128)}) custom-call(s32[1]{0:T(128)} %bitcast.3.device_ref, f32[128,2,16,512]{3,2,1,0:T(8,128)} %bitcast.40, f32[8,1,256]{2,1,0:T(1,128)S(1)} %copy.11.mask_ref, bf16[512,512]{1,0:T(8,128)(2,1)S(1)} %copy-done.3, bf16[512,512]{1,0:T(8,128)(2,1)S(1)} %copy-done.4, ...), custom_call_target="tpu_custom_call" | custom-call | flops 4831838208 | bytes 8388608 | tf_op jit(solution)/shard_map/data_transform/pallas_call | solution.py:527
  24.6 8.6 %data_transform.2 = (f32[2,4,2,128,256]{4,3,2,1,0:T(8,128)}, f32[2,4,2,128,256]{4,3,2,1,0:T(8,128)}) custom-call(s32[1]{0:T(128)} %bitcast.3.device_ref, f32[128,2,16,512]{3,2,1,0:T(8,128)} %bitcast.41, f32[8,1,256]{2,1,0:T(1,128)S(1)} %copy.11.mask_ref, bf16[512,512]{1,0:T(8,128)(2,1)S(1)} %copy-done.3, bf16[512,512]{1,0:T(8,128)(2,1)S(1)} %copy-done.4, ...), custom_call_target="tpu_custom_call" | custom-call | flops 4831838208 | bytes 8388608 | tf_op jit(solution)/shard_map/data_transform/pallas_call | solution.py:527
  33.3 1.2 %pad_maximum_fusion = f32[8,10,2,16,128]{4,3,2,1,0:T(8,128)} fusion(f32[8,3,2,16,128]{4,3,2,1,0:T(8,128)S(1)} %collective-permute-done, f32[8,7,2,16,128]{4,3,2,1,0:T(8,128)S(1)} %get-tuple-element.23), kind=kLoop, calls=%fused_computation | loop fusion | flops 327680 | bytes 2621440 | tf_op jit(solution)/shard_map/column_maps/concatenate | solution.py:513
  34.9 4.9 %all-to-all-start = ((f32[8,10,2,16,128]{4,3,2,1,0:T(8,128)}), f32[8,10,2,16,128]{4,3,2,1,0:T(8,128)S(1)}, u32[]{:S(2)}, u32[]{:S(2)}) async-start(f32[8,10,2,16,128]{4,3,2,1,0:T(8,128)} %pad_maximum_fusion), calls=%async_computation | async-start | bytes 2621440 | tf_op jit(solution)/shard_map/column_maps/all_to_all | solution.py:565
  39.8 3.6 %data_term.5 = f32[4,4,2,16,256]{4,3,2,1,0:T(8,128)} custom-call(s32[1]{0:T(128)} %bitcast.3.device_ref, f32[16,4,16,256]{3,2,1,0:T(8,128)} %all-to-all-done.1.maps_ref, f32[2,4,2,128,256]{4,3,2,1,0:T(8,128)} %get-tuple-element.28.kept_ref, f32[2,4,2,128,256]{4,3,2,1,0:T(8,128)} %collective-permute-done.2.got_ref), custom_call_target="tpu_custom_call" | custom-call | bytes 2621440 | tf_op jit(solution)/shard_map/data_term/pallas_call | solution.py:598
  43.4 1.1 collective-permute-start.3
  44.5 1.4 %copy-done.9 = f32[2,4,2,128,256]{4,3,2,1,0:T(8,128)} copy-done((f32[2,4,2,128,256]{4,3,2,1,0:T(8,128)}, f32[2,4,2,128,256]{4,3,2,1,0:T(8,128)S(1)}, u32[]{:S(2)}) %copy-start.9) | copy-done | bytes 2097176
  45.9 3.6 %data_term.7 = f32[4,4,2,16,256]{4,3,2,1,0:T(8,128)} custom-call(s32[1]{0:T(128)} %bitcast.3.device_ref, f32[16,4,16,256]{3,2,1,0:T(8,128)} %all-to-all-done.1.maps_ref, f32[2,4,2,128,256]{4,3,2,1,0:T(8,128)} %get-tuple-element.30.kept_ref, f32[2,4,2,128,256]{4,3,2,1,0:T(8,128)} %copy-done.9), custom_call_target="tpu_custom_call" | custom-call | bytes 2621440 | tf_op jit(solution)/shard_map/data_term/pallas_call | solution.py:598
  50.5 3.6 %data_term.4 = f32[4,4,2,16,256]{4,3,2,1,0:T(8,128)} custom-call(s32[1]{0:T(128)} %bitcast.3.device_ref, f32[16,4,16,256]{3,2,1,0:T(8,128)} %all-to-all-done.1.maps_ref, f32[2,4,2,128,256]{4,3,2,1,0:T(8,128)} %get-tuple-element.28.kept_ref, f32[2,4,2,128,256]{4,3,2,1,0:T(8,128)} %collective-permute-done.2.got_ref), custom_call_target="tpu_custom_call" | custom-call | bytes 2621440 | tf_op jit(solution)/shard_map/data_term/pallas_call | solution.py:598
  54.1 3.6 %data_term.6 = f32[4,4,2,16,256]{4,3,2,1,0:T(8,128)} custom-call(s32[1]{0:T(128)} %bitcast.3.device_ref, f32[16,4,16,256]{3,2,1,0:T(8,128)} %all-to-all-done.1.maps_ref, f32[2,4,2,128,256]{4,3,2,1,0:T(8,128)} %get-tuple-element.30.kept_ref, f32[2,4,2,128,256]{4,3,2,1,0:T(8,128)} %copy-done.9), custom_call_target="tpu_custom_call" | custom-call | bytes 2621440 | tf_op jit(solution)/shard_map/data_term/pallas_call | solution.py:598
  58.5 1.8 %dynamic-slice_add_fusion.3 = (f32[1,1,2,4,2,16,256]{6,5,4,3,2,1,0:T(8,128)S(1)}, f32[1,1,2,4,2,16,256]{6,5,4,3,2,1,0:T(8,128)}) fusion(f32[1,2,2,4,2,16,256]{6,5,4,3,2,1,0:T(8,128)} %collective-permute-done.3, s32[]{:T(128)S(6)} %select_n.26, f32[1,2,2,4,2,16,256]{6,5,4,3,2,1,0:T(8,128)S(1)} %bitcast.35, s32[]{:T(128)S(6)} %select_n.28), kind=kLoop, calls=%fused_computation.4 | loop fusion | flops 131072 | bytes 1572872 | tf_op jit(solution)/shard_map/data_term/add | solution.py:442
  60.3 2.1 %collective-permute-start.4 = (f32[1,1,2,4,2,16,256]{6,5,4,3,2,1,0:T(8,128)}, f32[1,1,2,4,2,16,256]{6,5,4,3,2,1,0:T(8,128)S(1)}, u32[]{:S(2)}, u32[]{:S(2)}) collective-permute-start(f32[1,1,2,4,2,16,256]{6,5,4,3,2,1,0:T(8,128)} %get-tuple-element.38), channel_id=1, source_target_pairs={{0,4},{1,5},{2,6},{3,7},{4,0},{5,1},{6,2},{7,3},{8,12},{9,13},{10,... | collective-permute-start | bytes 786440 | tf_op jit(solution)/shard_map/data_term/ppermute | solution.py:435
  62.4 6.9 %collective-permute-done.6 = f32[1,2,2,4,2,16,256]{6,5,4,3,2,1,0:T(8,128)S(1)} collective-permute-done((f32[1,2,2,4,2,16,256]{6,5,4,3,2,1,0:T(8,128)}, f32[1,2,2,4,2,16,256]{6,5,4,3,2,1,0:T(8,128)S(1)}, u32[]{:S(2)}, u32[]{:S(2)}) %collective-permute-start.6) | collective-permute-done | bytes 524320 | tf_op jit(solution)/shard_map/data_term/ppermute | solution.py:435
  69.2 1.1 dynamic-slice_add_fusion.1
  70.4 1.7 %collective-permute-start.7 = (f32[1,1,2,4,2,16,256]{6,5,4,3,2,1,0:T(8,128)S(1)}, f32[1,1,2,4,2,16,256]{6,5,4,3,2,1,0:T(8,128)S(1)}, u32[]{:S(2)}, u32[]{:S(2)}) collective-permute-start(f32[1,1,2,4,2,16,256]{6,5,4,3,2,1,0:T(8,128)S(1)} %get-tuple-element.36), channel_id=1, source_target_pairs={{0,4},{1,5},{2,6},{3,7},{4,0},{5,1},{6,2},{7,3},{8,12},{9,13},{10,... | collective-permute-start | bytes 786440 | tf_op jit(solution)/shard_map/data_term/ppermute | solution.py:435
  73.4 2.5 %collective-permute-start.8 = (f32[1,1,1,4,2,16,256]{6,5,4,3,2,1,0:T(8,128)S(1)}, f32[1,1,1,4,2,16,256]{6,5,4,3,2,1,0:T(8,128)S(1)}, u32[]{:S(2)}, u32[]{:S(2)}) collective-permute-start(f32[1,1,1,4,2,16,256]{6,5,4,3,2,1,0:T(8,128)S(1)} %get-tuple-element.42.refs_0_), channel_id=1, source_target_pairs={{0,8},{1,9},{2,10},{3,11},{4,12},{5,13},{6,14},{7,15},{8,0},{9,1},... | collective-permute-start | bytes 393224 | tf_op jit(solution)/shard_map/data_term/ppermute | solution.py:435
  75.9 5.6 %collective-permute-done.7 = f32[1,1,2,4,2,16,256]{6,5,4,3,2,1,0:T(8,128)S(1)} collective-permute-done((f32[1,1,2,4,2,16,256]{6,5,4,3,2,1,0:T(8,128)S(1)}, f32[1,1,2,4,2,16,256]{6,5,4,3,2,1,0:T(8,128)S(1)}, u32[]{:S(2)}, u32[]{:S(2)}) %collective-permute-start.7) | collective-permute-done | bytes 262176 | tf_op jit(solution)/shard_map/data_term/ppermute | solution.py:435
  82.5 7.4 %first_gradient.1 = (f32[32,2,16,256]{3,2,1,0:T(8,128)S(1)}, f32[8,2,16,256]{3,2,1,0:T(8,128)S(1)}, f32[8,2,16,256]{3,2,1,0:T(8,128)S(1)}) custom-call(s32[1]{0:T(128)} %bitcast.3.device_ref, f32[8,10,2,16,128]{4,3,2,1,0:T(8,128)S(1)} %all-to-all-done.got_ref, f32[8,2,2,16,128]{4,3,2,1,0:T(8,128)S(1)} %collective-permute-done.1.late_ref, ...), custom_call_target="tpu_custom_call" | custom-call | flops 3221225472 | bytes 4194304 | tf_op jit(solution)/shard_map/data_term/first_gradient/pallas_call | solution.py:578
  90.0 6.8 %outer_steps.1 = f32[16,2,16,128]{3,2,1,0:T(8,128)S(1)} custom-call(f32[8,2,16,256]{3,2,1,0:T(8,128)S(1)} %get-tuple-element.32.field_ref, f32[8,2,16,256]{3,2,1,0:T(8,128)S(1)} %get-tuple-element.33.grad_ref, f32[32,2,16,256]{3,2,1,0:T(8,128)S(1)} %get-tuple-element.34.maps_ref, f32[2,8,128]{2,1,0:T(8,128)S(1)} %pad_maximum_fusion.1.mask_ref, ...), custom_call_target="tpu_custom_call" | custom-call | flops 3221225472 | bytes 4194304 | tf_op jit(solution)/shard_map/outer_steps/pallas_call | solution.py:634
  96.9 14.2 %all_to_all.15.got_ref = f32[16,2,16,128]{3,2,1,0:T(8,128)S(1)} all-to-all(f32[16,2,16,128]{3,2,1,0:T(8,128)S(1)} %outer_steps.1), channel_id=1, replica_groups=mesh['plane'=2,'coil'=16] {'coil'}, dimensions={0} | all-to-all | bytes 524288 | tf_op jit(solution)/shard_map/result_rows/all_to_all | solution.py:643
  (48 shorter events, 9.0 us)
Async XLA Ops:
  0.0 1.2 %copy-start = (f32[16,32,512]{2,1,0:T(8,128)S(1)}, f32[16,32,512]{2,1,0:T(8,128)}, u32[]{:S(2)}) copy-start(f32[16,32,512]{2,1,0:T(8,128)} %param.11) | copy-start | bytes 3145732
  2.9 7.6 %copy-start.1 = (f32[16,32,512]{2,1,0:T(8,128)S(1)}, f32[16,32,512]{2,1,0:T(8,128)}, u32[]{:S(2)}) copy-start(f32[16,32,512]{2,1,0:T(8,128)} %param.11) | copy-start | bytes 3145732
  2.9 7.6 %copy-start.2 = (f32[16,8,512]{2,1,0:T(8,128)S(1)}, f32[16,8,512]{2,1,0:T(8,128)}, u32[]{:S(2)}) copy-start(f32[16,8,512]{2,1,0:T(8,128)} %param.10) | copy-start | bytes 786436
  2.9 32.0 %all-to-all-start.1 = ((f32[16,4,16,256]{3,2,1,0:T(8,128)}), f32[16,4,16,256]{3,2,1,0:T(8,128)}, u32[]{:S(2)}, u32[]{:S(2)}) async-start(f32[16,4,16,256]{3,2,1,0:T(8,128)} %coil_maps.1), calls=%async_computation.1 | async-start | bytes 2097152 | tf_op jit(solution)/shard_map/coil_maps/all_to_all | solution.py:493
  10.5 3.0 %copy-start.11 = (s32[8,256]{1,0:T(8,128)S(1)}, s32[8,256]{1,0:T(8,128)}, u32[]{:S(2)}) copy-start(s32[8,256]{1,0:T(8,128)} %param.13) | copy-start | bytes 24580
  10.5 3.4 %copy-start.3 = (bf16[512,512]{1,0:T(8,128)(2,1)S(1)}, bf16[512,512]{1,0:T(8,128)(2,1)}, u32[]{:S(2)}) copy-start(bf16[512,512]{1,0:T(8,128)(2,1)} %constant.61.clone.refs_0_) | copy-start | bytes 1572868
  10.5 3.4 %copy-start.5 = (bf16[2,256,256]{2,1,0:T(8,128)(2,1)S(1)}, bf16[2,256,256]{2,1,0:T(8,128)(2,1)}, u32[]{:S(2)}) copy-start(bf16[2,256,256]{2,1,0:T(8,128)(2,1)} %constant.63.clone.refs_2_) | copy-start | bytes 786436
  11.5 21.7 %collective-permute-start = (f32[8,3,2,16,128]{4,3,2,1,0:T(8,128)S(1)}, f32[8,3,2,16,128]{4,3,2,1,0:T(8,128)S(1)}, u32[]{:S(2)}, u32[]{:S(2)}) collective-permute-start(f32[8,3,2,16,128]{4,3,2,1,0:T(8,128)S(1)} %get-tuple-element.24), channel_id=1, source_target_pairs={{0,2},{1,3},{2,0},{3,1},{4,6},{5,7},{6,4},{7,5},{8,10},{9,11},{10,... | collective-permute-start | bytes 1179656 | tf_op jit(solution)/shard_map/column_maps/ppermute | solution.py:435
  14.0 1.0 copy-start.4
  15.0 0.9 copy-start.6
  24.5 15.3 %collective-permute-start.2 = (f32[2,4,2,128,256]{4,3,2,1,0:T(8,128)}, f32[2,4,2,128,256]{4,3,2,1,0:T(8,128)}, u32[]{:S(2)}, u32[]{:S(2)}) collective-permute-start(f32[2,4,2,128,256]{4,3,2,1,0:T(8,128)} %get-tuple-element.29), channel_id=1, source_target_pairs={{0,1},{1,0},{2,3},{3,2},{4,5},{5,4},{6,7},{7,6},{8,9},{9,8},{10,11... | collective-permute-start | bytes 6291464 | tf_op jit(solution)/shard_map/ppermute | solution.py:435
  34.4 10.0 %collective-permute-start.5 = (f32[2,4,2,128,256]{4,3,2,1,0:T(8,128)}, f32[2,4,2,128,256]{4,3,2,1,0:T(8,128)S(1)}, u32[]{:S(2)}, u32[]{:S(2)}) collective-permute-start(f32[2,4,2,128,256]{4,3,2,1,0:T(8,128)} %get-tuple-element.31), channel_id=1, source_target_pairs={{0,1},{1,0},{2,3},{3,2},{4,5},{5,4},{6,7},{7,6},{8,9},{9,8},{10,11... | collective-permute-start | bytes 6291464 | tf_op jit(solution)/shard_map/ppermute | solution.py:435
  34.9 37.2 %all-to-all-start = ((f32[8,10,2,16,128]{4,3,2,1,0:T(8,128)}), f32[8,10,2,16,128]{4,3,2,1,0:T(8,128)S(1)}, u32[]{:S(2)}, u32[]{:S(2)}) async-start(f32[8,10,2,16,128]{4,3,2,1,0:T(8,128)} %pad_maximum_fusion), calls=%async_computation | async-start | bytes 2621440 | tf_op jit(solution)/shard_map/column_maps/all_to_all | solution.py:565
  43.4 15.1 %collective-permute-start.3 = (f32[1,2,2,4,2,16,256]{6,5,4,3,2,1,0:T(8,128)}, f32[1,2,2,4,2,16,256]{6,5,4,3,2,1,0:T(8,128)}, u32[]{:S(2)}, u32[]{:S(2)}) collective-permute-start(f32[1,2,2,4,2,16,256]{6,5,4,3,2,1,0:T(8,128)} %bitcast.37), channel_id=1, source_target_pairs={{0,2},{1,3},{2,0},{3,1},{4,6},{5,7},{6,4},{7,5},{8,10},{9,11},{10,... | collective-permute-start | bytes 1572872 | tf_op jit(solution)/shard_map/data_term/ppermute | solution.py:435
  44.5 1.4 %copy-start.9 = (f32[2,4,2,128,256]{4,3,2,1,0:T(8,128)}, f32[2,4,2,128,256]{4,3,2,1,0:T(8,128)S(1)}, u32[]{:S(2)}) copy-start(f32[2,4,2,128,256]{4,3,2,1,0:T(8,128)S(1)} %collective-permute-done.5.got_ref) | copy-start | bytes 6291460
  49.5 19.8 %collective-permute-start.6 = (f32[1,2,2,4,2,16,256]{6,5,4,3,2,1,0:T(8,128)}, f32[1,2,2,4,2,16,256]{6,5,4,3,2,1,0:T(8,128)S(1)}, u32[]{:S(2)}, u32[]{:S(2)}) collective-permute-start(f32[1,2,2,4,2,16,256]{6,5,4,3,2,1,0:T(8,128)} %bitcast.36), channel_id=1, source_target_pairs={{0,2},{1,3},{2,0},{3,1},{4,6},{5,7},{6,4},{7,5},{8,10},{9,11},{10,... | collective-permute-start | bytes 1572872 | tf_op jit(solution)/shard_map/data_term/ppermute | solution.py:435
  54.1 4.4 %copy-start.10 = (f32[4,4,2,16,256]{4,3,2,1,0:T(8,128)S(1)}, f32[4,4,2,16,256]{4,3,2,1,0:T(8,128)}, u32[]{:S(2)}) copy-start(f32[4,4,2,16,256]{4,3,2,1,0:T(8,128)} %data_term.4) | copy-start | bytes 1572868
  60.3 22.2 %copy-start.7 = (bf16[2,128,256]{2,1,0:T(8,128)(2,1)S(1)}, bf16[2,128,256]{2,1,0:T(8,128)(2,1)}, u32[]{:S(2)}) copy-start(bf16[2,128,256]{2,1,0:T(8,128)(2,1)} %constant.65.clone.wave_hi.refs_0_) | copy-start | bytes 393220
  60.3 22.2 %copy-start.8 = (bf16[2,128,256]{2,1,0:T(8,128)(2,1)S(1)}, bf16[2,128,256]{2,1,0:T(8,128)(2,1)}, u32[]{:S(2)}) copy-start(bf16[2,128,256]{2,1,0:T(8,128)(2,1)} %constant.66.clone.wave_lo.refs_1_) | copy-start | bytes 393220
  60.3 13.0 %collective-permute-start.4 = (f32[1,1,2,4,2,16,256]{6,5,4,3,2,1,0:T(8,128)}, f32[1,1,2,4,2,16,256]{6,5,4,3,2,1,0:T(8,128)S(1)}, u32[]{:S(2)}, u32[]{:S(2)}) collective-permute-start(f32[1,1,2,4,2,16,256]{6,5,4,3,2,1,0:T(8,128)} %get-tuple-element.38), channel_id=1, source_target_pairs={{0,4},{1,5},{2,6},{3,7},{4,0},{5,1},{6,2},{7,3},{8,12},{9,13},{10,... | collective-permute-start | bytes 786440 | tf_op jit(solution)/shard_map/data_term/ppermute | solution.py:435
  70.4 11.1 %collective-permute-start.7 = (f32[1,1,2,4,2,16,256]{6,5,4,3,2,1,0:T(8,128)S(1)}, f32[1,1,2,4,2,16,256]{6,5,4,3,2,1,0:T(8,128)S(1)}, u32[]{:S(2)}, u32[]{:S(2)}) collective-permute-start(f32[1,1,2,4,2,16,256]{6,5,4,3,2,1,0:T(8,128)S(1)} %get-tuple-element.36), channel_id=1, source_target_pairs={{0,4},{1,5},{2,6},{3,7},{4,0},{5,1},{6,2},{7,3},{8,12},{9,13},{10,... | collective-permute-start | bytes 786440 | tf_op jit(solution)/shard_map/data_term/ppermute | solution.py:435
  72.1 10.4 %collective-permute-start.1 = (f32[8,2,2,16,128]{4,3,2,1,0:T(8,128)S(1)}, f32[8,2,2,16,128]{4,3,2,1,0:T(8,128)S(1)}, u32[]{:S(2)}, u32[]{:S(2)}) collective-permute-start(f32[8,2,2,16,128]{4,3,2,1,0:T(8,128)S(1)} %slice.12), channel_id=1, source_target_pairs={{0,2},{1,3},{2,0},{3,1},{4,6},{5,7},{6,4},{7,5},{8,10},{9,11},{10,... | collective-permute-start | bytes 786440 | tf_op jit(solution)/shard_map/column_maps/ppermute | solution.py:435
  73.4 16.6 %collective-permute-start.8 = (f32[1,1,1,4,2,16,256]{6,5,4,3,2,1,0:T(8,128)S(1)}, f32[1,1,1,4,2,16,256]{6,5,4,3,2,1,0:T(8,128)S(1)}, u32[]{:S(2)}, u32[]{:S(2)}) collective-permute-start(f32[1,1,1,4,2,16,256]{6,5,4,3,2,1,0:T(8,128)S(1)} %get-tuple-element.42.refs_0_), channel_id=1, source_target_pairs={{0,8},{1,9},{2,10},{3,11},{4,12},{5,13},{6,14},{7,15},{8,0},{9,1},... | collective-permute-start | bytes 393224 | tf_op jit(solution)/shard_map/data_term/ppermute | solution.py:435
  81.5 8.5 %collective-permute-start.9 = (f32[1,1,1,4,2,16,256]{6,5,4,3,2,1,0:T(8,128)S(1)}, f32[1,1,1,4,2,16,256]{6,5,4,3,2,1,0:T(8,128)S(1)}, u32[]{:S(2)}, u32[]{:S(2)}) collective-permute-start(f32[1,1,1,4,2,16,256]{6,5,4,3,2,1,0:T(8,128)S(1)} %get-tuple-element.40.refs_1_), channel_id=1, source_target_pairs={{0,8},{1,9},{2,10},{3,11},{4,12},{5,13},{6,14},{7,15},{8,0},{9,1},... | collective-permute-start | bytes 393224 | tf_op jit(solution)/shard_map/data_term/ppermute | solution.py:435

commit v7 on v6

--- a/solution.py
+++ b/solution.py
@@ -106,9 +106,22 @@
     return primal
 
 
+def parted_mask(mask_ref):
+    length = mask_ref.shape[1]
+    line = lax.broadcasted_iota(jnp.int32, (length, length), 0)
+    lane = lax.broadcasted_iota(jnp.int32, (length, length), 1)
+    half = length // 2
+    place = jnp.where(lane < half, 2 * lane, 2 * (lane - half) + 1)
+    permutation = (line == place).astype(jnp.float32).astype(jnp.bfloat16)
+    mask = mask_ref[...].astype(jnp.float32).astype(jnp.bfloat16)
+    return jnp.dot(mask, permutation, preferred_element_type=jnp.float32)
+
+
 def mask_responses(mask_ref, wave_hi, wave_lo, out_ref):
+    parted = parted_mask(mask_ref).astype(jnp.bfloat16)
+    half = parted.shape[1] // 2
     for side in range(2):
-        mask = mask_ref[side].astype(jnp.bfloat16)
+        mask = parted[:, side * half : (side + 1) * half]
         terms = [
             jnp.dot(mask, wave[side], preferred_element_type=jnp.float32)
             for wave in (wave_hi, wave_lo)
@@ -216,7 +229,7 @@
 
 
 def base_kernel(start, frames, device_ref, kspace_ref, mask_ref, *refs):
-    col_hi, col_lo, row_hi, row_lo, keep_ref, send_ref, data, near_hi, near_lo, arrived = refs
+    cols_ref, rows_ref, keep_ref, send_ref, data, near_hi, near_lo, masks, arrived = refs
     own, _, _, span, length = keep_ref.shape
     bit = device_ref[0] & 1
     half = length // 2
@@ -237,11 +250,12 @@
     def _():
         for copy in fetch(0, 0):
             copy.start()
-        for far, near in ((col_hi, near_hi), (col_lo, near_lo)):
+        masks[...] = parted_mask(mask_ref)
+        for term, near in enumerate((near_hi, near_lo)):
             for i, which in enumerate((bit, 1 - bit)):
                 for part in range(2):
                     at = pl.multiple_of((2 * part + which) * span, span)
-                    near[pl.ds((2 * i + part) * span, span)] = far[pl.ds(at, span)]
+                    near[pl.ds((2 * i + part) * span, span)] = cols_ref[term, pl.ds(at, span)]
 
     @pl.when(frame + 1 < pl.num_programs(0))
     def _():
@@ -252,7 +266,8 @@
     for copy in fetch(frame, slot):
         copy.wait()
     columns = [
-        dot3((near_hi[...], near_lo[...]), split(data[slot, c]), ((1,), (1,))) * mask_ref[0]
+        dot3((near_hi[...], near_lo[...]), split(data[slot, c]), ((1,), (1,)))
+        * masks[pl.ds(start + frame, 1), :]
         for c in range(own)
     ]
     blocks = [v[2 * i * span : (2 * i + 2) * span] for v in columns for i in range(2)]
@@ -266,7 +281,7 @@
             ],
             0,
         )
-        sides.append(dot3(split(stacked), (row_hi[odd], row_lo[odd])))
+        sides.append(dot3(split(stacked), (rows_ref[0, odd], rows_ref[1, odd])))
     for c in range(own):
         for i, ref in enumerate((keep_ref, send_ref)):
             rows = (2 * c + i) * span
@@ -278,7 +293,7 @@
 
 
 def weigh_kernel(outer, level, flip, device_ref, maps_ref, kept_ref, got_ref, out_ref, *refs):
-    turned, kept, got, total, arrived, left = refs
+    turned, maps, kept, got, total, maps_arrived, arrived, left = refs
     devices, pair_coils, rows, lanes = maps_ref.shape
     own, count = got_ref.shape[:2]
     inner, _, _, cols, length = total.shape
@@ -287,6 +302,12 @@
     bit, which = device_ref[0] & 1, ((device_ref[0] >> level) & 1) ^ flip
     far = [pl.multiple_of((2 * i + which) * span, span) for i in range(outer)]
 
+    map_copies = [
+        pltpu.make_async_copy(maps_ref.at[:, c], maps.at[c], maps_arrived.at[c])
+        for c in range(pair_coils)
+    ]
+    for copy in map_copies:
+        copy.start()
     copies = [
         [
             pltpu.make_async_copy(
@@ -303,7 +324,8 @@
         for copy in group:
             copy.start()
     for c in range(pair_coils):
-        one = maps_ref[:, c].reshape(length, lanes).T
+        map_copies[c].wait()
+        one = maps[c].reshape(length, lanes).T
         turned[c, 0] = one[: lanes // 2]
         turned[c, 1] = one[lanes // 2 :]
 
@@ -363,7 +385,7 @@
         )
         return 0
 
-    lax.fori_loop(0, frames, one, 0, unroll=2)
+    lax.fori_loop(0, frames, one, 0, unroll=4)
 
 
 def steps_kernel(field_ref, grad_ref, maps_ref, mask_ref, *refs):
@@ -383,7 +405,7 @@
             )
             return 0
 
-        lax.fori_loop(0, frames, one, 0, unroll=2)
+        lax.fori_loop(0, frames, one, 0, unroll=4)
         field[...] = tv_step(field[...] - step_size * (grad[...] - data_term))
     per = frames
     for h in range(devices // per):
@@ -465,16 +487,12 @@
     k = np.arange(length)
     z = np.arange(half)
     y = np.arange(hl)
-    col_hi, col_lo = two_terms(packed_left(dft(z, z, half) / np.sqrt(half)))
+    col_tables = np.stack(two_terms(packed_left(dft(z, z, half) / np.sqrt(half))))
     lanes_k = [k[0::2], k[1::2]]
     inverse = [packed_right(dft(y, ks, length)) for ks in lanes_k]
-    row_hi, row_lo = two_terms(np.stack(inverse) / np.sqrt(length))
+    row_tables = np.stack(two_terms(np.stack(inverse) / np.sqrt(length)))
     waves = [dft(ks, y, length) * 0.5 / hl for ks in lanes_k]
     wave_hi, wave_lo = two_terms(np.stack([np.concatenate([w.real, w.imag], 1) for w in waves]))
-
-    sampled = mask.astype(jnp.float32)
-    mask_sides = jnp.stack([sampled[:, 0::2], sampled[:, 1::2]])
-    mask_lanes = jnp.concatenate([mask_sides[0], mask_sides[1]], 1)[:, None, :]
 
     sens_rows = sens.reshape(rows * coils, packed)
     image_rows = image.reshape(rows * frames, packed)
@@ -531,17 +549,16 @@
                 in_specs=[
                     smem,
                     pl.BlockSpec(memory_space=pltpu.HBM),
-                    pl.BlockSpec((1, 1, length), lambda f, start=start: (start + f, 0, 0)),
-                    whole((packed, packed)),
-                    whole((packed, packed)),
-                    whole((2, length, length)),
-                    whole((2, length, length)),
+                    whole((frames, length)),
+                    whole((2, packed, packed)),
+                    whole((2, 2, length, length)),
                 ],
                 out_specs=(block, block),
                 scratch_shapes=[
                     pltpu.VMEM((2, own, length, packed), jnp.float32),
                     pltpu.VMEM((packed, packed), jnp.bfloat16),
                     pltpu.VMEM((packed, packed), jnp.bfloat16),
+                    pltpu.VMEM((frames, length), jnp.float32),
                     pltpu.SemaphoreType.DMA((2, own, 2)),
                 ],
                 compiler_params=params(TRANSFORM_LIMIT),
@@ -551,11 +568,9 @@
             )(
                 device[None],
                 kspace.reshape(hl, 2, pairs, packed),
-                mask_lanes,
-                col_hi,
-                col_lo,
-                row_hi,
-                row_lo,
+                mask,
+                col_tables,
+                row_tables,
             )
         if len(kept) == len(plans) - 1:
             column_blocks, send = lax.optimization_barrier((column_blocks, send))
@@ -585,7 +600,7 @@
             compiler_params=params(),
             cost_estimate=cost(normal_cost, 4 * sens.size * 4),
             name="first_gradient",
-        )(device[None], column_maps, column_late, mask_sides, wave_hi, wave_lo, *before)
+        )(device[None], column_maps, column_late, mask, wave_hi, wave_lo, *before)
 
     with jax.named_scope("data_term"):
 
@@ -593,18 +608,19 @@
             count, order = plans[stream]
             outer = 2 ** (order[0] - 1)
             out = f32(devices // 4, count, 2, cols, length)
-            vmem, anywhere = pl.BlockSpec(memory_space=pltpu.VMEM), pl.BlockSpec(memory_space=pl.ANY)
             base = pltpu.VMEM((own, count, 2, span // 2, length), jnp.float32)
             value = pl.pallas_call(
                 functools.partial(weigh_kernel, outer, order[0], flip),
                 out_shape=out,
-                in_specs=[smem, vmem, anywhere, anywhere],
+                in_specs=[smem, anywhere, anywhere, anywhere],
                 out_specs=anywhere,
                 scratch_shapes=[
                     pltpu.VMEM((2 * own, 2, span, length), jnp.float32),
+                    pltpu.VMEM((2 * own, devices, rows, half), jnp.float32),
                     base,
                     base,
                     pltpu.VMEM(out.shape, jnp.float32),
+                    pltpu.SemaphoreType.DMA((2 * own,)),
                     pltpu.SemaphoreType.DMA((2, count, outer)),
                     pltpu.SemaphoreType.DMA((count,)),
                 ],
@@ -637,7 +653,7 @@
             scratch_shapes=[pltpu.VMEM(field.shape, jnp.float32)] * 2 + [responses],
             compiler_params=params(),
             cost_estimate=cost(normal_cost, 4 * sens.size * 4),
-        )(field0, grad0, maps, mask_sides, wave_hi, wave_lo, *terms)
+        )(field0, grad0, maps, mask, wave_hi, wave_lo, *terms)
 
     with jax.named_scope("result_rows"):
         got = lax.all_to_all(blocks, "coil", 0, 0, tiled=True)

time: 113 us -> 111 us (0.982)
  waiting for transfers between devices: 13.3 us -> 19.9 us
  local copies, waits for them, and re-layouts: 5.09 us -> 1.28 us
  Pallas kernels: 49.4 us -> 45.8 us
    ppermute x10, waiting for transfers between devices: 13.3 us -> 18.2 us  [exchange(): lax.ppermute(send, 'coil', [(i, i ^ 1 << bit) for i in range(devices)])]
    pallas_call x4, Pallas kernels: 14.4 us -> 10.9 us  [weigh(): pl.pallas_call(functools.partial(weigh_kernel, outer, order[0], flip), ou...]
    unnamed x24 -> x20, local copies, waits for them, and re-layouts: 4.65 us -> 1.27 us
    all_to_all x1, starting transfers between devices: 4.91 us -> 6.34 us  [kernel_path(): lax.all_to_all(column_blocks, 'coil', 0, 0, tiled=True, axis_index_groups...]
  transfers between devices with their start and end apart: 12 -> 12, of which waited for: 4 -> 5; matrix products, arithmetic and copies ran while one was open for 4% -> 3% of each run, Pallas kernels for 36% -> 33%
where the time goes in v7:
time: 111 us
  Pallas kernels  45.8 us (41%)
  starting transfers between devices  26.1 us (24%)
  waiting for transfers between devices  19.9 us (18%)
  blocking collectives  14.2 us (13%)
  other arithmetic  3.15 us (3%)
  local copies, waits for them, and re-layouts  1.28 us (1%)
    ppermute x10, waiting for transfers between devices, exchange(): lax.ppermute(send, 'coil', [(i, i ^ 1 << bit) for i in range(devices)])  18.2 us
    pallas_call x2, Pallas kernels, kernel_path(): pl.pallas_call(functools.partial(base_kernel, start, frames), grid=(count...  17.3 us
    all_to_all x1, blocking collectives, kernel_path(): got = lax.all_to_all(blocks, 'coil', 0, 0, tiled=True)  14.2 us
    ppermute x10, starting transfers between devices, exchange(): lax.ppermute(send, 'coil', [(i, i ^ 1 << bit) for i in range(devices)])  12.3 us
    pallas_call x4, Pallas kernels, weigh(): pl.pallas_call(functools.partial(weigh_kernel, outer, order[0], flip), ou...  10.9 us
    all_to_all x1, starting transfers between devices, kernel_path(): coil_maps = lax.all_to_all(blocks, 'coil', 0, 0, tiled=True)  7.52 us
    pallas_call x1, Pallas kernels, first_gradient(): pl.pallas_call(functools.partial(first_normal_kernel, coils, level), in_s...  7.32 us
    pallas_call x1, Pallas kernels, kernel_path(): pl.pallas_call(steps_kernel, out_shape=f32(devices, 2, cols, LANES), scra...  6.72 us
  transfers between devices with their start and end apart: 12, of which 5 were waited for; matrix products, arithmetic and copies ran while one was open for 3% of the time, Pallas kernels for 33%

profile of v7, /device:TPU:0, one launch (start us, length us, event | category | flops | bytes accessed | tf_op | source)
XLA Modules:
  0.0 110.5 jit_solution(9610105492897895796)
XLA Ops:
  0.0 1.2 %copy-done = f32[16,32,512]{2,1,0:T(8,128)S(1)} copy-done((f32[16,32,512]{2,1,0:T(8,128)S(1)}, f32[16,32,512]{2,1,0:T(8,128)}, u32[]{:S(2)}) %copy-start) | copy-done | bytes 1048600
  1.2 1.6 %coil_maps.1 = f32[16,4,16,256]{3,2,1,0:T(8,128)} custom-call(f32[512,512]{1,0:T(8,128)S(1)} %bitcast.16, f32[512,512]{1,0:T(8,128)S(1)} %bitcast.17, f32[512,512]{1,0:T(8,128)S(1)} %bitcast.18, f32[512,512]{1,0:T(8,128)S(1)} %bitcast.19), custom_call_target="tpu_custom_call" | custom-call | bytes 2097152 | tf_op jit(solution)/shard_map/coil_maps/pallas_call | solution.py:501
  2.9 7.5 %all-to-all-start.1 = ((f32[16,4,16,256]{3,2,1,0:T(8,128)}), f32[16,4,16,256]{3,2,1,0:T(8,128)S(1)}, u32[]{:S(2)}, u32[]{:S(2)}) async-start(f32[16,4,16,256]{3,2,1,0:T(8,128)} %coil_maps.1), calls=%async_computation.1 | async-start | bytes 2097152 | tf_op jit(solution)/shard_map/coil_maps/all_to_all | solution.py:511
  11.5 2.0 %collective-permute-start = (f32[8,3,2,16,128]{4,3,2,1,0:T(8,128)S(1)}, f32[8,3,2,16,128]{4,3,2,1,0:T(8,128)S(1)}, u32[]{:S(2)}, u32[]{:S(2)}) collective-permute-start(f32[8,3,2,16,128]{4,3,2,1,0:T(8,128)S(1)} %get-tuple-element.24), channel_id=1, source_target_pairs={{0,2},{1,3},{2,0},{3,1},{4,6},{5,7},{6,4},{7,5},{8,10},{9,11},{10,... | collective-permute-start | bytes 1179656 | tf_op jit(solution)/shard_map/column_maps/ppermute | solution.py:457
  13.5 8.6 %data_transform.3 = (f32[2,4,2,128,256]{4,3,2,1,0:T(8,128)}, f32[2,4,2,128,256]{4,3,2,1,0:T(8,128)}) custom-call(s32[1]{0:T(128)} %bitcast.3.device_ref, f32[128,2,16,512]{3,2,1,0:T(8,128)} %bitcast.34, s32[8,256]{1,0:T(8,128)S(1)} %copy-done.3, bf16[2,512,512]{2,1,0:T(8,128)(2,1)S(1)} %copy-done.4, bf16[2,2,256,256]{3,2,1,0:T(8,128)(2,1)S(1)} %copy-done.5), custom_call_target="tpu_custom_call" | custom-call | flops 4831838208 | bytes 8388608 | tf_op jit(solution)/shard_map/data_transform/pallas_call | solution.py:545
  22.2 8.7 %data_transform.2 = (f32[2,4,2,128,256]{4,3,2,1,0:T(8,128)}, f32[2,4,2,128,256]{4,3,2,1,0:T(8,128)}) custom-call(s32[1]{0:T(128)} %bitcast.3.device_ref, f32[128,2,16,512]{3,2,1,0:T(8,128)} %bitcast.35, s32[8,256]{1,0:T(8,128)S(1)} %copy-done.3, bf16[2,512,512]{2,1,0:T(8,128)(2,1)S(1)} %copy-done.4, bf16[2,2,256,256]{3,2,1,0:T(8,128)(2,1)S(1)} %copy-done.5), custom_call_target="tpu_custom_call" | custom-call | flops 4831838208 | bytes 8388608 | tf_op jit(solution)/shard_map/data_transform/pallas_call | solution.py:545
  30.9 1.2 %pad_maximum_fusion = f32[8,10,2,16,128]{4,3,2,1,0:T(8,128)} fusion(f32[8,3,2,16,128]{4,3,2,1,0:T(8,128)S(1)} %collective-permute-done, f32[8,7,2,16,128]{4,3,2,1,0:T(8,128)S(1)} %get-tuple-element.23), kind=kLoop, calls=%fused_computation | loop fusion | flops 327680 | bytes 2621440 | tf_op jit(solution)/shard_map/column_maps/concatenate | solution.py:531
  33.3 6.3 %all-to-all-start = ((f32[8,10,2,16,128]{4,3,2,1,0:T(8,128)}), f32[8,10,2,16,128]{4,3,2,1,0:T(8,128)S(1)}, u32[]{:S(2)}, u32[]{:S(2)}) async-start(f32[8,10,2,16,128]{4,3,2,1,0:T(8,128)} %pad_maximum_fusion), calls=%async_computation | async-start | bytes 2621440 | tf_op jit(solution)/shard_map/column_maps/all_to_all | solution.py:580
  39.7 2.7 %data_term.5 = f32[4,4,2,16,256]{4,3,2,1,0:T(8,128)} custom-call(s32[1]{0:T(128)} %bitcast.3.device_ref, f32[16,4,16,256]{3,2,1,0:T(8,128)} %copy-done.8, f32[2,4,2,128,256]{4,3,2,1,0:T(8,128)} %get-tuple-element.28.kept_ref, f32[2,4,2,128,256]{4,3,2,1,0:T(8,128)} %collective-permute-done.2.got_ref), custom_call_target="tpu_custom_call" | custom-call | bytes 2621440 | tf_op jit(solution)/shard_map/data_term/pallas_call | solution.py:612
  42.4 1.1 collective-permute-start.3
  43.5 2.7 %data_term.7 = f32[4,4,2,16,256]{4,3,2,1,0:T(8,128)} custom-call(s32[1]{0:T(128)} %bitcast.3.device_ref, f32[16,4,16,256]{3,2,1,0:T(8,128)} %copy-done.8, f32[2,4,2,128,256]{4,3,2,1,0:T(8,128)} %get-tuple-element.30.kept_ref, f32[2,4,2,128,256]{4,3,2,1,0:T(8,128)} %collective-permute-done.5.got_ref), custom_call_target="tpu_custom_call" | custom-call | bytes 2621440 | tf_op jit(solution)/shard_map/data_term/pallas_call | solution.py:612
  47.3 2.7 %data_term.4 = f32[4,4,2,16,256]{4,3,2,1,0:T(8,128)} custom-call(s32[1]{0:T(128)} %bitcast.3.device_ref, f32[16,4,16,256]{3,2,1,0:T(8,128)} %copy-done.8, f32[2,4,2,128,256]{4,3,2,1,0:T(8,128)} %get-tuple-element.28.kept_ref, f32[2,4,2,128,256]{4,3,2,1,0:T(8,128)} %collective-permute-done.2.got_ref), custom_call_target="tpu_custom_call" | custom-call | bytes 2621440 | tf_op jit(solution)/shard_map/data_term/pallas_call | solution.py:612
  50.0 2.8 %data_term.6 = f32[4,4,2,16,256]{4,3,2,1,0:T(8,128)} custom-call(s32[1]{0:T(128)} %bitcast.3.device_ref, f32[16,4,16,256]{3,2,1,0:T(8,128)} %copy-done.8, f32[2,4,2,128,256]{4,3,2,1,0:T(8,128)} %get-tuple-element.30.kept_ref, f32[2,4,2,128,256]{4,3,2,1,0:T(8,128)} %collective-permute-done.5.got_ref), custom_call_target="tpu_custom_call" | custom-call | bytes 2621440 | tf_op jit(solution)/shard_map/data_term/pallas_call | solution.py:612
  52.8 4.6 %collective-permute-done.3 = f32[1,2,2,4,2,16,256]{6,5,4,3,2,1,0:T(8,128)S(1)} collective-permute-done((f32[1,2,2,4,2,16,256]{6,5,4,3,2,1,0:T(8,128)}, f32[1,2,2,4,2,16,256]{6,5,4,3,2,1,0:T(8,128)S(1)}, u32[]{:S(2)}, u32[]{:S(2)}) %collective-permute-start.3) | collective-permute-done | bytes 524320 | tf_op jit(solution)/shard_map/data_term/ppermute | solution.py:457
  58.2 2.1 %collective-permute-start.4 = (f32[1,1,2,4,2,16,256]{6,5,4,3,2,1,0:T(8,128)}, f32[1,1,2,4,2,16,256]{6,5,4,3,2,1,0:T(8,128)S(1)}, u32[]{:S(2)}, u32[]{:S(2)}) collective-permute-start(f32[1,1,2,4,2,16,256]{6,5,4,3,2,1,0:T(8,128)} %get-tuple-element.38), channel_id=1, source_target_pairs={{0,4},{1,5},{2,6},{3,7},{4,0},{5,1},{6,2},{7,3},{8,12},{9,13},{10,... | collective-permute-start | bytes 786440 | tf_op jit(solution)/shard_map/data_term/ppermute | solution.py:457
  60.3 8.0 %collective-permute-done.6 = f32[1,2,2,4,2,16,256]{6,5,4,3,2,1,0:T(8,128)S(1)} collective-permute-done((f32[1,2,2,4,2,16,256]{6,5,4,3,2,1,0:T(8,128)}, f32[1,2,2,4,2,16,256]{6,5,4,3,2,1,0:T(8,128)S(1)}, u32[]{:S(2)}, u32[]{:S(2)}) %collective-permute-start.6) | collective-permute-done | bytes 524320 | tf_op jit(solution)/shard_map/data_term/ppermute | solution.py:457
  68.3 1.1 %dynamic-slice_add_fusion.1 = (f32[1,1,2,4,2,16,256]{6,5,4,3,2,1,0:T(8,128)S(1)}, f32[1,1,2,4,2,16,256]{6,5,4,3,2,1,0:T(8,128)S(1)}) fusion(f32[1,2,2,4,2,16,256]{6,5,4,3,2,1,0:T(8,128)S(1)} %collective-permute-done.6, s32[]{:T(128)S(6)} %select_n.26, f32[1,2,2,4,2,16,256]{6,5,4,3,2,1,0:T(8,128)} %bitcast.30, s32[]{:T(128)S(6)} %select_n.28), kind=kLoop, calls=%fused_computation.2 | loop fusion | flops 131072 | bytes 1572872 | tf_op jit(solution)/shard_map/data_term/add | solution.py:464
  69.4 1.7 %collective-permute-start.7 = (f32[1,1,2,4,2,16,256]{6,5,4,3,2,1,0:T(8,128)S(1)}, f32[1,1,2,4,2,16,256]{6,5,4,3,2,1,0:T(8,128)S(1)}, u32[]{:S(2)}, u32[]{:S(2)}) collective-permute-start(f32[1,1,2,4,2,16,256]{6,5,4,3,2,1,0:T(8,128)S(1)} %get-tuple-element.36), channel_id=1, source_target_pairs={{0,4},{1,5},{2,6},{3,7},{4,0},{5,1},{6,2},{7,3},{8,12},{9,13},{10,... | collective-permute-start | bytes 786440 | tf_op jit(solution)/shard_map/data_term/ppermute | solution.py:457
  71.9 1.1 collective-permute-start.1
  73.1 1.6 %collective-permute-start.8 = (f32[1,1,1,4,2,16,256]{6,5,4,3,2,1,0:T(8,128)S(1)}, f32[1,1,1,4,2,16,256]{6,5,4,3,2,1,0:T(8,128)S(1)}, u32[]{:S(2)}, u32[]{:S(2)}) collective-permute-start(f32[1,1,1,4,2,16,256]{6,5,4,3,2,1,0:T(8,128)S(1)} %get-tuple-element.42.refs_0_), channel_id=1, source_target_pairs={{0,8},{1,9},{2,10},{3,11},{4,12},{5,13},{6,14},{7,15},{8,0},{9,1},... | collective-permute-start | bytes 393224 | tf_op jit(solution)/shard_map/data_term/ppermute | solution.py:457
  74.7 5.6 %collective-permute-done.7 = f32[1,1,2,4,2,16,256]{6,5,4,3,2,1,0:T(8,128)S(1)} collective-permute-done((f32[1,1,2,4,2,16,256]{6,5,4,3,2,1,0:T(8,128)S(1)}, f32[1,1,2,4,2,16,256]{6,5,4,3,2,1,0:T(8,128)S(1)}, u32[]{:S(2)}, u32[]{:S(2)}) %collective-permute-start.7) | collective-permute-done | bytes 262176 | tf_op jit(solution)/shard_map/data_term/ppermute | solution.py:457
  81.4 7.3 %first_gradient.1 = (f32[32,2,16,256]{3,2,1,0:T(8,128)S(1)}, f32[8,2,16,256]{3,2,1,0:T(8,128)S(1)}, f32[8,2,16,256]{3,2,1,0:T(8,128)S(1)}) custom-call(s32[1]{0:T(128)} %bitcast.3.device_ref, f32[8,10,2,16,128]{4,3,2,1,0:T(8,128)S(1)} %all-to-all-done.got_ref, f32[8,2,2,16,128]{4,3,2,1,0:T(8,128)S(1)} %collective-permute-done.1.late_ref, ...), custom_call_target="tpu_custom_call" | custom-call | flops 3221225472 | bytes 4194304 | tf_op jit(solution)/shard_map/data_term/first_gradient/pallas_call | solution.py:593
  88.8 6.7 %outer_steps.1 = f32[16,2,16,128]{3,2,1,0:T(8,128)S(1)} custom-call(f32[8,2,16,256]{3,2,1,0:T(8,128)S(1)} %get-tuple-element.32.field_ref, f32[8,2,16,256]{3,2,1,0:T(8,128)S(1)} %get-tuple-element.33.grad_ref, f32[32,2,16,256]{3,2,1,0:T(8,128)S(1)} %get-tuple-element.34.maps_ref, s32[8,256]{1,0:T(8,128)S(1)} %copy-done.3, ...), custom_call_target="tpu_custom_call" | custom-call | flops 3221225472 | bytes 4194304 | tf_op jit(solution)/shard_map/outer_steps/pallas_call | solution.py:650
  95.5 14.2 %all_to_all.15.got_ref = f32[16,2,16,128]{3,2,1,0:T(8,128)S(1)} all-to-all(f32[16,2,16,128]{3,2,1,0:T(8,128)S(1)} %outer_steps.1), channel_id=1, replica_groups=mesh['plane'=2,'coil'=16] {'coil'}, dimensions={0} | all-to-all | bytes 524288 | tf_op jit(solution)/shard_map/result_rows/all_to_all | solution.py:659
  (38 shorter events, 7.1 us)
Async XLA Ops:
  0.0 1.2 %copy-start = (f32[16,32,512]{2,1,0:T(8,128)S(1)}, f32[16,32,512]{2,1,0:T(8,128)}, u32[]{:S(2)}) copy-start(f32[16,32,512]{2,1,0:T(8,128)} %param.9) | copy-start | bytes 3145732
  2.9 7.5 %copy-start.1 = (f32[16,32,512]{2,1,0:T(8,128)S(1)}, f32[16,32,512]{2,1,0:T(8,128)}, u32[]{:S(2)}) copy-start(f32[16,32,512]{2,1,0:T(8,128)} %param.9) | copy-start | bytes 3145732
  2.9 7.5 %copy-start.2 = (f32[16,8,512]{2,1,0:T(8,128)S(1)}, f32[16,8,512]{2,1,0:T(8,128)}, u32[]{:S(2)}) copy-start(f32[16,8,512]{2,1,0:T(8,128)} %param.8) | copy-start | bytes 786436
  2.9 30.5 %all-to-all-start.1 = ((f32[16,4,16,256]{3,2,1,0:T(8,128)}), f32[16,4,16,256]{3,2,1,0:T(8,128)S(1)}, u32[]{:S(2)}, u32[]{:S(2)}) async-start(f32[16,4,16,256]{3,2,1,0:T(8,128)} %coil_maps.1), calls=%async_computation.1 | async-start | bytes 2097152 | tf_op jit(solution)/shard_map/coil_maps/all_to_all | solution.py:511
  10.4 3.0 %copy-start.3 = (s32[8,256]{1,0:T(8,128)S(1)}, s32[8,256]{1,0:T(8,128)}, u32[]{:S(2)}) copy-start(s32[8,256]{1,0:T(8,128)} %mask_ref.7) | copy-start | bytes 24580
  10.4 3.0 %copy-start.4 = (bf16[2,512,512]{2,1,0:T(8,128)(2,1)S(1)}, bf16[2,512,512]{2,1,0:T(8,128)(2,1)}, u32[]{:S(2)}) copy-start(bf16[2,512,512]{2,1,0:T(8,128)(2,1)} %constant.57.clone.refs_0_) | copy-start | bytes 3145732
  10.4 3.0 %copy-start.5 = (bf16[2,2,256,256]{3,2,1,0:T(8,128)(2,1)S(1)}, bf16[2,2,256,256]{3,2,1,0:T(8,128)(2,1)}, u32[]{:S(2)}) copy-start(bf16[2,2,256,256]{3,2,1,0:T(8,128)(2,1)} %constant.58.clone.refs_1_) | copy-start | bytes 1572868
  11.5 19.4 %collective-permute-start = (f32[8,3,2,16,128]{4,3,2,1,0:T(8,128)S(1)}, f32[8,3,2,16,128]{4,3,2,1,0:T(8,128)S(1)}, u32[]{:S(2)}, u32[]{:S(2)}) collective-permute-start(f32[8,3,2,16,128]{4,3,2,1,0:T(8,128)S(1)} %get-tuple-element.24), channel_id=1, source_target_pairs={{0,2},{1,3},{2,0},{3,1},{4,6},{5,7},{6,4},{7,5},{8,10},{9,11},{10,... | collective-permute-start | bytes 1179656 | tf_op jit(solution)/shard_map/column_maps/ppermute | solution.py:457
  22.1 17.6 %collective-permute-start.2 = (f32[2,4,2,128,256]{4,3,2,1,0:T(8,128)}, f32[2,4,2,128,256]{4,3,2,1,0:T(8,128)}, u32[]{:S(2)}, u32[]{:S(2)}) collective-permute-start(f32[2,4,2,128,256]{4,3,2,1,0:T(8,128)} %get-tuple-element.29), channel_id=1, source_target_pairs={{0,1},{1,0},{2,3},{3,2},{4,5},{5,4},{6,7},{7,6},{8,9},{9,8},{10,11... | collective-permute-start | bytes 6291464 | tf_op jit(solution)/shard_map/ppermute | solution.py:457
  32.1 11.5 %collective-permute-start.5 = (f32[2,4,2,128,256]{4,3,2,1,0:T(8,128)}, f32[2,4,2,128,256]{4,3,2,1,0:T(8,128)}, u32[]{:S(2)}, u32[]{:S(2)}) collective-permute-start(f32[2,4,2,128,256]{4,3,2,1,0:T(8,128)} %get-tuple-element.31), channel_id=1, source_target_pairs={{0,1},{1,0},{2,3},{3,2},{4,5},{5,4},{6,7},{7,6},{8,9},{9,8},{10,11... | collective-permute-start | bytes 6291464 | tf_op jit(solution)/shard_map/ppermute | solution.py:457
  33.3 6.4 %copy-start.8 = (f32[16,4,16,256]{3,2,1,0:T(8,128)}, f32[16,4,16,256]{3,2,1,0:T(8,128)S(1)}, u32[]{:S(2)}) copy-start(f32[16,4,16,256]{3,2,1,0:T(8,128)S(1)} %all-to-all-done.1.maps_ref) | copy-start | bytes 3145732
  33.3 38.6 %all-to-all-start = ((f32[8,10,2,16,128]{4,3,2,1,0:T(8,128)}), f32[8,10,2,16,128]{4,3,2,1,0:T(8,128)S(1)}, u32[]{:S(2)}, u32[]{:S(2)}) async-start(f32[8,10,2,16,128]{4,3,2,1,0:T(8,128)} %pad_maximum_fusion), calls=%async_computation | async-start | bytes 2621440 | tf_op jit(solution)/shard_map/column_maps/all_to_all | solution.py:580
  42.4 15.0 %collective-permute-start.3 = (f32[1,2,2,4,2,16,256]{6,5,4,3,2,1,0:T(8,128)}, f32[1,2,2,4,2,16,256]{6,5,4,3,2,1,0:T(8,128)S(1)}, u32[]{:S(2)}, u32[]{:S(2)}) collective-permute-start(f32[1,2,2,4,2,16,256]{6,5,4,3,2,1,0:T(8,128)} %bitcast.33), channel_id=1, source_target_pairs={{0,2},{1,3},{2,0},{3,1},{4,6},{5,7},{6,4},{7,5},{8,10},{9,11},{10,... | collective-permute-start | bytes 1572872 | tf_op jit(solution)/shard_map/data_term/ppermute | solution.py:457
  46.2 22.0 %collective-permute-start.6 = (f32[1,2,2,4,2,16,256]{6,5,4,3,2,1,0:T(8,128)}, f32[1,2,2,4,2,16,256]{6,5,4,3,2,1,0:T(8,128)S(1)}, u32[]{:S(2)}, u32[]{:S(2)}) collective-permute-start(f32[1,2,2,4,2,16,256]{6,5,4,3,2,1,0:T(8,128)} %bitcast.32), channel_id=1, source_target_pairs={{0,2},{1,3},{2,0},{3,1},{4,6},{5,7},{6,4},{7,5},{8,10},{9,11},{10,... | collective-permute-start | bytes 1572872 | tf_op jit(solution)/shard_map/data_term/ppermute | solution.py:457
  50.0 7.4 %copy-start.9 = (f32[4,4,2,16,256]{4,3,2,1,0:T(8,128)S(1)}, f32[4,4,2,16,256]{4,3,2,1,0:T(8,128)}, u32[]{:S(2)}) copy-start(f32[4,4,2,16,256]{4,3,2,1,0:T(8,128)} %data_term.4) | copy-start | bytes 1572868
  58.2 23.2 %copy-start.6 = (bf16[2,128,256]{2,1,0:T(8,128)(2,1)S(1)}, bf16[2,128,256]{2,1,0:T(8,128)(2,1)}, u32[]{:S(2)}) copy-start(bf16[2,128,256]{2,1,0:T(8,128)(2,1)} %constant.59.clone.wave_hi.refs_0_) | copy-start | bytes 393220
  58.2 23.2 %copy-start.7 = (bf16[2,128,256]{2,1,0:T(8,128)(2,1)S(1)}, bf16[2,128,256]{2,1,0:T(8,128)(2,1)}, u32[]{:S(2)}) copy-start(bf16[2,128,256]{2,1,0:T(8,128)(2,1)} %constant.60.clone.wave_lo.refs_1_) | copy-start | bytes 393220
  58.2 14.8 %collective-permute-start.4 = (f32[1,1,2,4,2,16,256]{6,5,4,3,2,1,0:T(8,128)}, f32[1,1,2,4,2,16,256]{6,5,4,3,2,1,0:T(8,128)S(1)}, u32[]{:S(2)}, u32[]{:S(2)}) collective-permute-start(f32[1,1,2,4,2,16,256]{6,5,4,3,2,1,0:T(8,128)} %get-tuple-element.38), channel_id=1, source_target_pairs={{0,4},{1,5},{2,6},{3,7},{4,0},{5,1},{6,2},{7,3},{8,12},{9,13},{10,... | collective-permute-start | bytes 786440 | tf_op jit(solution)/shard_map/data_term/ppermute | solution.py:457
  69.4 10.9 %collective-permute-start.7 = (f32[1,1,2,4,2,16,256]{6,5,4,3,2,1,0:T(8,128)S(1)}, f32[1,1,2,4,2,16,256]{6,5,4,3,2,1,0:T(8,128)S(1)}, u32[]{:S(2)}, u32[]{:S(2)}) collective-permute-start(f32[1,1,2,4,2,16,256]{6,5,4,3,2,1,0:T(8,128)S(1)} %get-tuple-element.36), channel_id=1, source_target_pairs={{0,4},{1,5},{2,6},{3,7},{4,0},{5,1},{6,2},{7,3},{8,12},{9,13},{10,... | collective-permute-start | bytes 786440 | tf_op jit(solution)/shard_map/data_term/ppermute | solution.py:457
  71.9 9.5 %collective-permute-start.1 = (f32[8,2,2,16,128]{4,3,2,1,0:T(8,128)S(1)}, f32[8,2,2,16,128]{4,3,2,1,0:T(8,128)S(1)}, u32[]{:S(2)}, u32[]{:S(2)}) collective-permute-start(f32[8,2,2,16,128]{4,3,2,1,0:T(8,128)S(1)} %slice.4), channel_id=1, source_target_pairs={{0,2},{1,3},{2,0},{3,1},{4,6},{5,7},{6,4},{7,5},{8,10},{9,11},{10,... | collective-permute-start | bytes 786440 | tf_op jit(solution)/shard_map/column_maps/ppermute | solution.py:457
  73.1 15.7 %collective-permute-start.8 = (f32[1,1,1,4,2,16,256]{6,5,4,3,2,1,0:T(8,128)S(1)}, f32[1,1,1,4,2,16,256]{6,5,4,3,2,1,0:T(8,128)S(1)}, u32[]{:S(2)}, u32[]{:S(2)}) collective-permute-start(f32[1,1,1,4,2,16,256]{6,5,4,3,2,1,0:T(8,128)S(1)} %get-tuple-element.42.refs_0_), channel_id=1, source_target_pairs={{0,8},{1,9},{2,10},{3,11},{4,12},{5,13},{6,14},{7,15},{8,0},{9,1},... | collective-permute-start | bytes 393224 | tf_op jit(solution)/shard_map/data_term/ppermute | solution.py:457
  80.4 8.4 %collective-permute-start.9 = (f32[1,1,1,4,2,16,256]{6,5,4,3,2,1,0:T(8,128)S(1)}, f32[1,1,1,4,2,16,256]{6,5,4,3,2,1,0:T(8,128)S(1)}, u32[]{:S(2)}, u32[]{:S(2)}) collective-permute-start(f32[1,1,1,4,2,16,256]{6,5,4,3,2,1,0:T(8,128)S(1)} %get-tuple-element.40.refs_1_), channel_id=1, source_target_pairs={{0,8},{1,9},{2,10},{3,11},{4,12},{5,13},{6,14},{7,15},{8,0},{9,1},... | collective-permute-start | bytes 393224 | tf_op jit(solution)/shard_map/data_term/ppermute | solution.py:457

commit v8 on v7

--- a/solution.py
+++ b/solution.py
@@ -151,7 +151,7 @@
     return tables
 
 
-def normal_frame(maps_ref, field_re, field_im, tables):
+def normal_coils(maps_ref, field_re, field_im, tables):
     coils, _, cols, length = maps_ref.shape
     half = length // 2
     maps_re, maps_im = maps_ref[:, 0], maps_ref[:, 1]
@@ -182,6 +182,13 @@
     )
 
 
+def normal_frame(maps_ref, field_re, field_im, tables):
+    middle = maps_ref.shape[0] // 2
+    first = normal_coils(maps_ref.at[:middle], field_re, field_im, tables)
+    second = normal_coils(maps_ref.at[middle:], field_re, field_im, tables)
+    return first[0] + second[0], first[1] + second[1]
+
+
 def coil_blocks_kernel(coils, *refs):
     *tiles, out_ref = refs
     devices, pair_coils, rows, lanes = out_ref.shape
@@ -385,7 +392,7 @@
         )
         return 0
 
-    lax.fori_loop(0, frames, one, 0, unroll=4)
+    lax.fori_loop(0, frames, one, 0, unroll=frames)
 
 
 def steps_kernel(field_ref, grad_ref, maps_ref, mask_ref, *refs):
@@ -405,7 +412,7 @@
             )
             return 0
 
-        lax.fori_loop(0, frames, one, 0, unroll=4)
+        lax.fori_loop(0, frames, one, 0, unroll=frames)
         field[...] = tv_step(field[...] - step_size * (grad[...] - data_term))
     per = frames
     for h in range(devices // per):

time: 111 us -> 109 us (0.982)
  Pallas kernels: 45.8 us -> 43.7 us
    pallas_call x1, Pallas kernels: 7.32 us -> 5.6 us  [first_gradient(): pl.pallas_call(functools.partial(first_normal_kernel, coils, level), in_s...]
  transfers between devices with their start and end apart: 12 -> 12, of which waited for: 5 -> 6; matrix products, arithmetic and copies ran while one was open for 3% -> 3% of each run, Pallas kernels for 33% -> 32%
where the time goes in v8:
time: 109 us
  Pallas kernels  43.7 us (40%)
  starting transfers between devices  26.1 us (24%)
  waiting for transfers between devices  20.5 us (19%)
  blocking collectives  13.6 us (12%)
  other arithmetic  3.15 us (3%)
  local copies, waits for them, and re-layouts  1.28 us (1%)
    ppermute x10, waiting for transfers between devices, exchange(): lax.ppermute(send, 'coil', [(i, i ^ 1 << bit) for i in range(devices)])  18.9 us
    pallas_call x2, Pallas kernels, kernel_path(): pl.pallas_call(functools.partial(base_kernel, start, frames), grid=(count...  17.3 us
    all_to_all x1, blocking collectives, kernel_path(): got = lax.all_to_all(blocks, 'coil', 0, 0, tiled=True)  13.6 us
    ppermute x10, starting transfers between devices, exchange(): lax.ppermute(send, 'coil', [(i, i ^ 1 << bit) for i in range(devices)])  12.3 us
    pallas_call x4, Pallas kernels, weigh(): pl.pallas_call(functools.partial(weigh_kernel, outer, order[0], flip), ou...  10.9 us
    all_to_all x1, starting transfers between devices, kernel_path(): coil_maps = lax.all_to_all(blocks, 'coil', 0, 0, tiled=True)  7.52 us
    pallas_call x1, Pallas kernels, kernel_path(): pl.pallas_call(steps_kernel, out_shape=f32(devices, 2, cols, LANES), scra...  6.4 us
    all_to_all x1, starting transfers between devices, kernel_path(): lax.all_to_all(column_blocks, 'coil', 0, 0, tiled=True, axis_index_groups...  6.34 us
  transfers between devices with their start and end apart: 12, of which 6 were waited for; matrix products, arithmetic and copies ran while one was open for 3% of the time, Pallas kernels for 32%

profile of v8, /device:TPU:0, one launch (start us, length us, event | category | flops | bytes accessed | tf_op | source)
XLA Modules:
  0.0 108.6 jit_solution(8946327853359932459)
XLA Ops:
  0.0 1.2 %copy-done = f32[16,32,512]{2,1,0:T(8,128)S(1)} copy-done((f32[16,32,512]{2,1,0:T(8,128)S(1)}, f32[16,32,512]{2,1,0:T(8,128)}, u32[]{:S(2)}) %copy-start) | copy-done | bytes 1048600
  1.2 1.6 %coil_maps.1 = f32[16,4,16,256]{3,2,1,0:T(8,128)} custom-call(f32[512,512]{1,0:T(8,128)S(1)} %bitcast.16, f32[512,512]{1,0:T(8,128)S(1)} %bitcast.17, f32[512,512]{1,0:T(8,128)S(1)} %bitcast.18, f32[512,512]{1,0:T(8,128)S(1)} %bitcast.19), custom_call_target="tpu_custom_call" | custom-call | bytes 2097152 | tf_op jit(solution)/shard_map/coil_maps/pallas_call | solution.py:508
  2.9 7.5 %all-to-all-start.1 = ((f32[16,4,16,256]{3,2,1,0:T(8,128)}), f32[16,4,16,256]{3,2,1,0:T(8,128)S(1)}, u32[]{:S(2)}, u32[]{:S(2)}) async-start(f32[16,4,16,256]{3,2,1,0:T(8,128)} %coil_maps.1), calls=%async_computation.1 | async-start | bytes 2097152 | tf_op jit(solution)/shard_map/coil_maps/all_to_all | solution.py:518
  11.5 2.0 %collective-permute-start = (f32[8,3,2,16,128]{4,3,2,1,0:T(8,128)S(1)}, f32[8,3,2,16,128]{4,3,2,1,0:T(8,128)S(1)}, u32[]{:S(2)}, u32[]{:S(2)}) collective-permute-start(f32[8,3,2,16,128]{4,3,2,1,0:T(8,128)S(1)} %get-tuple-element.24), channel_id=1, source_target_pairs={{0,2},{1,3},{2,0},{3,1},{4,6},{5,7},{6,4},{7,5},{8,10},{9,11},{10,... | collective-permute-start | bytes 1179656 | tf_op jit(solution)/shard_map/column_maps/ppermute | solution.py:464
  13.5 8.6 %data_transform.3 = (f32[2,4,2,128,256]{4,3,2,1,0:T(8,128)}, f32[2,4,2,128,256]{4,3,2,1,0:T(8,128)}) custom-call(s32[1]{0:T(128)} %bitcast.3.device_ref, f32[128,2,16,512]{3,2,1,0:T(8,128)} %bitcast.34, s32[8,256]{1,0:T(8,128)S(1)} %copy-done.3, bf16[2,512,512]{2,1,0:T(8,128)(2,1)S(1)} %copy-done.4, bf16[2,2,256,256]{3,2,1,0:T(8,128)(2,1)S(1)} %copy-done.5), custom_call_target="tpu_custom_call" | custom-call | flops 4831838208 | bytes 8388608 | tf_op jit(solution)/shard_map/data_transform/pallas_call | solution.py:552
  22.2 8.7 %data_transform.2 = (f32[2,4,2,128,256]{4,3,2,1,0:T(8,128)}, f32[2,4,2,128,256]{4,3,2,1,0:T(8,128)}) custom-call(s32[1]{0:T(128)} %bitcast.3.device_ref, f32[128,2,16,512]{3,2,1,0:T(8,128)} %bitcast.35, s32[8,256]{1,0:T(8,128)S(1)} %copy-done.3, bf16[2,512,512]{2,1,0:T(8,128)(2,1)S(1)} %copy-done.4, bf16[2,2,256,256]{3,2,1,0:T(8,128)(2,1)S(1)} %copy-done.5), custom_call_target="tpu_custom_call" | custom-call | flops 4831838208 | bytes 8388608 | tf_op jit(solution)/shard_map/data_transform/pallas_call | solution.py:552
  30.9 1.2 %pad_maximum_fusion = f32[8,10,2,16,128]{4,3,2,1,0:T(8,128)} fusion(f32[8,3,2,16,128]{4,3,2,1,0:T(8,128)S(1)} %collective-permute-done, f32[8,7,2,16,128]{4,3,2,1,0:T(8,128)S(1)} %get-tuple-element.23), kind=kLoop, calls=%fused_computation | loop fusion | flops 327680 | bytes 2621440 | tf_op jit(solution)/shard_map/column_maps/concatenate | solution.py:538
  33.3 6.3 %all-to-all-start = ((f32[8,10,2,16,128]{4,3,2,1,0:T(8,128)}), f32[8,10,2,16,128]{4,3,2,1,0:T(8,128)S(1)}, u32[]{:S(2)}, u32[]{:S(2)}) async-start(f32[8,10,2,16,128]{4,3,2,1,0:T(8,128)} %pad_maximum_fusion), calls=%async_computation | async-start | bytes 2621440 | tf_op jit(solution)/shard_map/column_maps/all_to_all | solution.py:587
  39.7 2.7 %data_term.5 = f32[4,4,2,16,256]{4,3,2,1,0:T(8,128)} custom-call(s32[1]{0:T(128)} %bitcast.3.device_ref, f32[16,4,16,256]{3,2,1,0:T(8,128)} %copy-done.8, f32[2,4,2,128,256]{4,3,2,1,0:T(8,128)} %get-tuple-element.28.kept_ref, f32[2,4,2,128,256]{4,3,2,1,0:T(8,128)} %collective-permute-done.2.got_ref), custom_call_target="tpu_custom_call" | custom-call | bytes 2621440 | tf_op jit(solution)/shard_map/data_term/pallas_call | solution.py:619
  42.4 1.1 %collective-permute-start.3 = (f32[1,2,2,4,2,16,256]{6,5,4,3,2,1,0:T(8,128)}, f32[1,2,2,4,2,16,256]{6,5,4,3,2,1,0:T(8,128)S(1)}, u32[]{:S(2)}, u32[]{:S(2)}) collective-permute-start(f32[1,2,2,4,2,16,256]{6,5,4,3,2,1,0:T(8,128)} %bitcast.33), channel_id=1, source_target_pairs={{0,2},{1,3},{2,0},{3,1},{4,6},{5,7},{6,4},{7,5},{8,10},{9,11},{10,... | collective-permute-start | bytes 1572872 | tf_op jit(solution)/shard_map/data_term/ppermute | solution.py:464
  43.5 2.7 %data_term.7 = f32[4,4,2,16,256]{4,3,2,1,0:T(8,128)} custom-call(s32[1]{0:T(128)} %bitcast.3.device_ref, f32[16,4,16,256]{3,2,1,0:T(8,128)} %copy-done.8, f32[2,4,2,128,256]{4,3,2,1,0:T(8,128)} %get-tuple-element.30.kept_ref, f32[2,4,2,128,256]{4,3,2,1,0:T(8,128)} %collective-permute-done.5.got_ref), custom_call_target="tpu_custom_call" | custom-call | bytes 2621440 | tf_op jit(solution)/shard_map/data_term/pallas_call | solution.py:619
  47.3 2.7 %data_term.4 = f32[4,4,2,16,256]{4,3,2,1,0:T(8,128)} custom-call(s32[1]{0:T(128)} %bitcast.3.device_ref, f32[16,4,16,256]{3,2,1,0:T(8,128)} %copy-done.8, f32[2,4,2,128,256]{4,3,2,1,0:T(8,128)} %get-tuple-element.28.kept_ref, f32[2,4,2,128,256]{4,3,2,1,0:T(8,128)} %collective-permute-done.2.got_ref), custom_call_target="tpu_custom_call" | custom-call | bytes 2621440 | tf_op jit(solution)/shard_map/data_term/pallas_call | solution.py:619
  50.0 2.8 %data_term.6 = f32[4,4,2,16,256]{4,3,2,1,0:T(8,128)} custom-call(s32[1]{0:T(128)} %bitcast.3.device_ref, f32[16,4,16,256]{3,2,1,0:T(8,128)} %copy-done.8, f32[2,4,2,128,256]{4,3,2,1,0:T(8,128)} %get-tuple-element.30.kept_ref, f32[2,4,2,128,256]{4,3,2,1,0:T(8,128)} %collective-permute-done.5.got_ref), custom_call_target="tpu_custom_call" | custom-call | bytes 2621440 | tf_op jit(solution)/shard_map/data_term/pallas_call | solution.py:619
  52.8 4.6 %collective-permute-done.3 = f32[1,2,2,4,2,16,256]{6,5,4,3,2,1,0:T(8,128)S(1)} collective-permute-done((f32[1,2,2,4,2,16,256]{6,5,4,3,2,1,0:T(8,128)}, f32[1,2,2,4,2,16,256]{6,5,4,3,2,1,0:T(8,128)S(1)}, u32[]{:S(2)}, u32[]{:S(2)}) %collective-permute-start.3) | collective-permute-done | bytes 524320 | tf_op jit(solution)/shard_map/data_term/ppermute | solution.py:464
  58.2 2.1 %collective-permute-start.4 = (f32[1,1,2,4,2,16,256]{6,5,4,3,2,1,0:T(8,128)}, f32[1,1,2,4,2,16,256]{6,5,4,3,2,1,0:T(8,128)S(1)}, u32[]{:S(2)}, u32[]{:S(2)}) collective-permute-start(f32[1,1,2,4,2,16,256]{6,5,4,3,2,1,0:T(8,128)} %get-tuple-element.38), channel_id=1, source_target_pairs={{0,4},{1,5},{2,6},{3,7},{4,0},{5,1},{6,2},{7,3},{8,12},{9,13},{10,... | collective-permute-start | bytes 786440 | tf_op jit(solution)/shard_map/data_term/ppermute | solution.py:464
  60.3 8.0 %collective-permute-done.6 = f32[1,2,2,4,2,16,256]{6,5,4,3,2,1,0:T(8,128)S(1)} collective-permute-done((f32[1,2,2,4,2,16,256]{6,5,4,3,2,1,0:T(8,128)}, f32[1,2,2,4,2,16,256]{6,5,4,3,2,1,0:T(8,128)S(1)}, u32[]{:S(2)}, u32[]{:S(2)}) %collective-permute-start.6) | collective-permute-done | bytes 524320 | tf_op jit(solution)/shard_map/data_term/ppermute | solution.py:464
  68.3 1.1 %dynamic-slice_add_fusion.1 = (f32[1,1,2,4,2,16,256]{6,5,4,3,2,1,0:T(8,128)S(1)}, f32[1,1,2,4,2,16,256]{6,5,4,3,2,1,0:T(8,128)S(1)}) fusion(f32[1,2,2,4,2,16,256]{6,5,4,3,2,1,0:T(8,128)S(1)} %collective-permute-done.6, s32[]{:T(128)S(6)} %select_n.26, f32[1,2,2,4,2,16,256]{6,5,4,3,2,1,0:T(8,128)} %bitcast.30, s32[]{:T(128)S(6)} %select_n.28), kind=kLoop, calls=%fused_computation.2 | loop fusion | flops 131072 | bytes 1572872 | tf_op jit(solution)/shard_map/data_term/add | solution.py:471
  69.4 1.7 %collective-permute-start.7 = (f32[1,1,2,4,2,16,256]{6,5,4,3,2,1,0:T(8,128)S(1)}, f32[1,1,2,4,2,16,256]{6,5,4,3,2,1,0:T(8,128)S(1)}, u32[]{:S(2)}, u32[]{:S(2)}) collective-permute-start(f32[1,1,2,4,2,16,256]{6,5,4,3,2,1,0:T(8,128)S(1)} %get-tuple-element.36), channel_id=1, source_target_pairs={{0,4},{1,5},{2,6},{3,7},{4,0},{5,1},{6,2},{7,3},{8,12},{9,13},{10,... | collective-permute-start | bytes 786440 | tf_op jit(solution)/shard_map/data_term/ppermute | solution.py:464
  71.9 1.1 %collective-permute-start.1 = (f32[8,2,2,16,128]{4,3,2,1,0:T(8,128)S(1)}, f32[8,2,2,16,128]{4,3,2,1,0:T(8,128)S(1)}, u32[]{:S(2)}, u32[]{:S(2)}) collective-permute-start(f32[8,2,2,16,128]{4,3,2,1,0:T(8,128)S(1)} %slice.4), channel_id=1, source_target_pairs={{0,2},{1,3},{2,0},{3,1},{4,6},{5,7},{6,4},{7,5},{8,10},{9,11},{10,... | collective-permute-start | bytes 786440 | tf_op jit(solution)/shard_map/column_maps/ppermute | solution.py:464
  73.1 1.6 %collective-permute-start.8 = (f32[1,1,1,4,2,16,256]{6,5,4,3,2,1,0:T(8,128)S(1)}, f32[1,1,1,4,2,16,256]{6,5,4,3,2,1,0:T(8,128)S(1)}, u32[]{:S(2)}, u32[]{:S(2)}) collective-permute-start(f32[1,1,1,4,2,16,256]{6,5,4,3,2,1,0:T(8,128)S(1)} %get-tuple-element.42.refs_0_), channel_id=1, source_target_pairs={{0,8},{1,9},{2,10},{3,11},{4,12},{5,13},{6,14},{7,15},{8,0},{9,1},... | collective-permute-start | bytes 393224 | tf_op jit(solution)/shard_map/data_term/ppermute | solution.py:464
  74.7 5.6 %collective-permute-done.7 = f32[1,1,2,4,2,16,256]{6,5,4,3,2,1,0:T(8,128)S(1)} collective-permute-done((f32[1,1,2,4,2,16,256]{6,5,4,3,2,1,0:T(8,128)S(1)}, f32[1,1,2,4,2,16,256]{6,5,4,3,2,1,0:T(8,128)S(1)}, u32[]{:S(2)}, u32[]{:S(2)}) %collective-permute-start.7) | collective-permute-done | bytes 262176 | tf_op jit(solution)/shard_map/data_term/ppermute | solution.py:464
  81.4 5.6 %first_gradient.1 = (f32[32,2,16,256]{3,2,1,0:T(8,128)S(1)}, f32[8,2,16,256]{3,2,1,0:T(8,128)S(1)}, f32[8,2,16,256]{3,2,1,0:T(8,128)S(1)}) custom-call(s32[1]{0:T(128)} %bitcast.3.device_ref, f32[8,10,2,16,128]{4,3,2,1,0:T(8,128)S(1)} %all-to-all-done.got_ref, f32[8,2,2,16,128]{4,3,2,1,0:T(8,128)S(1)} %collective-permute-done.1.late_ref, ...), custom_call_target="tpu_custom_call" | custom-call | flops 3221225472 | bytes 4194304 | tf_op jit(solution)/shard_map/data_term/first_gradient/pallas_call | solution.py:600
  87.7 6.4 %outer_steps.1 = f32[16,2,16,128]{3,2,1,0:T(8,128)S(1)} custom-call(f32[8,2,16,256]{3,2,1,0:T(8,128)S(1)} %get-tuple-element.32.field_ref, f32[8,2,16,256]{3,2,1,0:T(8,128)S(1)} %get-tuple-element.33.grad_ref, f32[32,2,16,256]{3,2,1,0:T(8,128)S(1)} %get-tuple-element.34.maps_ref, s32[8,256]{1,0:T(8,128)S(1)} %copy-done.3, ...), custom_call_target="tpu_custom_call" | custom-call | flops 3221225472 | bytes 4194304 | tf_op jit(solution)/shard_map/outer_steps/pallas_call | solution.py:657
  94.1 13.6 %all_to_all.15.got_ref = f32[16,2,16,128]{3,2,1,0:T(8,128)S(1)} all-to-all(f32[16,2,16,128]{3,2,1,0:T(8,128)S(1)} %outer_steps.1), channel_id=1, replica_groups=mesh['plane'=2,'coil'=16] {'coil'}, dimensions={0} | all-to-all | bytes 524288 | tf_op jit(solution)/shard_map/result_rows/all_to_all | solution.py:666
  (38 shorter events, 7.7 us)
Async XLA Ops:
  0.0 1.2 %copy-start = (f32[16,32,512]{2,1,0:T(8,128)S(1)}, f32[16,32,512]{2,1,0:T(8,128)}, u32[]{:S(2)}) copy-start(f32[16,32,512]{2,1,0:T(8,128)} %param.9) | copy-start | bytes 3145732
  2.9 7.5 %copy-start.1 = (f32[16,32,512]{2,1,0:T(8,128)S(1)}, f32[16,32,512]{2,1,0:T(8,128)}, u32[]{:S(2)}) copy-start(f32[16,32,512]{2,1,0:T(8,128)} %param.9) | copy-start | bytes 3145732
  2.9 7.5 %copy-start.2 = (f32[16,8,512]{2,1,0:T(8,128)S(1)}, f32[16,8,512]{2,1,0:T(8,128)}, u32[]{:S(2)}) copy-start(f32[16,8,512]{2,1,0:T(8,128)} %param.8) | copy-start | bytes 786436
  2.9 30.5 %all-to-all-start.1 = ((f32[16,4,16,256]{3,2,1,0:T(8,128)}), f32[16,4,16,256]{3,2,1,0:T(8,128)S(1)}, u32[]{:S(2)}, u32[]{:S(2)}) async-start(f32[16,4,16,256]{3,2,1,0:T(8,128)} %coil_maps.1), calls=%async_computation.1 | async-start | bytes 2097152 | tf_op jit(solution)/shard_map/coil_maps/all_to_all | solution.py:518
  10.4 3.0 %copy-start.3 = (s32[8,256]{1,0:T(8,128)S(1)}, s32[8,256]{1,0:T(8,128)}, u32[]{:S(2)}) copy-start(s32[8,256]{1,0:T(8,128)} %mask_ref.7) | copy-start | bytes 24580
  10.4 3.0 %copy-start.4 = (bf16[2,512,512]{2,1,0:T(8,128)(2,1)S(1)}, bf16[2,512,512]{2,1,0:T(8,128)(2,1)}, u32[]{:S(2)}) copy-start(bf16[2,512,512]{2,1,0:T(8,128)(2,1)} %constant.57.clone.refs_0_) | copy-start | bytes 3145732
  10.4 3.0 %copy-start.5 = (bf16[2,2,256,256]{3,2,1,0:T(8,128)(2,1)S(1)}, bf16[2,2,256,256]{3,2,1,0:T(8,128)(2,1)}, u32[]{:S(2)}) copy-start(bf16[2,2,256,256]{3,2,1,0:T(8,128)(2,1)} %constant.58.clone.refs_1_) | copy-start | bytes 1572868
  11.5 19.4 %collective-permute-start = (f32[8,3,2,16,128]{4,3,2,1,0:T(8,128)S(1)}, f32[8,3,2,16,128]{4,3,2,1,0:T(8,128)S(1)}, u32[]{:S(2)}, u32[]{:S(2)}) collective-permute-start(f32[8,3,2,16,128]{4,3,2,1,0:T(8,128)S(1)} %get-tuple-element.24), channel_id=1, source_target_pairs={{0,2},{1,3},{2,0},{3,1},{4,6},{5,7},{6,4},{7,5},{8,10},{9,11},{10,... | collective-permute-start | bytes 1179656 | tf_op jit(solution)/shard_map/column_maps/ppermute | solution.py:464
  22.1 17.6 %collective-permute-start.2 = (f32[2,4,2,128,256]{4,3,2,1,0:T(8,128)}, f32[2,4,2,128,256]{4,3,2,1,0:T(8,128)}, u32[]{:S(2)}, u32[]{:S(2)}) collective-permute-start(f32[2,4,2,128,256]{4,3,2,1,0:T(8,128)} %get-tuple-element.29), channel_id=1, source_target_pairs={{0,1},{1,0},{2,3},{3,2},{4,5},{5,4},{6,7},{7,6},{8,9},{9,8},{10,11... | collective-permute-start | bytes 6291464 | tf_op jit(solution)/shard_map/ppermute | solution.py:464
  32.1 11.5 %collective-permute-start.5 = (f32[2,4,2,128,256]{4,3,2,1,0:T(8,128)}, f32[2,4,2,128,256]{4,3,2,1,0:T(8,128)}, u32[]{:S(2)}, u32[]{:S(2)}) collective-permute-start(f32[2,4,2,128,256]{4,3,2,1,0:T(8,128)} %get-tuple-element.31), channel_id=1, source_target_pairs={{0,1},{1,0},{2,3},{3,2},{4,5},{5,4},{6,7},{7,6},{8,9},{9,8},{10,11... | collective-permute-start | bytes 6291464 | tf_op jit(solution)/shard_map/ppermute | solution.py:464
  33.3 6.4 %copy-start.8 = (f32[16,4,16,256]{3,2,1,0:T(8,128)}, f32[16,4,16,256]{3,2,1,0:T(8,128)S(1)}, u32[]{:S(2)}) copy-start(f32[16,4,16,256]{3,2,1,0:T(8,128)S(1)} %all-to-all-done.1.maps_ref) | copy-start | bytes 3145732
  33.3 38.6 %all-to-all-start = ((f32[8,10,2,16,128]{4,3,2,1,0:T(8,128)}), f32[8,10,2,16,128]{4,3,2,1,0:T(8,128)S(1)}, u32[]{:S(2)}, u32[]{:S(2)}) async-start(f32[8,10,2,16,128]{4,3,2,1,0:T(8,128)} %pad_maximum_fusion), calls=%async_computation | async-start | bytes 2621440 | tf_op jit(solution)/shard_map/column_maps/all_to_all | solution.py:587
  42.4 15.0 %collective-permute-start.3 = (f32[1,2,2,4,2,16,256]{6,5,4,3,2,1,0:T(8,128)}, f32[1,2,2,4,2,16,256]{6,5,4,3,2,1,0:T(8,128)S(1)}, u32[]{:S(2)}, u32[]{:S(2)}) collective-permute-start(f32[1,2,2,4,2,16,256]{6,5,4,3,2,1,0:T(8,128)} %bitcast.33), channel_id=1, source_target_pairs={{0,2},{1,3},{2,0},{3,1},{4,6},{5,7},{6,4},{7,5},{8,10},{9,11},{10,... | collective-permute-start | bytes 1572872 | tf_op jit(solution)/shard_map/data_term/ppermute | solution.py:464
  46.2 22.0 %collective-permute-start.6 = (f32[1,2,2,4,2,16,256]{6,5,4,3,2,1,0:T(8,128)}, f32[1,2,2,4,2,16,256]{6,5,4,3,2,1,0:T(8,128)S(1)}, u32[]{:S(2)}, u32[]{:S(2)}) collective-permute-start(f32[1,2,2,4,2,16,256]{6,5,4,3,2,1,0:T(8,128)} %bitcast.32), channel_id=1, source_target_pairs={{0,2},{1,3},{2,0},{3,1},{4,6},{5,7},{6,4},{7,5},{8,10},{9,11},{10,... | collective-permute-start | bytes 1572872 | tf_op jit(solution)/shard_map/data_term/ppermute | solution.py:464
  50.0 7.4 %copy-start.9 = (f32[4,4,2,16,256]{4,3,2,1,0:T(8,128)S(1)}, f32[4,4,2,16,256]{4,3,2,1,0:T(8,128)}, u32[]{:S(2)}) copy-start(f32[4,4,2,16,256]{4,3,2,1,0:T(8,128)} %data_term.4) | copy-start | bytes 1572868
  58.2 23.2 %copy-start.6 = (bf16[2,128,256]{2,1,0:T(8,128)(2,1)S(1)}, bf16[2,128,256]{2,1,0:T(8,128)(2,1)}, u32[]{:S(2)}) copy-start(bf16[2,128,256]{2,1,0:T(8,128)(2,1)} %constant.59.clone.wave_hi.refs_0_) | copy-start | bytes 393220
  58.2 23.2 %copy-start.7 = (bf16[2,128,256]{2,1,0:T(8,128)(2,1)S(1)}, bf16[2,128,256]{2,1,0:T(8,128)(2,1)}, u32[]{:S(2)}) copy-start(bf16[2,128,256]{2,1,0:T(8,128)(2,1)} %constant.60.clone.wave_lo.refs_1_) | copy-start | bytes 393220
  58.2 14.8 %collective-permute-start.4 = (f32[1,1,2,4,2,16,256]{6,5,4,3,2,1,0:T(8,128)}, f32[1,1,2,4,2,16,256]{6,5,4,3,2,1,0:T(8,128)S(1)}, u32[]{:S(2)}, u32[]{:S(2)}) collective-permute-start(f32[1,1,2,4,2,16,256]{6,5,4,3,2,1,0:T(8,128)} %get-tuple-element.38), channel_id=1, source_target_pairs={{0,4},{1,5},{2,6},{3,7},{4,0},{5,1},{6,2},{7,3},{8,12},{9,13},{10,... | collective-permute-start | bytes 786440 | tf_op jit(solution)/shard_map/data_term/ppermute | solution.py:464
  69.4 10.9 %collective-permute-start.7 = (f32[1,1,2,4,2,16,256]{6,5,4,3,2,1,0:T(8,128)S(1)}, f32[1,1,2,4,2,16,256]{6,5,4,3,2,1,0:T(8,128)S(1)}, u32[]{:S(2)}, u32[]{:S(2)}) collective-permute-start(f32[1,1,2,4,2,16,256]{6,5,4,3,2,1,0:T(8,128)S(1)} %get-tuple-element.36), channel_id=1, source_target_pairs={{0,4},{1,5},{2,6},{3,7},{4,0},{5,1},{6,2},{7,3},{8,12},{9,13},{10,... | collective-permute-start | bytes 786440 | tf_op jit(solution)/shard_map/data_term/ppermute | solution.py:464
  71.9 9.5 %collective-permute-start.1 = (f32[8,2,2,16,128]{4,3,2,1,0:T(8,128)S(1)}, f32[8,2,2,16,128]{4,3,2,1,0:T(8,128)S(1)}, u32[]{:S(2)}, u32[]{:S(2)}) collective-permute-start(f32[8,2,2,16,128]{4,3,2,1,0:T(8,128)S(1)} %slice.4), channel_id=1, source_target_pairs={{0,2},{1,3},{2,0},{3,1},{4,6},{5,7},{6,4},{7,5},{8,10},{9,11},{10,... | collective-permute-start | bytes 786440 | tf_op jit(solution)/shard_map/column_maps/ppermute | solution.py:464
  73.1 14.0 %collective-permute-start.8 = (f32[1,1,1,4,2,16,256]{6,5,4,3,2,1,0:T(8,128)S(1)}, f32[1,1,1,4,2,16,256]{6,5,4,3,2,1,0:T(8,128)S(1)}, u32[]{:S(2)}, u32[]{:S(2)}) collective-permute-start(f32[1,1,1,4,2,16,256]{6,5,4,3,2,1,0:T(8,128)S(1)} %get-tuple-element.42.refs_0_), channel_id=1, source_target_pairs={{0,8},{1,9},{2,10},{3,11},{4,12},{5,13},{6,14},{7,15},{8,0},{9,1},... | collective-permute-start | bytes 393224 | tf_op jit(solution)/shard_map/data_term/ppermute | solution.py:464
  80.4 7.3 %collective-permute-start.9 = (f32[1,1,1,4,2,16,256]{6,5,4,3,2,1,0:T(8,128)S(1)}, f32[1,1,1,4,2,16,256]{6,5,4,3,2,1,0:T(8,128)S(1)}, u32[]{:S(2)}, u32[]{:S(2)}) collective-permute-start(f32[1,1,1,4,2,16,256]{6,5,4,3,2,1,0:T(8,128)S(1)} %get-tuple-element.40.refs_1_), channel_id=1, source_target_pairs={{0,8},{1,9},{2,10},{3,11},{4,12},{5,13},{6,14},{7,15},{8,0},{9,1},... | collective-permute-start | bytes 393224 | tf_op jit(solution)/shard_map/data_term/ppermute | solution.py:464

commit v9 on v8

--- a/solution.py
+++ b/solution.py
@@ -194,14 +194,20 @@
     devices, pair_coils, rows, lanes = out_ref.shape
     halves = len(tiles) // 2
     each = lanes // (2 * LANES)
-    for d in range(devices):
-        for c in range(pair_coils):
-            for part in range(2):
-                for t in range(each):
-                    at = (part * each + t) * LANES
-                    out_ref[d, c, :, at : at + LANES] = tiles[part * halves + (d & 1) * each + t][
-                        pl.ds((d >> 1) * pair_coils + c, rows, stride=coils), :
-                    ]
+    step = 8
+    for part in range(2):
+        for side in range(2):
+            for t in range(each):
+                ref = tiles[part * halves + side * each + t]
+                at = (part * each + t) * LANES
+                for first in range(0, coils, step):
+                    for row in range(0, rows, step):
+                        turned = jnp.swapaxes(ref[row : row + step, first : first + step], 0, 1)
+                        for c in range(first, first + step):
+                            d = c // pair_coils * 2 + side
+                            out_ref[d, c % pair_coils, row : row + step, at : at + LANES] = turned[
+                                c - first
+                            ]
 
 
 def with_bit(index, bit, value):
@@ -509,11 +515,14 @@
             functools.partial(coil_blocks_kernel, coils),
             grid=(1,),
             out_shape=f32(devices, 2 * own, rows, half),
-            in_specs=lane_tiles(rows * coils, packed),
+            in_specs=[
+                pl.BlockSpec((rows, coils, LANES), lambda *_, t=t: (0, 0, t))
+                for t in range(packed // LANES)
+            ],
             out_specs=whole((devices, 2 * own, rows, half)),
             compiler_params=params(),
             cost_estimate=cost(0, 2 * sens.size * 4),
-        )(*[sens_rows] * (packed // LANES))
+        )(*[sens] * (packed // LANES))
         blocks, device = lax.optimization_barrier((blocks, device))
         coil_maps = lax.all_to_all(blocks, "coil", 0, 0, tiled=True)
 

time: 109 us -> 109 us (level)
  no operation moved by 1% of the time
where the time goes in v9:
time: 109 us; the launch traced here: 108 us
  Pallas kernels  43.2 us (40%)
  starting transfers between devices  26.1 us (24%)
  waiting for transfers between devices  20.5 us (19%)
  blocking collectives  13.6 us (12%)
  other arithmetic  3.15 us (3%)
  local copies, waits for them, and re-layouts  1.28 us (1%)
    ppermute x10, waiting for transfers between devices, exchange(): lax.ppermute(send, 'coil', [(i, i ^ 1 << bit) for i in range(devices)])  18.9 us
    pallas_call x2, Pallas kernels, kernel_path(): pl.pallas_call(functools.partial(base_kernel, start, frames), grid=(count...  17.3 us
    all_to_all x1, blocking collectives, kernel_path(): got = lax.all_to_all(blocks, 'coil', 0, 0, tiled=True)  13.6 us
    ppermute x10, starting transfers between devices, exchange(): lax.ppermute(send, 'coil', [(i, i ^ 1 << bit) for i in range(devices)])  12.3 us
    pallas_call x4, Pallas kernels, weigh(): pl.pallas_call(functools.partial(weigh_kernel, outer, order[0], flip), ou...  10.9 us
    all_to_all x1, starting transfers between devices, kernel_path(): coil_maps = lax.all_to_all(blocks, 'coil', 0, 0, tiled=True)  7.52 us
    pallas_call x1, Pallas kernels, kernel_path(): pl.pallas_call(steps_kernel, out_shape=f32(devices, 2, cols, LANES), scra...  6.41 us
    all_to_all x1, starting transfers between devices, kernel_path(): lax.all_to_all(column_blocks, 'coil', 0, 0, tiled=True, axis_index_groups...  6.34 us
  transfers between devices with their start and end apart: 12, of which 6 were waited for; matrix products, arithmetic and copies ran while one was open for 3% of the time, Pallas kernels for 32%

profile of v9, /device:TPU:0, one launch (start us, length us, event | category | flops | bytes accessed | tf_op | source)
XLA Modules:
  0.0 108.1 jit_solution(3620286977189826377)
XLA Ops:
  0.0 1.2 %copy-done = f32[16,32,512]{2,1,0:T(8,128)S(1)} copy-done((f32[16,32,512]{2,1,0:T(8,128)S(1)}, f32[16,32,512]{2,1,0:T(8,128)}, u32[]{:S(2)}) %copy-start) | copy-done | bytes 1048600
  1.2 1.2 %coil_maps.1 = f32[16,4,16,256]{3,2,1,0:T(8,128)} custom-call(f32[16,32,512]{2,1,0:T(8,128)S(1)} %copy-done, f32[16,32,512]{2,1,0:T(8,128)S(1)} %copy-done, f32[16,32,512]{2,1,0:T(8,128)S(1)} %copy-done, f32[16,32,512]{2,1,0:T(8,128)S(1)} %copy-done), custom_call_target="tpu_custom_call" | custom-call | bytes 2097152 | tf_op jit(solution)/shard_map/coil_maps/pallas_call | solution.py:514
  2.4 7.5 %all-to-all-start.1 = ((f32[16,4,16,256]{3,2,1,0:T(8,128)}), f32[16,4,16,256]{3,2,1,0:T(8,128)S(1)}, u32[]{:S(2)}, u32[]{:S(2)}) async-start(f32[16,4,16,256]{3,2,1,0:T(8,128)} %coil_maps.1), calls=%async_computation.1 | async-start | bytes 2097152 | tf_op jit(solution)/shard_map/coil_maps/all_to_all | solution.py:527
  11.0 2.0 %collective-permute-start = (f32[8,3,2,16,128]{4,3,2,1,0:T(8,128)S(1)}, f32[8,3,2,16,128]{4,3,2,1,0:T(8,128)S(1)}, u32[]{:S(2)}, u32[]{:S(2)}) collective-permute-start(f32[8,3,2,16,128]{4,3,2,1,0:T(8,128)S(1)} %get-tuple-element.24), channel_id=1, source_target_pairs={{0,2},{1,3},{2,0},{3,1},{4,6},{5,7},{6,4},{7,5},{8,10},{9,11},{10,... | collective-permute-start | bytes 1179656 | tf_op jit(solution)/shard_map/column_maps/ppermute | solution.py:470
  13.0 8.6 %data_transform.3 = (f32[2,4,2,128,256]{4,3,2,1,0:T(8,128)}, f32[2,4,2,128,256]{4,3,2,1,0:T(8,128)}) custom-call(s32[1]{0:T(128)} %bitcast.3.device_ref, f32[128,2,16,512]{3,2,1,0:T(8,128)} %bitcast.30, s32[8,256]{1,0:T(8,128)S(1)} %copy-done.3, bf16[2,512,512]{2,1,0:T(8,128)(2,1)S(1)} %copy-done.4, bf16[2,2,256,256]{3,2,1,0:T(8,128)(2,1)S(1)} %copy-done.5), custom_call_target="tpu_custom_call" | custom-call | flops 4831838208 | bytes 8388608 | tf_op jit(solution)/shard_map/data_transform/pallas_call | solution.py:561
  21.7 8.6 %data_transform.2 = (f32[2,4,2,128,256]{4,3,2,1,0:T(8,128)}, f32[2,4,2,128,256]{4,3,2,1,0:T(8,128)}) custom-call(s32[1]{0:T(128)} %bitcast.3.device_ref, f32[128,2,16,512]{3,2,1,0:T(8,128)} %bitcast.31, s32[8,256]{1,0:T(8,128)S(1)} %copy-done.3, bf16[2,512,512]{2,1,0:T(8,128)(2,1)S(1)} %copy-done.4, bf16[2,2,256,256]{3,2,1,0:T(8,128)(2,1)S(1)} %copy-done.5), custom_call_target="tpu_custom_call" | custom-call | flops 4831838208 | bytes 8388608 | tf_op jit(solution)/shard_map/data_transform/pallas_call | solution.py:561
  30.4 1.2 %pad_maximum_fusion = f32[8,10,2,16,128]{4,3,2,1,0:T(8,128)} fusion(f32[8,3,2,16,128]{4,3,2,1,0:T(8,128)S(1)} %collective-permute-done, f32[8,7,2,16,128]{4,3,2,1,0:T(8,128)S(1)} %get-tuple-element.23), kind=kLoop, calls=%fused_computation | loop fusion | flops 327680 | bytes 2621440 | tf_op jit(solution)/shard_map/column_maps/concatenate | solution.py:547
  32.9 6.3 %all-to-all-start = ((f32[8,10,2,16,128]{4,3,2,1,0:T(8,128)}), f32[8,10,2,16,128]{4,3,2,1,0:T(8,128)S(1)}, u32[]{:S(2)}, u32[]{:S(2)}) async-start(f32[8,10,2,16,128]{4,3,2,1,0:T(8,128)} %pad_maximum_fusion), calls=%async_computation | async-start | bytes 2621440 | tf_op jit(solution)/shard_map/column_maps/all_to_all | solution.py:596
  39.2 2.7 %data_term.5 = f32[4,4,2,16,256]{4,3,2,1,0:T(8,128)} custom-call(s32[1]{0:T(128)} %bitcast.3.device_ref, f32[16,4,16,256]{3,2,1,0:T(8,128)} %copy-done.8, f32[2,4,2,128,256]{4,3,2,1,0:T(8,128)} %get-tuple-element.28.kept_ref, f32[2,4,2,128,256]{4,3,2,1,0:T(8,128)} %collective-permute-done.2.got_ref), custom_call_target="tpu_custom_call" | custom-call | bytes 2621440 | tf_op jit(solution)/shard_map/data_term/pallas_call | solution.py:628
  41.9 1.1 %collective-permute-start.3 = (f32[1,2,2,4,2,16,256]{6,5,4,3,2,1,0:T(8,128)}, f32[1,2,2,4,2,16,256]{6,5,4,3,2,1,0:T(8,128)S(1)}, u32[]{:S(2)}, u32[]{:S(2)}) collective-permute-start(f32[1,2,2,4,2,16,256]{6,5,4,3,2,1,0:T(8,128)} %bitcast.29), channel_id=1, source_target_pairs={{0,2},{1,3},{2,0},{3,1},{4,6},{5,7},{6,4},{7,5},{8,10},{9,11},{10,... | collective-permute-start | bytes 1572872 | tf_op jit(solution)/shard_map/data_term/ppermute | solution.py:470
  43.0 2.7 %data_term.7 = f32[4,4,2,16,256]{4,3,2,1,0:T(8,128)} custom-call(s32[1]{0:T(128)} %bitcast.3.device_ref, f32[16,4,16,256]{3,2,1,0:T(8,128)} %copy-done.8, f32[2,4,2,128,256]{4,3,2,1,0:T(8,128)} %get-tuple-element.30.kept_ref, f32[2,4,2,128,256]{4,3,2,1,0:T(8,128)} %collective-permute-done.5.got_ref), custom_call_target="tpu_custom_call" | custom-call | bytes 2621440 | tf_op jit(solution)/shard_map/data_term/pallas_call | solution.py:628
  46.8 2.7 %data_term.4 = f32[4,4,2,16,256]{4,3,2,1,0:T(8,128)} custom-call(s32[1]{0:T(128)} %bitcast.3.device_ref, f32[16,4,16,256]{3,2,1,0:T(8,128)} %copy-done.8, f32[2,4,2,128,256]{4,3,2,1,0:T(8,128)} %get-tuple-element.28.kept_ref, f32[2,4,2,128,256]{4,3,2,1,0:T(8,128)} %collective-permute-done.2.got_ref), custom_call_target="tpu_custom_call" | custom-call | bytes 2621440 | tf_op jit(solution)/shard_map/data_term/pallas_call | solution.py:628
  49.5 2.8 %data_term.6 = f32[4,4,2,16,256]{4,3,2,1,0:T(8,128)} custom-call(s32[1]{0:T(128)} %bitcast.3.device_ref, f32[16,4,16,256]{3,2,1,0:T(8,128)} %copy-done.8, f32[2,4,2,128,256]{4,3,2,1,0:T(8,128)} %get-tuple-element.30.kept_ref, f32[2,4,2,128,256]{4,3,2,1,0:T(8,128)} %collective-permute-done.5.got_ref), custom_call_target="tpu_custom_call" | custom-call | bytes 2621440 | tf_op jit(solution)/shard_map/data_term/pallas_call | solution.py:628
  52.3 4.6 %collective-permute-done.3 = f32[1,2,2,4,2,16,256]{6,5,4,3,2,1,0:T(8,128)S(1)} collective-permute-done((f32[1,2,2,4,2,16,256]{6,5,4,3,2,1,0:T(8,128)}, f32[1,2,2,4,2,16,256]{6,5,4,3,2,1,0:T(8,128)S(1)}, u32[]{:S(2)}, u32[]{:S(2)}) %collective-permute-start.3) | collective-permute-done | bytes 524320 | tf_op jit(solution)/shard_map/data_term/ppermute | solution.py:470
  57.7 2.1 %collective-permute-start.4 = (f32[1,1,2,4,2,16,256]{6,5,4,3,2,1,0:T(8,128)}, f32[1,1,2,4,2,16,256]{6,5,4,3,2,1,0:T(8,128)S(1)}, u32[]{:S(2)}, u32[]{:S(2)}) collective-permute-start(f32[1,1,2,4,2,16,256]{6,5,4,3,2,1,0:T(8,128)} %get-tuple-element.38), channel_id=1, source_target_pairs={{0,4},{1,5},{2,6},{3,7},{4,0},{5,1},{6,2},{7,3},{8,12},{9,13},{10,... | collective-permute-start | bytes 786440 | tf_op jit(solution)/shard_map/data_term/ppermute | solution.py:470
  59.8 8.0 %collective-permute-done.6 = f32[1,2,2,4,2,16,256]{6,5,4,3,2,1,0:T(8,128)S(1)} collective-permute-done((f32[1,2,2,4,2,16,256]{6,5,4,3,2,1,0:T(8,128)}, f32[1,2,2,4,2,16,256]{6,5,4,3,2,1,0:T(8,128)S(1)}, u32[]{:S(2)}, u32[]{:S(2)}) %collective-permute-start.6) | collective-permute-done | bytes 524320 | tf_op jit(solution)/shard_map/data_term/ppermute | solution.py:470
  67.8 1.1 %dynamic-slice_add_fusion.1 = (f32[1,1,2,4,2,16,256]{6,5,4,3,2,1,0:T(8,128)S(1)}, f32[1,1,2,4,2,16,256]{6,5,4,3,2,1,0:T(8,128)S(1)}) fusion(f32[1,2,2,4,2,16,256]{6,5,4,3,2,1,0:T(8,128)S(1)} %collective-permute-done.6, s32[]{:T(128)S(6)} %select_n.26, f32[1,2,2,4,2,16,256]{6,5,4,3,2,1,0:T(8,128)} %bitcast.26, s32[]{:T(128)S(6)} %select_n.28), kind=kLoop, calls=%fused_computation.2 | loop fusion | flops 131072 | bytes 1572872 | tf_op jit(solution)/shard_map/data_term/add | solution.py:477
  68.9 1.7 %collective-permute-start.7 = (f32[1,1,2,4,2,16,256]{6,5,4,3,2,1,0:T(8,128)S(1)}, f32[1,1,2,4,2,16,256]{6,5,4,3,2,1,0:T(8,128)S(1)}, u32[]{:S(2)}, u32[]{:S(2)}) collective-permute-start(f32[1,1,2,4,2,16,256]{6,5,4,3,2,1,0:T(8,128)S(1)} %get-tuple-element.36), channel_id=1, source_target_pairs={{0,4},{1,5},{2,6},{3,7},{4,0},{5,1},{6,2},{7,3},{8,12},{9,13},{10,... | collective-permute-start | bytes 786440 | tf_op jit(solution)/shard_map/data_term/ppermute | solution.py:470
  71.4 1.1 %collective-permute-start.1 = (f32[8,2,2,16,128]{4,3,2,1,0:T(8,128)S(1)}, f32[8,2,2,16,128]{4,3,2,1,0:T(8,128)S(1)}, u32[]{:S(2)}, u32[]{:S(2)}) collective-permute-start(f32[8,2,2,16,128]{4,3,2,1,0:T(8,128)S(1)} %slice.4), channel_id=1, source_target_pairs={{0,2},{1,3},{2,0},{3,1},{4,6},{5,7},{6,4},{7,5},{8,10},{9,11},{10,... | collective-permute-start | bytes 786440 | tf_op jit(solution)/shard_map/column_maps/ppermute | solution.py:470
  72.6 1.6 %collective-permute-start.8 = (f32[1,1,1,4,2,16,256]{6,5,4,3,2,1,0:T(8,128)S(1)}, f32[1,1,1,4,2,16,256]{6,5,4,3,2,1,0:T(8,128)S(1)}, u32[]{:S(2)}, u32[]{:S(2)}) collective-permute-start(f32[1,1,1,4,2,16,256]{6,5,4,3,2,1,0:T(8,128)S(1)} %get-tuple-element.42.refs_0_), channel_id=1, source_target_pairs={{0,8},{1,9},{2,10},{3,11},{4,12},{5,13},{6,14},{7,15},{8,0},{9,1},... | collective-permute-start | bytes 393224 | tf_op jit(solution)/shard_map/data_term/ppermute | solution.py:470
  74.2 5.6 %collective-permute-done.7 = f32[1,1,2,4,2,16,256]{6,5,4,3,2,1,0:T(8,128)S(1)} collective-permute-done((f32[1,1,2,4,2,16,256]{6,5,4,3,2,1,0:T(8,128)S(1)}, f32[1,1,2,4,2,16,256]{6,5,4,3,2,1,0:T(8,128)S(1)}, u32[]{:S(2)}, u32[]{:S(2)}) %collective-permute-start.7) | collective-permute-done | bytes 262176 | tf_op jit(solution)/shard_map/data_term/ppermute | solution.py:470
  81.0 5.6 %first_gradient.1 = (f32[32,2,16,256]{3,2,1,0:T(8,128)S(1)}, f32[8,2,16,256]{3,2,1,0:T(8,128)S(1)}, f32[8,2,16,256]{3,2,1,0:T(8,128)S(1)}) custom-call(s32[1]{0:T(128)} %bitcast.3.device_ref, f32[8,10,2,16,128]{4,3,2,1,0:T(8,128)S(1)} %all-to-all-done.got_ref, f32[8,2,2,16,128]{4,3,2,1,0:T(8,128)S(1)} %collective-permute-done.1.late_ref, ...), custom_call_target="tpu_custom_call" | custom-call | flops 3221225472 | bytes 4194304 | tf_op jit(solution)/shard_map/data_term/first_gradient/pallas_call | solution.py:609
  87.2 6.4 %outer_steps.1 = f32[16,2,16,128]{3,2,1,0:T(8,128)S(1)} custom-call(f32[8,2,16,256]{3,2,1,0:T(8,128)S(1)} %get-tuple-element.32.field_ref, f32[8,2,16,256]{3,2,1,0:T(8,128)S(1)} %get-tuple-element.33.grad_ref, f32[32,2,16,256]{3,2,1,0:T(8,128)S(1)} %get-tuple-element.34.maps_ref, s32[8,256]{1,0:T(8,128)S(1)} %copy-done.3, ...), custom_call_target="tpu_custom_call" | custom-call | flops 3221225472 | bytes 4194304 | tf_op jit(solution)/shard_map/outer_steps/pallas_call | solution.py:666
  93.6 13.6 %all_to_all.15.got_ref = f32[16,2,16,128]{3,2,1,0:T(8,128)S(1)} all-to-all(f32[16,2,16,128]{3,2,1,0:T(8,128)S(1)} %outer_steps.1), channel_id=1, replica_groups=mesh['plane'=2,'coil'=16] {'coil'}, dimensions={0} | all-to-all | bytes 524288 | tf_op jit(solution)/shard_map/result_rows/all_to_all | solution.py:675
  (38 shorter events, 7.8 us)
Async XLA Ops:
  0.0 1.2 %copy-start = (f32[16,32,512]{2,1,0:T(8,128)S(1)}, f32[16,32,512]{2,1,0:T(8,128)}, u32[]{:S(2)}) copy-start(f32[16,32,512]{2,1,0:T(8,128)} %refs_3_.1) | copy-start | bytes 3145732
  2.4 7.5 %copy-start.1 = (f32[16,32,512]{2,1,0:T(8,128)S(1)}, f32[16,32,512]{2,1,0:T(8,128)}, u32[]{:S(2)}) copy-start(f32[16,32,512]{2,1,0:T(8,128)} %refs_3_.1) | copy-start | bytes 3145732
  2.4 7.5 %copy-start.2 = (f32[16,8,512]{2,1,0:T(8,128)S(1)}, f32[16,8,512]{2,1,0:T(8,128)}, u32[]{:S(2)}) copy-start(f32[16,8,512]{2,1,0:T(8,128)} %param.8) | copy-start | bytes 786436
  2.4 30.5 %all-to-all-start.1 = ((f32[16,4,16,256]{3,2,1,0:T(8,128)}), f32[16,4,16,256]{3,2,1,0:T(8,128)S(1)}, u32[]{:S(2)}, u32[]{:S(2)}) async-start(f32[16,4,16,256]{3,2,1,0:T(8,128)} %coil_maps.1), calls=%async_computation.1 | async-start | bytes 2097152 | tf_op jit(solution)/shard_map/coil_maps/all_to_all | solution.py:527
  9.9 3.0 %copy-start.3 = (s32[8,256]{1,0:T(8,128)S(1)}, s32[8,256]{1,0:T(8,128)}, u32[]{:S(2)}) copy-start(s32[8,256]{1,0:T(8,128)} %mask_ref.7) | copy-start | bytes 24580
  9.9 3.0 %copy-start.4 = (bf16[2,512,512]{2,1,0:T(8,128)(2,1)S(1)}, bf16[2,512,512]{2,1,0:T(8,128)(2,1)}, u32[]{:S(2)}) copy-start(bf16[2,512,512]{2,1,0:T(8,128)(2,1)} %constant.57.clone.refs_0_) | copy-start | bytes 3145732
  10.0 3.0 %copy-start.5 = (bf16[2,2,256,256]{3,2,1,0:T(8,128)(2,1)S(1)}, bf16[2,2,256,256]{3,2,1,0:T(8,128)(2,1)}, u32[]{:S(2)}) copy-start(bf16[2,2,256,256]{3,2,1,0:T(8,128)(2,1)} %constant.58.clone.refs_1_) | copy-start | bytes 1572868
  11.0 19.4 %collective-permute-start = (f32[8,3,2,16,128]{4,3,2,1,0:T(8,128)S(1)}, f32[8,3,2,16,128]{4,3,2,1,0:T(8,128)S(1)}, u32[]{:S(2)}, u32[]{:S(2)}) collective-permute-start(f32[8,3,2,16,128]{4,3,2,1,0:T(8,128)S(1)} %get-tuple-element.24), channel_id=1, source_target_pairs={{0,2},{1,3},{2,0},{3,1},{4,6},{5,7},{6,4},{7,5},{8,10},{9,11},{10,... | collective-permute-start | bytes 1179656 | tf_op jit(solution)/shard_map/column_maps/ppermute | solution.py:470
  21.6 17.6 %collective-permute-start.2 = (f32[2,4,2,128,256]{4,3,2,1,0:T(8,128)}, f32[2,4,2,128,256]{4,3,2,1,0:T(8,128)}, u32[]{:S(2)}, u32[]{:S(2)}) collective-permute-start(f32[2,4,2,128,256]{4,3,2,1,0:T(8,128)} %get-tuple-element.29), channel_id=1, source_target_pairs={{0,1},{1,0},{2,3},{3,2},{4,5},{5,4},{6,7},{7,6},{8,9},{9,8},{10,11... | collective-permute-start | bytes 6291464 | tf_op jit(solution)/shard_map/ppermute | solution.py:470
  31.5 11.5 %collective-permute-start.5 = (f32[2,4,2,128,256]{4,3,2,1,0:T(8,128)}, f32[2,4,2,128,256]{4,3,2,1,0:T(8,128)}, u32[]{:S(2)}, u32[]{:S(2)}) collective-permute-start(f32[2,4,2,128,256]{4,3,2,1,0:T(8,128)} %get-tuple-element.31), channel_id=1, source_target_pairs={{0,1},{1,0},{2,3},{3,2},{4,5},{5,4},{6,7},{7,6},{8,9},{9,8},{10,11... | collective-permute-start | bytes 6291464 | tf_op jit(solution)/shard_map/ppermute | solution.py:470
  32.9 6.4 %copy-start.8 = (f32[16,4,16,256]{3,2,1,0:T(8,128)}, f32[16,4,16,256]{3,2,1,0:T(8,128)S(1)}, u32[]{:S(2)}) copy-start(f32[16,4,16,256]{3,2,1,0:T(8,128)S(1)} %all-to-all-done.1.maps_ref) | copy-start | bytes 3145732
  32.9 38.6 %all-to-all-start = ((f32[8,10,2,16,128]{4,3,2,1,0:T(8,128)}), f32[8,10,2,16,128]{4,3,2,1,0:T(8,128)S(1)}, u32[]{:S(2)}, u32[]{:S(2)}) async-start(f32[8,10,2,16,128]{4,3,2,1,0:T(8,128)} %pad_maximum_fusion), calls=%async_computation | async-start | bytes 2621440 | tf_op jit(solution)/shard_map/column_maps/all_to_all | solution.py:596
  41.9 15.0 %collective-permute-start.3 = (f32[1,2,2,4,2,16,256]{6,5,4,3,2,1,0:T(8,128)}, f32[1,2,2,4,2,16,256]{6,5,4,3,2,1,0:T(8,128)S(1)}, u32[]{:S(2)}, u32[]{:S(2)}) collective-permute-start(f32[1,2,2,4,2,16,256]{6,5,4,3,2,1,0:T(8,128)} %bitcast.29), channel_id=1, source_target_pairs={{0,2},{1,3},{2,0},{3,1},{4,6},{5,7},{6,4},{7,5},{8,10},{9,11},{10,... | collective-permute-start | bytes 1572872 | tf_op jit(solution)/shard_map/data_term/ppermute | solution.py:470
  45.8 22.0 %collective-permute-start.6 = (f32[1,2,2,4,2,16,256]{6,5,4,3,2,1,0:T(8,128)}, f32[1,2,2,4,2,16,256]{6,5,4,3,2,1,0:T(8,128)S(1)}, u32[]{:S(2)}, u32[]{:S(2)}) collective-permute-start(f32[1,2,2,4,2,16,256]{6,5,4,3,2,1,0:T(8,128)} %bitcast.28), channel_id=1, source_target_pairs={{0,2},{1,3},{2,0},{3,1},{4,6},{5,7},{6,4},{7,5},{8,10},{9,11},{10,... | collective-permute-start | bytes 1572872 | tf_op jit(solution)/shard_map/data_term/ppermute | solution.py:470
  49.5 7.4 %copy-start.9 = (f32[4,4,2,16,256]{4,3,2,1,0:T(8,128)S(1)}, f32[4,4,2,16,256]{4,3,2,1,0:T(8,128)}, u32[]{:S(2)}) copy-start(f32[4,4,2,16,256]{4,3,2,1,0:T(8,128)} %data_term.4) | copy-start | bytes 1572868
  57.7 23.2 %copy-start.6 = (bf16[2,128,256]{2,1,0:T(8,128)(2,1)S(1)}, bf16[2,128,256]{2,1,0:T(8,128)(2,1)}, u32[]{:S(2)}) copy-start(bf16[2,128,256]{2,1,0:T(8,128)(2,1)} %constant.59.clone.wave_hi.refs_0_) | copy-start | bytes 393220
  57.7 23.2 %copy-start.7 = (bf16[2,128,256]{2,1,0:T(8,128)(2,1)S(1)}, bf16[2,128,256]{2,1,0:T(8,128)(2,1)}, u32[]{:S(2)}) copy-start(bf16[2,128,256]{2,1,0:T(8,128)(2,1)} %constant.60.clone.wave_lo.refs_1_) | copy-start | bytes 393220
  57.7 14.8 %collective-permute-start.4 = (f32[1,1,2,4,2,16,256]{6,5,4,3,2,1,0:T(8,128)}, f32[1,1,2,4,2,16,256]{6,5,4,3,2,1,0:T(8,128)S(1)}, u32[]{:S(2)}, u32[]{:S(2)}) collective-permute-start(f32[1,1,2,4,2,16,256]{6,5,4,3,2,1,0:T(8,128)} %get-tuple-element.38), channel_id=1, source_target_pairs={{0,4},{1,5},{2,6},{3,7},{4,0},{5,1},{6,2},{7,3},{8,12},{9,13},{10,... | collective-permute-start | bytes 786440 | tf_op jit(solution)/shard_map/data_term/ppermute | solution.py:470
  68.9 10.9 %collective-permute-start.7 = (f32[1,1,2,4,2,16,256]{6,5,4,3,2,1,0:T(8,128)S(1)}, f32[1,1,2,4,2,16,256]{6,5,4,3,2,1,0:T(8,128)S(1)}, u32[]{:S(2)}, u32[]{:S(2)}) collective-permute-start(f32[1,1,2,4,2,16,256]{6,5,4,3,2,1,0:T(8,128)S(1)} %get-tuple-element.36), channel_id=1, source_target_pairs={{0,4},{1,5},{2,6},{3,7},{4,0},{5,1},{6,2},{7,3},{8,12},{9,13},{10,... | collective-permute-start | bytes 786440 | tf_op jit(solution)/shard_map/data_term/ppermute | solution.py:470
  71.4 9.5 %collective-permute-start.1 = (f32[8,2,2,16,128]{4,3,2,1,0:T(8,128)S(1)}, f32[8,2,2,16,128]{4,3,2,1,0:T(8,128)S(1)}, u32[]{:S(2)}, u32[]{:S(2)}) collective-permute-start(f32[8,2,2,16,128]{4,3,2,1,0:T(8,128)S(1)} %slice.4), channel_id=1, source_target_pairs={{0,2},{1,3},{2,0},{3,1},{4,6},{5,7},{6,4},{7,5},{8,10},{9,11},{10,... | collective-permute-start | bytes 786440 | tf_op jit(solution)/shard_map/column_maps/ppermute | solution.py:470
  72.6 14.0 %collective-permute-start.8 = (f32[1,1,1,4,2,16,256]{6,5,4,3,2,1,0:T(8,128)S(1)}, f32[1,1,1,4,2,16,256]{6,5,4,3,2,1,0:T(8,128)S(1)}, u32[]{:S(2)}, u32[]{:S(2)}) collective-permute-start(f32[1,1,1,4,2,16,256]{6,5,4,3,2,1,0:T(8,128)S(1)} %get-tuple-element.42.refs_0_), channel_id=1, source_target_pairs={{0,8},{1,9},{2,10},{3,11},{4,12},{5,13},{6,14},{7,15},{8,0},{9,1},... | collective-permute-start | bytes 393224 | tf_op jit(solution)/shard_map/data_term/ppermute | solution.py:470
  79.9 7.3 %collective-permute-start.9 = (f32[1,1,1,4,2,16,256]{6,5,4,3,2,1,0:T(8,128)S(1)}, f32[1,1,1,4,2,16,256]{6,5,4,3,2,1,0:T(8,128)S(1)}, u32[]{:S(2)}, u32[]{:S(2)}) collective-permute-start(f32[1,1,1,4,2,16,256]{6,5,4,3,2,1,0:T(8,128)S(1)} %get-tuple-element.40.refs_1_), channel_id=1, source_target_pairs={{0,8},{1,9},{2,10},{3,11},{4,12},{5,13},{6,14},{7,15},{8,0},{9,1},... | collective-permute-start | bytes 393224 | tf_op jit(solution)/shard_map/data_term/ppermute | solution.py:470

commit v10 on v9

--- a/solution.py
+++ b/solution.py
@@ -520,7 +520,7 @@
                 for t in range(packed // LANES)
             ],
             out_specs=whole((devices, 2 * own, rows, half)),
-            compiler_params=params(),
+            compiler_params=params(WEIGH_LIMIT),
             cost_estimate=cost(0, 2 * sens.size * 4),
         )(*[sens] * (packed // LANES))
         blocks, device = lax.optimization_barrier((blocks, device))

time: 109 us -> 109 us (level)
  Pallas kernels: 43.2 us -> 44.5 us
  local copies, waits for them, and re-layouts: 1.28 us -> 0.06 us
    unnamed x20 -> x18, local copies, waits for them, and re-layouts: 1.27 us -> 0.04 us
    pallas_call x1, Pallas kernels: 1.16 us -> 2.34 us  [kernel_path(): pl.pallas_call(functools.partial(coil_blocks_kernel, coils), grid=(1,), o...]
where the time goes in v10:
time: 109 us; the launch traced here: 108 us
  Pallas kernels  44.5 us (41%)
  starting transfers between devices  26.1 us (24%)
  waiting for transfers between devices  20.4 us (19%)
  blocking collectives  13.6 us (12%)
  other arithmetic  3.17 us (3%)
    ppermute x10, waiting for transfers between devices, exchange(): lax.ppermute(send, 'coil', [(i, i ^ 1 << bit) for i in range(devices)])  18.8 us
    pallas_call x2, Pallas kernels, kernel_path(): pl.pallas_call(functools.partial(base_kernel, start, frames), grid=(count...  17.3 us
    all_to_all x1, blocking collectives, kernel_path(): got = lax.all_to_all(blocks, 'coil', 0, 0, tiled=True)  13.6 us
    ppermute x10, starting transfers between devices, exchange(): lax.ppermute(send, 'coil', [(i, i ^ 1 << bit) for i in range(devices)])  12.3 us
    pallas_call x4, Pallas kernels, weigh(): pl.pallas_call(functools.partial(weigh_kernel, outer, order[0], flip), ou...  11 us
    all_to_all x1, starting transfers between devices, kernel_path(): coil_maps = lax.all_to_all(blocks, 'coil', 0, 0, tiled=True)  7.52 us
    pallas_call x1, Pallas kernels, kernel_path(): pl.pallas_call(steps_kernel, out_shape=f32(devices, 2, cols, LANES), scra...  6.41 us
    all_to_all x1, starting transfers between devices, kernel_path(): lax.all_to_all(column_blocks, 'coil', 0, 0, tiled=True, axis_index_groups...  6.34 us
  transfers between devices with their start and end apart: 12, of which 6 were waited for; matrix products, arithmetic and copies ran while one was open for 3% of the time, Pallas kernels for 32%

profile of v10, /device:TPU:0, one launch (start us, length us, event | category | flops | bytes accessed | tf_op | source)
XLA Modules:
  0.0 108.1 jit_solution(1113625779838839954)
XLA Ops:
  0.0 2.3 %coil_maps.1 = f32[16,4,16,256]{3,2,1,0:T(8,128)} custom-call(f32[16,32,512]{2,1,0:T(8,128)} %refs_3_.1, f32[16,32,512]{2,1,0:T(8,128)} %refs_3_.1, f32[16,32,512]{2,1,0:T(8,128)} %refs_3_.1, f32[16,32,512]{2,1,0:T(8,128)} %refs_3_.1), custom_call_target="tpu_custom_call" | custom-call | bytes 2097152 | tf_op jit(solution)/shard_map/coil_maps/pallas_call | solution.py:514
  2.4 7.5 %all-to-all-start.1 = ((f32[16,4,16,256]{3,2,1,0:T(8,128)}), f32[16,4,16,256]{3,2,1,0:T(8,128)S(1)}, u32[]{:S(2)}, u32[]{:S(2)}) async-start(f32[16,4,16,256]{3,2,1,0:T(8,128)} %coil_maps.1), calls=%async_computation.1 | async-start | bytes 2097152 | tf_op jit(solution)/shard_map/coil_maps/all_to_all | solution.py:527
  11.0 2.0 %collective-permute-start = (f32[8,3,2,16,128]{4,3,2,1,0:T(8,128)S(1)}, f32[8,3,2,16,128]{4,3,2,1,0:T(8,128)S(1)}, u32[]{:S(2)}, u32[]{:S(2)}) collective-permute-start(f32[8,3,2,16,128]{4,3,2,1,0:T(8,128)S(1)} %get-tuple-element.24), channel_id=1, source_target_pairs={{0,2},{1,3},{2,0},{3,1},{4,6},{5,7},{6,4},{7,5},{8,10},{9,11},{10,... | collective-permute-start | bytes 1179656 | tf_op jit(solution)/shard_map/column_maps/ppermute | solution.py:470
  12.9 8.6 %data_transform.3 = (f32[2,4,2,128,256]{4,3,2,1,0:T(8,128)}, f32[2,4,2,128,256]{4,3,2,1,0:T(8,128)}) custom-call(s32[1]{0:T(128)} %bitcast.3.device_ref, f32[128,2,16,512]{3,2,1,0:T(8,128)} %bitcast.30, s32[8,256]{1,0:T(8,128)S(1)} %copy-done.2, bf16[2,512,512]{2,1,0:T(8,128)(2,1)S(1)} %copy-done.3, bf16[2,2,256,256]{3,2,1,0:T(8,128)(2,1)S(1)} %copy-done.4), custom_call_target="tpu_custom_call" | custom-call | flops 4831838208 | bytes 8388608 | tf_op jit(solution)/shard_map/data_transform/pallas_call | solution.py:561
  21.6 8.6 %data_transform.2 = (f32[2,4,2,128,256]{4,3,2,1,0:T(8,128)}, f32[2,4,2,128,256]{4,3,2,1,0:T(8,128)}) custom-call(s32[1]{0:T(128)} %bitcast.3.device_ref, f32[128,2,16,512]{3,2,1,0:T(8,128)} %bitcast.31, s32[8,256]{1,0:T(8,128)S(1)} %copy-done.2, bf16[2,512,512]{2,1,0:T(8,128)(2,1)S(1)} %copy-done.3, bf16[2,2,256,256]{3,2,1,0:T(8,128)(2,1)S(1)} %copy-done.4), custom_call_target="tpu_custom_call" | custom-call | flops 4831838208 | bytes 8388608 | tf_op jit(solution)/shard_map/data_transform/pallas_call | solution.py:561
  30.3 1.2 %pad_maximum_fusion = f32[8,10,2,16,128]{4,3,2,1,0:T(8,128)} fusion(f32[8,3,2,16,128]{4,3,2,1,0:T(8,128)S(1)} %collective-permute-done, f32[8,7,2,16,128]{4,3,2,1,0:T(8,128)S(1)} %get-tuple-element.23), kind=kLoop, calls=%fused_computation | loop fusion | flops 327680 | bytes 2621440 | tf_op jit(solution)/shard_map/column_maps/concatenate | solution.py:547
  32.8 6.3 %all-to-all-start = ((f32[8,10,2,16,128]{4,3,2,1,0:T(8,128)}), f32[8,10,2,16,128]{4,3,2,1,0:T(8,128)S(1)}, u32[]{:S(2)}, u32[]{:S(2)}) async-start(f32[8,10,2,16,128]{4,3,2,1,0:T(8,128)} %pad_maximum_fusion), calls=%async_computation | async-start | bytes 2621440 | tf_op jit(solution)/shard_map/column_maps/all_to_all | solution.py:596
  39.2 2.7 %data_term.5 = f32[4,4,2,16,256]{4,3,2,1,0:T(8,128)} custom-call(s32[1]{0:T(128)} %bitcast.3.device_ref, f32[16,4,16,256]{3,2,1,0:T(8,128)} %copy-done.7, f32[2,4,2,128,256]{4,3,2,1,0:T(8,128)} %get-tuple-element.28.kept_ref, f32[2,4,2,128,256]{4,3,2,1,0:T(8,128)} %collective-permute-done.2.got_ref), custom_call_target="tpu_custom_call" | custom-call | bytes 2621440 | tf_op jit(solution)/shard_map/data_term/pallas_call | solution.py:628
  41.9 1.1 %collective-permute-start.3 = (f32[1,2,2,4,2,16,256]{6,5,4,3,2,1,0:T(8,128)}, f32[1,2,2,4,2,16,256]{6,5,4,3,2,1,0:T(8,128)S(1)}, u32[]{:S(2)}, u32[]{:S(2)}) collective-permute-start(f32[1,2,2,4,2,16,256]{6,5,4,3,2,1,0:T(8,128)} %bitcast.29), channel_id=1, source_target_pairs={{0,2},{1,3},{2,0},{3,1},{4,6},{5,7},{6,4},{7,5},{8,10},{9,11},{10,... | collective-permute-start | bytes 1572872 | tf_op jit(solution)/shard_map/data_term/ppermute | solution.py:470
  43.0 2.7 %data_term.7 = f32[4,4,2,16,256]{4,3,2,1,0:T(8,128)} custom-call(s32[1]{0:T(128)} %bitcast.3.device_ref, f32[16,4,16,256]{3,2,1,0:T(8,128)} %copy-done.7, f32[2,4,2,128,256]{4,3,2,1,0:T(8,128)} %get-tuple-element.30.kept_ref, f32[2,4,2,128,256]{4,3,2,1,0:T(8,128)} %collective-permute-done.5.got_ref), custom_call_target="tpu_custom_call" | custom-call | bytes 2621440 | tf_op jit(solution)/shard_map/data_term/pallas_call | solution.py:628
  46.8 2.7 %data_term.4 = f32[4,4,2,16,256]{4,3,2,1,0:T(8,128)} custom-call(s32[1]{0:T(128)} %bitcast.3.device_ref, f32[16,4,16,256]{3,2,1,0:T(8,128)} %copy-done.7, f32[2,4,2,128,256]{4,3,2,1,0:T(8,128)} %get-tuple-element.28.kept_ref, f32[2,4,2,128,256]{4,3,2,1,0:T(8,128)} %collective-permute-done.2.got_ref), custom_call_target="tpu_custom_call" | custom-call | bytes 2621440 | tf_op jit(solution)/shard_map/data_term/pallas_call | solution.py:628
  49.6 2.8 %data_term.6 = f32[4,4,2,16,256]{4,3,2,1,0:T(8,128)} custom-call(s32[1]{0:T(128)} %bitcast.3.device_ref, f32[16,4,16,256]{3,2,1,0:T(8,128)} %copy-done.7, f32[2,4,2,128,256]{4,3,2,1,0:T(8,128)} %get-tuple-element.30.kept_ref, f32[2,4,2,128,256]{4,3,2,1,0:T(8,128)} %collective-permute-done.5.got_ref), custom_call_target="tpu_custom_call" | custom-call | bytes 2621440 | tf_op jit(solution)/shard_map/data_term/pallas_call | solution.py:628
  52.4 4.6 %collective-permute-done.3 = f32[1,2,2,4,2,16,256]{6,5,4,3,2,1,0:T(8,128)S(1)} collective-permute-done((f32[1,2,2,4,2,16,256]{6,5,4,3,2,1,0:T(8,128)}, f32[1,2,2,4,2,16,256]{6,5,4,3,2,1,0:T(8,128)S(1)}, u32[]{:S(2)}, u32[]{:S(2)}) %collective-permute-start.3) | collective-permute-done | bytes 524320 | tf_op jit(solution)/shard_map/data_term/ppermute | solution.py:470
  57.7 2.1 %collective-permute-start.4 = (f32[1,1,2,4,2,16,256]{6,5,4,3,2,1,0:T(8,128)}, f32[1,1,2,4,2,16,256]{6,5,4,3,2,1,0:T(8,128)S(1)}, u32[]{:S(2)}, u32[]{:S(2)}) collective-permute-start(f32[1,1,2,4,2,16,256]{6,5,4,3,2,1,0:T(8,128)} %get-tuple-element.38), channel_id=1, source_target_pairs={{0,4},{1,5},{2,6},{3,7},{4,0},{5,1},{6,2},{7,3},{8,12},{9,13},{10,... | collective-permute-start | bytes 786440 | tf_op jit(solution)/shard_map/data_term/ppermute | solution.py:470
  59.8 8.0 %collective-permute-done.6 = f32[1,2,2,4,2,16,256]{6,5,4,3,2,1,0:T(8,128)S(1)} collective-permute-done((f32[1,2,2,4,2,16,256]{6,5,4,3,2,1,0:T(8,128)}, f32[1,2,2,4,2,16,256]{6,5,4,3,2,1,0:T(8,128)S(1)}, u32[]{:S(2)}, u32[]{:S(2)}) %collective-permute-start.6) | collective-permute-done | bytes 524320 | tf_op jit(solution)/shard_map/data_term/ppermute | solution.py:470
  67.8 1.1 %dynamic-slice_add_fusion.1 = (f32[1,1,2,4,2,16,256]{6,5,4,3,2,1,0:T(8,128)S(1)}, f32[1,1,2,4,2,16,256]{6,5,4,3,2,1,0:T(8,128)S(1)}) fusion(f32[1,2,2,4,2,16,256]{6,5,4,3,2,1,0:T(8,128)S(1)} %collective-permute-done.6, s32[]{:T(128)S(6)} %select_n.26, f32[1,2,2,4,2,16,256]{6,5,4,3,2,1,0:T(8,128)} %bitcast.26, s32[]{:T(128)S(6)} %select_n.28), kind=kLoop, calls=%fused_computation.2 | loop fusion | flops 131072 | bytes 1572872 | tf_op jit(solution)/shard_map/data_term/add | solution.py:477
  68.9 1.7 %collective-permute-start.7 = (f32[1,1,2,4,2,16,256]{6,5,4,3,2,1,0:T(8,128)S(1)}, f32[1,1,2,4,2,16,256]{6,5,4,3,2,1,0:T(8,128)S(1)}, u32[]{:S(2)}, u32[]{:S(2)}) collective-permute-start(f32[1,1,2,4,2,16,256]{6,5,4,3,2,1,0:T(8,128)S(1)} %get-tuple-element.36), channel_id=1, source_target_pairs={{0,4},{1,5},{2,6},{3,7},{4,0},{5,1},{6,2},{7,3},{8,12},{9,13},{10,... | collective-permute-start | bytes 786440 | tf_op jit(solution)/shard_map/data_term/ppermute | solution.py:470
  71.4 1.1 %collective-permute-start.1 = (f32[8,2,2,16,128]{4,3,2,1,0:T(8,128)S(1)}, f32[8,2,2,16,128]{4,3,2,1,0:T(8,128)S(1)}, u32[]{:S(2)}, u32[]{:S(2)}) collective-permute-start(f32[8,2,2,16,128]{4,3,2,1,0:T(8,128)S(1)} %slice.4), channel_id=1, source_target_pairs={{0,2},{1,3},{2,0},{3,1},{4,6},{5,7},{6,4},{7,5},{8,10},{9,11},{10,... | collective-permute-start | bytes 786440 | tf_op jit(solution)/shard_map/column_maps/ppermute | solution.py:470
  72.5 1.7 %collective-permute-start.8 = (f32[1,1,1,4,2,16,256]{6,5,4,3,2,1,0:T(8,128)S(1)}, f32[1,1,1,4,2,16,256]{6,5,4,3,2,1,0:T(8,128)S(1)}, u32[]{:S(2)}, u32[]{:S(2)}) collective-permute-start(f32[1,1,1,4,2,16,256]{6,5,4,3,2,1,0:T(8,128)S(1)} %get-tuple-element.42.refs_0_), channel_id=1, source_target_pairs={{0,8},{1,9},{2,10},{3,11},{4,12},{5,13},{6,14},{7,15},{8,0},{9,1},... | collective-permute-start | bytes 393224 | tf_op jit(solution)/shard_map/data_term/ppermute | solution.py:470
  74.2 5.6 %collective-permute-done.7 = f32[1,1,2,4,2,16,256]{6,5,4,3,2,1,0:T(8,128)S(1)} collective-permute-done((f32[1,1,2,4,2,16,256]{6,5,4,3,2,1,0:T(8,128)S(1)}, f32[1,1,2,4,2,16,256]{6,5,4,3,2,1,0:T(8,128)S(1)}, u32[]{:S(2)}, u32[]{:S(2)}) %collective-permute-start.7) | collective-permute-done | bytes 262176 | tf_op jit(solution)/shard_map/data_term/ppermute | solution.py:470
  79.8 1.1 %collective-permute-start.9 = (f32[1,1,1,4,2,16,256]{6,5,4,3,2,1,0:T(8,128)S(1)}, f32[1,1,1,4,2,16,256]{6,5,4,3,2,1,0:T(8,128)S(1)}, u32[]{:S(2)}, u32[]{:S(2)}) collective-permute-start(f32[1,1,1,4,2,16,256]{6,5,4,3,2,1,0:T(8,128)S(1)} %get-tuple-element.40.refs_1_), channel_id=1, source_target_pairs={{0,8},{1,9},{2,10},{3,11},{4,12},{5,13},{6,14},{7,15},{8,0},{9,1},... | collective-permute-start | bytes 393224 | tf_op jit(solution)/shard_map/data_term/ppermute | solution.py:470
  81.0 5.6 %first_gradient.1 = (f32[32,2,16,256]{3,2,1,0:T(8,128)S(1)}, f32[8,2,16,256]{3,2,1,0:T(8,128)S(1)}, f32[8,2,16,256]{3,2,1,0:T(8,128)S(1)}) custom-call(s32[1]{0:T(128)} %bitcast.3.device_ref, f32[8,10,2,16,128]{4,3,2,1,0:T(8,128)S(1)} %all-to-all-done.got_ref, f32[8,2,2,16,128]{4,3,2,1,0:T(8,128)S(1)} %collective-permute-done.1.late_ref, ...), custom_call_target="tpu_custom_call" | custom-call | flops 3221225472 | bytes 4194304 | tf_op jit(solution)/shard_map/data_term/first_gradient/pallas_call | solution.py:609
  87.2 6.4 %outer_steps.1 = f32[16,2,16,128]{3,2,1,0:T(8,128)S(1)} custom-call(f32[8,2,16,256]{3,2,1,0:T(8,128)S(1)} %get-tuple-element.32.field_ref, f32[8,2,16,256]{3,2,1,0:T(8,128)S(1)} %get-tuple-element.33.grad_ref, f32[32,2,16,256]{3,2,1,0:T(8,128)S(1)} %get-tuple-element.34.maps_ref, s32[8,256]{1,0:T(8,128)S(1)} %copy-done.2, ...), custom_call_target="tpu_custom_call" | custom-call | flops 3221225472 | bytes 4194304 | tf_op jit(solution)/shard_map/outer_steps/pallas_call | solution.py:666
  93.6 13.6 %all_to_all.15.got_ref = f32[16,2,16,128]{3,2,1,0:T(8,128)S(1)} all-to-all(f32[16,2,16,128]{3,2,1,0:T(8,128)S(1)} %outer_steps.1), channel_id=1, replica_groups=mesh['plane'=2,'coil'=16] {'coil'}, dimensions={0} | all-to-all | bytes 524288 | tf_op jit(solution)/shard_map/result_rows/all_to_all | solution.py:675
  (36 shorter events, 6.6 us)
Async XLA Ops:
  2.3 7.5 %copy-start = (f32[16,32,512]{2,1,0:T(8,128)S(1)}, f32[16,32,512]{2,1,0:T(8,128)}, u32[]{:S(2)}) copy-start(f32[16,32,512]{2,1,0:T(8,128)} %refs_3_.1) | copy-start | bytes 3145732
  2.3 7.5 %copy-start.1 = (f32[16,8,512]{2,1,0:T(8,128)S(1)}, f32[16,8,512]{2,1,0:T(8,128)}, u32[]{:S(2)}) copy-start(f32[16,8,512]{2,1,0:T(8,128)} %param.8) | copy-start | bytes 786436
  2.4 30.5 %all-to-all-start.1 = ((f32[16,4,16,256]{3,2,1,0:T(8,128)}), f32[16,4,16,256]{3,2,1,0:T(8,128)S(1)}, u32[]{:S(2)}, u32[]{:S(2)}) async-start(f32[16,4,16,256]{3,2,1,0:T(8,128)} %coil_maps.1), calls=%async_computation.1 | async-start | bytes 2097152 | tf_op jit(solution)/shard_map/coil_maps/all_to_all | solution.py:527
  9.9 3.0 %copy-start.2 = (s32[8,256]{1,0:T(8,128)S(1)}, s32[8,256]{1,0:T(8,128)}, u32[]{:S(2)}) copy-start(s32[8,256]{1,0:T(8,128)} %mask_ref.7) | copy-start | bytes 24580
  9.9 3.0 %copy-start.3 = (bf16[2,512,512]{2,1,0:T(8,128)(2,1)S(1)}, bf16[2,512,512]{2,1,0:T(8,128)(2,1)}, u32[]{:S(2)}) copy-start(bf16[2,512,512]{2,1,0:T(8,128)(2,1)} %constant.57.clone.refs_0_) | copy-start | bytes 3145732
  9.9 3.0 %copy-start.4 = (bf16[2,2,256,256]{3,2,1,0:T(8,128)(2,1)S(1)}, bf16[2,2,256,256]{3,2,1,0:T(8,128)(2,1)}, u32[]{:S(2)}) copy-start(bf16[2,2,256,256]{3,2,1,0:T(8,128)(2,1)} %constant.58.clone.refs_1_) | copy-start | bytes 1572868
  11.0 19.4 %collective-permute-start = (f32[8,3,2,16,128]{4,3,2,1,0:T(8,128)S(1)}, f32[8,3,2,16,128]{4,3,2,1,0:T(8,128)S(1)}, u32[]{:S(2)}, u32[]{:S(2)}) collective-permute-start(f32[8,3,2,16,128]{4,3,2,1,0:T(8,128)S(1)} %get-tuple-element.24), channel_id=1, source_target_pairs={{0,2},{1,3},{2,0},{3,1},{4,6},{5,7},{6,4},{7,5},{8,10},{9,11},{10,... | collective-permute-start | bytes 1179656 | tf_op jit(solution)/shard_map/column_maps/ppermute | solution.py:470
  21.6 17.6 %collective-permute-start.2 = (f32[2,4,2,128,256]{4,3,2,1,0:T(8,128)}, f32[2,4,2,128,256]{4,3,2,1,0:T(8,128)}, u32[]{:S(2)}, u32[]{:S(2)}) collective-permute-start(f32[2,4,2,128,256]{4,3,2,1,0:T(8,128)} %get-tuple-element.29), channel_id=1, source_target_pairs={{0,1},{1,0},{2,3},{3,2},{4,5},{5,4},{6,7},{7,6},{8,9},{9,8},{10,11... | collective-permute-start | bytes 6291464 | tf_op jit(solution)/shard_map/ppermute | solution.py:470
  31.5 11.5 %collective-permute-start.5 = (f32[2,4,2,128,256]{4,3,2,1,0:T(8,128)}, f32[2,4,2,128,256]{4,3,2,1,0:T(8,128)}, u32[]{:S(2)}, u32[]{:S(2)}) collective-permute-start(f32[2,4,2,128,256]{4,3,2,1,0:T(8,128)} %get-tuple-element.31), channel_id=1, source_target_pairs={{0,1},{1,0},{2,3},{3,2},{4,5},{5,4},{6,7},{7,6},{8,9},{9,8},{10,11... | collective-permute-start | bytes 6291464 | tf_op jit(solution)/shard_map/ppermute | solution.py:470
  32.8 6.4 %copy-start.7 = (f32[16,4,16,256]{3,2,1,0:T(8,128)}, f32[16,4,16,256]{3,2,1,0:T(8,128)S(1)}, u32[]{:S(2)}) copy-start(f32[16,4,16,256]{3,2,1,0:T(8,128)S(1)} %all-to-all-done.1.maps_ref) | copy-start | bytes 3145732
  32.8 38.6 %all-to-all-start = ((f32[8,10,2,16,128]{4,3,2,1,0:T(8,128)}), f32[8,10,2,16,128]{4,3,2,1,0:T(8,128)S(1)}, u32[]{:S(2)}, u32[]{:S(2)}) async-start(f32[8,10,2,16,128]{4,3,2,1,0:T(8,128)} %pad_maximum_fusion), calls=%async_computation | async-start | bytes 2621440 | tf_op jit(solution)/shard_map/column_maps/all_to_all | solution.py:596
  41.9 15.0 %collective-permute-start.3 = (f32[1,2,2,4,2,16,256]{6,5,4,3,2,1,0:T(8,128)}, f32[1,2,2,4,2,16,256]{6,5,4,3,2,1,0:T(8,128)S(1)}, u32[]{:S(2)}, u32[]{:S(2)}) collective-permute-start(f32[1,2,2,4,2,16,256]{6,5,4,3,2,1,0:T(8,128)} %bitcast.29), channel_id=1, source_target_pairs={{0,2},{1,3},{2,0},{3,1},{4,6},{5,7},{6,4},{7,5},{8,10},{9,11},{10,... | collective-permute-start | bytes 1572872 | tf_op jit(solution)/shard_map/data_term/ppermute | solution.py:470
  45.8 22.0 %collective-permute-start.6 = (f32[1,2,2,4,2,16,256]{6,5,4,3,2,1,0:T(8,128)}, f32[1,2,2,4,2,16,256]{6,5,4,3,2,1,0:T(8,128)S(1)}, u32[]{:S(2)}, u32[]{:S(2)}) collective-permute-start(f32[1,2,2,4,2,16,256]{6,5,4,3,2,1,0:T(8,128)} %bitcast.28), channel_id=1, source_target_pairs={{0,2},{1,3},{2,0},{3,1},{4,6},{5,7},{6,4},{7,5},{8,10},{9,11},{10,... | collective-permute-start | bytes 1572872 | tf_op jit(solution)/shard_map/data_term/ppermute | solution.py:470
  49.6 7.4 %copy-start.8 = (f32[4,4,2,16,256]{4,3,2,1,0:T(8,128)S(1)}, f32[4,4,2,16,256]{4,3,2,1,0:T(8,128)}, u32[]{:S(2)}) copy-start(f32[4,4,2,16,256]{4,3,2,1,0:T(8,128)} %data_term.4) | copy-start | bytes 1572868
  57.7 23.2 %copy-start.5 = (bf16[2,128,256]{2,1,0:T(8,128)(2,1)S(1)}, bf16[2,128,256]{2,1,0:T(8,128)(2,1)}, u32[]{:S(2)}) copy-start(bf16[2,128,256]{2,1,0:T(8,128)(2,1)} %constant.59.clone.wave_hi.refs_0_) | copy-start | bytes 393220
  57.7 23.2 %copy-start.6 = (bf16[2,128,256]{2,1,0:T(8,128)(2,1)S(1)}, bf16[2,128,256]{2,1,0:T(8,128)(2,1)}, u32[]{:S(2)}) copy-start(bf16[2,128,256]{2,1,0:T(8,128)(2,1)} %constant.60.clone.wave_lo.refs_1_) | copy-start | bytes 393220
  57.7 14.8 %collective-permute-start.4 = (f32[1,1,2,4,2,16,256]{6,5,4,3,2,1,0:T(8,128)}, f32[1,1,2,4,2,16,256]{6,5,4,3,2,1,0:T(8,128)S(1)}, u32[]{:S(2)}, u32[]{:S(2)}) collective-permute-start(f32[1,1,2,4,2,16,256]{6,5,4,3,2,1,0:T(8,128)} %get-tuple-element.38), channel_id=1, source_target_pairs={{0,4},{1,5},{2,6},{3,7},{4,0},{5,1},{6,2},{7,3},{8,12},{9,13},{10,... | collective-permute-start | bytes 786440 | tf_op jit(solution)/shard_map/data_term/ppermute | solution.py:470
  68.9 10.9 %collective-permute-start.7 = (f32[1,1,2,4,2,16,256]{6,5,4,3,2,1,0:T(8,128)S(1)}, f32[1,1,2,4,2,16,256]{6,5,4,3,2,1,0:T(8,128)S(1)}, u32[]{:S(2)}, u32[]{:S(2)}) collective-permute-start(f32[1,1,2,4,2,16,256]{6,5,4,3,2,1,0:T(8,128)S(1)} %get-tuple-element.36), channel_id=1, source_target_pairs={{0,4},{1,5},{2,6},{3,7},{4,0},{5,1},{6,2},{7,3},{8,12},{9,13},{10,... | collective-permute-start | bytes 786440 | tf_op jit(solution)/shard_map/data_term/ppermute | solution.py:470
  71.4 9.5 %collective-permute-start.1 = (f32[8,2,2,16,128]{4,3,2,1,0:T(8,128)S(1)}, f32[8,2,2,16,128]{4,3,2,1,0:T(8,128)S(1)}, u32[]{:S(2)}, u32[]{:S(2)}) collective-permute-start(f32[8,2,2,16,128]{4,3,2,1,0:T(8,128)S(1)} %slice.4), channel_id=1, source_target_pairs={{0,2},{1,3},{2,0},{3,1},{4,6},{5,7},{6,4},{7,5},{8,10},{9,11},{10,... | collective-permute-start | bytes 786440 | tf_op jit(solution)/shard_map/column_maps/ppermute | solution.py:470
  72.5 14.0 %collective-permute-start.8 = (f32[1,1,1,4,2,16,256]{6,5,4,3,2,1,0:T(8,128)S(1)}, f32[1,1,1,4,2,16,256]{6,5,4,3,2,1,0:T(8,128)S(1)}, u32[]{:S(2)}, u32[]{:S(2)}) collective-permute-start(f32[1,1,1,4,2,16,256]{6,5,4,3,2,1,0:T(8,128)S(1)} %get-tuple-element.42.refs_0_), channel_id=1, source_target_pairs={{0,8},{1,9},{2,10},{3,11},{4,12},{5,13},{6,14},{7,15},{8,0},{9,1},... | collective-permute-start | bytes 393224 | tf_op jit(solution)/shard_map/data_term/ppermute | solution.py:470
  79.8 7.3 %collective-permute-start.9 = (f32[1,1,1,4,2,16,256]{6,5,4,3,2,1,0:T(8,128)S(1)}, f32[1,1,1,4,2,16,256]{6,5,4,3,2,1,0:T(8,128)S(1)}, u32[]{:S(2)}, u32[]{:S(2)}) collective-permute-start(f32[1,1,1,4,2,16,256]{6,5,4,3,2,1,0:T(8,128)S(1)} %get-tuple-element.40.refs_1_), channel_id=1, source_target_pairs={{0,8},{1,9},{2,10},{3,11},{4,12},{5,13},{6,14},{7,15},{8,0},{9,1},... | collective-permute-start | bytes 393224 | tf_op jit(solution)/shard_map/data_term/ppermute | solution.py:470
